TPU v7x, 32 devices: a whole 2x2x4 slice. The times are simulated.
32 devices in a mesh: section: 4 (over z), neuron: 8 (over y, x, core).
Axes of the slice: x: 2, y: 2, z: 4, core: 2. Of those that a mesh axis runs over, the one named last changes fastest.
Arguments:
- inputs: bfloat16 [2, 256, 16384], P(None, None, 'neuron'), may hold values from -6 to 6
- weights: bfloat16 [8, 128, 3, 128, 128], P('section', 'neuron'), may hold values from -0.4375 to 0.4375
- bias: bfloat16 [8, 16384], P('section', 'neuron'), may hold values from -0.19921875 to 0.19921875
- offsets: int32 [8, 3], P('section'), may hold values from -3 to 3, as said below
Outputs:
- outputs: bfloat16 [2, 256, 16384], P(None, 'section', 'neuron')
Inputs may be any that keep to these rules, and one draw needn't show every extreme that they name: `offsets`: band 0 has offset 0; band 1 lies in 1 .. 3 and band 2 in -3 .. -1; some layer has 3 in band 1 and some layer -3 in band 2.
All inputs are finite; a program needn't handle non-finite values.
Results may differ from a plain program's by a relative error of at most 0.029.
Values may be sent and summed in bfloat16 or wider, within the bound.
No kernel may reach another device: no remote copies, remote signals or barrier semaphores. Data moves between devices by JAX's collectives and lax.ppermute only.
A program may use at most 128 MiB of HBM per device.

v0:
```python
import jax
import jax.numpy as jnp
from jax import lax
from jax.sharding import PartitionSpec as P

HALO = 3


ceiling = 2.0


def padded(block, sides, width):
    for axis, dim in sides:
        count = lax.axis_size(axis)
        forward = [(i, i + 1) for i in range(count - 1)]
        forward.append((count - 1, 0))
        backward = [(target, source) for source, target in forward]
        low = lax.ppermute(
            lax.slice_in_dim(block, block.shape[dim] - width, None, axis=dim), axis, forward
        )
        high = lax.ppermute(lax.slice_in_dim(block, 0, width, axis=dim), axis, backward)
        block = jnp.concatenate([low, block, high], axis=dim)
    return block


def from_behind(value, axis, steps):
    count = lax.axis_size(axis)
    first, last = (max(0, -steps), min(count, count - steps))
    return lax.ppermute(value, axis, [(source, source + steps) for source in range(first, last)])


def spread(value, axis, source):
    kept = jnp.where(lax.axis_index(axis) == source, value, 0).astype(value.dtype)
    return lax.psum(kept, axis)


def shards(inputs, weights, bias, offsets):
    sections = lax.axis_size("section")
    section_index = lax.axis_index("section")
    micro_count, row_count, local_width = inputs.shape
    layer_count, block_count, band_count, block_size = (
        weights.shape[0],
        weights.shape[1],
        weights.shape[2],
        weights.shape[3],
    )
    packed = jnp.concatenate(
        [
            weights.reshape(layer_count, block_count, band_count * block_size, block_size),
            bias.reshape(layer_count, block_count, 1, block_size),
        ],
        axis=2,
    )
    table_edge = (packed.shape[1] - block_count) // 2

    def apply_layer(extended, table, layer_offsets, layer, margin):
        rows_here = extended.shape[0]
        out_blocks = block_count + 2 * margin
        first = table_edge - margin
        layer_weights = table[layer, first : first + out_blocks]
        summed = jnp.zeros((rows_here, out_blocks, block_size), jnp.float32)
        for band_index in range(band_count):
            start_col = (HALO + layer_offsets[layer, band_index]) * block_size
            shifted = lax.dynamic_slice_in_dim(
                extended, start_col, out_blocks * block_size, 1
            ).reshape(rows_here, out_blocks, block_size)
            block_weights = layer_weights[
                :, band_index * block_size : (band_index + 1) * block_size
            ]
            summed = summed + jnp.einsum(
                "rjk,jkn->rjn", shifted, block_weights, preferred_element_type=jnp.float32
            )
        bias_rows = layer_weights[:, band_count * block_size].astype(jnp.float32)
        preact = summed + bias_rows[None]
        return (
            jnp.clip(preact, 0.0, ceiling)
            .astype(jnp.bfloat16)
            .reshape(rows_here, out_blocks * block_size)
        )

    def run_section(current, table, layer_offsets):
        for layer in range(layer_count):
            extended = padded(current, (("neuron", 1),), HALO * block_size)
            current = apply_layer(extended, table, layer_offsets, layer, 0)
        return current

    share_rows = row_count // sections

    def advance(step_index, carry):
        incoming, finished_rows = carry
        arriving = lax.dynamic_index_in_dim(
            inputs, jnp.minimum(step_index, micro_count - 1), 0, keepdims=False
        )
        current = jnp.where(section_index == 0, arriving, incoming)
        produced = run_section(current, packed, offsets)
        slot_index = jnp.clip(step_index - (sections - 1), 0, micro_count - 1)
        finished = jnp.logical_and(section_index == sections - 1, step_index >= sections - 1)
        previous = lax.dynamic_index_in_dim(finished_rows, slot_index, 0, keepdims=False)
        finished_rows = lax.dynamic_update_index_in_dim(
            finished_rows, jnp.where(finished, produced, previous), slot_index, 0
        )
        incoming = from_behind(produced, "section", 1)
        return (incoming, finished_rows)

    initial = (
        jnp.zeros((row_count, local_width), jnp.bfloat16),
        jnp.zeros((micro_count, row_count, local_width), jnp.bfloat16),
    )
    incoming, finished_rows = lax.fori_loop(0, micro_count + sections - 1, advance, initial)
    everything = spread(finished_rows, "section", sections - 1)
    return lax.dynamic_slice_in_dim(everything, section_index * share_rows, share_rows, 1)


def solution(mesh):
    in_specs = (
        P(None, None, "neuron"),
        P("section", "neuron", None, None, None),
        P("section", "neuron"),
        P("section", None),
    )
    out_specs = P(None, "section", "neuron")
    return jax.shard_map(shards, mesh=mesh, in_specs=in_specs, out_specs=out_specs, check_vma=False)
```

profile of v0, /device:TPU:16, one launch (start us, length us, event | category | flops | bytes accessed | tf_op | source)
XLA Modules:
  0.0 369.6 jit_solution(7111104696531133256)
XLA Ops:
  12.7 2.2 pad_maximum_fusion.2
  14.9 5.1 %copy.18 = bf16[2,16,385,128]{2,3,1,0:T(8,128)(2,1)} copy(bf16[2,16,385,128]{3,2,1,0:T(8,128)(2,1)S(1)} %pad_maximum_fusion.2) | data formatting | bytes 6307840 | tf_op jit(solution)/shard_map/while | solution.py:109
  20.0 1.6 broadcast_in_dim.19.clone2
  22.6 246.7 %while.17 = (s32[]{:T(128)}, bf16[256,2048]{0,1:T(8,128)(2,1)}, bf16[2,256,2048]{2,1,0:T(8,128)(2,1)}, pred[]{:T(512)}, bf16[2,256,2048]{2,1,0:T(8,128)(2,1)}, /...) while((s32[]{:T(128)}, bf16[256,2048]{0,1:T(8,128)(2,1)}, ...), condition=%wide.region_1.2_spmd, body=%wide.region_0.1_spmd.sunk | while | flops 820252672 | bytes 80798200 | solution.py:109
  22.6 1.7 constant_dynamic-slice_fusion.12
  26.2 1.9 collective-permute-start
  28.2 2.5 slice_bitcast_fusion.3
  32.6 1.9 collective-permute-done.1
  37.2 4.2 %collective-permute-done.2 = bf16[256,384]{0,1:T(8,128)(2,1)S(1)} collective-permute-done((bf16[256,384]{0,1:T(8,128)(2,1)S(1)}, bf16[256,384]{0,1:T(8,128)(2,1)S(1)}, u32[]{:S(2)}, u32[]{:S(2)}) %collective-permute-start.2) | collective-permute-done | bytes 196640 | tf_op jit(solution)/shard_map/while/body/eval_jaxpr/ppermute | solution.py:21
  41.4 2.0 collective-permute-done.3
  44.6 1.6 clamp_convert_fusion.5
  46.2 3.5 collective-permute-start.4
  52.1 18.4 %collective-permute-done.4 = bf16[256,2048]{0,1:T(8,128)(2,1)} collective-permute-done((bf16[256,2048]{0,1:T(8,128)(2,1)}, bf16[256,2048]{0,1:T(8,128)(2,1)}, u32[]{:S(2)}, u32[]{:S(2)}) %collective-permute-start.4) | collective-permute-done | bytes 1048608 | tf_op jit(solution)/shard_map/while/body/eval_jaxpr/ppermute | solution.py:29
  70.5 1.7 constant_dynamic-slice_fusion.12
  74.1 3.4 collective-permute-start
  77.4 2.5 slice_bitcast_fusion.3
  81.3 2.8 collective-permute-done.1
  86.4 4.6 %collective-permute-done.2 = bf16[256,384]{0,1:T(8,128)(2,1)S(1)} collective-permute-done((bf16[256,384]{0,1:T(8,128)(2,1)S(1)}, bf16[256,384]{0,1:T(8,128)(2,1)S(1)}, u32[]{:S(2)}, u32[]{:S(2)}) %collective-permute-start.2) | collective-permute-done | bytes 196640 | tf_op jit(solution)/shard_map/while/body/eval_jaxpr/ppermute | solution.py:21
  91.0 2.1 collective-permute-done.3
  94.3 1.6 clamp_convert_fusion.5
  95.9 3.5 collective-permute-start.4
  101.7 19.2 %collective-permute-done.4 = bf16[256,2048]{0,1:T(8,128)(2,1)} collective-permute-done((bf16[256,2048]{0,1:T(8,128)(2,1)}, bf16[256,2048]{0,1:T(8,128)(2,1)}, u32[]{:S(2)}, u32[]{:S(2)}) %collective-permute-start.4) | collective-permute-done | bytes 1048608 | tf_op jit(solution)/shard_map/while/body/eval_jaxpr/ppermute | solution.py:29
  120.9 1.7 constant_dynamic-slice_fusion.12
  124.5 2.5 collective-permute-start
  127.0 2.5 slice_bitcast_fusion.3
  129.9 2.3 collective-permute-done
  136.8 4.6 %collective-permute-done.2 = bf16[256,384]{0,1:T(8,128)(2,1)S(1)} collective-permute-done((bf16[256,384]{0,1:T(8,128)(2,1)S(1)}, bf16[256,384]{0,1:T(8,128)(2,1)S(1)}, u32[]{:S(2)}, u32[]{:S(2)}) %collective-permute-start.2) | collective-permute-done | bytes 196640 | tf_op jit(solution)/shard_map/while/body/eval_jaxpr/ppermute | solution.py:21
  145.6 3.4 collective-permute-start.4
  151.4 19.5 %collective-permute-done.4 = bf16[256,2048]{0,1:T(8,128)(2,1)} collective-permute-done((bf16[256,2048]{0,1:T(8,128)(2,1)}, bf16[256,2048]{0,1:T(8,128)(2,1)}, u32[]{:S(2)}, u32[]{:S(2)}) %collective-permute-start.4) | collective-permute-done | bytes 1048608 | tf_op jit(solution)/shard_map/while/body/eval_jaxpr/ppermute | solution.py:29
  170.9 1.7 constant_dynamic-slice_fusion.12
  174.5 2.0 collective-permute-start
  176.4 2.5 slice_bitcast_fusion.3
  179.3 2.1 collective-permute-done
  184.2 1.9 collective-permute-start.2
  186.1 4.7 %collective-permute-done.2 = bf16[256,384]{0,1:T(8,128)(2,1)S(1)} collective-permute-done((bf16[256,384]{0,1:T(8,128)(2,1)S(1)}, bf16[256,384]{0,1:T(8,128)(2,1)S(1)}, u32[]{:S(2)}, u32[]{:S(2)}) %collective-permute-start.2) | collective-permute-done | bytes 196640 | tf_op jit(solution)/shard_map/while/body/eval_jaxpr/ppermute | solution.py:21
  193.2 1.6 clamp_convert_fusion.5
  194.8 3.6 collective-permute-start.4
  200.7 20.0 %collective-permute-done.4 = bf16[256,2048]{0,1:T(8,128)(2,1)} collective-permute-done((bf16[256,2048]{0,1:T(8,128)(2,1)}, bf16[256,2048]{0,1:T(8,128)(2,1)}, u32[]{:S(2)}, u32[]{:S(2)}) %collective-permute-start.4) | collective-permute-done | bytes 1048608 | tf_op jit(solution)/shard_map/while/body/eval_jaxpr/ppermute | solution.py:29
  220.7 1.7 constant_dynamic-slice_fusion.12
  224.3 3.0 collective-permute-start
  227.3 2.5 slice_bitcast_fusion.3
  231.6 1.9 collective-permute-done.1
  236.2 4.2 %collective-permute-done.2 = bf16[256,384]{0,1:T(8,128)(2,1)S(1)} collective-permute-done((bf16[256,384]{0,1:T(8,128)(2,1)S(1)}, bf16[256,384]{0,1:T(8,128)(2,1)S(1)}, u32[]{:S(2)}, u32[]{:S(2)}) %collective-permute-start.2) | collective-permute-done | bytes 196640 | tf_op jit(solution)/shard_map/while/body/eval_jaxpr/ppermute | solution.py:21
  240.4 1.8 collective-permute-done.3
  244.9 3.5 collective-permute-start.4
  250.9 18.5 %collective-permute-done.4 = bf16[256,2048]{0,1:T(8,128)(2,1)} collective-permute-done((bf16[256,2048]{0,1:T(8,128)(2,1)}, bf16[256,2048]{0,1:T(8,128)(2,1)}, u32[]{:S(2)}, u32[]{:S(2)}) %collective-permute-start.4) | collective-permute-done | bytes 1048608 | tf_op jit(solution)/shard_map/while/body/eval_jaxpr/ppermute | solution.py:29
  270.9 90.0 %all-reduce.2.cloned.1.call-done = bf16[2,256,2048]{2,1,0:T(8,128)(2,1)} async-done(((bf16[2,256,2048]{2,1,0:T(8,128)(2,1)}), bf16[2,256,2048]{2,1,0:T(8,128)(2,1)}) %all-reduce.2.cloned.1.call-update) | async-done | bytes 2097168 | tf_op jit(solution)/shard_map/psum | solution.py:34
  360.9 1.9 constant_dynamic-slice_fusion.8
  (119 shorter events, 58.3 us)
Async XLA Ops:
  6.5 354.4 %all-reduce.2.cloned.1.call-start = ((), (), s32[]{:S(2)}) async-start(), calls=%async_computation | async-start | bytes 4194304 | tf_op jit(solution)/shard_map/psum | solution.py:34
  26.2 6.3 %collective-permute-start = (bf16[256,384]{0,1:T(8,128)(2,1)S(1)}, bf16[256,384]{0,1:T(8,128)(2,1)S(1)}, u32[]{:S(2)}, u32[]{:S(2)}) collective-permute-start(bf16[256,384]{0,1:T(8,128)(2,1)S(1)} %get-tuple-element.410), channel_id=1, source_target_pairs={{1,0},{2,1},{3,2},{4,3},{5,4},{6,5},{7,6},{0,7},{9,8},{10,9},{11,1... | collective-permute-start | bytes 589832 | tf_op jit(solution)/shard_map/while/body/eval_jaxpr/ppermute | solution.py:21
  28.2 6.3 %collective-permute-start.1 = (bf16[256,384]{0,1:T(8,128)(2,1)S(1)}, bf16[256,384]{0,1:T(8,128)(2,1)S(1)}, u32[]{:S(2)}, u32[]{:S(2)}) collective-permute-start(bf16[256,384]{0,1:T(8,128)(2,1)S(1)} %get-tuple-element.411), channel_id=1, source_target_pairs={{0,1},{1,2},{2,3},{3,4},{4,5},{5,6},{6,7},{7,0},{8,9},{9,10},{10,1... | collective-permute-start | bytes 589832 | tf_op jit(solution)/shard_map/while/body/eval_jaxpr/ppermute | solution.py:18
  36.3 5.2 %collective-permute-start.2 = (bf16[256,384]{0,1:T(8,128)(2,1)S(1)}, bf16[256,384]{0,1:T(8,128)(2,1)S(1)}, u32[]{:S(2)}, u32[]{:S(2)}) collective-permute-start(bf16[256,384]{0,1:T(8,128)(2,1)S(1)} %get-tuple-element.418), channel_id=1, source_target_pairs={{1,0},{2,1},{3,2},{4,3},{5,4},{6,5},{7,6},{0,7},{9,8},{10,9},{11,1... | collective-permute-start | bytes 589832 | tf_op jit(solution)/shard_map/while/body/eval_jaxpr/ppermute | solution.py:21
  37.2 6.3 %collective-permute-start.3 = (bf16[256,384]{0,1:T(8,128)(2,1)S(1)}, bf16[256,384]{0,1:T(8,128)(2,1)S(1)}, u32[]{:S(2)}, u32[]{:S(2)}) collective-permute-start(bf16[256,384]{0,1:T(8,128)(2,1)S(1)} %get-tuple-element.419), channel_id=1, source_target_pairs={{0,1},{1,2},{2,3},{3,4},{4,5},{5,6},{6,7},{7,0},{8,9},{9,10},{10,1... | collective-permute-start | bytes 589832 | tf_op jit(solution)/shard_map/while/body/eval_jaxpr/ppermute | solution.py:18
  46.2 24.3 %collective-permute-start.4 = (bf16[256,2048]{0,1:T(8,128)(2,1)}, bf16[256,2048]{0,1:T(8,128)(2,1)}, u32[]{:S(2)}, u32[]{:S(2)}) collective-permute-start(bf16[256,2048]{0,1:T(8,128)(2,1)} %bitcast.67), channel_id=1, source_target_pairs={{0,8},{8,16},{16,24},{1,9},{9,17},{17,25},{2,10},{10,18},{18,26},{... | collective-permute-start | bytes 3145736 | tf_op jit(solution)/shard_map/while/body/eval_jaxpr/ppermute | solution.py:29
  74.1 7.2 %collective-permute-start = (bf16[256,384]{0,1:T(8,128)(2,1)S(1)}, bf16[256,384]{0,1:T(8,128)(2,1)S(1)}, u32[]{:S(2)}, u32[]{:S(2)}) collective-permute-start(bf16[256,384]{0,1:T(8,128)(2,1)S(1)} %get-tuple-element.410), channel_id=1, source_target_pairs={{1,0},{2,1},{3,2},{4,3},{5,4},{6,5},{7,6},{0,7},{9,8},{10,9},{11,1... | collective-permute-start | bytes 589832 | tf_op jit(solution)/shard_map/while/body/eval_jaxpr/ppermute | solution.py:21
  77.4 6.6 %collective-permute-start.1 = (bf16[256,384]{0,1:T(8,128)(2,1)S(1)}, bf16[256,384]{0,1:T(8,128)(2,1)S(1)}, u32[]{:S(2)}, u32[]{:S(2)}) collective-permute-start(bf16[256,384]{0,1:T(8,128)(2,1)S(1)} %get-tuple-element.411), channel_id=1, source_target_pairs={{0,1},{1,2},{2,3},{3,4},{4,5},{5,6},{6,7},{7,0},{8,9},{9,10},{10,1... | collective-permute-start | bytes 589832 | tf_op jit(solution)/shard_map/while/body/eval_jaxpr/ppermute | solution.py:18
  85.8 5.2 %collective-permute-start.2 = (bf16[256,384]{0,1:T(8,128)(2,1)S(1)}, bf16[256,384]{0,1:T(8,128)(2,1)S(1)}, u32[]{:S(2)}, u32[]{:S(2)}) collective-permute-start(bf16[256,384]{0,1:T(8,128)(2,1)S(1)} %get-tuple-element.418), channel_id=1, source_target_pairs={{1,0},{2,1},{3,2},{4,3},{5,4},{6,5},{7,6},{0,7},{9,8},{10,9},{11,1... | collective-permute-start | bytes 589832 | tf_op jit(solution)/shard_map/while/body/eval_jaxpr/ppermute | solution.py:21
  85.9 7.2 %collective-permute-start.3 = (bf16[256,384]{0,1:T(8,128)(2,1)S(1)}, bf16[256,384]{0,1:T(8,128)(2,1)S(1)}, u32[]{:S(2)}, u32[]{:S(2)}) collective-permute-start(bf16[256,384]{0,1:T(8,128)(2,1)S(1)} %get-tuple-element.419), channel_id=1, source_target_pairs={{0,1},{1,2},{2,3},{3,4},{4,5},{5,6},{6,7},{7,0},{8,9},{9,10},{10,1... | collective-permute-start | bytes 589832 | tf_op jit(solution)/shard_map/while/body/eval_jaxpr/ppermute | solution.py:18
  95.9 25.0 %collective-permute-start.4 = (bf16[256,2048]{0,1:T(8,128)(2,1)}, bf16[256,2048]{0,1:T(8,128)(2,1)}, u32[]{:S(2)}, u32[]{:S(2)}) collective-permute-start(bf16[256,2048]{0,1:T(8,128)(2,1)} %bitcast.67), channel_id=1, source_target_pairs={{0,8},{8,16},{16,24},{1,9},{9,17},{17,25},{2,10},{10,18},{18,26},{... | collective-permute-start | bytes 3145736 | tf_op jit(solution)/shard_map/while/body/eval_jaxpr/ppermute | solution.py:29
  124.5 7.7 %collective-permute-start = (bf16[256,384]{0,1:T(8,128)(2,1)S(1)}, bf16[256,384]{0,1:T(8,128)(2,1)S(1)}, u32[]{:S(2)}, u32[]{:S(2)}) collective-permute-start(bf16[256,384]{0,1:T(8,128)(2,1)S(1)} %get-tuple-element.410), channel_id=1, source_target_pairs={{1,0},{2,1},{3,2},{4,3},{5,4},{6,5},{7,6},{0,7},{9,8},{10,9},{11,1... | collective-permute-start | bytes 589832 | tf_op jit(solution)/shard_map/while/body/eval_jaxpr/ppermute | solution.py:21
  127.0 6.6 %collective-permute-start.1 = (bf16[256,384]{0,1:T(8,128)(2,1)S(1)}, bf16[256,384]{0,1:T(8,128)(2,1)S(1)}, u32[]{:S(2)}, u32[]{:S(2)}) collective-permute-start(bf16[256,384]{0,1:T(8,128)(2,1)S(1)} %get-tuple-element.411), channel_id=1, source_target_pairs={{0,1},{1,2},{2,3},{3,4},{4,5},{5,6},{6,7},{7,0},{8,9},{9,10},{10,1... | collective-permute-start | bytes 589832 | tf_op jit(solution)/shard_map/while/body/eval_jaxpr/ppermute | solution.py:18
  135.4 6.0 %collective-permute-start.2 = (bf16[256,384]{0,1:T(8,128)(2,1)S(1)}, bf16[256,384]{0,1:T(8,128)(2,1)S(1)}, u32[]{:S(2)}, u32[]{:S(2)}) collective-permute-start(bf16[256,384]{0,1:T(8,128)(2,1)S(1)} %get-tuple-element.418), channel_id=1, source_target_pairs={{1,0},{2,1},{3,2},{4,3},{5,4},{6,5},{7,6},{0,7},{9,8},{10,9},{11,1... | collective-permute-start | bytes 589832 | tf_op jit(solution)/shard_map/while/body/eval_jaxpr/ppermute | solution.py:21
  136.8 6.0 %collective-permute-start.3 = (bf16[256,384]{0,1:T(8,128)(2,1)S(1)}, bf16[256,384]{0,1:T(8,128)(2,1)S(1)}, u32[]{:S(2)}, u32[]{:S(2)}) collective-permute-start(bf16[256,384]{0,1:T(8,128)(2,1)S(1)} %get-tuple-element.419), channel_id=1, source_target_pairs={{0,1},{1,2},{2,3},{3,4},{4,5},{5,6},{6,7},{7,0},{8,9},{9,10},{10,1... | collective-permute-start | bytes 589832 | tf_op jit(solution)/shard_map/while/body/eval_jaxpr/ppermute | solution.py:18
  145.6 25.3 %collective-permute-start.4 = (bf16[256,2048]{0,1:T(8,128)(2,1)}, bf16[256,2048]{0,1:T(8,128)(2,1)}, u32[]{:S(2)}, u32[]{:S(2)}) collective-permute-start(bf16[256,2048]{0,1:T(8,128)(2,1)} %bitcast.67), channel_id=1, source_target_pairs={{0,8},{8,16},{16,24},{1,9},{9,17},{17,25},{2,10},{10,18},{18,26},{... | collective-permute-start | bytes 3145736 | tf_op jit(solution)/shard_map/while/body/eval_jaxpr/ppermute | solution.py:29
  174.5 7.0 %collective-permute-start = (bf16[256,384]{0,1:T(8,128)(2,1)S(1)}, bf16[256,384]{0,1:T(8,128)(2,1)S(1)}, u32[]{:S(2)}, u32[]{:S(2)}) collective-permute-start(bf16[256,384]{0,1:T(8,128)(2,1)S(1)} %get-tuple-element.410), channel_id=1, source_target_pairs={{1,0},{2,1},{3,2},{4,3},{5,4},{6,5},{7,6},{0,7},{9,8},{10,9},{11,1... | collective-permute-start | bytes 589832 | tf_op jit(solution)/shard_map/while/body/eval_jaxpr/ppermute | solution.py:21
  176.4 6.0 %collective-permute-start.1 = (bf16[256,384]{0,1:T(8,128)(2,1)S(1)}, bf16[256,384]{0,1:T(8,128)(2,1)S(1)}, u32[]{:S(2)}, u32[]{:S(2)}) collective-permute-start(bf16[256,384]{0,1:T(8,128)(2,1)S(1)} %get-tuple-element.411), channel_id=1, source_target_pairs={{0,1},{1,2},{2,3},{3,4},{4,5},{5,6},{6,7},{7,0},{8,9},{9,10},{10,1... | collective-permute-start | bytes 589832 | tf_op jit(solution)/shard_map/while/body/eval_jaxpr/ppermute | solution.py:18
  184.2 6.6 %collective-permute-start.2 = (bf16[256,384]{0,1:T(8,128)(2,1)S(1)}, bf16[256,384]{0,1:T(8,128)(2,1)S(1)}, u32[]{:S(2)}, u32[]{:S(2)}) collective-permute-start(bf16[256,384]{0,1:T(8,128)(2,1)S(1)} %get-tuple-element.418), channel_id=1, source_target_pairs={{1,0},{2,1},{3,2},{4,3},{5,4},{6,5},{7,6},{0,7},{9,8},{10,9},{11,1... | collective-permute-start | bytes 589832 | tf_op jit(solution)/shard_map/while/body/eval_jaxpr/ppermute | solution.py:21
  186.1 6.0 %collective-permute-start.3 = (bf16[256,384]{0,1:T(8,128)(2,1)S(1)}, bf16[256,384]{0,1:T(8,128)(2,1)S(1)}, u32[]{:S(2)}, u32[]{:S(2)}) collective-permute-start(bf16[256,384]{0,1:T(8,128)(2,1)S(1)} %get-tuple-element.419), channel_id=1, source_target_pairs={{0,1},{1,2},{2,3},{3,4},{4,5},{5,6},{6,7},{7,0},{8,9},{9,10},{10,1... | collective-permute-start | bytes 589832 | tf_op jit(solution)/shard_map/while/body/eval_jaxpr/ppermute | solution.py:18
  194.8 25.9 %collective-permute-start.4 = (bf16[256,2048]{0,1:T(8,128)(2,1)}, bf16[256,2048]{0,1:T(8,128)(2,1)}, u32[]{:S(2)}, u32[]{:S(2)}) collective-permute-start(bf16[256,2048]{0,1:T(8,128)(2,1)} %bitcast.67), channel_id=1, source_target_pairs={{0,8},{8,16},{16,24},{1,9},{9,17},{17,25},{2,10},{10,18},{18,26},{... | collective-permute-start | bytes 3145736 | tf_op jit(solution)/shard_map/while/body/eval_jaxpr/ppermute | solution.py:29
  224.3 7.3 %collective-permute-start = (bf16[256,384]{0,1:T(8,128)(2,1)S(1)}, bf16[256,384]{0,1:T(8,128)(2,1)S(1)}, u32[]{:S(2)}, u32[]{:S(2)}) collective-permute-start(bf16[256,384]{0,1:T(8,128)(2,1)S(1)} %get-tuple-element.410), channel_id=1, source_target_pairs={{1,0},{2,1},{3,2},{4,3},{5,4},{6,5},{7,6},{0,7},{9,8},{10,9},{11,1... | collective-permute-start | bytes 589832 | tf_op jit(solution)/shard_map/while/body/eval_jaxpr/ppermute | solution.py:21
  227.3 6.1 %collective-permute-start.1 = (bf16[256,384]{0,1:T(8,128)(2,1)S(1)}, bf16[256,384]{0,1:T(8,128)(2,1)S(1)}, u32[]{:S(2)}, u32[]{:S(2)}) collective-permute-start(bf16[256,384]{0,1:T(8,128)(2,1)S(1)} %get-tuple-element.411), channel_id=1, source_target_pairs={{0,1},{1,2},{2,3},{3,4},{4,5},{5,6},{6,7},{7,0},{8,9},{9,10},{10,1... | collective-permute-start | bytes 589832 | tf_op jit(solution)/shard_map/while/body/eval_jaxpr/ppermute | solution.py:18
  235.2 5.2 %collective-permute-start.2 = (bf16[256,384]{0,1:T(8,128)(2,1)S(1)}, bf16[256,384]{0,1:T(8,128)(2,1)S(1)}, u32[]{:S(2)}, u32[]{:S(2)}) collective-permute-start(bf16[256,384]{0,1:T(8,128)(2,1)S(1)} %get-tuple-element.418), channel_id=1, source_target_pairs={{1,0},{2,1},{3,2},{4,3},{5,4},{6,5},{7,6},{0,7},{9,8},{10,9},{11,1... | collective-permute-start | bytes 589832 | tf_op jit(solution)/shard_map/while/body/eval_jaxpr/ppermute | solution.py:21
  236.2 6.0 %collective-permute-start.3 = (bf16[256,384]{0,1:T(8,128)(2,1)S(1)}, bf16[256,384]{0,1:T(8,128)(2,1)S(1)}, u32[]{:S(2)}, u32[]{:S(2)}) collective-permute-start(bf16[256,384]{0,1:T(8,128)(2,1)S(1)} %get-tuple-element.419), channel_id=1, source_target_pairs={{0,1},{1,2},{2,3},{3,4},{4,5},{5,6},{6,7},{7,0},{8,9},{9,10},{10,1... | collective-permute-start | bytes 589832 | tf_op jit(solution)/shard_map/while/body/eval_jaxpr/ppermute | solution.py:18
  244.9 24.4 %collective-permute-start.4 = (bf16[256,2048]{0,1:T(8,128)(2,1)}, bf16[256,2048]{0,1:T(8,128)(2,1)}, u32[]{:S(2)}, u32[]{:S(2)}) collective-permute-start(bf16[256,2048]{0,1:T(8,128)(2,1)} %bitcast.67), channel_id=1, source_target_pairs={{0,8},{8,16},{16,24},{1,9},{9,17},{17,25},{2,10},{10,18},{18,26},{... | collective-permute-start | bytes 3145736 | tf_op jit(solution)/shard_map/while/body/eval_jaxpr/ppermute | solution.py:29
Sparse Core Ops, SparseCore 0:
  271.0 89.8 all-reduce.1
where the time goes:
time: 373 us; the launch traced here: 370 us
  waiting for transfers between devices  234 us (63%)
  local copies, waits for them, and re-layouts  48.9 us (13%)
  starting transfers between devices  36.1 us (10%)
  matrix products  19.1 us (5%)
  between operations  17.3 us (5%)
  other arithmetic  13.7 us (4%)
    ppermute x5, waiting for transfers between devices, from_behind(): lax.ppermute(value, axis, [(source, source + steps) for source in range(f...  95.5 us
    psum x1, waiting for transfers between devices, spread(): return lax.psum(kept, axis)  90 us
    ppermute x10, waiting for transfers between devices, padded(): lax.ppermute(lax.slice_in_dim(block, 0, width, axis=dim), axis, backward)  30.7 us
    dot_general x30, matrix products, apply_layer(): jnp.einsum('rjk,jkn->rjn', shifted, block_weights, preferred_element_type...  19.1 us
    ppermute x10, starting transfers between devices, padded(): lax.ppermute(lax.slice_in_dim(block, 0, width, axis=dim), axis, backward)  18.1 us
    ppermute x10, waiting for transfers between devices, padded(): lax.ppermute(lax.slice_in_dim(block, block.shape[dim] - width, None, axis...  17.6 us
    ppermute x5, starting transfers between devices, from_behind(): lax.ppermute(value, axis, [(source, source + steps) for source in range(f...  17.5 us
    squeeze x5, local copies, waits for them, and re-layouts, apply_layer(): layer_weights = table[layer, first:first + out_blocks]  12.5 us
  transfers between devices with their start and end apart: 26, of which 26 were waited for; matrix products, arithmetic and copies ran while one was open for 7% of the time, Pallas kernels for 0%

commit v1 on v0

v1 whole, which is shorter than its diff:
```python
import jax
import jax.numpy as jnp
from jax import lax
from jax.experimental import pallas as pl
from jax.experimental.pallas import tpu as pltpu
from jax.sharding import PartitionSpec as P

HALO = 3
CEILING = 2.0
CHUNK_ROWS = 32
LAG = 3


def layers_kernel(sizes, step, chunks, *refs):
    layer_count, block_count, band_count, block, margin = sizes
    where_ref, offsets_ref, bias_ref, weights_ref = refs[:4]
    margin_refs = refs[4 : 4 + 2 * (layer_count - 1)]
    refs = refs[4 + 2 * (layer_count - 1) :]
    own_ref, own_before_ref, own_after_ref = refs[:3]
    before_ref, low_ref, mid_ref, high_ref, after_ref = refs[3:8]
    out_low_ref, out_mid_ref, out_high_ref, out_ref = refs[8:12]
    buffers = refs[12:]
    section = where_ref[0]
    chunk = step - LAG * section
    edge = margin * block
    width = block_count * block

    @pl.when(jnp.logical_and(chunk >= 0, chunk < chunks))
    def _():
        first = buffers[0]

        @pl.when(section == 0)
        def _():
            first[:, :edge] = own_before_ref[...]
            first[:, edge : edge + width] = own_ref[0]
            first[:, edge + width :] = own_after_ref[...]

        @pl.when(section != 0)
        def _():
            first[:, :edge] = before_ref[...]
            first[:, edge : 2 * edge] = low_ref[...]
            first[:, 2 * edge : width] = mid_ref[...]
            first[:, width : edge + width] = high_ref[...]
            first[:, edge + width :] = after_ref[...]

        bias = bias_ref[...].astype(jnp.float32)
        for layer in range(layer_count):
            side = (layer_count - 1 - layer) * HALO
            source = buffers[layer]
            shift = [offsets_ref[layer, band] for band in range(band_count)]
            for j in range(block_count + 2 * side):
                own = j - side
                x = jnp.concatenate(
                    [
                        source[:, pl.ds(pl.multiple_of((j + HALO + s) * block, block), block)]
                        for s in shift
                    ],
                    axis=1,
                )
                depth = band_count * block
                if own < 0 or own >= block_count:
                    table = margin_refs[2 * layer + (own >= block_count)]
                    k = j if own < 0 else own - block_count
                    w = table[k * depth : (k + 1) * depth]
                    b = table[side * depth : side * depth + 16].astype(jnp.float32)[k : k + 1]
                else:
                    w = weights_ref[layer, own].reshape(depth, block)
                    b = bias[layer : layer + 1, own * block : (own + 1) * block]
                y = jnp.dot(x, w, preferred_element_type=jnp.float32) + b
                y = jnp.clip(y, 0.0, CEILING).astype(jnp.bfloat16)
                if layer < layer_count - 1:
                    buffers[layer + 1][:, j * block : (j + 1) * block] = y
                else:
                    out_ref[:, j * block : (j + 1) * block] = y
                    if j < margin:
                        out_low_ref[:, j * block : (j + 1) * block] = y
                    elif j < block_count - margin:
                        out_mid_ref[:, (j - margin) * block : (j - margin + 1) * block] = y
                    else:
                        k = j - (block_count - margin)
                        out_high_ref[:, k * block : (k + 1) * block] = y


def shards(inputs, weights, bias, offsets):
    sections = lax.axis_size("section")
    neurons = lax.axis_size("neuron")
    both = ("section", "neuron")
    section = lax.axis_index("section")
    batches, rows, width = inputs.shape
    layer_count, block_count, band_count, block, _ = weights.shape
    margin = layer_count * HALO
    edge = margin * block
    share = rows // sections
    chunk_rows = min(CHUNK_ROWS, share)
    places = [
        (batch, target * share + part * chunk_rows)
        for target in range(sections)
        for batch in range(batches)
        for part in range(share // chunk_rows)
    ]
    chunks = len(places)
    per_section = chunks // sections

    def sideways(value, which, step):
        pairs = [
            (s * neurons + n, s * neurons + (n + step) % neurons)
            for s in which
            for n in range(neurons)
        ]
        return lax.ppermute(value, both, pairs)

    def active(step):
        return [s for s in range(sections) if 0 <= step - LAG * s < chunks]

    tables = []
    for layer in range(layer_count - 1):
        side = (layer_count - 1 - layer) * HALO
        for lo, hi, step in ((block_count - side, block_count, 1), (0, side, -1)):
            b = bias[layer, lo * block : hi * block].reshape(side, block)
            b = jnp.pad(b, ((0, 16 - side), (0, 0)))
            table = jnp.concatenate([weights[layer, lo:hi].reshape(-1, block), b], axis=0)
            tables.append(sideways(table, range(sections), step))

    def input_edges(picked):
        x = jnp.concatenate(
            [inputs[b, r : r + chunk_rows] for b, r in picked], axis=0
        )
        return (
            sideways(x[:, -edge:], [0], 1),
            sideways(x[:, :edge], [0], -1),
        )

    first_edges = input_edges(places[:1])
    rest_edges = input_edges(places[1:])

    where = section.astype(jnp.int32).reshape(1)
    sizes = (layer_count, block_count, band_count, block, margin)
    smem = pl.BlockSpec(memory_space=pltpu.SMEM)
    vmem = pl.BlockSpec(memory_space=pltpu.VMEM)
    bf16 = jnp.bfloat16
    inner = width - 2 * edge

    def run(step, edges, at, pieces):
        batch, row = places[min(step, chunks - 1)]
        row_block = row // chunk_rows
        in_specs = [smem, smem, vmem, vmem] + [vmem] * len(tables)
        in_specs.append(
            pl.BlockSpec((1, chunk_rows, width), lambda i: (batch, row_block, 0))
        )
        in_specs += [pl.BlockSpec((chunk_rows, edge), lambda i: (at, 0))] * 2
        in_specs += [vmem] * 5
        widths = (edge, inner, edge, width)
        scratch = [pltpu.VMEM((chunk_rows, width + 2 * edge), bf16)]
        for layer in range(1, layer_count):
            side = (layer_count - layer) * HALO
            scratch.append(pltpu.VMEM((chunk_rows, width + 2 * side * block), bf16))
        return pl.pallas_call(
            lambda *refs: layers_kernel(sizes, step, chunks, *refs),
            grid=(1,),
            in_specs=in_specs,
            out_specs=[vmem] * 4,
            out_shape=[jax.ShapeDtypeStruct((chunk_rows, w), bf16) for w in widths],
            scratch_shapes=scratch,
            compiler_params=pltpu.CompilerParams(vmem_limit_bytes=40 * 1024 * 1024),
        )(where, offsets, bias, weights, *tables, inputs, *edges, *pieces)

    zeros = [jnp.zeros((chunk_rows, w), bf16) for w in (edge, edge, inner, edge, edge)]
    hops = {}
    returned = []
    kept = []
    for step in range(chunks + LAG * (sections - 1)):
        if step < LAG:
            pieces = zeros
        else:
            low, mid, high = hops[step - LAG]
            which = [s for s in active(step) if s > 0]
            before = sideways(high, which, 1)
            after = sideways(low, which, -1)
            pieces = [before, low, mid, high, after]
        at = min(step, chunks - 1)
        edges, at = (first_edges, 0) if at == 0 else (rest_edges, at - 1)
        out_low, out_mid, out_high, out = run(step, edges, at, pieces)
        pairs = [
            (s * neurons + n, (s + 1) * neurons + n)
            for s in active(step)
            if s + 1 < sections
            for n in range(neurons)
        ]
        if pairs:
            hops[step] = [lax.ppermute(v, both, pairs) for v in (out_low, out_mid, out_high)]
        done = step - LAG * (sections - 1)
        if done >= 0:
            target = done // per_section
            if target == sections - 1:
                kept.append(out)
            else:
                back = [
                    ((sections - 1) * neurons + n, target * neurons + n) for n in range(neurons)
                ]
                returned.append(lax.ppermute(out, both, back))

    results = []
    for k in range(per_section):
        value = returned[k]
        for target in range(1, sections - 1):
            value = value + returned[target * per_section + k]
        results.append(jnp.where(section == sections - 1, kept[k], value))
    return jnp.concatenate(results, axis=0).reshape(batches, share, width)


def solution(mesh):
    in_specs = (
        P(None, None, "neuron"),
        P("section", "neuron", None, None, None),
        P("section", "neuron"),
        P("section", None),
    )
    out_specs = P(None, "section", "neuron")
    return jax.shard_map(shards, mesh=mesh, in_specs=in_specs, out_specs=out_specs, check_vma=False)
```

time: 373 us -> 472 us (1.27)
  starting transfers between devices: 36.1 us -> 393 us
  waiting for transfers between devices: 234 us -> 8.3 us
  Pallas kernels: 0 us -> 49.4 us
  local copies, waits for them, and re-layouts: 48.9 us -> 13.5 us
  matrix products: 19.1 us -> 0 us
  between operations: 17.3 us -> 2.3 us
  other arithmetic: 13.7 us -> 2.42 us
    ppermute x25 -> x128, starting transfers between devices: 36.1 us -> 393 us  [the longest x66 189 us: shards(): lax.ppermute(v, both, pairs)]
    ppermute x25 -> x128, waiting for transfers between devices: 144 us -> 8.3 us  [the longest x12 7.67 us: shards(): returned.append(lax.ppermute(out, both, back))]
    psum x1 -> x0, waiting for transfers between devices: 90 us -> none  [spread(): return lax.psum(kept, axis)]
    pallas_call x0 -> x25, Pallas kernels: none -> 49.4 us  [run(): pl.pallas_call(lambda *refs: layers_kernel(sizes, step, chunks, *refs), g...]
    dot_general x30 -> x0, matrix products: 19.1 us -> none  [apply_layer(): jnp.einsum('rjk,jkn->rjn', shifted, block_weights, preferred_element_type...]
    dynamic_slice x26 -> x0, local copies, waits for them, and re-layouts: 17.7 us -> none  [the longest x10 11 us: advance(): lax.dynamic_index_in_dim(finished_rows, slot_index, 0, keepdims=False)]
    squeeze x5 -> x1, local copies, waits for them, and re-layouts: 12.5 us -> 0.01 us  [input_edges(): inputs[b, r:r + chunk_rows]]
    unnamed x0 -> x90, local copies, waits for them, and re-layouts: none -> 9.57 us
  transfers between devices with their start and end apart: 26 -> 128, of which waited for: 26 -> 2; matrix products, arithmetic and copies ran while one was open for 7% -> 1% of each run, Pallas kernels for 0% -> 11%
where the time goes in v1:
time: 472 us; the launch traced here: 469 us
  starting transfers between devices  393 us (83%)
  Pallas kernels  49.4 us (10%)
  local copies, waits for them, and re-layouts  13.5 us (3%)
  waiting for transfers between devices  8.3 us (2%)
    ppermute x66, starting transfers between devices, shards(): lax.ppermute(v, both, pairs)  189 us
    ppermute x50, starting transfers between devices, sideways(): return lax.ppermute(value, both, pairs)  178 us
    pallas_call x25, Pallas kernels, run(): pl.pallas_call(lambda *refs: layers_kernel(sizes, step, chunks, *refs), g...  49.4 us
    ppermute x12, starting transfers between devices, shards(): returned.append(lax.ppermute(out, both, back))  26.1 us
    unnamed x90, local copies, waits for them, and re-layouts  9.57 us
  transfers between devices with their start and end apart: 128, of which 2 were waited for; matrix products, arithmetic and copies ran while one was open for 1% of the time, Pallas kernels for 11%

profile of v1, /device:TPU:16, one launch (start us, length us, event | category | flops | bytes accessed | tf_op | source)
XLA Modules:
  0.0 468.8 jit_solution(8833649734790724188)
XLA Ops:
  2.7 5.8 %collective-permute-start = (bf16[1168,128]{1,0:T(8,128)(2,1)}, bf16[1168,128]{1,0:T(8,128)(2,1)S(1)}, u32[]{:S(2)}, u32[]{:S(2)}) collective-permute-start(bf16[1168,128]{1,0:T(8,128)(2,1)} %fusion.2), channel_id=1, source_target_pairs={{0,1},{1,2},{2,3},{3,4},{4,5},{5,6},{6,7},{7,0},{8,9},{9,10},{10,1... | collective-permute-start | bytes 897032 | tf_op jit(solution)/shard_map/ppermute | solution.py:110
  9.3 5.7 %collective-permute-start.1 = (bf16[1168,128]{1,0:T(8,128)(2,1)}, bf16[1168,128]{1,0:T(8,128)(2,1)}, u32[]{:S(2)}, u32[]{:S(2)}) collective-permute-start(bf16[1168,128]{1,0:T(8,128)(2,1)} %fusion.3), channel_id=1, source_target_pairs={{0,7},{1,0},{2,1},{3,2},{4,3},{5,4},{6,5},{7,6},{8,15},{9,8},{10,9... | collective-permute-start | bytes 897032 | tf_op jit(solution)/shard_map/ppermute | solution.py:110
  18.3 7.2 %collective-permute-start.3 = (bf16[480,768]{1,0:T(8,128)(2,1)}, bf16[480,768]{1,0:T(8,128)(2,1)}, u32[]{:S(2)}, u32[]{:S(2)}) collective-permute-start(bf16[480,768]{1,0:T(8,128)(2,1)} %get-tuple-element.173), channel_id=1, source_target_pairs={{0,7},{1,0},{2,1},{3,2},{4,3},{5,4},{6,5},{7,6}} | collective-permute-start | bytes 2211848 | tf_op jit(solution)/shard_map/ppermute | solution.py:110
  26.8 9.6 %collective-permute-start.5 = (bf16[32,768]{1,0:T(8,128)(2,1)}, bf16[32,768]{1,0:T(8,128)(2,1)S(1)}, u32[]{:S(2)}, u32[]{:S(2)}) collective-permute-start(bf16[32,768]{1,0:T(8,128)(2,1)} %get-tuple-element.175), channel_id=1, source_target_pairs={{0,7},{1,0},{2,1},{3,2},{4,3},{5,4},{6,5},{7,6}} | collective-permute-start | bytes 147464 | tf_op jit(solution)/shard_map/ppermute | solution.py:110
  45.5 18.5 %collective-permute-start.44 = (bf16[32,768]{1,0:T(8,128)(2,1)S(1)}, bf16[32,768]{1,0:T(8,128)(2,1)S(1)}, u32[]{:S(2)}, u32[]{:S(2)}) collective-permute-start(bf16[32,768]{1,0:T(8,128)(2,1)S(1)} %get-tuple-element.111), channel_id=1, source_target_pairs={{0,8},{1,9},{2,10},{3,11},{4,12},{5,13},{6,14},{7,15}} | collective-permute-start | bytes 147464 | tf_op jit(solution)/shard_map/ppermute | solution.py:190
  66.3 7.2 %collective-permute-start.66 = (bf16[32,512]{1,0:T(8,128)(2,1)S(1)}, bf16[32,512]{1,0:T(8,128)(2,1)S(1)}, u32[]{:S(2)}, u32[]{:S(2)}) collective-permute-start(bf16[32,512]{1,0:T(8,128)(2,1)S(1)} %get-tuple-element.125), channel_id=1, source_target_pairs={{0,8},{1,9},{2,10},{3,11},{4,12},{5,13},{6,14},{7,15}} | collective-permute-start | bytes 98312 | tf_op jit(solution)/shard_map/ppermute | solution.py:190
  73.5 6.4 %collective-permute-start.63 = (bf16[32,768]{1,0:T(8,128)(2,1)S(1)}, bf16[32,768]{1,0:T(8,128)(2,1)S(1)}, u32[]{:S(2)}, u32[]{:S(2)}) collective-permute-start(bf16[32,768]{1,0:T(8,128)(2,1)S(1)} %get-tuple-element.123), channel_id=1, source_target_pairs={{0,8},{1,9},{2,10},{3,11},{4,12},{5,13},{6,14},{7,15}} | collective-permute-start | bytes 147464 | tf_op jit(solution)/shard_map/ppermute | solution.py:190
  86.2 11.5 %collective-permute-start.64 = (bf16[32,768]{1,0:T(8,128)(2,1)S(1)}, bf16[32,768]{1,0:T(8,128)(2,1)S(1)}, u32[]{:S(2)}, u32[]{:S(2)}) collective-permute-start(bf16[32,768]{1,0:T(8,128)(2,1)S(1)} %collective-permute-done.63.refs_12_), channel_id=1, source_target_pairs={{8,9},{9,10},{10,11},{11,12},{12,13},{13,14},{14,15},{15,8}} | collective-permute-start | bytes 147464 | tf_op jit(solution)/shard_map/ppermute | solution.py:110
  97.7 6.4 %collective-permute-start.67 = (bf16[32,768]{1,0:T(8,128)(2,1)S(1)}, bf16[32,768]{1,0:T(8,128)(2,1)S(1)}, u32[]{:S(2)}, u32[]{:S(2)}) collective-permute-start(bf16[32,768]{1,0:T(8,128)(2,1)S(1)} %collective-permute-done.65.refs_10_), channel_id=1, source_target_pairs={{8,15},{9,8},{10,9},{11,10},{12,11},{13,12},{14,13},{15,14}} | collective-permute-start | bytes 147464 | tf_op jit(solution)/shard_map/ppermute | solution.py:110
  106.2 4.4 collective-permute-start.15
  114.9 7.8 %collective-permute-start.49 = (bf16[32,768]{1,0:T(8,128)(2,1)S(1)}, bf16[32,768]{1,0:T(8,128)(2,1)S(1)}, u32[]{:S(2)}, u32[]{:S(2)}) collective-permute-start(bf16[32,768]{1,0:T(8,128)(2,1)S(1)} %get-tuple-element.114), channel_id=1, source_target_pairs={{0,8},{1,9},{2,10},{3,11},{4,12},{5,13},{6,14},{7,15},{8,16},{9,17... | collective-permute-start | bytes 147464 | tf_op jit(solution)/shard_map/ppermute | solution.py:190
  125.6 7.2 %collective-permute-start.71 = (bf16[32,512]{1,0:T(8,128)(2,1)S(1)}, bf16[32,512]{1,0:T(8,128)(2,1)S(1)}, u32[]{:S(2)}, u32[]{:S(2)}) collective-permute-start(bf16[32,512]{1,0:T(8,128)(2,1)S(1)} %get-tuple-element.128), channel_id=1, source_target_pairs={{0,8},{1,9},{2,10},{3,11},{4,12},{5,13},{6,14},{7,15},{8,16},{9,17... | collective-permute-start | bytes 98312 | tf_op jit(solution)/shard_map/ppermute | solution.py:190
  132.9 6.4 %collective-permute-start.68 = (bf16[32,768]{1,0:T(8,128)(2,1)S(1)}, bf16[32,768]{1,0:T(8,128)(2,1)S(1)}, u32[]{:S(2)}, u32[]{:S(2)}) collective-permute-start(bf16[32,768]{1,0:T(8,128)(2,1)S(1)} %get-tuple-element.126), channel_id=1, source_target_pairs={{0,8},{1,9},{2,10},{3,11},{4,12},{5,13},{6,14},{7,15},{8,16},{9,17... | collective-permute-start | bytes 147464 | tf_op jit(solution)/shard_map/ppermute | solution.py:190
  139.2 2.6 shard_map.48
  149.1 4.4 collective-permute-start.51
  153.5 6.3 %collective-permute-start.69 = (bf16[32,768]{1,0:T(8,128)(2,1)S(1)}, bf16[32,768]{1,0:T(8,128)(2,1)S(1)}, u32[]{:S(2)}, u32[]{:S(2)}) collective-permute-start(bf16[32,768]{1,0:T(8,128)(2,1)S(1)} %collective-permute-done.68.refs_12_), channel_id=1, source_target_pairs={{8,9},{9,10},{10,11},{11,12},{12,13},{13,14},{14,15},{15,8},{16,17... | collective-permute-start | bytes 147464 | tf_op jit(solution)/shard_map/ppermute | solution.py:110
  159.8 6.3 %collective-permute-start.72 = (bf16[32,768]{1,0:T(8,128)(2,1)S(1)}, bf16[32,768]{1,0:T(8,128)(2,1)S(1)}, u32[]{:S(2)}, u32[]{:S(2)}) collective-permute-start(bf16[32,768]{1,0:T(8,128)(2,1)S(1)} %collective-permute-done.70.refs_10_), channel_id=1, source_target_pairs={{8,15},{9,8},{10,9},{11,10},{12,11},{13,12},{14,13},{15,14},{16,23... | collective-permute-start | bytes 147464 | tf_op jit(solution)/shard_map/ppermute | solution.py:110
  168.3 4.4 collective-permute-start.20
  172.7 2.8 collective-permute-start.19
  175.5 2.6 shard_map.56
  180.0 2.6 shard_map.61
  190.3 2.2 collective-permute-start.54
  198.5 6.3 %collective-permute-start.74 = (bf16[32,768]{1,0:T(8,128)(2,1)S(1)}, bf16[32,768]{1,0:T(8,128)(2,1)S(1)}, u32[]{:S(2)}, u32[]{:S(2)}) collective-permute-start(bf16[32,768]{1,0:T(8,128)(2,1)S(1)} %collective-permute-done.73.refs_12_), channel_id=1, source_target_pairs={{8,9},{9,10},{10,11},{11,12},{12,13},{13,14},{14,15},{15,8},{16,17... | collective-permute-start | bytes 147464 | tf_op jit(solution)/shard_map/ppermute | solution.py:110
  204.8 7.0 %collective-permute-start.77 = (bf16[32,768]{1,0:T(8,128)(2,1)S(1)}, bf16[32,768]{1,0:T(8,128)(2,1)S(1)}, u32[]{:S(2)}, u32[]{:S(2)}) collective-permute-start(bf16[32,768]{1,0:T(8,128)(2,1)S(1)} %collective-permute-done.75.refs_10_), channel_id=1, source_target_pairs={{8,15},{9,8},{10,9},{11,10},{12,11},{13,12},{14,13},{15,14},{16,23... | collective-permute-start | bytes 147464 | tf_op jit(solution)/shard_map/ppermute | solution.py:110
  213.9 4.4 collective-permute-start.56
  220.3 4.5 collective-permute-start.25
  224.8 3.4 collective-permute-start.24
  249.0 8.1 %collective-permute-start.28 = (bf16[32,768]{1,0:T(8,128)(2,1)S(1)}, bf16[32,768]{1,0:T(8,128)(2,1)S(1)}, u32[]{:S(2)}, u32[]{:S(2)}) collective-permute-start(bf16[32,768]{1,0:T(8,128)(2,1)S(1)} %get-tuple-element.100), channel_id=1, source_target_pairs={{0,8},{1,9},{2,10},{3,11},{4,12},{5,13},{6,14},{7,15},{8,16},{9,17... | collective-permute-start | bytes 147464 | tf_op jit(solution)/shard_map/ppermute | solution.py:190
  259.1 4.5 collective-permute-start.82
  265.6 4.5 collective-permute-start.30
  272.1 4.5 collective-permute-start.61
  303.8 4.5 collective-permute-start.87
  312.4 4.5 collective-permute-start.35
  319.2 4.5 collective-permute-start.93
  325.7 7.0 %collective-permute-start.39 = (bf16[32,512]{1,0:T(8,128)(2,1)S(1)}, bf16[32,512]{1,0:T(8,128)(2,1)S(1)}, u32[]{:S(2)}, u32[]{:S(2)}) collective-permute-start(bf16[32,512]{1,0:T(8,128)(2,1)S(1)} %get-tuple-element.107), channel_id=1, source_target_pairs={{8,16},{9,17},{10,18},{11,19},{12,20},{13,21},{14,22},{15,23},{16,... | collective-permute-start | bytes 98312 | tf_op jit(solution)/shard_map/ppermute | solution.py:190
  343.1 5.7 %collective-permute-start.38 = (bf16[32,768]{1,0:T(8,128)(2,1)S(1)}, bf16[32,768]{1,0:T(8,128)(2,1)S(1)}, u32[]{:S(2)}, u32[]{:S(2)}) collective-permute-start(bf16[32,768]{1,0:T(8,128)(2,1)S(1)} %get-tuple-element.106), channel_id=1, source_target_pairs={{8,16},{9,17},{10,18},{11,19},{12,20},{13,21},{14,22},{15,23},{16,... | collective-permute-start | bytes 147464 | tf_op jit(solution)/shard_map/ppermute | solution.py:190
  349.4 2.8 collective-permute-start.94
  359.9 6.3 %collective-permute-start.95 = (bf16[32,768]{1,0:T(8,128)(2,1)S(1)}, bf16[32,768]{1,0:T(8,128)(2,1)S(1)}, u32[]{:S(2)}, u32[]{:S(2)}) collective-permute-start(bf16[32,768]{1,0:T(8,128)(2,1)S(1)} %collective-permute-done.94.refs_12_), channel_id=1, source_target_pairs={{16,17},{17,18},{18,19},{19,20},{20,21},{21,22},{22,23},{23,16},{2... | collective-permute-start | bytes 147464 | tf_op jit(solution)/shard_map/ppermute | solution.py:110
  368.9 4.1 collective-permute-start.98
  373.6 6.1 %collective-permute-start.40 = (bf16[32,768]{1,0:T(8,128)(2,1)S(1)}, bf16[32,768]{1,0:T(8,128)(2,1)S(1)}, u32[]{:S(2)}, u32[]{:S(2)}) collective-permute-start(bf16[32,768]{1,0:T(8,128)(2,1)S(1)} %collective-permute-done.38.refs_10_), channel_id=1, source_target_pairs={{16,23},{17,16},{18,17},{19,18},{20,19},{21,20},{22,21},{23,22},{2... | collective-permute-start | bytes 147464 | tf_op jit(solution)/shard_map/ppermute | solution.py:110
  381.8 4.4 collective-permute-start.111
  388.4 4.0 collective-permute-start.99
  395.6 2.6 shard_map.68
  398.9 5.8 %collective-permute-start.112 = (bf16[32,768]{1,0:T(8,128)(2,1)}, bf16[32,768]{1,0:T(8,128)(2,1)}, u32[]{:S(2)}, u32[]{:S(2)}) collective-permute-start(bf16[32,768]{1,0:T(8,128)(2,1)} %get-tuple-element.155), channel_id=1, source_target_pairs={{16,24},{17,25},{18,26},{19,27},{20,28},{21,29},{22,30},{23,31}} | collective-permute-start | bytes 147464 | tf_op jit(solution)/shard_map/ppermute | solution.py:190
  404.7 6.6 %collective-permute-start.114 = (bf16[32,768]{1,0:T(8,128)(2,1)}, bf16[32,768]{1,0:T(8,128)(2,1)}, u32[]{:S(2)}, u32[]{:S(2)}) collective-permute-start(bf16[32,768]{1,0:T(8,128)(2,1)} %get-tuple-element.156), channel_id=1, source_target_pairs={{16,24},{17,25},{18,26},{19,27},{20,28},{21,29},{22,30},{23,31}} | collective-permute-start | bytes 147464 | tf_op jit(solution)/shard_map/ppermute | solution.py:190
  414.5 6.7 %collective-permute-start.115 = (bf16[32,512]{1,0:T(8,128)(2,1)}, bf16[32,512]{1,0:T(8,128)(2,1)}, u32[]{:S(2)}, u32[]{:S(2)}) collective-permute-start(bf16[32,512]{1,0:T(8,128)(2,1)} %get-tuple-element.157), channel_id=1, source_target_pairs={{16,24},{17,25},{18,26},{19,27},{20,28},{21,29},{22,30},{23,31}} | collective-permute-start | bytes 98312 | tf_op jit(solution)/shard_map/ppermute | solution.py:190
  440.3 16.1 %collective-permute-start.125 = (bf16[32,2048]{1,0:T(8,128)(2,1)S(1)}, bf16[32,2048]{1,0:T(8,128)(2,1)S(1)}, u32[]{:S(2)}, u32[]{:S(2)}) collective-permute-start(bf16[32,2048]{1,0:T(8,128)(2,1)S(1)} %copy-done.17), channel_id=1, source_target_pairs={{24,0},{25,1},{26,2},{27,3},{28,4},{29,5},{30,6},{31,7}} | collective-permute-start | bytes 393224 | tf_op jit(solution)/shard_map/ppermute | solution.py:200
  460.3 7.6 %collective-permute-done.127 = bf16[32,2048]{1,0:T(8,128)(2,1)S(1)} collective-permute-done((bf16[32,2048]{1,0:T(8,128)(2,1)S(1)}, bf16[32,2048]{1,0:T(8,128)(2,1)S(1)}, u32[]{:S(2)}, u32[]{:S(2)}) %collective-permute-start.127) | collective-permute-done | bytes 131104 | tf_op jit(solution)/shard_map/ppermute | solution.py:200
  (338 shorter events, 181.4 us)
Async XLA Ops:
  2.7 33.7 %collective-permute-start = (bf16[1168,128]{1,0:T(8,128)(2,1)}, bf16[1168,128]{1,0:T(8,128)(2,1)S(1)}, u32[]{:S(2)}, u32[]{:S(2)}) collective-permute-start(bf16[1168,128]{1,0:T(8,128)(2,1)} %fusion.2), channel_id=1, source_target_pairs={{0,1},{1,2},{2,3},{3,4},{4,5},{5,6},{6,7},{7,0},{8,9},{9,10},{10,1... | collective-permute-start | bytes 897032 | tf_op jit(solution)/shard_map/ppermute | solution.py:110
  9.3 27.2 %collective-permute-start.1 = (bf16[1168,128]{1,0:T(8,128)(2,1)}, bf16[1168,128]{1,0:T(8,128)(2,1)}, u32[]{:S(2)}, u32[]{:S(2)}) collective-permute-start(bf16[1168,128]{1,0:T(8,128)(2,1)} %fusion.3), channel_id=1, source_target_pairs={{0,7},{1,0},{2,1},{3,2},{4,3},{5,4},{6,5},{7,6},{8,15},{9,8},{10,9... | collective-permute-start | bytes 897032 | tf_op jit(solution)/shard_map/ppermute | solution.py:110
  16.6 26.5 %collective-permute-start.2 = (bf16[480,768]{1,0:T(8,128)(2,1)}, bf16[480,768]{1,0:T(8,128)(2,1)}, u32[]{:S(2)}, u32[]{:S(2)}) collective-permute-start(bf16[480,768]{1,0:T(8,128)(2,1)} %get-tuple-element.174), channel_id=1, source_target_pairs={{0,1},{1,2},{2,3},{3,4},{4,5},{5,6},{6,7},{7,0}} | collective-permute-start | bytes 2211848 | tf_op jit(solution)/shard_map/ppermute | solution.py:110
  18.3 24.9 %collective-permute-start.3 = (bf16[480,768]{1,0:T(8,128)(2,1)}, bf16[480,768]{1,0:T(8,128)(2,1)}, u32[]{:S(2)}, u32[]{:S(2)}) collective-permute-start(bf16[480,768]{1,0:T(8,128)(2,1)} %get-tuple-element.173), channel_id=1, source_target_pairs={{0,7},{1,0},{2,1},{3,2},{4,3},{5,4},{6,5},{7,6}} | collective-permute-start | bytes 2211848 | tf_op jit(solution)/shard_map/ppermute | solution.py:110
  41.1 25.3 %collective-permute-start.10 = (bf16[32,768]{1,0:T(8,128)(2,1)S(1)}, bf16[32,768]{1,0:T(8,128)(2,1)S(1)}, u32[]{:S(2)}, u32[]{:S(2)}) collective-permute-start(bf16[32,768]{1,0:T(8,128)(2,1)S(1)} %collective-permute-done.8.refs_10_), channel_id=1, source_target_pairs={{8,15},{9,8},{10,9},{11,10},{12,11},{13,12},{14,13},{15,14}} | collective-permute-start | bytes 147464 | tf_op jit(solution)/shard_map/ppermute | solution.py:110
  41.8 31.8 %collective-permute-start.7 = (bf16[32,768]{1,0:T(8,128)(2,1)S(1)}, bf16[32,768]{1,0:T(8,128)(2,1)S(1)}, u32[]{:S(2)}, u32[]{:S(2)}) collective-permute-start(bf16[32,768]{1,0:T(8,128)(2,1)S(1)} %collective-permute-done.6.refs_12_), channel_id=1, source_target_pairs={{8,9},{9,10},{10,11},{11,12},{12,13},{13,14},{14,15},{15,8}} | collective-permute-start | bytes 147464 | tf_op jit(solution)/shard_map/ppermute | solution.py:110
  42.4 21.6 %collective-permute-start.9 = (bf16[32,512]{1,0:T(8,128)(2,1)S(1)}, bf16[32,512]{1,0:T(8,128)(2,1)S(1)}, u32[]{:S(2)}, u32[]{:S(2)}) collective-permute-start(bf16[32,512]{1,0:T(8,128)(2,1)S(1)} %get-tuple-element.89), channel_id=1, source_target_pairs={{0,8},{1,9},{2,10},{3,11},{4,12},{5,13},{6,14},{7,15}} | collective-permute-start | bytes 98312 | tf_op jit(solution)/shard_map/ppermute | solution.py:190
  44.8 38.7 %collective-permute-start.42 = (bf16[32,768]{1,0:T(8,128)(2,1)S(1)}, bf16[32,768]{1,0:T(8,128)(2,1)S(1)}, u32[]{:S(2)}, u32[]{:S(2)}) collective-permute-start(bf16[32,768]{1,0:T(8,128)(2,1)S(1)} %get-tuple-element.110), channel_id=1, source_target_pairs={{0,8},{1,9},{2,10},{3,11},{4,12},{5,13},{6,14},{7,15}} | collective-permute-start | bytes 147464 | tf_op jit(solution)/shard_map/ppermute | solution.py:190
  45.5 39.4 %collective-permute-start.44 = (bf16[32,768]{1,0:T(8,128)(2,1)S(1)}, bf16[32,768]{1,0:T(8,128)(2,1)S(1)}, u32[]{:S(2)}, u32[]{:S(2)}) collective-permute-start(bf16[32,768]{1,0:T(8,128)(2,1)S(1)} %get-tuple-element.111), channel_id=1, source_target_pairs={{0,8},{1,9},{2,10},{3,11},{4,12},{5,13},{6,14},{7,15}} | collective-permute-start | bytes 147464 | tf_op jit(solution)/shard_map/ppermute | solution.py:190
  83.5 20.6 %collective-permute-start.13 = (bf16[32,768]{1,0:T(8,128)(2,1)S(1)}, bf16[32,768]{1,0:T(8,128)(2,1)S(1)}, u32[]{:S(2)}, u32[]{:S(2)}) collective-permute-start(bf16[32,768]{1,0:T(8,128)(2,1)S(1)} %get-tuple-element.91), channel_id=1, source_target_pairs={{0,8},{1,9},{2,10},{3,11},{4,12},{5,13},{6,14},{7,15},{8,16},{9,17... | collective-permute-start | bytes 147464 | tf_op jit(solution)/shard_map/ppermute | solution.py:190
  84.9 21.3 %collective-permute-start.43 = (bf16[32,768]{1,0:T(8,128)(2,1)S(1)}, bf16[32,768]{1,0:T(8,128)(2,1)S(1)}, u32[]{:S(2)}, u32[]{:S(2)}) collective-permute-start(bf16[32,768]{1,0:T(8,128)(2,1)S(1)} %collective-permute-done.42.refs_12_), channel_id=1, source_target_pairs={{8,9},{9,10},{10,11},{11,12},{12,13},{13,14},{14,15},{15,8}} | collective-permute-start | bytes 147464 | tf_op jit(solution)/shard_map/ppermute | solution.py:110
  85.5 25.0 %collective-permute-start.46 = (bf16[32,768]{1,0:T(8,128)(2,1)S(1)}, bf16[32,768]{1,0:T(8,128)(2,1)S(1)}, u32[]{:S(2)}, u32[]{:S(2)}) collective-permute-start(bf16[32,768]{1,0:T(8,128)(2,1)S(1)} %collective-permute-done.44.refs_10_), channel_id=1, source_target_pairs={{8,15},{9,8},{10,9},{11,10},{12,11},{13,12},{14,13},{15,14}} | collective-permute-start | bytes 147464 | tf_op jit(solution)/shard_map/ppermute | solution.py:110
  86.2 27.4 %collective-permute-start.64 = (bf16[32,768]{1,0:T(8,128)(2,1)S(1)}, bf16[32,768]{1,0:T(8,128)(2,1)S(1)}, u32[]{:S(2)}, u32[]{:S(2)}) collective-permute-start(bf16[32,768]{1,0:T(8,128)(2,1)S(1)} %collective-permute-done.63.refs_12_), channel_id=1, source_target_pairs={{8,9},{9,10},{10,11},{11,12},{12,13},{13,14},{14,15},{15,8}} | collective-permute-start | bytes 147464 | tf_op jit(solution)/shard_map/ppermute | solution.py:110
  104.1 21.5 %collective-permute-start.12 = (bf16[32,768]{1,0:T(8,128)(2,1)S(1)}, bf16[32,768]{1,0:T(8,128)(2,1)S(1)}, u32[]{:S(2)}, u32[]{:S(2)}) collective-permute-start(bf16[32,768]{1,0:T(8,128)(2,1)S(1)} %collective-permute-done.11.refs_12_), channel_id=1, source_target_pairs={{8,9},{9,10},{10,11},{11,12},{12,13},{13,14},{14,15},{15,8},{16,17... | collective-permute-start | bytes 147464 | tf_op jit(solution)/shard_map/ppermute | solution.py:110
  106.2 26.7 %collective-permute-start.15 = (bf16[32,768]{1,0:T(8,128)(2,1)S(1)}, bf16[32,768]{1,0:T(8,128)(2,1)S(1)}, u32[]{:S(2)}, u32[]{:S(2)}) collective-permute-start(bf16[32,768]{1,0:T(8,128)(2,1)S(1)} %collective-permute-done.13.refs_10_), channel_id=1, source_target_pairs={{8,15},{9,8},{10,9},{11,10},{12,11},{13,12},{14,13},{15,14},{16,23... | collective-permute-start | bytes 147464 | tf_op jit(solution)/shard_map/ppermute | solution.py:110
  113.6 31.5 %collective-permute-start.47 = (bf16[32,768]{1,0:T(8,128)(2,1)S(1)}, bf16[32,768]{1,0:T(8,128)(2,1)S(1)}, u32[]{:S(2)}, u32[]{:S(2)}) collective-permute-start(bf16[32,768]{1,0:T(8,128)(2,1)S(1)} %get-tuple-element.113), channel_id=1, source_target_pairs={{0,8},{1,9},{2,10},{3,11},{4,12},{5,13},{6,14},{7,15},{8,16},{9,17... | collective-permute-start | bytes 147464 | tf_op jit(solution)/shard_map/ppermute | solution.py:190
  114.9 32.1 %collective-permute-start.49 = (bf16[32,768]{1,0:T(8,128)(2,1)S(1)}, bf16[32,768]{1,0:T(8,128)(2,1)S(1)}, u32[]{:S(2)}, u32[]{:S(2)}) collective-permute-start(bf16[32,768]{1,0:T(8,128)(2,1)S(1)} %get-tuple-element.114), channel_id=1, source_target_pairs={{0,8},{1,9},{2,10},{3,11},{4,12},{5,13},{6,14},{7,15},{8,16},{9,17... | collective-permute-start | bytes 147464 | tf_op jit(solution)/shard_map/ppermute | solution.py:190
  145.0 21.1 %collective-permute-start.18 = (bf16[32,768]{1,0:T(8,128)(2,1)S(1)}, bf16[32,768]{1,0:T(8,128)(2,1)S(1)}, u32[]{:S(2)}, u32[]{:S(2)}) collective-permute-start(bf16[32,768]{1,0:T(8,128)(2,1)S(1)} %get-tuple-element.94), channel_id=1, source_target_pairs={{0,8},{1,9},{2,10},{3,11},{4,12},{5,13},{6,14},{7,15},{8,16},{9,17... | collective-permute-start | bytes 147464 | tf_op jit(solution)/shard_map/ppermute | solution.py:190
  147.0 21.3 %collective-permute-start.48 = (bf16[32,768]{1,0:T(8,128)(2,1)S(1)}, bf16[32,768]{1,0:T(8,128)(2,1)S(1)}, u32[]{:S(2)}, u32[]{:S(2)}) collective-permute-start(bf16[32,768]{1,0:T(8,128)(2,1)S(1)} %collective-permute-done.47.refs_12_), channel_id=1, source_target_pairs={{8,9},{9,10},{10,11},{11,12},{12,13},{13,14},{14,15},{15,8},{16,17... | collective-permute-start | bytes 147464 | tf_op jit(solution)/shard_map/ppermute | solution.py:110
  149.1 23.6 %collective-permute-start.51 = (bf16[32,768]{1,0:T(8,128)(2,1)S(1)}, bf16[32,768]{1,0:T(8,128)(2,1)S(1)}, u32[]{:S(2)}, u32[]{:S(2)}) collective-permute-start(bf16[32,768]{1,0:T(8,128)(2,1)S(1)} %collective-permute-done.49.refs_10_), channel_id=1, source_target_pairs={{8,15},{9,8},{10,9},{11,10},{12,11},{13,12},{14,13},{15,14},{16,23... | collective-permute-start | bytes 147464 | tf_op jit(solution)/shard_map/ppermute | solution.py:110
  153.5 24.6 %collective-permute-start.69 = (bf16[32,768]{1,0:T(8,128)(2,1)S(1)}, bf16[32,768]{1,0:T(8,128)(2,1)S(1)}, u32[]{:S(2)}, u32[]{:S(2)}) collective-permute-start(bf16[32,768]{1,0:T(8,128)(2,1)S(1)} %collective-permute-done.68.refs_12_), channel_id=1, source_target_pairs={{8,9},{9,10},{10,11},{11,12},{12,13},{13,14},{14,15},{15,8},{16,17... | collective-permute-start | bytes 147464 | tf_op jit(solution)/shard_map/ppermute | solution.py:110
  159.8 20.2 %collective-permute-start.72 = (bf16[32,768]{1,0:T(8,128)(2,1)S(1)}, bf16[32,768]{1,0:T(8,128)(2,1)S(1)}, u32[]{:S(2)}, u32[]{:S(2)}) collective-permute-start(bf16[32,768]{1,0:T(8,128)(2,1)S(1)} %collective-permute-done.70.refs_10_), channel_id=1, source_target_pairs={{8,15},{9,8},{10,9},{11,10},{12,11},{13,12},{14,13},{15,14},{16,23... | collective-permute-start | bytes 147464 | tf_op jit(solution)/shard_map/ppermute | solution.py:110
  166.2 20.3 %collective-permute-start.17 = (bf16[32,768]{1,0:T(8,128)(2,1)S(1)}, bf16[32,768]{1,0:T(8,128)(2,1)S(1)}, u32[]{:S(2)}, u32[]{:S(2)}) collective-permute-start(bf16[32,768]{1,0:T(8,128)(2,1)S(1)} %collective-permute-done.16.refs_12_), channel_id=1, source_target_pairs={{8,9},{9,10},{10,11},{11,12},{12,13},{13,14},{14,15},{15,8},{16,17... | collective-permute-start | bytes 147464 | tf_op jit(solution)/shard_map/ppermute | solution.py:110
  168.3 20.1 %collective-permute-start.20 = (bf16[32,768]{1,0:T(8,128)(2,1)S(1)}, bf16[32,768]{1,0:T(8,128)(2,1)S(1)}, u32[]{:S(2)}, u32[]{:S(2)}) collective-permute-start(bf16[32,768]{1,0:T(8,128)(2,1)S(1)} %collective-permute-done.18.refs_10_), channel_id=1, source_target_pairs={{8,15},{9,8},{10,9},{11,10},{12,11},{13,12},{14,13},{15,14},{16,23... | collective-permute-start | bytes 147464 | tf_op jit(solution)/shard_map/ppermute | solution.py:110
  190.3 21.5 %collective-permute-start.54 = (bf16[32,768]{1,0:T(8,128)(2,1)S(1)}, bf16[32,768]{1,0:T(8,128)(2,1)S(1)}, u32[]{:S(2)}, u32[]{:S(2)}) collective-permute-start(bf16[32,768]{1,0:T(8,128)(2,1)S(1)} %get-tuple-element.117), channel_id=1, source_target_pairs={{0,8},{1,9},{2,10},{3,11},{4,12},{5,13},{6,14},{7,15},{8,16},{9,17... | collective-permute-start | bytes 147464 | tf_op jit(solution)/shard_map/ppermute | solution.py:190
  196.6 21.7 %collective-permute-start.23 = (bf16[32,768]{1,0:T(8,128)(2,1)S(1)}, bf16[32,768]{1,0:T(8,128)(2,1)S(1)}, u32[]{:S(2)}, u32[]{:S(2)}) collective-permute-start(bf16[32,768]{1,0:T(8,128)(2,1)S(1)} %get-tuple-element.97), channel_id=1, source_target_pairs={{0,8},{1,9},{2,10},{3,11},{4,12},{5,13},{6,14},{7,15},{8,16},{9,17... | collective-permute-start | bytes 147464 | tf_op jit(solution)/shard_map/ppermute | solution.py:190
  198.5 21.7 %collective-permute-start.74 = (bf16[32,768]{1,0:T(8,128)(2,1)S(1)}, bf16[32,768]{1,0:T(8,128)(2,1)S(1)}, u32[]{:S(2)}, u32[]{:S(2)}) collective-permute-start(bf16[32,768]{1,0:T(8,128)(2,1)S(1)} %collective-permute-done.73.refs_12_), channel_id=1, source_target_pairs={{8,9},{9,10},{10,11},{11,12},{12,13},{13,14},{14,15},{15,8},{16,17... | collective-permute-start | bytes 147464 | tf_op jit(solution)/shard_map/ppermute | solution.py:110
  204.8 20.0 %collective-permute-start.77 = (bf16[32,768]{1,0:T(8,128)(2,1)S(1)}, bf16[32,768]{1,0:T(8,128)(2,1)S(1)}, u32[]{:S(2)}, u32[]{:S(2)}) collective-permute-start(bf16[32,768]{1,0:T(8,128)(2,1)S(1)} %collective-permute-done.75.refs_10_), channel_id=1, source_target_pairs={{8,15},{9,8},{10,9},{11,10},{12,11},{13,12},{14,13},{15,14},{16,23... | collective-permute-start | bytes 147464 | tf_op jit(solution)/shard_map/ppermute | solution.py:110
  218.3 19.7 %collective-permute-start.22 = (bf16[32,768]{1,0:T(8,128)(2,1)S(1)}, bf16[32,768]{1,0:T(8,128)(2,1)S(1)}, u32[]{:S(2)}, u32[]{:S(2)}) collective-permute-start(bf16[32,768]{1,0:T(8,128)(2,1)S(1)} %collective-permute-done.21.refs_12_), channel_id=1, source_target_pairs={{8,9},{9,10},{10,11},{11,12},{12,13},{13,14},{14,15},{15,8},{16,17... | collective-permute-start | bytes 147464 | tf_op jit(solution)/shard_map/ppermute | solution.py:110
  248.3 43.8 %collective-permute-start.41 = (bf16[32,2048]{1,0:T(8,128)(2,1)S(1)}, bf16[32,2048]{1,0:T(8,128)(2,1)S(1)}, u32[]{:S(2)}, u32[]{:S(2)}) collective-permute-start(bf16[32,2048]{1,0:T(8,128)(2,1)S(1)} %get-tuple-element.109), channel_id=1, source_target_pairs={{24,0},{25,1},{26,2},{27,3},{28,4},{29,5},{30,6},{31,7}} | collective-permute-start | bytes 393224 | tf_op jit(solution)/shard_map/ppermute | solution.py:200
  308.4 30.8 %collective-permute-start.104 = (bf16[32,2048]{1,0:T(8,128)(2,1)S(1)}, bf16[32,2048]{1,0:T(8,128)(2,1)S(1)}, u32[]{:S(2)}, u32[]{:S(2)}) collective-permute-start(bf16[32,2048]{1,0:T(8,128)(2,1)S(1)} %get-tuple-element.149), channel_id=1, source_target_pairs={{24,0},{25,1},{26,2},{27,3},{28,4},{29,5},{30,6},{31,7}} | collective-permute-start | bytes 393224 | tf_op jit(solution)/shard_map/ppermute | solution.py:200
  309.1 32.1 %collective-permute-start.62 = (bf16[32,2048]{1,0:T(8,128)(2,1)S(1)}, bf16[32,2048]{1,0:T(8,128)(2,1)S(1)}, u32[]{:S(2)}, u32[]{:S(2)}) collective-permute-start(bf16[32,2048]{1,0:T(8,128)(2,1)S(1)} %get-tuple-element.122), channel_id=1, source_target_pairs={{24,8},{25,9},{26,10},{27,11},{28,12},{29,13},{30,14},{31,15}} | collective-permute-start | bytes 393224 | tf_op jit(solution)/shard_map/ppermute | solution.py:200
  309.7 33.3 %collective-permute-start.105 = (bf16[32,2048]{1,0:T(8,128)(2,1)S(1)}, bf16[32,2048]{1,0:T(8,128)(2,1)S(1)}, u32[]{:S(2)}, u32[]{:S(2)}) collective-permute-start(bf16[32,2048]{1,0:T(8,128)(2,1)S(1)} %get-tuple-element.150), channel_id=1, source_target_pairs={{24,8},{25,9},{26,10},{27,11},{28,12},{29,13},{30,14},{31,15}} | collective-permute-start | bytes 393224 | tf_op jit(solution)/shard_map/ppermute | solution.py:200
  325.7 23.1 %collective-permute-start.39 = (bf16[32,512]{1,0:T(8,128)(2,1)S(1)}, bf16[32,512]{1,0:T(8,128)(2,1)S(1)}, u32[]{:S(2)}, u32[]{:S(2)}) collective-permute-start(bf16[32,512]{1,0:T(8,128)(2,1)S(1)} %get-tuple-element.107), channel_id=1, source_target_pairs={{8,16},{9,17},{10,18},{11,19},{12,20},{13,21},{14,22},{15,23},{16,... | collective-permute-start | bytes 98312 | tf_op jit(solution)/shard_map/ppermute | solution.py:190
  332.7 23.3 %collective-permute-start.36 = (bf16[32,768]{1,0:T(8,128)(2,1)S(1)}, bf16[32,768]{1,0:T(8,128)(2,1)S(1)}, u32[]{:S(2)}, u32[]{:S(2)}) collective-permute-start(bf16[32,768]{1,0:T(8,128)(2,1)S(1)} %get-tuple-element.105), channel_id=1, source_target_pairs={{8,16},{9,17},{10,18},{11,19},{12,20},{13,21},{14,22},{15,23},{16,... | collective-permute-start | bytes 147464 | tf_op jit(solution)/shard_map/ppermute | solution.py:190
  359.9 19.8 %collective-permute-start.95 = (bf16[32,768]{1,0:T(8,128)(2,1)S(1)}, bf16[32,768]{1,0:T(8,128)(2,1)S(1)}, u32[]{:S(2)}, u32[]{:S(2)}) collective-permute-start(bf16[32,768]{1,0:T(8,128)(2,1)S(1)} %collective-permute-done.94.refs_12_), channel_id=1, source_target_pairs={{16,17},{17,18},{18,19},{19,20},{20,21},{21,22},{22,23},{23,16},{2... | collective-permute-start | bytes 147464 | tf_op jit(solution)/shard_map/ppermute | solution.py:110
  366.3 32.6 %collective-permute-start.88 = (bf16[32,2048]{1,0:T(8,128)(2,1)S(1)}, bf16[32,2048]{1,0:T(8,128)(2,1)S(1)}, u32[]{:S(2)}, u32[]{:S(2)}) collective-permute-start(bf16[32,2048]{1,0:T(8,128)(2,1)S(1)} %get-tuple-element.138), channel_id=1, source_target_pairs={{24,16},{25,17},{26,18},{27,19},{28,20},{29,21},{30,22},{31,23}} | collective-permute-start | bytes 393224 | tf_op jit(solution)/shard_map/ppermute | solution.py:200
  367.6 37.1 %collective-permute-start.106 = (bf16[32,2048]{1,0:T(8,128)(2,1)S(1)}, bf16[32,2048]{1,0:T(8,128)(2,1)S(1)}, u32[]{:S(2)}, u32[]{:S(2)}) collective-permute-start(bf16[32,2048]{1,0:T(8,128)(2,1)S(1)} %get-tuple-element.151), channel_id=1, source_target_pairs={{24,16},{25,17},{26,18},{27,19},{28,20},{29,21},{30,22},{31,23}} | collective-permute-start | bytes 393224 | tf_op jit(solution)/shard_map/ppermute | solution.py:200
  388.4 22.9 %collective-permute-start.99 = (bf16[32,768]{1,0:T(8,128)(2,1)S(1)}, bf16[32,768]{1,0:T(8,128)(2,1)}, u32[]{:S(2)}, u32[]{:S(2)}) collective-permute-start(bf16[32,768]{1,0:T(8,128)(2,1)S(1)} %get-tuple-element.145), channel_id=1, source_target_pairs={{16,24},{17,25},{18,26},{19,27},{20,28},{21,29},{22,30},{23,31}} | collective-permute-start | bytes 147464 | tf_op jit(solution)/shard_map/ppermute | solution.py:190
  392.4 20.2 %collective-permute-start.101 = (bf16[32,768]{1,0:T(8,128)(2,1)S(1)}, bf16[32,768]{1,0:T(8,128)(2,1)}, u32[]{:S(2)}, u32[]{:S(2)}) collective-permute-start(bf16[32,768]{1,0:T(8,128)(2,1)S(1)} %get-tuple-element.146), channel_id=1, source_target_pairs={{16,24},{17,25},{18,26},{19,27},{20,28},{21,29},{22,30},{23,31}} | collective-permute-start | bytes 147464 | tf_op jit(solution)/shard_map/ppermute | solution.py:190
  394.3 19.5 %collective-permute-start.102 = (bf16[32,512]{1,0:T(8,128)(2,1)S(1)}, bf16[32,512]{1,0:T(8,128)(2,1)S(1)}, u32[]{:S(2)}, u32[]{:S(2)}) collective-permute-start(bf16[32,512]{1,0:T(8,128)(2,1)S(1)} %get-tuple-element.147), channel_id=1, source_target_pairs={{16,24},{17,25},{18,26},{19,27},{20,28},{21,29},{22,30},{23,31}} | collective-permute-start | bytes 98312 | tf_op jit(solution)/shard_map/ppermute | solution.py:190
  398.9 29.6 %collective-permute-start.112 = (bf16[32,768]{1,0:T(8,128)(2,1)}, bf16[32,768]{1,0:T(8,128)(2,1)}, u32[]{:S(2)}, u32[]{:S(2)}) collective-permute-start(bf16[32,768]{1,0:T(8,128)(2,1)} %get-tuple-element.155), channel_id=1, source_target_pairs={{16,24},{17,25},{18,26},{19,27},{20,28},{21,29},{22,30},{23,31}} | collective-permute-start | bytes 147464 | tf_op jit(solution)/shard_map/ppermute | solution.py:190
  404.7 25.1 %collective-permute-start.114 = (bf16[32,768]{1,0:T(8,128)(2,1)}, bf16[32,768]{1,0:T(8,128)(2,1)}, u32[]{:S(2)}, u32[]{:S(2)}) collective-permute-start(bf16[32,768]{1,0:T(8,128)(2,1)} %get-tuple-element.156), channel_id=1, source_target_pairs={{16,24},{17,25},{18,26},{19,27},{20,28},{21,29},{22,30},{23,31}} | collective-permute-start | bytes 147464 | tf_op jit(solution)/shard_map/ppermute | solution.py:190
  411.3 19.7 %collective-permute-start.100 = (bf16[32,768]{1,0:T(8,128)(2,1)}, bf16[32,768]{1,0:T(8,128)(2,1)}, u32[]{:S(2)}, u32[]{:S(2)}) collective-permute-start(bf16[32,768]{1,0:T(8,128)(2,1)} %collective-permute-done.99.refs_12_), channel_id=1, source_target_pairs={{24,25},{25,26},{26,27},{27,28},{28,29},{29,30},{30,31},{31,24}} | collective-permute-start | bytes 147464 | tf_op jit(solution)/shard_map/ppermute | solution.py:110
  434.4 24.6 %collective-permute-start.117 = (bf16[32,2048]{1,0:T(8,128)(2,1)S(1)}, bf16[32,2048]{1,0:T(8,128)(2,1)S(1)}, u32[]{:S(2)}, u32[]{:S(2)}) collective-permute-start(bf16[32,2048]{1,0:T(8,128)(2,1)S(1)} %copy-done.15), channel_id=1, source_target_pairs={{24,0},{25,1},{26,2},{27,3},{28,4},{29,5},{30,6},{31,7}} | collective-permute-start | bytes 393224 | tf_op jit(solution)/shard_map/ppermute | solution.py:200
  435.1 25.2 %collective-permute-start.118 = (bf16[32,2048]{1,0:T(8,128)(2,1)S(1)}, bf16[32,2048]{1,0:T(8,128)(2,1)S(1)}, u32[]{:S(2)}, u32[]{:S(2)}) collective-permute-start(bf16[32,2048]{1,0:T(8,128)(2,1)S(1)} %copy-done.19), channel_id=1, source_target_pairs={{24,8},{25,9},{26,10},{27,11},{28,12},{29,13},{30,14},{31,15}} | collective-permute-start | bytes 393224 | tf_op jit(solution)/shard_map/ppermute | solution.py:200
  435.8 24.5 %collective-permute-start.119 = (bf16[32,2048]{1,0:T(8,128)(2,1)S(1)}, bf16[32,2048]{1,0:T(8,128)(2,1)S(1)}, u32[]{:S(2)}, u32[]{:S(2)}) collective-permute-start(bf16[32,2048]{1,0:T(8,128)(2,1)S(1)} %copy-done.23), channel_id=1, source_target_pairs={{24,16},{25,17},{26,18},{27,19},{28,20},{29,21},{30,22},{31,23}} | collective-permute-start | bytes 393224 | tf_op jit(solution)/shard_map/ppermute | solution.py:200
  440.3 20.0 %collective-permute-start.125 = (bf16[32,2048]{1,0:T(8,128)(2,1)S(1)}, bf16[32,2048]{1,0:T(8,128)(2,1)S(1)}, u32[]{:S(2)}, u32[]{:S(2)}) collective-permute-start(bf16[32,2048]{1,0:T(8,128)(2,1)S(1)} %copy-done.17), channel_id=1, source_target_pairs={{24,0},{25,1},{26,2},{27,3},{28,4},{29,5},{30,6},{31,7}} | collective-permute-start | bytes 393224 | tf_op jit(solution)/shard_map/ppermute | solution.py:200
  (118 other events, 1376.1 us)

commit v2 on v1

v2 whole, which is shorter than its diff:
```python
import jax
import jax.numpy as jnp
from jax import lax
from jax.experimental import pallas as pl
from jax.experimental.pallas import tpu as pltpu
from jax.sharding import PartitionSpec as P

HALO = 3
CEILING = 2.0
LAG = 3


def tie(value, *after):
    return lax.optimization_barrier((value, *after))[0]


def stage_kernel(copies, bias_rows, bias_ref, weights_ref, inputs_ref, where_ref, *refs):
    outs, (sems,) = refs[:-1], refs[-1:]
    sources = {"weights": weights_ref, "inputs": inputs_ref}

    def run(side):
        started = []
        for k, (out, rows, name, index) in enumerate(copies[side]):
            target = outs[out].at[rows] if rows is not None else outs[out]
            started.append(pltpu.make_async_copy(sources[name].at[index], target, sems.at[k]))
            started[-1].start()
        for out, row, layer, first, count, block in bias_rows[side]:
            own = bias_ref[layer : layer + 1, first * block : (first + count) * block]
            own = own.astype(jnp.float32)
            parts = [own[:, k * block : (k + 1) * block] for k in range(count)]
            parts.append(jnp.zeros((16 - count, block), jnp.float32))
            outs[out][row : row + 16] = jnp.concatenate(parts, axis=0).astype(jnp.bfloat16)
        for copy in started:
            copy.wait()

    if len(copies) == 1:
        run(0)
    else:

        @pl.when(where_ref[1] == 0)
        def _():
            run(0)

        @pl.when(where_ref[1] != 0)
        def _():
            run(1)


def layers_kernel(sizes, step, chunks, halo_row, *refs):
    layer_count, block_count, band_count, block, margin, share = sizes
    where_ref, offsets_ref, bias_ref, weights_ref = refs[:4]
    table_refs = refs[4 : 4 + 2 * (layer_count - 1)]
    source_ref, near_ref, far_ref, out_ref = refs[4 + 2 * (layer_count - 1) :][:4]
    buffers = refs[8 + 2 * (layer_count - 1) :]
    even = where_ref[1] == 0
    chunk = step - LAG * where_ref[0]
    edge = margin * block
    width = block_count * block
    depth = band_count * block
    rows = pl.ds(halo_row, share)

    @pl.when(jnp.logical_and(chunk >= 0, chunk < chunks))
    def _():
        first = buffers[0]
        near, far = near_ref[rows, :], far_ref[rows, :]
        first[:, :edge] = jnp.where(even, far, near)
        first[:, edge + width :] = jnp.where(even, near, far)
        first[:, edge : edge + width] = source_ref[...].reshape(share, width)

        bias = bias_ref[...].astype(jnp.float32)
        for layer in range(layer_count):
            side = (layer_count - 1 - layer) * HALO
            source = buffers[layer]
            shift = [offsets_ref[layer, band] for band in range(band_count)]
            if side:
                tables = table_refs[2 * layer : 2 * layer + 2]
                last = slice(side * depth, side * depth + 16)
                sides = [table[last].astype(jnp.float32) for table in tables]
                before_bias = jnp.where(even, sides[1], sides[0])
                after_bias = jnp.where(even, sides[0], sides[1])
            for j in range(block_count + 2 * side):
                own = j - side
                x = jnp.concatenate(
                    [
                        source[:, pl.ds(pl.multiple_of((j + HALO + s) * block, block), block)]
                        for s in shift
                    ],
                    axis=1,
                )
                if own < 0:
                    k = slice(j * depth, (j + 1) * depth)
                    w = jnp.where(even, tables[1][k], tables[0][k])
                    b = before_bias[j : j + 1]
                elif own >= block_count:
                    k = own - block_count
                    b = after_bias[k : k + 1]
                    k = slice(k * depth, (k + 1) * depth)
                    w = jnp.where(even, tables[0][k], tables[1][k])
                else:
                    w = weights_ref[layer, own].reshape(depth, block)
                    b = bias[layer : layer + 1, own * block : (own + 1) * block]
                y = jnp.dot(x, w, preferred_element_type=jnp.float32) + b
                y = jnp.clip(y, 0.0, CEILING).astype(jnp.bfloat16)
                if layer < layer_count - 1:
                    buffers[layer + 1][:, j * block : (j + 1) * block] = y
                else:
                    out_ref[:, j * block : (j + 1) * block] = y


def shards(inputs, weights, bias, offsets):
    sections = lax.axis_size("section")
    neurons = lax.axis_size("neuron")
    both = ("section", "neuron")
    section = lax.axis_index("section")
    odd = lax.axis_index("neuron") % 2
    even = odd == 0
    batches, rows, width = inputs.shape
    layer_count, block_count, band_count, block, _ = weights.shape
    margin = layer_count * HALO
    edge = margin * block
    share = rows // sections
    depth = band_count * block
    places = [(batch, target) for target in range(sections) for batch in range(batches)]
    chunks = len(places)
    assert chunks <= sections * LAG and neurons % 2 == 0 and chunks >= LAG

    near_pairs = [
        (s * neurons + n, s * neurons + (n ^ 1)) for s in range(sections) for n in range(neurons)
    ]
    far_pairs = [
        (s * neurons + n, s * neurons + (n + (1 if n % 2 else -1)) % neurons)
        for s in range(sections)
        for n in range(neurons)
    ]

    def send_near(value):
        return lax.ppermute(value, both, near_pairs)

    def send_far(value):
        return lax.ppermute(value, both, far_pairs)

    where = jnp.stack([section, odd]).astype(jnp.int32)
    sizes = (layer_count, block_count, band_count, block, margin, share)
    smem = pl.BlockSpec(memory_space=pltpu.SMEM)
    vmem = pl.BlockSpec(memory_space=pltpu.VMEM)
    hbm = pl.BlockSpec(memory_space=pltpu.HBM)
    bf16 = jnp.bfloat16
    limit = pltpu.CompilerParams(vmem_limit_bytes=12 * 1024 * 1024)

    def away(value):
        return pltpu.with_memory_space_constraint(value, pltpu.HBM)

    def stage(copies, bias_rows, shapes):
        return pl.pallas_call(
            lambda *refs: stage_kernel(copies, bias_rows, *refs),
            in_specs=[vmem, hbm, hbm, smem],
            out_specs=[vmem] * len(shapes),
            out_shape=[pltpu.VMEM(shape, bf16) for shape in shapes],
            scratch_shapes=[pltpu.SemaphoreType.DMA((max(map(len, copies)),))],
            compiler_params=limit,
        )(bias, away(weights.reshape(layer_count, block_count * depth, block)), away(inputs), where)

    ends = (pl.ds(0, edge), pl.ds(width - edge, edge))
    copies, bias_rows, shapes = [[], []], [[], []], []
    for layer in range(layer_count - 1):
        side = (layer_count - 1 - layer) * HALO
        for far in (False, True):
            for parity in range(2):
                first = 0 if far == (parity == 0) else block_count - side
                index = (layer, pl.ds(first * depth, side * depth))
                copies[parity].append((len(shapes), pl.ds(0, side * depth), "weights", index))
                bias_rows[parity].append((len(shapes), side * depth, layer, first, side, block))
            shapes.append((side * depth + 16, block))
    for steps in ((0,), range(1, LAG)):
        for far in (False, True):
            for parity in range(2):
                end = ends[0 if far == (parity == 0) else 1]
                for k, step in enumerate(steps):
                    batch, target = places[step]
                    index = (batch, pl.ds(target * share, share), end)
                    copies[parity].append((len(shapes), pl.ds(k * share, share), "inputs", index))
            shapes.append((len(steps) * share, edge))
    packed = stage(copies, bias_rows, shapes)
    tables = []
    first_halo = [send_far(packed[-3])]
    for layer in range(layer_count - 1):
        far = send_far(packed[2 * layer + 1])
        tables += [send_near(packed[2 * layer]), far]
    first_halo.insert(0, send_near(packed[-4]))
    early_far = send_far(packed[-1])
    early_halo = [send_near(packed[-2]), early_far]
    chunk_shape = (chunks, share, width)
    copies = [
        (0, k, "inputs", (batch, pl.ds(target * share, share)))
        for k, (batch, target) in enumerate(places)
    ]
    (staged,) = stage([copies], [[]], [chunk_shape])

    outputs = sum(block_count + 2 * k * HALO for k in range(layer_count))
    cost = pl.CostEstimate(
        flops=2 * outputs * share * depth * block,
        bytes_accessed=2 * (outputs * depth * block + 4 * share * width),
        transcendentals=0,
    )

    def run(step, halo_row, source, halo):
        scratch = [pltpu.VMEM((share, width + 2 * edge), bf16)]
        for layer in range(1, layer_count):
            side = (layer_count - layer) * HALO
            scratch.append(pltpu.VMEM((share, width + 2 * side * block), bf16))
        return pl.pallas_call(
            lambda *refs: layers_kernel(sizes, step, chunks, halo_row, *refs),
            in_specs=[smem, smem] + [vmem] * (5 + len(tables)),
            out_specs=vmem,
            out_shape=jax.ShapeDtypeStruct((share, width), bf16),
            scratch_shapes=scratch,
            compiler_params=limit,
            cost_estimate=cost,
        )(where, offsets, bias, weights, *tables, source, *halo)

    last = sections - 1

    def hop(step, out):
        moves = [(s, s + 1) for s in range(last) if 0 <= step - LAG * s < chunks]
        done = step - LAG * last
        if done >= 0 and places[done][1] < last:
            moves.append((last, places[done][1]))
        idle = [s for s in range(sections) if s not in [a for a, _ in moves]]
        open_ = [s for s in range(sections) if s not in [b for _, b in moves]]
        pairs = [(a * neurons + n, b * neurons + n) for a, b in moves for n in range(neurons)]
        for a, b in zip(
            [s for s in idle if s not in open_] + [s for s in idle if s in open_],
            [s for s in open_ if s not in idle] + [s for s in open_ if s in idle],
        ):
            pairs += [
                (a * neurons + n, b * neurons + (n ^ 1 if a == b else n)) for n in range(neurons)
            ]
        return lax.ppermute(out, both, pairs)

    steps = chunks + LAG * last
    hops, halos, sources, kept = {}, {}, {}, {}
    for step in range(steps):
        if step < LAG:
            source = staged[step]
            halo, halo_row = (early_halo, (step - 1) * share) if step else (first_halo, 0)
        else:
            source, halo, halo_row = sources[step], halos[step], 0
        coming = step + LAG - 2
        if coming in halos:
            source = tie(source, *halo, *sources[coming, "edges"])
        out = run(step, halo_row, source, halo)
        done = step - LAG * last
        if done < 0 or places[done][1] < last:
            hops[step] = hop(step, out)
            if done >= 0:
                kept[places[done]] = hops[step]
        else:
            kept[places[done]] = out
        coming = step + LAG - 1
        if LAG <= coming < steps:
            here = tie(hops[coming - LAG], out)
            if coming < chunks:
                here = jnp.where(section == 0, staged[coming], here)
            low, high = here[:, :edge], here[:, width - edge :]
            far, near = jnp.where(even, low, high), jnp.where(even, high, low)
            sources[coming], sources[coming, "edges"] = here, (far, near)
            far = send_far(far)
            halos[coming] = [send_near(near), far]

    results = []
    for batch in range(batches):
        value = kept[batch, last]
        for target in range(last):
            value = jnp.where(section == target, kept[batch, target], value)
        results.append(value)
    return jnp.stack(results, axis=0)


def solution(mesh):
    in_specs = (
        P(None, None, "neuron"),
        P("section", "neuron", None, None, None),
        P("section", "neuron"),
        P("section", None),
    )
    out_specs = P(None, "section", "neuron")
    return jax.shard_map(shards, mesh=mesh, in_specs=in_specs, out_specs=out_specs, check_vma=False)
```

time: 472 us -> 137 us (0.29)
  starting transfers between devices: 393 us -> 45.6 us
  waiting for transfers between devices: 8.3 us -> 52.1 us
  Pallas kernels: 49.4 us -> 26.8 us
  local copies, waits for them, and re-layouts: 13.5 us -> 5.98 us
    ppermute x128 -> x49, starting transfers between devices: 393 us -> 45.6 us  [the longest x17 21.7 us: send_far(): return lax.ppermute(value, both, far_pairs)]
    ppermute x128 -> x49, waiting for transfers between devices: 8.3 us -> 52.1 us  [the longest x17 39.4 us: send_far(): return lax.ppermute(value, both, far_pairs)]
    pallas_call x25 -> x19, Pallas kernels: 49.4 us -> 26.8 us  [the longest x17 21.8 us: run(): pl.pallas_call(lambda *refs: layers_kernel(sizes, step, chunks, halo_row,...]
    unnamed x90 -> x36, local copies, waits for them, and re-layouts: 9.57 us -> 5.06 us
  transfers between devices with their start and end apart: 128 -> 49, of which waited for: 2 -> 20; matrix products, arithmetic and copies ran while one was open for 1% -> 4% of each run, Pallas kernels for 11% -> 17%
where the time goes in v2:
time: 137 us
  waiting for transfers between devices  52.1 us (38%)
  starting transfers between devices  45.6 us (33%)
  Pallas kernels  26.8 us (20%)
  other arithmetic  6 us (4%)
  local copies, waits for them, and re-layouts  5.98 us (4%)
    ppermute x17, waiting for transfers between devices, send_far(): return lax.ppermute(value, both, far_pairs)  39.4 us
    pallas_call x17, Pallas kernels, run(): pl.pallas_call(lambda *refs: layers_kernel(sizes, step, chunks, halo_row,...  21.8 us
    ppermute x17, starting transfers between devices, send_far(): return lax.ppermute(value, both, far_pairs)  21.7 us
    ppermute x15, starting transfers between devices, hop(): return lax.ppermute(out, both, pairs)  21.1 us
    ppermute x15, waiting for transfers between devices, hop(): return lax.ppermute(out, both, pairs)  8.73 us
    unnamed x36, local copies, waits for them, and re-layouts  5.06 us
    pallas_call x2, Pallas kernels, stage(): pl.pallas_call(lambda *refs: stage_kernel(copies, bias_rows, *refs), in_s...  4.97 us
    ppermute x17, waiting for transfers between devices, send_near(): return lax.ppermute(value, both, near_pairs)  3.99 us
  transfers between devices with their start and end apart: 49, of which 20 were waited for; matrix products, arithmetic and copies ran while one was open for 4% of the time, Pallas kernels for 17%

profile of v2, /device:TPU:16, one launch (start us, length us, event | category | flops | bytes accessed | tf_op | source)
XLA Modules:
  0.0 137.0 jit_solution(5273317464646708957)
XLA Ops:
  0.8 2.6 %shard_map.46 = (bf16[1168,128]{1,0:T(8,128)(2,1)S(1)}, bf16[1168,128]{1,0:T(8,128)(2,1)S(1)}, bf16[64,768]{1,0:T(8,128)(2,1)S(1)}, bf16[64,768]{1,0:T(8,128)(2,...) custom-call(bf16[2,2048]{1,0:T(2,128)(2,1)S(1)} %copy-done.6, bf16[2,6144,128]{2,1,0:T(8,128)(2,1)} %bitcast.33, ...), custom_call_target="tpu_custom_call" | custom-call | tf_op jit(solution)/shard_map/pallas_call | solution.py:154
  3.5 2.5 %collective-permute-start.1 = (bf16[1168,128]{1,0:T(8,128)(2,1)S(1)}, bf16[1168,128]{1,0:T(8,128)(2,1)S(1)}, u32[]{:S(2)}, u32[]{:S(2)}) collective-permute-start(bf16[1168,128]{1,0:T(8,128)(2,1)S(1)} %get-tuple-element.40), channel_id=1, source_target_pairs={{0,7},{1,2},{2,1},{3,4},{4,3},{5,6},{6,5},{7,0},{8,15},{9,10},{10,... | collective-permute-start | bytes 897032 | tf_op jit(solution)/shard_map/ppermute | solution.py:140
  6.7 2.4 %shard_map.47 = bf16[8,64,2048]{2,1,0:T(8,128)(2,1)S(1)} custom-call(bf16[2,2048]{1,0:T(2,128)(2,1)S(1)} %copy-done.6, bf16[2,6144,128]{2,1,0:T(8,128)(2,1)} %bitcast.34, bf16[2,256,2048]{2,1,0:T(8,128)(2,1)} %refs_2_.20, s32[2]{0:T(128)S(1)} %pad_add_fusion.refs_3_.refs_0_), custom_call_target="tpu_custom_call" | custom-call | tf_op jit(solution)/shard_map/pallas_call | solution.py:154
  10.0 5.3 %collective-permute-done.6.refs_8_ = bf16[64,768]{1,0:T(8,128)(2,1)S(1)} collective-permute-done((bf16[64,768]{1,0:T(8,128)(2,1)S(1)}, bf16[64,768]{1,0:T(8,128)(2,1)S(1)}, u32[]{:S(2)}, u32[]{:S(2)}) %collective-permute-start.6) | collective-permute-done | bytes 98336 | tf_op jit(solution)/shard_map/ppermute | solution.py:140
  15.4 1.3 shard_map.49
  17.1 1.5 %collective-permute-start.3 = (bf16[128,768]{1,0:T(8,128)(2,1)}, bf16[128,768]{1,0:T(8,128)(2,1)}, u32[]{:S(2)}, u32[]{:S(2)}) collective-permute-start(bf16[128,768]{1,0:T(8,128)(2,1)} %get-tuple-element.42), channel_id=1, source_target_pairs={{0,7},{1,2},{2,1},{3,4},{4,3},{5,6},{6,5},{7,0},{8,15},{9,10},{10,... | collective-permute-start | bytes 589832 | tf_op jit(solution)/shard_map/ppermute | solution.py:140
  18.8 6.3 %collective-permute-done.3.refs_8_ = bf16[128,768]{1,0:T(8,128)(2,1)} collective-permute-done((bf16[128,768]{1,0:T(8,128)(2,1)}, bf16[128,768]{1,0:T(8,128)(2,1)}, u32[]{:S(2)}, u32[]{:S(2)}) %collective-permute-start.3) | collective-permute-done | bytes 196640 | tf_op jit(solution)/shard_map/ppermute | solution.py:140
  27.0 1.2 shard_map.48
  28.8 1.0 fusion.2.refs_6_
  29.9 1.4 %collective-permute-start.12 = (bf16[64,768]{1,0:T(8,128)(2,1)S(1)}, bf16[64,768]{1,0:T(8,128)(2,1)S(1)}, u32[]{:S(2)}, u32[]{:S(2)}) collective-permute-start(bf16[64,768]{1,0:T(8,128)(2,1)S(1)} %get-tuple-element.103), channel_id=1, source_target_pairs={{0,7},{1,2},{2,1},{3,4},{4,3},{5,6},{6,5},{7,0},{8,15},{9,10},{10,... | collective-permute-start | bytes 294920 | tf_op jit(solution)/shard_map/ppermute | solution.py:140
  31.3 1.0 shard_map.50
  33.1 1.3 collective-permute-start.9
  34.4 1.2 collective-permute-done.12.refs_8_
  36.2 5.2 %collective-permute-start.16 = (bf16[64,2048]{1,0:T(8,128)(2,1)S(1)}, bf16[64,2048]{1,0:T(8,128)(2,1)S(1)}, u32[]{:S(2)}, u32[]{:S(2)}) collective-permute-start(bf16[64,2048]{1,0:T(8,128)(2,1)S(1)} %shard_map.51), channel_id=1, source_target_pairs={{0,8},{1,9},{2,10},{3,11},{4,12},{5,13},{6,14},{7,15},{8,16},{9,17... | collective-permute-start | bytes 786440 | tf_op jit(solution)/shard_map/ppermute | solution.py:238
  42.3 3.0 %collective-permute-start.15 = (bf16[64,768]{1,0:T(8,128)(2,1)S(1)}, bf16[64,768]{1,0:T(8,128)(2,1)S(1)}, u32[]{:S(2)}, u32[]{:S(2)}) collective-permute-start(bf16[64,768]{1,0:T(8,128)(2,1)S(1)} %get-tuple-element.98), channel_id=1, source_target_pairs={{0,7},{1,2},{2,1},{3,4},{4,3},{5,6},{6,5},{7,0},{8,15},{9,10},{10,... | collective-permute-start | bytes 294920 | tf_op jit(solution)/shard_map/ppermute | solution.py:140
  45.8 1.7 %collective-permute-start.13 = (bf16[64,2048]{1,0:T(8,128)(2,1)S(1)}, bf16[64,2048]{1,0:T(8,128)(2,1)S(1)}, u32[]{:S(2)}, u32[]{:S(2)}) collective-permute-start(bf16[64,2048]{1,0:T(8,128)(2,1)S(1)} %shard_map.52), channel_id=1, source_target_pairs={{0,8},{1,9},{2,10},{3,11},{4,12},{5,13},{6,14},{7,15},{8,16},{9,17... | collective-permute-start | bytes 786440 | tf_op jit(solution)/shard_map/ppermute | solution.py:238
  48.3 2.6 %collective-permute-start.21 = (bf16[64,768]{1,0:T(8,128)(2,1)S(1)}, bf16[64,768]{1,0:T(8,128)(2,1)S(1)}, u32[]{:S(2)}, u32[]{:S(2)}) collective-permute-start(bf16[64,768]{1,0:T(8,128)(2,1)S(1)} %get-tuple-element.97), channel_id=1, source_target_pairs={{0,7},{1,2},{2,1},{3,4},{4,3},{5,6},{6,5},{7,0},{8,15},{9,10},{10,... | collective-permute-start | bytes 294920 | tf_op jit(solution)/shard_map/ppermute | solution.py:140
  51.5 4.5 %collective-permute-start.19 = (bf16[64,2048]{1,0:T(8,128)(2,1)S(1)}, bf16[64,2048]{1,0:T(8,128)(2,1)S(1)}, u32[]{:S(2)}, u32[]{:S(2)}) collective-permute-start(bf16[64,2048]{1,0:T(8,128)(2,1)S(1)} %shard_map.53), channel_id=1, source_target_pairs={{0,8},{1,9},{2,10},{3,11},{4,12},{5,13},{6,14},{7,15},{8,16},{9,17... | collective-permute-start | bytes 786440 | tf_op jit(solution)/shard_map/ppermute | solution.py:238
  56.1 1.6 %shard_map.54 = bf16[64,2048]{1,0:T(8,128)(2,1)S(1)} custom-call(s32[2]{0:T(128)S(1)} %pad_add_fusion.refs_3_.refs_0_, s32[2,3]{1,0:T(2,128)S(1)} %copy-done.17, bf16[2,2048]{1,0:T(2,128)(2,1)S(1)} %copy-done.7, bf16[2,16,3,128,128]{4,3,2,1,0:T(8,128)(2,1)S(1)} %copy-done, bf16[1168,128]{1,0:T(8,128)(2,1)S(1)} %collective-permute-done.refs_4_, ...), custom_call_target="tpu_custom_call" | custom-call | flops 239075328 | bytes 4784128 | tf_op jit(solution)/shard_map/pallas_call | solution.py:211
  57.8 1.4 %collective-permute-start.18 = (bf16[64,768]{1,0:T(8,128)(2,1)S(1)}, bf16[64,768]{1,0:T(8,128)(2,1)S(1)}, u32[]{:S(2)}, u32[]{:S(2)}) collective-permute-start(bf16[64,768]{1,0:T(8,128)(2,1)S(1)} %get-tuple-element.95), channel_id=1, source_target_pairs={{0,7},{1,2},{2,1},{3,4},{4,3},{5,6},{6,5},{7,0},{8,15},{9,10},{10,... | collective-permute-start | bytes 294920 | tf_op jit(solution)/shard_map/ppermute | solution.py:140
  59.2 8.2 %collective-permute-done.19.refs_6_ = bf16[64,2048]{1,0:T(8,128)(2,1)S(1)} collective-permute-done((bf16[64,2048]{1,0:T(8,128)(2,1)S(1)}, bf16[64,2048]{1,0:T(8,128)(2,1)S(1)}, u32[]{:S(2)}, u32[]{:S(2)}) %collective-permute-start.19) | collective-permute-done | bytes 262176 | tf_op jit(solution)/shard_map/ppermute | solution.py:238
  67.5 1.6 %shard_map.55 = bf16[64,2048]{1,0:T(8,128)(2,1)S(1)} custom-call(s32[2]{0:T(128)S(1)} %pad_add_fusion.refs_3_.refs_0_, s32[2,3]{1,0:T(2,128)S(1)} %copy-done.17, bf16[2,2048]{1,0:T(2,128)(2,1)S(1)} %copy-done.7, bf16[2,16,3,128,128]{4,3,2,1,0:T(8,128)(2,1)S(1)} %copy-done, bf16[1168,128]{1,0:T(8,128)(2,1)S(1)} %collective-permute-done.refs_4_, ...), custom_call_target="tpu_custom_call" | custom-call | flops 239075328 | bytes 4784128 | tf_op jit(solution)/shard_map/pallas_call | solution.py:211
  69.3 1.2 collective-permute-done.23.refs_7_
  70.5 4.5 %collective-permute-done.24.refs_8_ = bf16[64,768]{1,0:T(8,128)(2,1)S(1)} collective-permute-done((bf16[64,768]{1,0:T(8,128)(2,1)S(1)}, bf16[64,768]{1,0:T(8,128)(2,1)S(1)}, u32[]{:S(2)}, u32[]{:S(2)}) %collective-permute-start.24) | collective-permute-done | bytes 98336 | tf_op jit(solution)/shard_map/ppermute | solution.py:140
  74.9 1.6 %shard_map.56 = bf16[64,2048]{1,0:T(8,128)(2,1)S(1)} custom-call(s32[2]{0:T(128)S(1)} %pad_add_fusion.refs_3_.refs_0_, s32[2,3]{1,0:T(2,128)S(1)} %copy-done.17, bf16[2,2048]{1,0:T(2,128)(2,1)S(1)} %copy-done.7, bf16[2,16,3,128,128]{4,3,2,1,0:T(8,128)(2,1)S(1)} %copy-done, bf16[1168,128]{1,0:T(8,128)(2,1)S(1)} %collective-permute-done.refs_4_, ...), custom_call_target="tpu_custom_call" | custom-call | flops 239075328 | bytes 4784128 | tf_op jit(solution)/shard_map/pallas_call | solution.py:211
  76.5 4.0 %collective-permute-start.28 = (bf16[64,2048]{1,0:T(8,128)(2,1)S(1)}, bf16[64,2048]{1,0:T(8,128)(2,1)S(1)}, u32[]{:S(2)}, u32[]{:S(2)}) collective-permute-start(bf16[64,2048]{1,0:T(8,128)(2,1)S(1)} %shard_map.56), channel_id=1, source_target_pairs={{8,16},{9,17},{10,18},{11,19},{12,20},{13,21},{14,22},{15,23},{16,... | collective-permute-start | bytes 786440 | tf_op jit(solution)/shard_map/ppermute | solution.py:238
  80.6 1.3 collective-permute-done.29.refs_7_
  81.8 4.0 %collective-permute-done.30.refs_8_ = bf16[64,768]{1,0:T(8,128)(2,1)S(1)} collective-permute-done((bf16[64,768]{1,0:T(8,128)(2,1)S(1)}, bf16[64,768]{1,0:T(8,128)(2,1)S(1)}, u32[]{:S(2)}, u32[]{:S(2)}) %collective-permute-start.30) | collective-permute-done | bytes 98336 | tf_op jit(solution)/shard_map/ppermute | solution.py:140
  85.8 1.6 %shard_map.57 = bf16[64,2048]{1,0:T(8,128)(2,1)S(1)} custom-call(s32[2]{0:T(128)S(1)} %pad_add_fusion.refs_3_.refs_0_, s32[2,3]{1,0:T(2,128)S(1)} %copy-done.17, bf16[2,2048]{1,0:T(2,128)(2,1)S(1)} %copy-done.7, bf16[2,16,3,128,128]{4,3,2,1,0:T(8,128)(2,1)S(1)} %copy-done, bf16[1168,128]{1,0:T(8,128)(2,1)S(1)} %collective-permute-done.refs_4_, ...), custom_call_target="tpu_custom_call" | custom-call | flops 239075328 | bytes 4784128 | tf_op jit(solution)/shard_map/pallas_call | solution.py:211
  88.9 3.8 %collective-permute-done.27.refs_8_ = bf16[64,768]{1,0:T(8,128)(2,1)S(1)} collective-permute-done((bf16[64,768]{1,0:T(8,128)(2,1)S(1)}, bf16[64,768]{1,0:T(8,128)(2,1)S(1)}, u32[]{:S(2)}, u32[]{:S(2)}) %collective-permute-start.27) | collective-permute-done | bytes 98336 | tf_op jit(solution)/shard_map/ppermute | solution.py:140
  92.6 1.6 %shard_map.58 = bf16[64,2048]{1,0:T(8,128)(2,1)S(1)} custom-call(s32[2]{0:T(128)S(1)} %pad_add_fusion.refs_3_.refs_0_, s32[2,3]{1,0:T(2,128)S(1)} %copy-done.17, bf16[2,2048]{1,0:T(2,128)(2,1)S(1)} %copy-done.7, bf16[2,16,3,128,128]{4,3,2,1,0:T(8,128)(2,1)S(1)} %copy-done, bf16[1168,128]{1,0:T(8,128)(2,1)S(1)} %collective-permute-done.refs_4_, ...), custom_call_target="tpu_custom_call" | custom-call | flops 239075328 | bytes 4784128 | tf_op jit(solution)/shard_map/pallas_call | solution.py:211
  95.7 3.8 %collective-permute-done.33.refs_8_ = bf16[64,768]{1,0:T(8,128)(2,1)S(1)} collective-permute-done((bf16[64,768]{1,0:T(8,128)(2,1)S(1)}, bf16[64,768]{1,0:T(8,128)(2,1)S(1)}, u32[]{:S(2)}, u32[]{:S(2)}) %collective-permute-start.33) | collective-permute-done | bytes 98336 | tf_op jit(solution)/shard_map/ppermute | solution.py:140
  99.4 1.6 %shard_map.59 = bf16[64,2048]{1,0:T(8,128)(2,1)S(1)} custom-call(s32[2]{0:T(128)S(1)} %pad_add_fusion.refs_3_.refs_0_, s32[2,3]{1,0:T(2,128)S(1)} %copy-done.17, bf16[2,2048]{1,0:T(2,128)(2,1)S(1)} %copy-done.7, bf16[2,16,3,128,128]{4,3,2,1,0:T(8,128)(2,1)S(1)} %copy-done, bf16[1168,128]{1,0:T(8,128)(2,1)S(1)} %collective-permute-done.refs_4_, ...), custom_call_target="tpu_custom_call" | custom-call | flops 239075328 | bytes 4784128 | tf_op jit(solution)/shard_map/pallas_call | solution.py:211
  102.8 3.7 %collective-permute-done.39.refs_8_ = bf16[64,768]{1,0:T(8,128)(2,1)S(1)} collective-permute-done((bf16[64,768]{1,0:T(8,128)(2,1)S(1)}, bf16[64,768]{1,0:T(8,128)(2,1)S(1)}, u32[]{:S(2)}, u32[]{:S(2)}) %collective-permute-start.39) | collective-permute-done | bytes 98336 | tf_op jit(solution)/shard_map/ppermute | solution.py:140
  106.5 2.3 %shard_map.60 = bf16[64,2048]{1,0:T(8,128)(2,1)} custom-call(s32[2]{0:T(128)S(1)} %pad_add_fusion.refs_3_.refs_0_, s32[2,3]{1,0:T(2,128)S(1)} %copy-done.17, bf16[2,2048]{1,0:T(2,128)(2,1)S(1)} %copy-done.7, bf16[2,16,3,128,128]{4,3,2,1,0:T(8,128)(2,1)S(1)} %copy-done, bf16[1168,128]{1,0:T(8,128)(2,1)S(1)} %collective-permute-done.refs_4_, ...), custom_call_target="tpu_custom_call" | custom-call | flops 239075328 | bytes 4784128 | tf_op jit(solution)/shard_map/pallas_call | solution.py:211
  108.8 1.8 %collective-permute-start.41 = (bf16[64,2048]{1,0:T(8,128)(2,1)}, bf16[64,2048]{1,0:T(8,128)(2,1)}, u32[]{:S(2)}, u32[]{:S(2)}) collective-permute-start(bf16[64,2048]{1,0:T(8,128)(2,1)} %shard_map.60), channel_id=1, source_target_pairs={{16,24},{17,25},{18,26},{19,27},{20,28},{21,29},{22,30},{23,31},{2... | collective-permute-start | bytes 786440 | tf_op jit(solution)/shard_map/ppermute | solution.py:238
  110.7 1.0 collective-permute-start.36
  112.4 3.3 %collective-permute-done.36.refs_8_ = bf16[64,768]{1,0:T(8,128)(2,1)S(1)} collective-permute-done((bf16[64,768]{1,0:T(8,128)(2,1)S(1)}, bf16[64,768]{1,0:T(8,128)(2,1)S(1)}, u32[]{:S(2)}, u32[]{:S(2)}) %collective-permute-start.36) | collective-permute-done | bytes 98336 | tf_op jit(solution)/shard_map/ppermute | solution.py:140
  115.7 2.3 %shard_map.61 = bf16[64,2048]{1,0:T(8,128)(2,1)} custom-call(s32[2]{0:T(128)S(1)} %pad_add_fusion.refs_3_.refs_0_, s32[2,3]{1,0:T(2,128)S(1)} %copy-done.17, bf16[2,2048]{1,0:T(2,128)(2,1)S(1)} %copy-done.7, bf16[2,16,3,128,128]{4,3,2,1,0:T(8,128)(2,1)S(1)} %copy-done, bf16[1168,128]{1,0:T(8,128)(2,1)S(1)} %collective-permute-done.refs_4_, ...), custom_call_target="tpu_custom_call" | custom-call | flops 239075328 | bytes 4784128 | tf_op jit(solution)/shard_map/pallas_call | solution.py:211
  118.4 1.1 collective-permute-start.45
  120.5 1.6 %collective-permute-start.43 = (bf16[64,768]{1,0:T(8,128)(2,1)S(1)}, bf16[64,768]{1,0:T(8,128)(2,1)S(1)}, u32[]{:S(2)}, u32[]{:S(2)}) collective-permute-start(bf16[64,768]{1,0:T(8,128)(2,1)S(1)} %get-tuple-element.79), channel_id=1, source_target_pairs={{0,7},{1,2},{2,1},{3,4},{4,3},{5,6},{6,5},{7,0},{8,15},{9,10},{10,... | collective-permute-start | bytes 294920 | tf_op jit(solution)/shard_map/ppermute | solution.py:140
  122.1 1.6 %collective-permute-done.45.refs_8_ = bf16[64,768]{1,0:T(8,128)(2,1)S(1)} collective-permute-done((bf16[64,768]{1,0:T(8,128)(2,1)}, bf16[64,768]{1,0:T(8,128)(2,1)S(1)}, u32[]{:S(2)}, u32[]{:S(2)}) %collective-permute-start.45) | collective-permute-done | bytes 98336 | tf_op jit(solution)/shard_map/ppermute | solution.py:140
  126.2 2.6 %collective-permute-start.46 = (bf16[64,2048]{1,0:T(8,128)(2,1)S(1)}, bf16[64,2048]{1,0:T(8,128)(2,1)S(1)}, u32[]{:S(2)}, u32[]{:S(2)}) collective-permute-start(bf16[64,2048]{1,0:T(8,128)(2,1)S(1)} %shard_map.62), channel_id=1, source_target_pairs={{24,16},{25,17},{26,18},{27,19},{28,20},{29,21},{30,22},{31,23},{1... | collective-permute-start | bytes 786440 | tf_op jit(solution)/shard_map/ppermute | solution.py:238
  129.8 1.2 collective-permute-start.48
  131.1 1.0 shard_map.63
  132.1 1.0 select_bitcast_fusion.1
  133.1 1.9 %collective-permute-done.48.refs_8_ = bf16[64,768]{1,0:T(8,128)(2,1)S(1)} collective-permute-done((bf16[64,768]{1,0:T(8,128)(2,1)S(1)}, bf16[64,768]{1,0:T(8,128)(2,1)S(1)}, u32[]{:S(2)}, u32[]{:S(2)}) %collective-permute-start.48) | collective-permute-done | bytes 98336 | tf_op jit(solution)/shard_map/ppermute | solution.py:140
  135.0 1.0 shard_map.64
  (129 shorter events, 21.5 us)
Async XLA Ops:
  3.4 11.9 %collective-permute-start = (bf16[1168,128]{1,0:T(8,128)(2,1)S(1)}, bf16[1168,128]{1,0:T(8,128)(2,1)S(1)}, u32[]{:S(2)}, u32[]{:S(2)}) collective-permute-start(bf16[1168,128]{1,0:T(8,128)(2,1)S(1)} %get-tuple-element.39), channel_id=1, source_target_pairs={{0,1},{1,0},{2,3},{3,2},{4,5},{5,4},{6,7},{7,6},{8,9},{9,8},{10,11... | collective-permute-start | bytes 897032 | tf_op jit(solution)/shard_map/ppermute | solution.py:137
  3.5 11.9 %collective-permute-start.1 = (bf16[1168,128]{1,0:T(8,128)(2,1)S(1)}, bf16[1168,128]{1,0:T(8,128)(2,1)S(1)}, u32[]{:S(2)}, u32[]{:S(2)}) collective-permute-start(bf16[1168,128]{1,0:T(8,128)(2,1)S(1)} %get-tuple-element.40), channel_id=1, source_target_pairs={{0,7},{1,2},{2,1},{3,4},{4,3},{5,6},{6,5},{7,0},{8,15},{9,10},{10,... | collective-permute-start | bytes 897032 | tf_op jit(solution)/shard_map/ppermute | solution.py:140
  6.0 4.0 %collective-permute-start.5 = (bf16[64,768]{1,0:T(8,128)(2,1)S(1)}, bf16[64,768]{1,0:T(8,128)(2,1)S(1)}, u32[]{:S(2)}, u32[]{:S(2)}) collective-permute-start(bf16[64,768]{1,0:T(8,128)(2,1)S(1)} %get-tuple-element.43), channel_id=1, source_target_pairs={{0,1},{1,0},{2,3},{3,2},{4,5},{5,4},{6,7},{7,6},{8,9},{9,8},{10,11... | collective-permute-start | bytes 294920 | tf_op jit(solution)/shard_map/ppermute | solution.py:137
  6.0 9.3 %collective-permute-start.6 = (bf16[64,768]{1,0:T(8,128)(2,1)S(1)}, bf16[64,768]{1,0:T(8,128)(2,1)S(1)}, u32[]{:S(2)}, u32[]{:S(2)}) collective-permute-start(bf16[64,768]{1,0:T(8,128)(2,1)S(1)} %get-tuple-element.44), channel_id=1, source_target_pairs={{0,7},{1,2},{2,1},{3,4},{4,3},{5,6},{6,5},{7,0},{8,15},{9,10},{10,... | collective-permute-start | bytes 294920 | tf_op jit(solution)/shard_map/ppermute | solution.py:140
  16.6 11.7 %collective-permute-start.7 = (bf16[64,2048]{1,0:T(8,128)(2,1)}, bf16[64,2048]{1,0:T(8,128)(2,1)}, u32[]{:S(2)}, u32[]{:S(2)}) collective-permute-start(bf16[64,2048]{1,0:T(8,128)(2,1)} %shard_map.49), channel_id=1, source_target_pairs={{0,8},{1,9},{2,10},{3,11},{4,12},{5,13},{6,14},{7,15},{8,0},{9,1},... | collective-permute-start | bytes 786440 | tf_op jit(solution)/shard_map/ppermute | solution.py:238
  16.7 2.1 %collective-permute-start.2 = (bf16[128,768]{1,0:T(8,128)(2,1)}, bf16[128,768]{1,0:T(8,128)(2,1)}, u32[]{:S(2)}, u32[]{:S(2)}) collective-permute-start(bf16[128,768]{1,0:T(8,128)(2,1)} %get-tuple-element.41), channel_id=1, source_target_pairs={{0,1},{1,0},{2,3},{3,2},{4,5},{5,4},{6,7},{7,6},{8,9},{9,8},{10,11... | collective-permute-start | bytes 589832 | tf_op jit(solution)/shard_map/ppermute | solution.py:137
  17.1 8.0 %collective-permute-start.3 = (bf16[128,768]{1,0:T(8,128)(2,1)}, bf16[128,768]{1,0:T(8,128)(2,1)}, u32[]{:S(2)}, u32[]{:S(2)}) collective-permute-start(bf16[128,768]{1,0:T(8,128)(2,1)} %get-tuple-element.42), channel_id=1, source_target_pairs={{0,7},{1,2},{2,1},{3,4},{4,3},{5,6},{6,5},{7,0},{8,15},{9,10},{10,... | collective-permute-start | bytes 589832 | tf_op jit(solution)/shard_map/ppermute | solution.py:140
  28.2 4.2 %collective-permute-start.4 = (bf16[64,2048]{1,0:T(8,128)(2,1)S(1)}, bf16[64,2048]{1,0:T(8,128)(2,1)S(1)}, u32[]{:S(2)}, u32[]{:S(2)}) collective-permute-start(bf16[64,2048]{1,0:T(8,128)(2,1)S(1)} %shard_map.48), channel_id=1, source_target_pairs={{0,8},{1,9},{2,10},{3,11},{4,12},{5,13},{6,14},{7,15},{8,0},{9,1},... | collective-permute-start | bytes 786440 | tf_op jit(solution)/shard_map/ppermute | solution.py:238
  29.8 4.6 %collective-permute-start.11 = (bf16[64,768]{1,0:T(8,128)(2,1)S(1)}, bf16[64,768]{1,0:T(8,128)(2,1)S(1)}, u32[]{:S(2)}, u32[]{:S(2)}) collective-permute-start(bf16[64,768]{1,0:T(8,128)(2,1)S(1)} %get-tuple-element.102), channel_id=1, source_target_pairs={{0,1},{1,0},{2,3},{3,2},{4,5},{5,4},{6,7},{7,6},{8,9},{9,8},{10,11... | collective-permute-start | bytes 294920 | tf_op jit(solution)/shard_map/ppermute | solution.py:137
  29.9 5.7 %collective-permute-start.12 = (bf16[64,768]{1,0:T(8,128)(2,1)S(1)}, bf16[64,768]{1,0:T(8,128)(2,1)S(1)}, u32[]{:S(2)}, u32[]{:S(2)}) collective-permute-start(bf16[64,768]{1,0:T(8,128)(2,1)S(1)} %get-tuple-element.103), channel_id=1, source_target_pairs={{0,7},{1,2},{2,1},{3,4},{4,3},{5,6},{6,5},{7,0},{8,15},{9,10},{10,... | collective-permute-start | bytes 294920 | tf_op jit(solution)/shard_map/ppermute | solution.py:140
  32.4 9.0 %collective-permute-start.10 = (bf16[64,2048]{1,0:T(8,128)(2,1)S(1)}, bf16[64,2048]{1,0:T(8,128)(2,1)S(1)}, u32[]{:S(2)}, u32[]{:S(2)}) collective-permute-start(bf16[64,2048]{1,0:T(8,128)(2,1)S(1)} %shard_map.50), channel_id=1, source_target_pairs={{0,8},{1,9},{2,10},{3,11},{4,12},{5,13},{6,14},{7,15},{8,0},{9,1},... | collective-permute-start | bytes 786440 | tf_op jit(solution)/shard_map/ppermute | solution.py:238
  32.5 12.8 %collective-permute-start.8 = (bf16[64,768]{1,0:T(8,128)(2,1)S(1)}, bf16[64,768]{1,0:T(8,128)(2,1)S(1)}, u32[]{:S(2)}, u32[]{:S(2)}) collective-permute-start(bf16[64,768]{1,0:T(8,128)(2,1)S(1)} %get-tuple-element.100), channel_id=1, source_target_pairs={{0,1},{1,0},{2,3},{3,2},{4,5},{5,4},{6,7},{7,6},{8,9},{9,8},{10,11... | collective-permute-start | bytes 294920 | tf_op jit(solution)/shard_map/ppermute | solution.py:137
  33.1 12.2 %collective-permute-start.9 = (bf16[64,768]{1,0:T(8,128)(2,1)S(1)}, bf16[64,768]{1,0:T(8,128)(2,1)S(1)}, u32[]{:S(2)}, u32[]{:S(2)}) collective-permute-start(bf16[64,768]{1,0:T(8,128)(2,1)S(1)} %get-tuple-element.101), channel_id=1, source_target_pairs={{0,7},{1,2},{2,1},{3,4},{4,3},{5,6},{6,5},{7,0},{8,15},{9,10},{10,... | collective-permute-start | bytes 294920 | tf_op jit(solution)/shard_map/ppermute | solution.py:140
  36.2 11.7 %collective-permute-start.16 = (bf16[64,2048]{1,0:T(8,128)(2,1)S(1)}, bf16[64,2048]{1,0:T(8,128)(2,1)S(1)}, u32[]{:S(2)}, u32[]{:S(2)}) collective-permute-start(bf16[64,2048]{1,0:T(8,128)(2,1)S(1)} %shard_map.51), channel_id=1, source_target_pairs={{0,8},{1,9},{2,10},{3,11},{4,12},{5,13},{6,14},{7,15},{8,16},{9,17... | collective-permute-start | bytes 786440 | tf_op jit(solution)/shard_map/ppermute | solution.py:238
  41.4 9.6 %collective-permute-start.14 = (bf16[64,768]{1,0:T(8,128)(2,1)S(1)}, bf16[64,768]{1,0:T(8,128)(2,1)S(1)}, u32[]{:S(2)}, u32[]{:S(2)}) collective-permute-start(bf16[64,768]{1,0:T(8,128)(2,1)S(1)} %get-tuple-element.99), channel_id=1, source_target_pairs={{0,1},{1,0},{2,3},{3,2},{4,5},{5,4},{6,7},{7,6},{8,9},{9,8},{10,11... | collective-permute-start | bytes 294920 | tf_op jit(solution)/shard_map/ppermute | solution.py:137
  42.3 8.6 %collective-permute-start.15 = (bf16[64,768]{1,0:T(8,128)(2,1)S(1)}, bf16[64,768]{1,0:T(8,128)(2,1)S(1)}, u32[]{:S(2)}, u32[]{:S(2)}) collective-permute-start(bf16[64,768]{1,0:T(8,128)(2,1)S(1)} %get-tuple-element.98), channel_id=1, source_target_pairs={{0,7},{1,2},{2,1},{3,4},{4,3},{5,6},{6,5},{7,0},{8,15},{9,10},{10,... | collective-permute-start | bytes 294920 | tf_op jit(solution)/shard_map/ppermute | solution.py:140
  45.8 10.1 %collective-permute-start.13 = (bf16[64,2048]{1,0:T(8,128)(2,1)S(1)}, bf16[64,2048]{1,0:T(8,128)(2,1)S(1)}, u32[]{:S(2)}, u32[]{:S(2)}) collective-permute-start(bf16[64,2048]{1,0:T(8,128)(2,1)S(1)} %shard_map.52), channel_id=1, source_target_pairs={{0,8},{1,9},{2,10},{3,11},{4,12},{5,13},{6,14},{7,15},{8,16},{9,17... | collective-permute-start | bytes 786440 | tf_op jit(solution)/shard_map/ppermute | solution.py:238
  47.9 8.2 %collective-permute-start.20 = (bf16[64,768]{1,0:T(8,128)(2,1)S(1)}, bf16[64,768]{1,0:T(8,128)(2,1)S(1)}, u32[]{:S(2)}, u32[]{:S(2)}) collective-permute-start(bf16[64,768]{1,0:T(8,128)(2,1)S(1)} %get-tuple-element.96), channel_id=1, source_target_pairs={{0,1},{1,0},{2,3},{3,2},{4,5},{5,4},{6,7},{7,6},{8,9},{9,8},{10,11... | collective-permute-start | bytes 294920 | tf_op jit(solution)/shard_map/ppermute | solution.py:137
  48.3 7.8 %collective-permute-start.21 = (bf16[64,768]{1,0:T(8,128)(2,1)S(1)}, bf16[64,768]{1,0:T(8,128)(2,1)S(1)}, u32[]{:S(2)}, u32[]{:S(2)}) collective-permute-start(bf16[64,768]{1,0:T(8,128)(2,1)S(1)} %get-tuple-element.97), channel_id=1, source_target_pairs={{0,7},{1,2},{2,1},{3,4},{4,3},{5,6},{6,5},{7,0},{8,15},{9,10},{10,... | collective-permute-start | bytes 294920 | tf_op jit(solution)/shard_map/ppermute | solution.py:140
  51.5 15.9 %collective-permute-start.19 = (bf16[64,2048]{1,0:T(8,128)(2,1)S(1)}, bf16[64,2048]{1,0:T(8,128)(2,1)S(1)}, u32[]{:S(2)}, u32[]{:S(2)}) collective-permute-start(bf16[64,2048]{1,0:T(8,128)(2,1)S(1)} %shard_map.53), channel_id=1, source_target_pairs={{0,8},{1,9},{2,10},{3,11},{4,12},{5,13},{6,14},{7,15},{8,16},{9,17... | collective-permute-start | bytes 786440 | tf_op jit(solution)/shard_map/ppermute | solution.py:238
  57.7 11.6 %collective-permute-start.25 = (bf16[64,2048]{1,0:T(8,128)(2,1)S(1)}, bf16[64,2048]{1,0:T(8,128)(2,1)S(1)}, u32[]{:S(2)}, u32[]{:S(2)}) collective-permute-start(bf16[64,2048]{1,0:T(8,128)(2,1)S(1)} %shard_map.54), channel_id=1, source_target_pairs={{0,8},{1,9},{2,10},{3,11},{4,12},{5,13},{6,14},{7,15},{8,16},{9,17... | collective-permute-start | bytes 786440 | tf_op jit(solution)/shard_map/ppermute | solution.py:238
  57.7 9.7 %collective-permute-start.17 = (bf16[64,768]{1,0:T(8,128)(2,1)S(1)}, bf16[64,768]{1,0:T(8,128)(2,1)S(1)}, u32[]{:S(2)}, u32[]{:S(2)}) collective-permute-start(bf16[64,768]{1,0:T(8,128)(2,1)S(1)} %get-tuple-element.94), channel_id=1, source_target_pairs={{0,1},{1,0},{2,3},{3,2},{4,5},{5,4},{6,7},{7,6},{8,9},{9,8},{10,11... | collective-permute-start | bytes 294920 | tf_op jit(solution)/shard_map/ppermute | solution.py:137
  57.8 9.7 %collective-permute-start.18 = (bf16[64,768]{1,0:T(8,128)(2,1)S(1)}, bf16[64,768]{1,0:T(8,128)(2,1)S(1)}, u32[]{:S(2)}, u32[]{:S(2)}) collective-permute-start(bf16[64,768]{1,0:T(8,128)(2,1)S(1)} %get-tuple-element.95), channel_id=1, source_target_pairs={{0,7},{1,2},{2,1},{3,4},{4,3},{5,6},{6,5},{7,0},{8,15},{9,10},{10,... | collective-permute-start | bytes 294920 | tf_op jit(solution)/shard_map/ppermute | solution.py:140
  69.1 11.5 %collective-permute-start.22 = (bf16[64,2048]{1,0:T(8,128)(2,1)S(1)}, bf16[64,2048]{1,0:T(8,128)(2,1)S(1)}, u32[]{:S(2)}, u32[]{:S(2)}) collective-permute-start(bf16[64,2048]{1,0:T(8,128)(2,1)S(1)} %shard_map.55), channel_id=1, source_target_pairs={{0,8},{1,9},{2,10},{3,11},{4,12},{5,13},{6,14},{7,15},{8,16},{9,17... | collective-permute-start | bytes 786440 | tf_op jit(solution)/shard_map/ppermute | solution.py:238
  69.1 1.4 collective-permute-start.23
  69.2 5.7 %collective-permute-start.24 = (bf16[64,768]{1,0:T(8,128)(2,1)S(1)}, bf16[64,768]{1,0:T(8,128)(2,1)S(1)}, u32[]{:S(2)}, u32[]{:S(2)}) collective-permute-start(bf16[64,768]{1,0:T(8,128)(2,1)S(1)} %get-tuple-element.92), channel_id=1, source_target_pairs={{0,7},{1,2},{2,1},{3,4},{4,3},{5,6},{6,5},{7,0},{8,15},{9,10},{10,... | collective-permute-start | bytes 294920 | tf_op jit(solution)/shard_map/ppermute | solution.py:140
  76.5 11.6 %collective-permute-start.28 = (bf16[64,2048]{1,0:T(8,128)(2,1)S(1)}, bf16[64,2048]{1,0:T(8,128)(2,1)S(1)}, u32[]{:S(2)}, u32[]{:S(2)}) collective-permute-start(bf16[64,2048]{1,0:T(8,128)(2,1)S(1)} %shard_map.56), channel_id=1, source_target_pairs={{8,16},{9,17},{10,18},{11,19},{12,20},{13,21},{14,22},{15,23},{16,... | collective-permute-start | bytes 786440 | tf_op jit(solution)/shard_map/ppermute | solution.py:238
  80.5 1.3 collective-permute-start.29
  80.5 5.3 %collective-permute-start.30 = (bf16[64,768]{1,0:T(8,128)(2,1)S(1)}, bf16[64,768]{1,0:T(8,128)(2,1)S(1)}, u32[]{:S(2)}, u32[]{:S(2)}) collective-permute-start(bf16[64,768]{1,0:T(8,128)(2,1)S(1)} %get-tuple-element.91), channel_id=1, source_target_pairs={{0,7},{1,2},{2,1},{3,4},{4,3},{5,6},{6,5},{7,0},{8,15},{9,10},{10,... | collective-permute-start | bytes 294920 | tf_op jit(solution)/shard_map/ppermute | solution.py:140
  87.4 7.8 %collective-permute-start.34 = (bf16[64,2048]{1,0:T(8,128)(2,1)S(1)}, bf16[64,2048]{1,0:T(8,128)(2,1)S(1)}, u32[]{:S(2)}, u32[]{:S(2)}) collective-permute-start(bf16[64,2048]{1,0:T(8,128)(2,1)S(1)} %shard_map.57), channel_id=1, source_target_pairs={{8,16},{9,17},{10,18},{11,19},{12,20},{13,21},{14,22},{15,23},{16,... | collective-permute-start | bytes 786440 | tf_op jit(solution)/shard_map/ppermute | solution.py:238
  87.6 1.3 collective-permute-start.26
  87.6 5.1 %collective-permute-start.27 = (bf16[64,768]{1,0:T(8,128)(2,1)S(1)}, bf16[64,768]{1,0:T(8,128)(2,1)S(1)}, u32[]{:S(2)}, u32[]{:S(2)}) collective-permute-start(bf16[64,768]{1,0:T(8,128)(2,1)S(1)} %get-tuple-element.89), channel_id=1, source_target_pairs={{0,7},{1,2},{2,1},{3,4},{4,3},{5,6},{6,5},{7,0},{8,15},{9,10},{10,... | collective-permute-start | bytes 294920 | tf_op jit(solution)/shard_map/ppermute | solution.py:140
  94.2 8.2 %collective-permute-start.31 = (bf16[64,2048]{1,0:T(8,128)(2,1)S(1)}, bf16[64,2048]{1,0:T(8,128)(2,1)S(1)}, u32[]{:S(2)}, u32[]{:S(2)}) collective-permute-start(bf16[64,2048]{1,0:T(8,128)(2,1)S(1)} %shard_map.58), channel_id=1, source_target_pairs={{8,16},{9,17},{10,18},{11,19},{12,20},{13,21},{14,22},{15,23},{16,... | collective-permute-start | bytes 786440 | tf_op jit(solution)/shard_map/ppermute | solution.py:238
  94.4 1.3 collective-permute-start.32
  94.4 5.0 %collective-permute-start.33 = (bf16[64,768]{1,0:T(8,128)(2,1)S(1)}, bf16[64,768]{1,0:T(8,128)(2,1)S(1)}, u32[]{:S(2)}, u32[]{:S(2)}) collective-permute-start(bf16[64,768]{1,0:T(8,128)(2,1)S(1)} %get-tuple-element.86), channel_id=1, source_target_pairs={{0,7},{1,2},{2,1},{3,4},{4,3},{5,6},{6,5},{7,0},{8,15},{9,10},{10,... | collective-permute-start | bytes 294920 | tf_op jit(solution)/shard_map/ppermute | solution.py:140
  101.0 10.6 %collective-permute-start.37 = (bf16[64,2048]{1,0:T(8,128)(2,1)S(1)}, bf16[64,2048]{1,0:T(8,128)(2,1)S(1)}, u32[]{:S(2)}, u32[]{:S(2)}) collective-permute-start(bf16[64,2048]{1,0:T(8,128)(2,1)S(1)} %shard_map.59), channel_id=1, source_target_pairs={{16,24},{17,25},{18,26},{19,27},{20,28},{21,29},{22,30},{23,31},{2... | collective-permute-start | bytes 786440 | tf_op jit(solution)/shard_map/ppermute | solution.py:238
  101.5 5.0 %collective-permute-start.39 = (bf16[64,768]{1,0:T(8,128)(2,1)S(1)}, bf16[64,768]{1,0:T(8,128)(2,1)S(1)}, u32[]{:S(2)}, u32[]{:S(2)}) collective-permute-start(bf16[64,768]{1,0:T(8,128)(2,1)S(1)} %get-tuple-element.85), channel_id=1, source_target_pairs={{0,7},{1,2},{2,1},{3,4},{4,3},{5,6},{6,5},{7,0},{8,15},{9,10},{10,... | collective-permute-start | bytes 294920 | tf_op jit(solution)/shard_map/ppermute | solution.py:140
  108.8 10.6 %collective-permute-start.41 = (bf16[64,2048]{1,0:T(8,128)(2,1)}, bf16[64,2048]{1,0:T(8,128)(2,1)}, u32[]{:S(2)}, u32[]{:S(2)}) collective-permute-start(bf16[64,2048]{1,0:T(8,128)(2,1)} %shard_map.60), channel_id=1, source_target_pairs={{16,24},{17,25},{18,26},{19,27},{20,28},{21,29},{22,30},{23,31},{2... | collective-permute-start | bytes 786440 | tf_op jit(solution)/shard_map/ppermute | solution.py:238
  110.6 1.7 %collective-permute-start.35 = (bf16[64,768]{1,0:T(8,128)(2,1)S(1)}, bf16[64,768]{1,0:T(8,128)(2,1)S(1)}, u32[]{:S(2)}, u32[]{:S(2)}) collective-permute-start(bf16[64,768]{1,0:T(8,128)(2,1)S(1)} %get-tuple-element.82), channel_id=1, source_target_pairs={{0,1},{1,0},{2,3},{3,2},{4,5},{5,4},{6,7},{7,6},{8,9},{9,8},{10,11... | collective-permute-start | bytes 294920 | tf_op jit(solution)/shard_map/ppermute | solution.py:137
  110.7 5.0 %collective-permute-start.36 = (bf16[64,768]{1,0:T(8,128)(2,1)S(1)}, bf16[64,768]{1,0:T(8,128)(2,1)S(1)}, u32[]{:S(2)}, u32[]{:S(2)}) collective-permute-start(bf16[64,768]{1,0:T(8,128)(2,1)S(1)} %get-tuple-element.83), channel_id=1, source_target_pairs={{0,7},{1,2},{2,1},{3,4},{4,3},{5,6},{6,5},{7,0},{8,15},{9,10},{10,... | collective-permute-start | bytes 294920 | tf_op jit(solution)/shard_map/ppermute | solution.py:140
  118.0 10.8 %collective-permute-start.40 = (bf16[64,2048]{1,0:T(8,128)(2,1)}, bf16[64,2048]{1,0:T(8,128)(2,1)}, u32[]{:S(2)}, u32[]{:S(2)}) collective-permute-start(bf16[64,2048]{1,0:T(8,128)(2,1)} %shard_map.61), channel_id=1, source_target_pairs={{16,24},{17,25},{18,26},{19,27},{20,28},{21,29},{22,30},{23,31},{2... | collective-permute-start | bytes 786440 | tf_op jit(solution)/shard_map/ppermute | solution.py:238
  118.4 3.8 %collective-permute-start.44 = (bf16[64,768]{1,0:T(8,128)(2,1)}, bf16[64,768]{1,0:T(8,128)(2,1)S(1)}, u32[]{:S(2)}, u32[]{:S(2)}) collective-permute-start(bf16[64,768]{1,0:T(8,128)(2,1)} %get-tuple-element.81), channel_id=1, source_target_pairs={{0,1},{1,0},{2,3},{3,2},{4,5},{5,4},{6,7},{7,6},{8,9},{9,8},{10,11... | collective-permute-start | bytes 294920 | tf_op jit(solution)/shard_map/ppermute | solution.py:137
  118.4 5.3 %collective-permute-start.45 = (bf16[64,768]{1,0:T(8,128)(2,1)}, bf16[64,768]{1,0:T(8,128)(2,1)S(1)}, u32[]{:S(2)}, u32[]{:S(2)}) collective-permute-start(bf16[64,768]{1,0:T(8,128)(2,1)} %get-tuple-element.80), channel_id=1, source_target_pairs={{0,7},{1,2},{2,1},{3,4},{4,3},{5,6},{6,5},{7,0},{8,15},{9,10},{10,... | collective-permute-start | bytes 294920 | tf_op jit(solution)/shard_map/ppermute | solution.py:140
  120.4 10.7 %collective-permute-start.42 = (bf16[64,768]{1,0:T(8,128)(2,1)S(1)}, bf16[64,768]{1,0:T(8,128)(2,1)S(1)}, u32[]{:S(2)}, u32[]{:S(2)}) collective-permute-start(bf16[64,768]{1,0:T(8,128)(2,1)S(1)} %get-tuple-element.78), channel_id=1, source_target_pairs={{0,1},{1,0},{2,3},{3,2},{4,5},{5,4},{6,7},{7,6},{8,9},{9,8},{10,11... | collective-permute-start | bytes 294920 | tf_op jit(solution)/shard_map/ppermute | solution.py:137
  120.5 10.6 %collective-permute-start.43 = (bf16[64,768]{1,0:T(8,128)(2,1)S(1)}, bf16[64,768]{1,0:T(8,128)(2,1)S(1)}, u32[]{:S(2)}, u32[]{:S(2)}) collective-permute-start(bf16[64,768]{1,0:T(8,128)(2,1)S(1)} %get-tuple-element.79), channel_id=1, source_target_pairs={{0,7},{1,2},{2,1},{3,4},{4,3},{5,6},{6,5},{7,0},{8,15},{9,10},{10,... | collective-permute-start | bytes 294920 | tf_op jit(solution)/shard_map/ppermute | solution.py:140
  126.2 9.8 %collective-permute-start.46 = (bf16[64,2048]{1,0:T(8,128)(2,1)S(1)}, bf16[64,2048]{1,0:T(8,128)(2,1)S(1)}, u32[]{:S(2)}, u32[]{:S(2)}) collective-permute-start(bf16[64,2048]{1,0:T(8,128)(2,1)S(1)} %shard_map.62), channel_id=1, source_target_pairs={{24,16},{25,17},{26,18},{27,19},{28,20},{29,21},{30,22},{31,23},{1... | collective-permute-start | bytes 786440 | tf_op jit(solution)/shard_map/ppermute | solution.py:238
  129.7 3.4 %collective-permute-start.47 = (bf16[64,768]{1,0:T(8,128)(2,1)S(1)}, bf16[64,768]{1,0:T(8,128)(2,1)S(1)}, u32[]{:S(2)}, u32[]{:S(2)}) collective-permute-start(bf16[64,768]{1,0:T(8,128)(2,1)S(1)} %get-tuple-element.77), channel_id=1, source_target_pairs={{0,1},{1,0},{2,3},{3,2},{4,5},{5,4},{6,7},{7,6},{8,9},{9,8},{10,11... | collective-permute-start | bytes 294920 | tf_op jit(solution)/shard_map/ppermute | solution.py:137
  129.8 5.2 %collective-permute-start.48 = (bf16[64,768]{1,0:T(8,128)(2,1)S(1)}, bf16[64,768]{1,0:T(8,128)(2,1)S(1)}, u32[]{:S(2)}, u32[]{:S(2)}) collective-permute-start(bf16[64,768]{1,0:T(8,128)(2,1)S(1)} %get-tuple-element.76), channel_id=1, source_target_pairs={{0,7},{1,2},{2,1},{3,4},{4,3},{5,6},{6,5},{7,0},{8,15},{9,10},{10,... | collective-permute-start | bytes 294920 | tf_op jit(solution)/shard_map/ppermute | solution.py:140
  (19 other events, 85.1 us)

commit v3 on v2

v3 whole, which is shorter than its diff:
```python
import jax
import jax.numpy as jnp
from jax import lax
from jax.experimental import pallas as pl
from jax.experimental.pallas import tpu as pltpu
from jax.sharding import PartitionSpec as P

HALO = 3
CEILING = 2.0
LAG = 3
AHEAD = 2


def tie(value, *after):
    return lax.optimization_barrier((value, *after))[0]


def in_hbm(value):
    return pltpu.with_memory_space_constraint(value, pltpu.HBM)


def stage_kernel(copies, bias_rows, where_ref, bias_ref, weights_ref, inputs_ref, *refs):
    outs, bias_buffer, bias_sem, sems = refs[:-3], refs[-3], refs[-2], refs[-1]
    sources = {"weights": weights_ref, "inputs": inputs_ref}

    def run(side):
        bias_copy = pltpu.make_async_copy(bias_ref, bias_buffer, bias_sem)
        bias_copy.start()
        started = []
        for k, (out, rows, name, index) in enumerate(copies[side]):
            target = outs[out].at[rows]
            started.append(pltpu.make_async_copy(sources[name].at[index], target, sems.at[k]))
            started[-1].start()
        bias_copy.wait()
        for out, row, layer, first, count, block in bias_rows[side]:
            own = bias_buffer[layer : layer + 1, first * block : (first + count) * block]
            own = own.astype(jnp.float32)
            parts = [own[:, k * block : (k + 1) * block] for k in range(count)]
            parts.append(jnp.zeros((16 - count, block), jnp.float32))
            outs[out][row : row + 16] = jnp.concatenate(parts, axis=0).astype(jnp.bfloat16)
        for copy in started:
            copy.wait()

    @pl.when(where_ref[1] == 0)
    def _():
        run(0)

    @pl.when(where_ref[1] != 0)
    def _():
        run(1)


def layers_kernel(sizes, step, chunks, halo_row, next_place, final, *refs):
    layer_count, block_count, band_count, block, margin, share = sizes
    where_ref, offsets_ref, bias_ref, weights_ref = refs[:4]
    refs = refs[4:]
    table_refs, refs = refs[: 2 * (layer_count - 1)], refs[2 * (layer_count - 1) :]
    source_ref, near_ref, far_ref = refs[:3]
    refs = refs[3:]
    if next_place:
        inputs_ref, out_ref, next_ref, *buffers, sem = refs
        batch, target = next_place
        following = pltpu.make_async_copy(
            inputs_ref.at[batch, pl.ds(target * share, share)], next_ref, sem
        )
        following.start()
    elif final:
        *done_refs, last_ref, all_ref = refs[: final + 2]
        out_ref, buffers = all_ref.at[final - 1], refs[final + 2 :]
    else:
        out_ref, *buffers = refs
    even = where_ref[1] == 0
    chunk = step - LAG * where_ref[0]
    edge = margin * block
    width = block_count * block
    depth = band_count * block
    rows = pl.ds(halo_row, share)
    active = jnp.logical_and(chunk >= 0, chunk < chunks)

    @pl.when(active)
    def _():
        first = buffers[0]
        near, far = near_ref[rows, :], far_ref[rows, :]
        first[:, :edge] = jnp.where(even, far, near)
        first[:, edge + width :] = jnp.where(even, near, far)
        first[:, edge : edge + width] = source_ref[...]

        bias = bias_ref[...].astype(jnp.float32)
        for layer in range(layer_count):
            side = (layer_count - 1 - layer) * HALO
            source = buffers[layer]
            shift = [offsets_ref[layer, band] for band in range(band_count)]
            if side:
                tables = table_refs[2 * layer : 2 * layer + 2]
                last = slice(side * depth, side * depth + 16)
                sides = [table[last].astype(jnp.float32) for table in tables]
                before_bias = jnp.where(even, sides[1], sides[0])
                after_bias = jnp.where(even, sides[0], sides[1])
            for j in range(block_count + 2 * side):
                own = j - side
                x = jnp.concatenate(
                    [
                        source[:, pl.ds(pl.multiple_of((j + HALO + s) * block, block), block)]
                        for s in shift
                    ],
                    axis=1,
                )
                if own < 0:
                    k = slice(j * depth, (j + 1) * depth)
                    w = jnp.where(even, tables[1][k], tables[0][k])
                    b = before_bias[j : j + 1]
                elif own >= block_count:
                    k = own - block_count
                    b = after_bias[k : k + 1]
                    k = slice(k * depth, (k + 1) * depth)
                    w = jnp.where(even, tables[0][k], tables[1][k])
                else:
                    w = weights_ref[layer, own].reshape(depth, block)
                    b = bias[layer : layer + 1, own * block : (own + 1) * block]
                y = jnp.dot(x, w, preferred_element_type=jnp.float32) + b
                y = jnp.clip(y, 0.0, CEILING).astype(jnp.bfloat16)
                if layer < layer_count - 1:
                    buffers[layer + 1][:, j * block : (j + 1) * block] = y
                else:
                    out_ref[:, j * block : (j + 1) * block] = y

    if next_place:
        following.wait()
    if final:
        @pl.when(active)
        def _():
            for batch in range(final - 1):
                all_ref[batch] = last_ref[batch]

        @pl.when(jnp.logical_not(active))
        def _():
            for batch in range(final):
                all_ref[batch] = done_refs[batch][...]


def shards(inputs, weights, bias, offsets):
    sections = lax.axis_size("section")
    neurons = lax.axis_size("neuron")
    both = ("section", "neuron")
    section = lax.axis_index("section")
    odd = lax.axis_index("neuron") % 2
    batches, rows, width = inputs.shape
    layer_count, block_count, band_count, block, _ = weights.shape
    margin = layer_count * HALO
    edge = margin * block
    share = rows // sections
    depth = band_count * block
    places = [(batch, target) for target in range(sections) for batch in range(batches)]
    chunks = len(places)
    assert chunks <= sections * LAG and neurons % 2 == 0 and chunks > LAG

    def send_near(value):
        pairs = [
            (s * neurons + n, s * neurons + (n ^ 1))
            for s in range(sections)
            for n in range(neurons)
        ]
        return lax.ppermute(value, both, pairs)

    def send_far(value, which=range(sections)):
        pairs = []
        for s in range(sections):
            for n in range(neurons):
                other = (n + (1 if n % 2 else -1)) % neurons if s in which else n ^ 1
                pairs.append((s * neurons + n, s * neurons + other))
        return lax.ppermute(value, both, pairs)

    where = jnp.stack([section, odd]).astype(jnp.int32)
    here_is = [section == s for s in range(sections - 1)]
    even, inputs, weights, bias, offsets, where, *here_is = lax.optimization_barrier(
        (odd == 0, inputs, weights, bias, offsets, where, *here_is)
    )
    sizes = (layer_count, block_count, band_count, block, margin, share)
    smem = pl.BlockSpec(memory_space=pltpu.SMEM)
    vmem = pl.BlockSpec(memory_space=pltpu.VMEM)
    hbm = pl.BlockSpec(memory_space=pltpu.HBM)
    bf16 = jnp.bfloat16
    limit = pltpu.CompilerParams(vmem_limit_bytes=8 * 1024 * 1024)

    copies, bias_rows, shapes = [[], []], [[], []], []
    for far in (True, False):
        for parity in range(2):
            end = pl.ds(0 if far == (parity == 0) else width - edge, edge)
            for k in range(AHEAD):
                batch, target = places[k]
                index = (batch, pl.ds(target * share, share), end)
                copies[parity].append((len(shapes), pl.ds(k * share, share), "inputs", index))
        shapes.append((AHEAD * share, edge))
    for layer in range(layer_count - 1):
        side = (layer_count - 1 - layer) * HALO
        for far in (True, False):
            for parity in range(2):
                first = 0 if far == (parity == 0) else block_count - side
                index = (layer, pl.ds(first * depth, side * depth))
                copies[parity].append((len(shapes), pl.ds(0, side * depth), "weights", index))
                bias_rows[parity].append((len(shapes), side * depth, layer, first, side, block))
            shapes.append((side * depth + 16, block))
    for k in range(AHEAD):
        batch, target = places[k]
        index = (batch, pl.ds(target * share, share))
        for parity in range(2):
            copies[parity].append((len(shapes), pl.ds(0, share), "inputs", index))
        shapes.append((share, width))
    packed = pl.pallas_call(
        lambda *refs: stage_kernel(copies, bias_rows, *refs),
        in_specs=[smem, hbm, hbm, hbm],
        out_specs=[vmem] * len(shapes),
        out_shape=[pltpu.VMEM(shape, bf16) for shape in shapes],
        scratch_shapes=[
            pltpu.VMEM(bias.shape, bf16),
            pltpu.SemaphoreType.DMA,
            pltpu.SemaphoreType.DMA((len(copies[0]),)),
        ],
        compiler_params=limit,
    )(
        where,
        in_hbm(bias),
        in_hbm(weights.reshape(layer_count, block_count * depth, block)),
        in_hbm(inputs),
    )
    first_far = send_far(packed[0], [0])
    tables = []
    for layer in range(layer_count - 1):
        far = send_far(packed[2 + 2 * layer])
        tables += [send_near(packed[3 + 2 * layer]), far]
    first_halo = [send_near(packed[1]), first_far]

    def run(step, halo_row, source, halo, finished=None):
        scratch = [pltpu.VMEM((share, width + 2 * edge), bf16)]
        for layer in range(1, layer_count):
            side = (layer_count - layer) * HALO
            scratch.append(pltpu.VMEM((share, width + 2 * side * block), bf16))
        operands = [where, offsets, bias, weights, *tables, source, *halo]
        in_specs = [smem, smem] + [vmem] * (len(operands) - 2)
        out_shape = [jax.ShapeDtypeStruct((share, width), bf16)]
        next_place, final = None, 0
        if step + AHEAD < chunks:
            next_place = places[step + AHEAD]
            operands.append(in_hbm(inputs))
            in_specs.append(hbm)
            out_shape.append(pltpu.VMEM((share, width), bf16))
            scratch.append(pltpu.SemaphoreType.DMA)
        elif finished:
            final = batches
            operands += finished
            in_specs += [vmem] * len(finished)
            out_shape = [jax.ShapeDtypeStruct((batches, share, width), bf16)]
        return pl.pallas_call(
            lambda *refs: layers_kernel(sizes, step, chunks, halo_row, next_place, final, *refs),
            in_specs=in_specs,
            out_specs=[vmem] * len(out_shape),
            out_shape=out_shape,
            scratch_shapes=scratch,
            compiler_params=limit,
        )(*operands)

    last = sections - 1

    def hop(step, out):
        moves = [(s, s + 1) for s in range(last) if 0 <= step - LAG * s < chunks]
        done = step - LAG * last
        if done >= 0 and places[done][1] < last:
            moves.append((last, places[done][1]))
        idle = [s for s in range(sections) if s not in [a for a, _ in moves]]
        open_ = [s for s in range(sections) if s not in [b for _, b in moves]]
        pairs = [(a * neurons + n, b * neurons + n) for a, b in moves for n in range(neurons)]
        for a, b in zip(
            [s for s in idle if s not in open_] + [s for s in idle if s in open_],
            [s for s in open_ if s not in idle] + [s for s in open_ if s in idle],
        ):
            pairs += [
                (a * neurons + n, b * neurons + (n ^ 1 if a == b else n)) for n in range(neurons)
            ]
        return lax.ppermute(out, both, pairs)

    steps = chunks + LAG * last
    own = {k: packed[k - AHEAD] for k in range(AHEAD)}
    sources, halos, sent, hops = {}, {}, {}, {}
    finished = [None] * batches
    ended = []
    for step in range(steps):
        if step < AHEAD:
            source, halo, halo_row = own[step], first_halo, step * share
        else:
            source, halo, halo_row = sources[step], halos[step], 0
        source = tie(source, *halo, *sent.get(step + 1, ()))
        ending = step == steps - 1
        if ending:
            (result,) = run(step, halo_row, source, halo, finished + [jnp.stack(ended)])
            return result
        out, *following = run(step, halo_row, source, halo)
        if following:
            own[step + AHEAD] = following[0]
        done = step - LAG * last
        if done < 0 or places[done][1] < last:
            hops[step] = hop(step, out)
        else:
            ended.append(out)
        coming = step + AHEAD
        if coming < steps:
            after = (out, *halos.get(coming - 1, ()))
            if coming < LAG:
                here = tie(own[coming], *after)
            else:
                here = tie(hops[coming - LAG], *after)
                if coming < chunks:
                    here = jnp.where(here_is[0], own[coming], here)
            sources[coming] = here
            low, high = here[:, :edge], here[:, width - edge :]
            sent[coming] = (jnp.where(even, low, high), jnp.where(even, high, low))
            which = [s for s in range(sections) if 0 <= coming - LAG * s < chunks]
            far = send_far(sent[coming][0], which)
            halos[coming] = [send_near(sent[coming][1]), far]
        back = step - 1 - LAG * last
        if back >= 0 and places[back][1] < last:
            batch, target = places[back]
            arrived = hops[step - 1]
            if finished[batch] is not None:
                arrived = jnp.where(here_is[target], arrived, finished[batch])
            finished[batch] = arrived


def solution(mesh):
    in_specs = (
        P(None, None, "neuron"),
        P("section", "neuron", None, None, None),
        P("section", "neuron"),
        P("section", None),
    )
    out_specs = P(None, "section", "neuron")
    return jax.shard_map(shards, mesh=mesh, in_specs=in_specs, out_specs=out_specs, check_vma=False)
```

time: 137 us -> 111 us (0.81)
  waiting for transfers between devices: 52.1 us -> 23.2 us
  starting transfers between devices: 45.6 us -> 58.6 us
  local copies, waits for them, and re-layouts: 5.98 us -> 0.01 us
  other arithmetic: 6 us -> 0.6 us
    ppermute x34, waiting for transfers between devices: 43.4 us -> 10.3 us  [the longest x17 9.16 us: send_far(): return lax.ppermute(value, both, pairs)]
    ppermute x15, starting transfers between devices: 21.1 us -> 40.6 us  [hop(): return lax.ppermute(out, both, pairs)]
    ppermute x34, starting transfers between devices: 24.4 us -> 18 us  [the longest x17 15 us: send_far(): return lax.ppermute(value, both, pairs)]
    unnamed x36 -> x6, local copies, waits for them, and re-layouts: 5.06 us -> 0.01 us
    ppermute x15, waiting for transfers between devices: 8.73 us -> 13 us  [hop(): return lax.ppermute(out, both, pairs)]
    select_n x19 -> x22, other arithmetic: 3.99 us -> 0.52 us  [the longest x15 0.28 us: shards(): sent[coming] = (jnp.where(even, low, high), jnp.where(even, high, low))]
    pallas_call x17, Pallas kernels: 21.8 us -> 24.5 us  [run(): pl.pallas_call(lambda *refs: layers_kernel(sizes, step, chunks, halo_row,...]
    pallas_call x2 -> x1, Pallas kernels: 4.97 us -> 2.35 us  [shards(): pl.pallas_call(lambda *refs: stage_kernel(copies, bias_rows, *refs), in_s...]
  transfers between devices with their start and end apart: 49 -> 49, of which waited for: 20 -> 21; matrix products, arithmetic and copies ran while one was open for 4% -> 0% of each run, Pallas kernels for 17% -> 20%
where the time goes in v3:
time: 111 us; the launch traced here: 110 us
  starting transfers between devices  58.6 us (53%)
  Pallas kernels  26.9 us (24%)
  waiting for transfers between devices  23.2 us (21%)
    ppermute x15, starting transfers between devices, hop(): return lax.ppermute(out, both, pairs)  40.6 us
    pallas_call x17, Pallas kernels, run(): pl.pallas_call(lambda *refs: layers_kernel(sizes, step, chunks, halo_row,...  24.5 us
    ppermute x17, starting transfers between devices, send_far(): return lax.ppermute(value, both, pairs)  15 us
    ppermute x15, waiting for transfers between devices, hop(): return lax.ppermute(out, both, pairs)  13 us
    ppermute x17, waiting for transfers between devices, send_far(): return lax.ppermute(value, both, pairs)  9.16 us
    ppermute x17, starting transfers between devices, send_near(): return lax.ppermute(value, both, pairs)  3.03 us
    pallas_call x1, Pallas kernels, shards(): pl.pallas_call(lambda *refs: stage_kernel(copies, bias_rows, *refs), in_s...  2.35 us
  transfers between devices with their start and end apart: 49, of which 21 were waited for; matrix products, arithmetic and copies ran while one was open for 0% of the time, Pallas kernels for 20%

profile of v3, /device:TPU:16, one launch (start us, length us, event | category | flops | bytes accessed | tf_op | source)
XLA Modules:
  0.0 109.7 jit_solution(13370694444663254321)
XLA Ops:
  0.1 2.4 %shard_map.46 = (bf16[128,768]{1,0:T(8,128)(2,1)S(1)}, bf16[128,768]{1,0:T(8,128)(2,1)S(1)}, bf16[1168,128]{1,0:T(8,128)(2,1)S(1)}, bf16[1168,128]{1,0:T(8,128)(...) custom-call(s32[2]{0:T(128)S(1)} %pad_add_fusion.refs_0_, bf16[2,2048]{1,0:T(2,128)(2,1)} %refs_2_.16, ...), custom_call_target="tpu_custom_call" | custom-call | tf_op jit(solution)/shard_map/pallas_call | solution.py:209
  2.5 2.5 %collective-permute-start.1 = (bf16[1168,128]{1,0:T(8,128)(2,1)S(1)}, bf16[1168,128]{1,0:T(8,128)(2,1)S(1)}, u32[]{:S(2)}, u32[]{:S(2)}) collective-permute-start(bf16[1168,128]{1,0:T(8,128)(2,1)S(1)} %get-tuple-element.70), channel_id=1, source_target_pairs={{0,7},{1,2},{2,1},{3,4},{4,3},{5,6},{6,5},{7,0},{8,15},{9,10},{10,... | collective-permute-start | bytes 897032 | tf_op jit(solution)/shard_map/ppermute | solution.py:171
  5.6 0.9 collective-permute-done.2.refs_7_
  6.8 5.5 %collective-permute-done.1.refs_5_ = bf16[1168,128]{1,0:T(8,128)(2,1)S(1)} collective-permute-done((bf16[1168,128]{1,0:T(8,128)(2,1)S(1)}, bf16[1168,128]{1,0:T(8,128)(2,1)S(1)}, u32[]{:S(2)}, u32[]{:S(2)}) %collective-permute-start.1) | collective-permute-done | bytes 299040 | tf_op jit(solution)/shard_map/ppermute | solution.py:171
  12.3 1.5 %shard_map.47 = (bf16[64,2048]{1,0:T(8,128)(2,1)S(1)}, bf16[64,2048]{1,0:T(8,128)(2,1)S(1)}) custom-call(s32[2]{0:T(128)S(1)} %pad_add_fusion.refs_0_, s32[2,3]{1,0:T(2,128)S(1)} %copy-done.2, bf16[2,2048]{1,0:T(2,128)(2,1)S(1)} %copy-done.1, bf16[2,16,3,128,128]{4,3,2,1,0:T(8,128)(2,1)S(1)} %copy-done, bf16[1168,128]{1,0:T(8,128)(2,1)S(1)} %collective-permute-done.refs_4_, ...), custom_call_target="tpu_custom_call" | custom-call | tf_op jit(solution)/shard_map/pallas_call | solution.py:253
  14.6 1.5 %shard_map.48 = (bf16[64,2048]{1,0:T(8,128)(2,1)S(1)}, bf16[64,2048]{1,0:T(8,128)(2,1)S(1)}) custom-call(s32[2]{0:T(128)S(1)} %pad_add_fusion.refs_0_, s32[2,3]{1,0:T(2,128)S(1)} %copy-done.2, bf16[2,2048]{1,0:T(2,128)(2,1)S(1)} %copy-done.1, bf16[2,16,3,128,128]{4,3,2,1,0:T(8,128)(2,1)S(1)} %copy-done, bf16[1168,128]{1,0:T(8,128)(2,1)S(1)} %collective-permute-done.refs_4_, ...), custom_call_target="tpu_custom_call" | custom-call | tf_op jit(solution)/shard_map/pallas_call | solution.py:253
  17.2 1.5 %shard_map.49 = (bf16[64,2048]{1,0:T(8,128)(2,1)S(1)}, bf16[64,2048]{1,0:T(8,128)(2,1)S(1)}) custom-call(s32[2]{0:T(128)S(1)} %pad_add_fusion.refs_0_, s32[2,3]{1,0:T(2,128)S(1)} %copy-done.2, bf16[2,2048]{1,0:T(2,128)(2,1)S(1)} %copy-done.1, bf16[2,16,3,128,128]{4,3,2,1,0:T(8,128)(2,1)S(1)} %copy-done, bf16[1168,128]{1,0:T(8,128)(2,1)S(1)} %collective-permute-done.refs_4_, ...), custom_call_target="tpu_custom_call" | custom-call | tf_op jit(solution)/shard_map/pallas_call | solution.py:253
  19.6 1.5 %shard_map.50 = (bf16[64,2048]{1,0:T(8,128)(2,1)S(1)}, bf16[64,2048]{1,0:T(8,128)(2,1)S(1)}) custom-call(s32[2]{0:T(128)S(1)} %pad_add_fusion.refs_0_, s32[2,3]{1,0:T(2,128)S(1)} %copy-done.2, bf16[2,2048]{1,0:T(2,128)(2,1)S(1)} %copy-done.1, bf16[2,16,3,128,128]{4,3,2,1,0:T(8,128)(2,1)S(1)} %copy-done, bf16[1168,128]{1,0:T(8,128)(2,1)S(1)} %collective-permute-done.refs_4_, ...), custom_call_target="tpu_custom_call" | custom-call | tf_op jit(solution)/shard_map/pallas_call | solution.py:253
  21.1 15.2 %collective-permute-start.15 = (bf16[64,2048]{1,0:T(8,128)(2,1)S(1)}, bf16[64,2048]{1,0:T(8,128)(2,1)S(1)}, u32[]{:S(2)}, u32[]{:S(2)}) collective-permute-start(bf16[64,2048]{1,0:T(8,128)(2,1)S(1)} %get-tuple-element.91), channel_id=1, source_target_pairs={{0,8},{1,9},{2,10},{3,11},{4,12},{5,13},{6,14},{7,15},{8,16},{9,17... | collective-permute-start | bytes 786440 | tf_op jit(solution)/shard_map/ppermute | solution.py:279
  36.9 1.5 %shard_map.51 = (bf16[64,2048]{1,0:T(8,128)(2,1)S(1)}, bf16[64,2048]{1,0:T(8,128)(2,1)S(1)}) custom-call(s32[2]{0:T(128)S(1)} %pad_add_fusion.refs_0_, s32[2,3]{1,0:T(2,128)S(1)} %copy-done.2, bf16[2,2048]{1,0:T(2,128)(2,1)S(1)} %copy-done.1, bf16[2,16,3,128,128]{4,3,2,1,0:T(8,128)(2,1)S(1)} %copy-done, bf16[1168,128]{1,0:T(8,128)(2,1)S(1)} %collective-permute-done.refs_4_, ...), custom_call_target="tpu_custom_call" | custom-call | tf_op jit(solution)/shard_map/pallas_call | solution.py:253
  38.4 4.1 %collective-permute-start.16 = (bf16[64,2048]{1,0:T(8,128)(2,1)S(1)}, bf16[64,2048]{1,0:T(8,128)(2,1)S(1)}, u32[]{:S(2)}, u32[]{:S(2)}) collective-permute-start(bf16[64,2048]{1,0:T(8,128)(2,1)S(1)} %get-tuple-element.95), channel_id=1, source_target_pairs={{0,8},{1,9},{2,10},{3,11},{4,12},{5,13},{6,14},{7,15},{8,16},{9,17... | collective-permute-start | bytes 786440 | tf_op jit(solution)/shard_map/ppermute | solution.py:279
  42.7 0.7 collective-permute-start.18
  43.4 1.5 %shard_map.52 = (bf16[64,2048]{1,0:T(8,128)(2,1)S(1)}, bf16[64,2048]{1,0:T(8,128)(2,1)S(1)}) custom-call(s32[2]{0:T(128)S(1)} %pad_add_fusion.refs_0_, s32[2,3]{1,0:T(2,128)S(1)} %copy-done.2, bf16[2,2048]{1,0:T(2,128)(2,1)S(1)} %copy-done.1, bf16[2,16,3,128,128]{4,3,2,1,0:T(8,128)(2,1)S(1)} %copy-done, bf16[1168,128]{1,0:T(8,128)(2,1)S(1)} %collective-permute-done.refs_4_, ...), custom_call_target="tpu_custom_call" | custom-call | tf_op jit(solution)/shard_map/pallas_call | solution.py:253
  44.9 3.0 %collective-permute-start.21 = (bf16[64,2048]{1,0:T(8,128)(2,1)S(1)}, bf16[64,2048]{1,0:T(8,128)(2,1)S(1)}, u32[]{:S(2)}, u32[]{:S(2)}) collective-permute-start(bf16[64,2048]{1,0:T(8,128)(2,1)S(1)} %get-tuple-element.99), channel_id=1, source_target_pairs={{0,8},{1,9},{2,10},{3,11},{4,12},{5,13},{6,14},{7,15},{8,16},{9,17... | collective-permute-start | bytes 786440 | tf_op jit(solution)/shard_map/ppermute | solution.py:279
  48.3 1.6 %collective-permute-start.20 = (bf16[64,768]{1,0:T(8,128)(2,1)S(1)}, bf16[64,768]{1,0:T(8,128)(2,1)S(1)}, u32[]{:S(2)}, u32[]{:S(2)}) collective-permute-start(bf16[64,768]{1,0:T(8,128)(2,1)S(1)} %get-tuple-element.141), channel_id=1, source_target_pairs={{0,7},{1,2},{2,1},{3,4},{4,3},{5,6},{6,5},{7,0},{8,15},{9,10},{10,... | collective-permute-start | bytes 294920 | tf_op jit(solution)/shard_map/ppermute | solution.py:171
  49.9 1.6 %shard_map.53 = bf16[64,2048]{1,0:T(8,128)(2,1)S(1)} custom-call(s32[2]{0:T(128)S(1)} %pad_add_fusion.refs_0_, s32[2,3]{1,0:T(2,128)S(1)} %copy-done.2, bf16[2,2048]{1,0:T(2,128)(2,1)S(1)} %copy-done.1, bf16[2,16,3,128,128]{4,3,2,1,0:T(8,128)(2,1)S(1)} %copy-done, bf16[1168,128]{1,0:T(8,128)(2,1)S(1)} %collective-permute-done.refs_4_, ...), custom_call_target="tpu_custom_call" | custom-call | tf_op jit(solution)/shard_map/pallas_call | solution.py:253
  51.6 2.3 %collective-permute-done.21.refs_6_ = bf16[64,2048]{1,0:T(8,128)(2,1)S(1)} collective-permute-done((bf16[64,2048]{1,0:T(8,128)(2,1)S(1)}, bf16[64,2048]{1,0:T(8,128)(2,1)S(1)}, u32[]{:S(2)}, u32[]{:S(2)}) %collective-permute-start.21) | collective-permute-done | bytes 262176 | tf_op jit(solution)/shard_map/ppermute | solution.py:279
  54.0 2.3 %collective-permute-start.24 = (bf16[64,768]{1,0:T(8,128)(2,1)S(1)}, bf16[64,768]{1,0:T(8,128)(2,1)S(1)}, u32[]{:S(2)}, u32[]{:S(2)}) collective-permute-start(bf16[64,768]{1,0:T(8,128)(2,1)S(1)} %get-tuple-element.140), channel_id=1, source_target_pairs={{0,1},{1,0},{2,3},{3,2},{4,5},{5,4},{6,7},{7,6},{8,15},{9,10},{10,... | collective-permute-start | bytes 294920 | tf_op jit(solution)/shard_map/ppermute | solution.py:171
  56.3 1.6 %shard_map.54 = bf16[64,2048]{1,0:T(8,128)(2,1)S(1)} custom-call(s32[2]{0:T(128)S(1)} %pad_add_fusion.refs_0_, s32[2,3]{1,0:T(2,128)S(1)} %copy-done.2, bf16[2,2048]{1,0:T(2,128)(2,1)S(1)} %copy-done.1, bf16[2,16,3,128,128]{4,3,2,1,0:T(8,128)(2,1)S(1)} %copy-done, bf16[1168,128]{1,0:T(8,128)(2,1)S(1)} %collective-permute-done.refs_4_, ...), custom_call_target="tpu_custom_call" | custom-call | tf_op jit(solution)/shard_map/pallas_call | solution.py:253
  58.0 2.1 %collective-permute-done.24.refs_8_ = bf16[64,768]{1,0:T(8,128)(2,1)S(1)} collective-permute-done((bf16[64,768]{1,0:T(8,128)(2,1)S(1)}, bf16[64,768]{1,0:T(8,128)(2,1)S(1)}, u32[]{:S(2)}, u32[]{:S(2)}) %collective-permute-start.24) | collective-permute-done | bytes 98336 | tf_op jit(solution)/shard_map/ppermute | solution.py:171
  60.1 0.6 collective-permute-done.25.refs_6_
  60.8 1.1 %collective-permute-start.27 = (bf16[64,768]{1,0:T(8,128)(2,1)S(1)}, bf16[64,768]{1,0:T(8,128)(2,1)S(1)}, u32[]{:S(2)}, u32[]{:S(2)}) collective-permute-start(bf16[64,768]{1,0:T(8,128)(2,1)S(1)} %get-tuple-element.138), channel_id=1, source_target_pairs={{0,1},{1,0},{2,3},{3,2},{4,5},{5,4},{6,7},{7,6},{8,15},{9,10},{10,... | collective-permute-start | bytes 294920 | tf_op jit(solution)/shard_map/ppermute | solution.py:171
  61.9 1.6 %shard_map.55 = bf16[64,2048]{1,0:T(8,128)(2,1)S(1)} custom-call(s32[2]{0:T(128)S(1)} %pad_add_fusion.refs_0_, s32[2,3]{1,0:T(2,128)S(1)} %copy-done.2, bf16[2,2048]{1,0:T(2,128)(2,1)S(1)} %copy-done.1, bf16[2,16,3,128,128]{4,3,2,1,0:T(8,128)(2,1)S(1)} %copy-done, bf16[1168,128]{1,0:T(8,128)(2,1)S(1)} %collective-permute-done.refs_4_, ...), custom_call_target="tpu_custom_call" | custom-call | tf_op jit(solution)/shard_map/pallas_call | solution.py:253
  63.5 1.3 %collective-permute-start.30 = (bf16[64,2048]{1,0:T(8,128)(2,1)S(1)}, bf16[64,2048]{1,0:T(8,128)(2,1)S(1)}, u32[]{:S(2)}, u32[]{:S(2)}) collective-permute-start(bf16[64,2048]{1,0:T(8,128)(2,1)S(1)} %shard_map.55), channel_id=1, source_target_pairs={{8,16},{9,17},{10,18},{11,19},{12,20},{13,21},{14,22},{15,23},{16,... | collective-permute-start | bytes 786440 | tf_op jit(solution)/shard_map/ppermute | solution.py:279
  64.9 1.0 collective-permute-done.22.refs_6_
  66.3 0.6 collective-permute-start.29
  66.9 1.6 %shard_map.56 = bf16[64,2048]{1,0:T(8,128)(2,1)S(1)} custom-call(s32[2]{0:T(128)S(1)} %pad_add_fusion.refs_0_, s32[2,3]{1,0:T(2,128)S(1)} %copy-done.2, bf16[2,2048]{1,0:T(2,128)(2,1)S(1)} %copy-done.1, bf16[2,16,3,128,128]{4,3,2,1,0:T(8,128)(2,1)S(1)} %copy-done, bf16[1168,128]{1,0:T(8,128)(2,1)S(1)} %collective-permute-done.refs_4_, ...), custom_call_target="tpu_custom_call" | custom-call | tf_op jit(solution)/shard_map/pallas_call | solution.py:253
  68.6 2.4 %collective-permute-start.34 = (bf16[64,2048]{1,0:T(8,128)(2,1)S(1)}, bf16[64,2048]{1,0:T(8,128)(2,1)S(1)}, u32[]{:S(2)}, u32[]{:S(2)}) collective-permute-start(bf16[64,2048]{1,0:T(8,128)(2,1)S(1)} %shard_map.56), channel_id=1, source_target_pairs={{8,16},{9,17},{10,18},{11,19},{12,20},{13,21},{14,22},{15,23},{16,... | collective-permute-start | bytes 786440 | tf_op jit(solution)/shard_map/ppermute | solution.py:279
  71.7 1.9 %collective-permute-start.33 = (bf16[64,768]{1,0:T(8,128)(2,1)S(1)}, bf16[64,768]{1,0:T(8,128)(2,1)S(1)}, u32[]{:S(2)}, u32[]{:S(2)}) collective-permute-start(bf16[64,768]{1,0:T(8,128)(2,1)S(1)} %get-tuple-element.134), channel_id=1, source_target_pairs={{0,1},{1,0},{2,3},{3,2},{4,5},{5,4},{6,7},{7,6},{8,9},{9,8},{10,11... | collective-permute-start | bytes 294920 | tf_op jit(solution)/shard_map/ppermute | solution.py:171
  73.6 1.6 %shard_map.57 = bf16[64,2048]{1,0:T(8,128)(2,1)S(1)} custom-call(s32[2]{0:T(128)S(1)} %pad_add_fusion.refs_0_, s32[2,3]{1,0:T(2,128)S(1)} %copy-done.2, bf16[2,2048]{1,0:T(2,128)(2,1)S(1)} %copy-done.1, bf16[2,16,3,128,128]{4,3,2,1,0:T(8,128)(2,1)S(1)} %copy-done, bf16[1168,128]{1,0:T(8,128)(2,1)S(1)} %collective-permute-done.refs_4_, ...), custom_call_target="tpu_custom_call" | custom-call | tf_op jit(solution)/shard_map/pallas_call | solution.py:253
  75.2 1.8 %collective-permute-start.31 = (bf16[64,2048]{1,0:T(8,128)(2,1)S(1)}, bf16[64,2048]{1,0:T(8,128)(2,1)S(1)}, u32[]{:S(2)}, u32[]{:S(2)}) collective-permute-start(bf16[64,2048]{1,0:T(8,128)(2,1)S(1)} %shard_map.57), channel_id=1, source_target_pairs={{8,16},{9,17},{10,18},{11,19},{12,20},{13,21},{14,22},{15,23},{16,... | collective-permute-start | bytes 786440 | tf_op jit(solution)/shard_map/ppermute | solution.py:279
  77.0 0.6 collective-permute-done.34.refs_6_
  77.7 1.8 %collective-permute-start.36 = (bf16[64,768]{1,0:T(8,128)(2,1)S(1)}, bf16[64,768]{1,0:T(8,128)(2,1)S(1)}, u32[]{:S(2)}, u32[]{:S(2)}) collective-permute-start(bf16[64,768]{1,0:T(8,128)(2,1)S(1)} %get-tuple-element.132), channel_id=1, source_target_pairs={{0,1},{1,0},{2,3},{3,2},{4,5},{5,4},{6,7},{7,6},{8,9},{9,8},{10,11... | collective-permute-start | bytes 294920 | tf_op jit(solution)/shard_map/ppermute | solution.py:171
  79.5 1.6 %shard_map.58 = bf16[64,2048]{1,0:T(8,128)(2,1)S(1)} custom-call(s32[2]{0:T(128)S(1)} %pad_add_fusion.refs_0_, s32[2,3]{1,0:T(2,128)S(1)} %copy-done.2, bf16[2,2048]{1,0:T(2,128)(2,1)S(1)} %copy-done.1, bf16[2,16,3,128,128]{4,3,2,1,0:T(8,128)(2,1)S(1)} %copy-done, bf16[1168,128]{1,0:T(8,128)(2,1)S(1)} %collective-permute-done.refs_4_, ...), custom_call_target="tpu_custom_call" | custom-call | tf_op jit(solution)/shard_map/pallas_call | solution.py:253
  81.1 2.6 %collective-permute-start.39 = (bf16[64,2048]{1,0:T(8,128)(2,1)S(1)}, bf16[64,2048]{1,0:T(8,128)(2,1)S(1)}, u32[]{:S(2)}, u32[]{:S(2)}) collective-permute-start(bf16[64,2048]{1,0:T(8,128)(2,1)S(1)} %shard_map.58), channel_id=1, source_target_pairs={{16,24},{17,25},{18,26},{19,27},{20,28},{21,29},{22,30},{23,31},{2... | collective-permute-start | bytes 786440 | tf_op jit(solution)/shard_map/ppermute | solution.py:279
  83.7 0.8 collective-permute-done.31.refs_6_
  85.0 1.6 %shard_map.59 = bf16[64,2048]{1,0:T(8,128)(2,1)S(1)} custom-call(s32[2]{0:T(128)S(1)} %pad_add_fusion.refs_0_, s32[2,3]{1,0:T(2,128)S(1)} %copy-done.2, bf16[2,2048]{1,0:T(2,128)(2,1)S(1)} %copy-done.1, bf16[2,16,3,128,128]{4,3,2,1,0:T(8,128)(2,1)S(1)} %copy-done, bf16[1168,128]{1,0:T(8,128)(2,1)S(1)} %collective-permute-done.refs_4_, ...), custom_call_target="tpu_custom_call" | custom-call | tf_op jit(solution)/shard_map/pallas_call | solution.py:253
  86.6 2.1 %collective-permute-start.43 = (bf16[64,2048]{1,0:T(8,128)(2,1)S(1)}, bf16[64,2048]{1,0:T(8,128)(2,1)S(1)}, u32[]{:S(2)}, u32[]{:S(2)}) collective-permute-start(bf16[64,2048]{1,0:T(8,128)(2,1)S(1)} %shard_map.59), channel_id=1, source_target_pairs={{16,24},{17,25},{18,26},{19,27},{20,28},{21,29},{22,30},{23,31},{2... | collective-permute-start | bytes 786440 | tf_op jit(solution)/shard_map/ppermute | solution.py:279
  88.7 0.9 collective-permute-done.39.refs_6_
  90.6 1.6 %shard_map.60 = bf16[64,2048]{1,0:T(8,128)(2,1)S(1)} custom-call(s32[2]{0:T(128)S(1)} %pad_add_fusion.refs_0_, s32[2,3]{1,0:T(2,128)S(1)} %copy-done.2, bf16[2,2048]{1,0:T(2,128)(2,1)S(1)} %copy-done.1, bf16[2,16,3,128,128]{4,3,2,1,0:T(8,128)(2,1)S(1)} %copy-done, bf16[1168,128]{1,0:T(8,128)(2,1)S(1)} %collective-permute-done.refs_4_, ...), custom_call_target="tpu_custom_call" | custom-call | tf_op jit(solution)/shard_map/pallas_call | solution.py:253
  92.2 2.6 %collective-permute-start.40 = (bf16[64,2048]{1,0:T(8,128)(2,1)S(1)}, bf16[64,2048]{1,0:T(8,128)(2,1)S(1)}, u32[]{:S(2)}, u32[]{:S(2)}) collective-permute-start(bf16[64,2048]{1,0:T(8,128)(2,1)S(1)} %shard_map.60), channel_id=1, source_target_pairs={{16,24},{17,25},{18,26},{19,27},{20,28},{21,29},{22,30},{23,31},{2... | collective-permute-start | bytes 786440 | tf_op jit(solution)/shard_map/ppermute | solution.py:279
  94.7 0.6 collective-permute-done.43.refs_6_
  95.9 0.6 shard_map.61
  96.5 4.6 %collective-permute-start.48 = (bf16[64,2048]{1,0:T(8,128)(2,1)S(1)}, bf16[64,2048]{1,0:T(8,128)(2,1)S(1)}, u32[]{:S(2)}, u32[]{:S(2)}) collective-permute-start(bf16[64,2048]{1,0:T(8,128)(2,1)S(1)} %shard_map.61), channel_id=1, source_target_pairs={{24,16},{25,17},{26,18},{27,19},{28,20},{29,21},{30,22},{31,23},{1... | collective-permute-start | bytes 786440 | tf_op jit(solution)/shard_map/ppermute | solution.py:279
  101.1 2.4 %collective-permute-done.40.refs_6_ = bf16[64,2048]{1,0:T(8,128)(2,1)S(1)} collective-permute-done((bf16[64,2048]{1,0:T(8,128)(2,1)S(1)}, bf16[64,2048]{1,0:T(8,128)(2,1)S(1)}, u32[]{:S(2)}, u32[]{:S(2)}) %collective-permute-start.40) | collective-permute-done | bytes 262176 | tf_op jit(solution)/shard_map/ppermute | solution.py:279
  104.1 0.6 shard_map.62
  105.0 3.2 %collective-permute-done.48 = bf16[64,2048]{1,0:T(8,128)(2,1)S(1)} collective-permute-done((bf16[64,2048]{1,0:T(8,128)(2,1)S(1)}, bf16[64,2048]{1,0:T(8,128)(2,1)S(1)}, u32[]{:S(2)}, u32[]{:S(2)}) %collective-permute-start.48) | collective-permute-done | bytes 262176 | tf_op jit(solution)/shard_map/ppermute | solution.py:279
  108.3 1.4 %shard_map.63 = bf16[2,64,2048]{2,1,0:T(8,128)(2,1)} custom-call(s32[2]{0:T(128)S(1)} %pad_add_fusion.refs_0_, s32[2,3]{1,0:T(2,128)S(1)} %copy-done.2, bf16[2,2048]{1,0:T(2,128)(2,1)S(1)} %copy-done.1, bf16[2,16,3,128,128]{4,3,2,1,0:T(8,128)(2,1)S(1)} %copy-done, bf16[1168,128]{1,0:T(8,128)(2,1)S(1)} %collective-permute-done.refs_4_, ...), custom_call_target="tpu_custom_call" | custom-call | tf_op jit(solution)/shard_map/pallas_call | solution.py:253
  (97 shorter events, 9.3 us)
Async XLA Ops:
  2.5 4.4 %collective-permute-start = (bf16[1168,128]{1,0:T(8,128)(2,1)S(1)}, bf16[1168,128]{1,0:T(8,128)(2,1)S(1)}, u32[]{:S(2)}, u32[]{:S(2)}) collective-permute-start(bf16[1168,128]{1,0:T(8,128)(2,1)S(1)} %get-tuple-element.69), channel_id=1, source_target_pairs={{0,1},{1,0},{2,3},{3,2},{4,5},{5,4},{6,7},{7,6},{8,9},{9,8},{10,11... | collective-permute-start | bytes 897032 | tf_op jit(solution)/shard_map/ppermute | solution.py:163
  2.5 9.7 %collective-permute-start.1 = (bf16[1168,128]{1,0:T(8,128)(2,1)S(1)}, bf16[1168,128]{1,0:T(8,128)(2,1)S(1)}, u32[]{:S(2)}, u32[]{:S(2)}) collective-permute-start(bf16[1168,128]{1,0:T(8,128)(2,1)S(1)} %get-tuple-element.70), channel_id=1, source_target_pairs={{0,7},{1,2},{2,1},{3,4},{4,3},{5,6},{6,5},{7,0},{8,15},{9,10},{10,... | collective-permute-start | bytes 897032 | tf_op jit(solution)/shard_map/ppermute | solution.py:171
  5.1 1.4 %collective-permute-start.2 = (bf16[128,768]{1,0:T(8,128)(2,1)S(1)}, bf16[128,768]{1,0:T(8,128)(2,1)S(1)}, u32[]{:S(2)}, u32[]{:S(2)}) collective-permute-start(bf16[128,768]{1,0:T(8,128)(2,1)S(1)} %get-tuple-element.73), channel_id=1, source_target_pairs={{0,1},{1,0},{2,3},{3,2},{4,5},{5,4},{6,7},{7,6},{8,9},{9,8},{10,11... | collective-permute-start | bytes 589832 | tf_op jit(solution)/shard_map/ppermute | solution.py:163
  5.1 1.7 %collective-permute-start.3 = (bf16[128,768]{1,0:T(8,128)(2,1)S(1)}, bf16[128,768]{1,0:T(8,128)(2,1)S(1)}, u32[]{:S(2)}, u32[]{:S(2)}) collective-permute-start(bf16[128,768]{1,0:T(8,128)(2,1)S(1)} %get-tuple-element.74), channel_id=1, source_target_pairs={{0,7},{1,2},{2,1},{3,4},{4,3},{5,6},{6,5},{7,0},{8,9},{9,8},{10,11... | collective-permute-start | bytes 589832 | tf_op jit(solution)/shard_map/ppermute | solution.py:171
  13.8 2.8 %collective-permute-start.4 = (bf16[64,2048]{1,0:T(8,128)(2,1)S(1)}, bf16[64,2048]{1,0:T(8,128)(2,1)S(1)}, u32[]{:S(2)}, u32[]{:S(2)}) collective-permute-start(bf16[64,2048]{1,0:T(8,128)(2,1)S(1)} %get-tuple-element.79), channel_id=1, source_target_pairs={{0,8},{1,9},{2,10},{3,11},{4,12},{5,13},{6,14},{7,15},{8,0},{9,1},... | collective-permute-start | bytes 786440 | tf_op jit(solution)/shard_map/ppermute | solution.py:279
  14.0 2.6 %collective-permute-start.5 = (bf16[64,768]{1,0:T(8,128)(2,1)S(1)}, bf16[64,768]{1,0:T(8,128)(2,1)S(1)}, u32[]{:S(2)}, u32[]{:S(2)}) collective-permute-start(bf16[64,768]{1,0:T(8,128)(2,1)S(1)} %get-tuple-element.151), channel_id=1, source_target_pairs={{0,1},{1,0},{2,3},{3,2},{4,5},{5,4},{6,7},{7,6},{8,9},{9,8},{10,11... | collective-permute-start | bytes 294920 | tf_op jit(solution)/shard_map/ppermute | solution.py:163
  14.5 2.1 %collective-permute-start.6 = (bf16[64,768]{1,0:T(8,128)(2,1)S(1)}, bf16[64,768]{1,0:T(8,128)(2,1)S(1)}, u32[]{:S(2)}, u32[]{:S(2)}) collective-permute-start(bf16[64,768]{1,0:T(8,128)(2,1)S(1)} %get-tuple-element.152), channel_id=1, source_target_pairs={{0,7},{1,2},{2,1},{3,4},{4,3},{5,6},{6,5},{7,0},{8,9},{9,8},{10,11... | collective-permute-start | bytes 294920 | tf_op jit(solution)/shard_map/ppermute | solution.py:171
  16.1 2.8 %collective-permute-start.9 = (bf16[64,2048]{1,0:T(8,128)(2,1)S(1)}, bf16[64,2048]{1,0:T(8,128)(2,1)S(1)}, u32[]{:S(2)}, u32[]{:S(2)}) collective-permute-start(bf16[64,2048]{1,0:T(8,128)(2,1)S(1)} %get-tuple-element.83), channel_id=1, source_target_pairs={{0,8},{1,9},{2,10},{3,11},{4,12},{5,13},{6,14},{7,15},{8,0},{9,1},... | collective-permute-start | bytes 786440 | tf_op jit(solution)/shard_map/ppermute | solution.py:279
  16.6 2.3 %collective-permute-start.8 = (bf16[64,768]{1,0:T(8,128)(2,1)S(1)}, bf16[64,768]{1,0:T(8,128)(2,1)S(1)}, u32[]{:S(2)}, u32[]{:S(2)}) collective-permute-start(bf16[64,768]{1,0:T(8,128)(2,1)S(1)} %get-tuple-element.149), channel_id=1, source_target_pairs={{0,7},{1,2},{2,1},{3,4},{4,3},{5,6},{6,5},{7,0},{8,15},{9,10},{10,... | collective-permute-start | bytes 294920 | tf_op jit(solution)/shard_map/ppermute | solution.py:171
  16.8 2.1 %collective-permute-start.7 = (bf16[64,768]{1,0:T(8,128)(2,1)S(1)}, bf16[64,768]{1,0:T(8,128)(2,1)S(1)}, u32[]{:S(2)}, u32[]{:S(2)}) collective-permute-start(bf16[64,768]{1,0:T(8,128)(2,1)S(1)} %get-tuple-element.150), channel_id=1, source_target_pairs={{0,1},{1,0},{2,3},{3,2},{4,5},{5,4},{6,7},{7,6},{8,9},{9,8},{10,11... | collective-permute-start | bytes 294920 | tf_op jit(solution)/shard_map/ppermute | solution.py:163
  18.7 17.5 %collective-permute-start.10 = (bf16[64,2048]{1,0:T(8,128)(2,1)S(1)}, bf16[64,2048]{1,0:T(8,128)(2,1)S(1)}, u32[]{:S(2)}, u32[]{:S(2)}) collective-permute-start(bf16[64,2048]{1,0:T(8,128)(2,1)S(1)} %get-tuple-element.87), channel_id=1, source_target_pairs={{0,8},{1,9},{2,10},{3,11},{4,12},{5,13},{6,14},{7,15},{8,0},{9,1},... | collective-permute-start | bytes 786440 | tf_op jit(solution)/shard_map/ppermute | solution.py:279
  19.0 17.3 %collective-permute-start.11 = (bf16[64,768]{1,0:T(8,128)(2,1)S(1)}, bf16[64,768]{1,0:T(8,128)(2,1)S(1)}, u32[]{:S(2)}, u32[]{:S(2)}) collective-permute-start(bf16[64,768]{1,0:T(8,128)(2,1)S(1)} %get-tuple-element.147), channel_id=1, source_target_pairs={{0,1},{1,0},{2,3},{3,2},{4,5},{5,4},{6,7},{7,6},{8,9},{9,8},{10,11... | collective-permute-start | bytes 294920 | tf_op jit(solution)/shard_map/ppermute | solution.py:163
  19.5 16.8 %collective-permute-start.12 = (bf16[64,768]{1,0:T(8,128)(2,1)S(1)}, bf16[64,768]{1,0:T(8,128)(2,1)S(1)}, u32[]{:S(2)}, u32[]{:S(2)}) collective-permute-start(bf16[64,768]{1,0:T(8,128)(2,1)S(1)} %get-tuple-element.148), channel_id=1, source_target_pairs={{0,7},{1,2},{2,1},{3,4},{4,3},{5,6},{6,5},{7,0},{8,15},{9,10},{10,... | collective-permute-start | bytes 294920 | tf_op jit(solution)/shard_map/ppermute | solution.py:171
  21.1 21.5 %collective-permute-start.15 = (bf16[64,2048]{1,0:T(8,128)(2,1)S(1)}, bf16[64,2048]{1,0:T(8,128)(2,1)S(1)}, u32[]{:S(2)}, u32[]{:S(2)}) collective-permute-start(bf16[64,2048]{1,0:T(8,128)(2,1)S(1)} %get-tuple-element.91), channel_id=1, source_target_pairs={{0,8},{1,9},{2,10},{3,11},{4,12},{5,13},{6,14},{7,15},{8,16},{9,17... | collective-permute-start | bytes 786440 | tf_op jit(solution)/shard_map/ppermute | solution.py:279
  36.4 6.2 %collective-permute-start.14 = (bf16[64,768]{1,0:T(8,128)(2,1)S(1)}, bf16[64,768]{1,0:T(8,128)(2,1)S(1)}, u32[]{:S(2)}, u32[]{:S(2)}) collective-permute-start(bf16[64,768]{1,0:T(8,128)(2,1)S(1)} %get-tuple-element.145), channel_id=1, source_target_pairs={{0,7},{1,2},{2,1},{3,4},{4,3},{5,6},{6,5},{7,0},{8,15},{9,10},{10,... | collective-permute-start | bytes 294920 | tf_op jit(solution)/shard_map/ppermute | solution.py:171
  36.4 6.1 %collective-permute-start.13 = (bf16[64,768]{1,0:T(8,128)(2,1)S(1)}, bf16[64,768]{1,0:T(8,128)(2,1)S(1)}, u32[]{:S(2)}, u32[]{:S(2)}) collective-permute-start(bf16[64,768]{1,0:T(8,128)(2,1)S(1)} %get-tuple-element.146), channel_id=1, source_target_pairs={{0,1},{1,0},{2,3},{3,2},{4,5},{5,4},{6,7},{7,6},{8,9},{9,8},{10,11... | collective-permute-start | bytes 294920 | tf_op jit(solution)/shard_map/ppermute | solution.py:163
  38.4 9.8 %collective-permute-start.16 = (bf16[64,2048]{1,0:T(8,128)(2,1)S(1)}, bf16[64,2048]{1,0:T(8,128)(2,1)S(1)}, u32[]{:S(2)}, u32[]{:S(2)}) collective-permute-start(bf16[64,2048]{1,0:T(8,128)(2,1)S(1)} %get-tuple-element.95), channel_id=1, source_target_pairs={{0,8},{1,9},{2,10},{3,11},{4,12},{5,13},{6,14},{7,15},{8,16},{9,17... | collective-permute-start | bytes 786440 | tf_op jit(solution)/shard_map/ppermute | solution.py:279
  42.6 5.3 %collective-permute-start.17 = (bf16[64,768]{1,0:T(8,128)(2,1)S(1)}, bf16[64,768]{1,0:T(8,128)(2,1)S(1)}, u32[]{:S(2)}, u32[]{:S(2)}) collective-permute-start(bf16[64,768]{1,0:T(8,128)(2,1)S(1)} %get-tuple-element.143), channel_id=1, source_target_pairs={{0,1},{1,0},{2,3},{3,2},{4,5},{5,4},{6,7},{7,6},{8,9},{9,8},{10,11... | collective-permute-start | bytes 294920 | tf_op jit(solution)/shard_map/ppermute | solution.py:163
  42.7 5.3 %collective-permute-start.18 = (bf16[64,768]{1,0:T(8,128)(2,1)S(1)}, bf16[64,768]{1,0:T(8,128)(2,1)S(1)}, u32[]{:S(2)}, u32[]{:S(2)}) collective-permute-start(bf16[64,768]{1,0:T(8,128)(2,1)S(1)} %get-tuple-element.144), channel_id=1, source_target_pairs={{0,7},{1,2},{2,1},{3,4},{4,3},{5,6},{6,5},{7,0},{8,15},{9,10},{10,... | collective-permute-start | bytes 294920 | tf_op jit(solution)/shard_map/ppermute | solution.py:171
  44.9 9.0 %collective-permute-start.21 = (bf16[64,2048]{1,0:T(8,128)(2,1)S(1)}, bf16[64,2048]{1,0:T(8,128)(2,1)S(1)}, u32[]{:S(2)}, u32[]{:S(2)}) collective-permute-start(bf16[64,2048]{1,0:T(8,128)(2,1)S(1)} %get-tuple-element.99), channel_id=1, source_target_pairs={{0,8},{1,9},{2,10},{3,11},{4,12},{5,13},{6,14},{7,15},{8,16},{9,17... | collective-permute-start | bytes 786440 | tf_op jit(solution)/shard_map/ppermute | solution.py:279
  48.3 5.6 %collective-permute-start.20 = (bf16[64,768]{1,0:T(8,128)(2,1)S(1)}, bf16[64,768]{1,0:T(8,128)(2,1)S(1)}, u32[]{:S(2)}, u32[]{:S(2)}) collective-permute-start(bf16[64,768]{1,0:T(8,128)(2,1)S(1)} %get-tuple-element.141), channel_id=1, source_target_pairs={{0,7},{1,2},{2,1},{3,4},{4,3},{5,6},{6,5},{7,0},{8,15},{9,10},{10,... | collective-permute-start | bytes 294920 | tf_op jit(solution)/shard_map/ppermute | solution.py:171
  49.9 4.0 %collective-permute-start.19 = (bf16[64,768]{1,0:T(8,128)(2,1)S(1)}, bf16[64,768]{1,0:T(8,128)(2,1)S(1)}, u32[]{:S(2)}, u32[]{:S(2)}) collective-permute-start(bf16[64,768]{1,0:T(8,128)(2,1)S(1)} %get-tuple-element.142), channel_id=1, source_target_pairs={{0,1},{1,0},{2,3},{3,2},{4,5},{5,4},{6,7},{7,6},{8,9},{9,8},{10,11... | collective-permute-start | bytes 294920 | tf_op jit(solution)/shard_map/ppermute | solution.py:163
  51.5 9.2 %collective-permute-start.25 = (bf16[64,2048]{1,0:T(8,128)(2,1)S(1)}, bf16[64,2048]{1,0:T(8,128)(2,1)S(1)}, u32[]{:S(2)}, u32[]{:S(2)}) collective-permute-start(bf16[64,2048]{1,0:T(8,128)(2,1)S(1)} %shard_map.53), channel_id=1, source_target_pairs={{0,8},{1,9},{2,10},{3,11},{4,12},{5,13},{6,14},{7,15},{8,16},{9,17... | collective-permute-start | bytes 786440 | tf_op jit(solution)/shard_map/ppermute | solution.py:279
  53.9 4.1 %collective-permute-start.23 = (bf16[64,768]{1,0:T(8,128)(2,1)S(1)}, bf16[64,768]{1,0:T(8,128)(2,1)S(1)}, u32[]{:S(2)}, u32[]{:S(2)}) collective-permute-start(bf16[64,768]{1,0:T(8,128)(2,1)S(1)} %get-tuple-element.139), channel_id=1, source_target_pairs={{0,1},{1,0},{2,3},{3,2},{4,5},{5,4},{6,7},{7,6},{8,9},{9,8},{10,11... | collective-permute-start | bytes 294920 | tf_op jit(solution)/shard_map/ppermute | solution.py:163
  54.0 6.0 %collective-permute-start.24 = (bf16[64,768]{1,0:T(8,128)(2,1)S(1)}, bf16[64,768]{1,0:T(8,128)(2,1)S(1)}, u32[]{:S(2)}, u32[]{:S(2)}) collective-permute-start(bf16[64,768]{1,0:T(8,128)(2,1)S(1)} %get-tuple-element.140), channel_id=1, source_target_pairs={{0,1},{1,0},{2,3},{3,2},{4,5},{5,4},{6,7},{7,6},{8,15},{9,10},{10,... | collective-permute-start | bytes 294920 | tf_op jit(solution)/shard_map/ppermute | solution.py:171
  57.9 8.0 %collective-permute-start.22 = (bf16[64,2048]{1,0:T(8,128)(2,1)S(1)}, bf16[64,2048]{1,0:T(8,128)(2,1)S(1)}, u32[]{:S(2)}, u32[]{:S(2)}) collective-permute-start(bf16[64,2048]{1,0:T(8,128)(2,1)S(1)} %shard_map.54), channel_id=1, source_target_pairs={{0,8},{1,9},{2,10},{3,11},{4,12},{5,13},{6,14},{7,15},{8,16},{9,17... | collective-permute-start | bytes 786440 | tf_op jit(solution)/shard_map/ppermute | solution.py:279
  60.7 5.2 %collective-permute-start.26 = (bf16[64,768]{1,0:T(8,128)(2,1)S(1)}, bf16[64,768]{1,0:T(8,128)(2,1)S(1)}, u32[]{:S(2)}, u32[]{:S(2)}) collective-permute-start(bf16[64,768]{1,0:T(8,128)(2,1)S(1)} %get-tuple-element.137), channel_id=1, source_target_pairs={{0,1},{1,0},{2,3},{3,2},{4,5},{5,4},{6,7},{7,6},{8,9},{9,8},{10,11... | collective-permute-start | bytes 294920 | tf_op jit(solution)/shard_map/ppermute | solution.py:163
  60.8 5.5 %collective-permute-start.27 = (bf16[64,768]{1,0:T(8,128)(2,1)S(1)}, bf16[64,768]{1,0:T(8,128)(2,1)S(1)}, u32[]{:S(2)}, u32[]{:S(2)}) collective-permute-start(bf16[64,768]{1,0:T(8,128)(2,1)S(1)} %get-tuple-element.138), channel_id=1, source_target_pairs={{0,1},{1,0},{2,3},{3,2},{4,5},{5,4},{6,7},{7,6},{8,15},{9,10},{10,... | collective-permute-start | bytes 294920 | tf_op jit(solution)/shard_map/ppermute | solution.py:171
  63.5 8.1 %collective-permute-start.30 = (bf16[64,2048]{1,0:T(8,128)(2,1)S(1)}, bf16[64,2048]{1,0:T(8,128)(2,1)S(1)}, u32[]{:S(2)}, u32[]{:S(2)}) collective-permute-start(bf16[64,2048]{1,0:T(8,128)(2,1)S(1)} %shard_map.55), channel_id=1, source_target_pairs={{8,16},{9,17},{10,18},{11,19},{12,20},{13,21},{14,22},{15,23},{16,... | collective-permute-start | bytes 786440 | tf_op jit(solution)/shard_map/ppermute | solution.py:279
  66.3 5.0 %collective-permute-start.29 = (bf16[64,768]{1,0:T(8,128)(2,1)S(1)}, bf16[64,768]{1,0:T(8,128)(2,1)S(1)}, u32[]{:S(2)}, u32[]{:S(2)}) collective-permute-start(bf16[64,768]{1,0:T(8,128)(2,1)S(1)} %get-tuple-element.135), channel_id=1, source_target_pairs={{0,1},{1,0},{2,3},{3,2},{4,5},{5,4},{6,7},{7,6},{8,15},{9,10},{10,... | collective-permute-start | bytes 294920 | tf_op jit(solution)/shard_map/ppermute | solution.py:171
  66.9 4.4 %collective-permute-start.28 = (bf16[64,768]{1,0:T(8,128)(2,1)S(1)}, bf16[64,768]{1,0:T(8,128)(2,1)S(1)}, u32[]{:S(2)}, u32[]{:S(2)}) collective-permute-start(bf16[64,768]{1,0:T(8,128)(2,1)S(1)} %get-tuple-element.136), channel_id=1, source_target_pairs={{0,1},{1,0},{2,3},{3,2},{4,5},{5,4},{6,7},{7,6},{8,9},{9,8},{10,11... | collective-permute-start | bytes 294920 | tf_op jit(solution)/shard_map/ppermute | solution.py:163
  68.6 9.0 %collective-permute-start.34 = (bf16[64,2048]{1,0:T(8,128)(2,1)S(1)}, bf16[64,2048]{1,0:T(8,128)(2,1)S(1)}, u32[]{:S(2)}, u32[]{:S(2)}) collective-permute-start(bf16[64,2048]{1,0:T(8,128)(2,1)S(1)} %shard_map.56), channel_id=1, source_target_pairs={{8,16},{9,17},{10,18},{11,19},{12,20},{13,21},{14,22},{15,23},{16,... | collective-permute-start | bytes 786440 | tf_op jit(solution)/shard_map/ppermute | solution.py:279
  71.6 6.0 %collective-permute-start.32 = (bf16[64,768]{1,0:T(8,128)(2,1)S(1)}, bf16[64,768]{1,0:T(8,128)(2,1)S(1)}, u32[]{:S(2)}, u32[]{:S(2)}) collective-permute-start(bf16[64,768]{1,0:T(8,128)(2,1)S(1)} %get-tuple-element.133), channel_id=1, source_target_pairs={{0,1},{1,0},{2,3},{3,2},{4,5},{5,4},{6,7},{7,6},{8,9},{9,8},{10,11... | collective-permute-start | bytes 294920 | tf_op jit(solution)/shard_map/ppermute | solution.py:163
  71.7 5.9 %collective-permute-start.33 = (bf16[64,768]{1,0:T(8,128)(2,1)S(1)}, bf16[64,768]{1,0:T(8,128)(2,1)S(1)}, u32[]{:S(2)}, u32[]{:S(2)}) collective-permute-start(bf16[64,768]{1,0:T(8,128)(2,1)S(1)} %get-tuple-element.134), channel_id=1, source_target_pairs={{0,1},{1,0},{2,3},{3,2},{4,5},{5,4},{6,7},{7,6},{8,9},{9,8},{10,11... | collective-permute-start | bytes 294920 | tf_op jit(solution)/shard_map/ppermute | solution.py:171
  75.2 9.3 %collective-permute-start.31 = (bf16[64,2048]{1,0:T(8,128)(2,1)S(1)}, bf16[64,2048]{1,0:T(8,128)(2,1)S(1)}, u32[]{:S(2)}, u32[]{:S(2)}) collective-permute-start(bf16[64,2048]{1,0:T(8,128)(2,1)S(1)} %shard_map.57), channel_id=1, source_target_pairs={{8,16},{9,17},{10,18},{11,19},{12,20},{13,21},{14,22},{15,23},{16,... | collective-permute-start | bytes 786440 | tf_op jit(solution)/shard_map/ppermute | solution.py:279
  77.6 6.1 %collective-permute-start.35 = (bf16[64,768]{1,0:T(8,128)(2,1)S(1)}, bf16[64,768]{1,0:T(8,128)(2,1)S(1)}, u32[]{:S(2)}, u32[]{:S(2)}) collective-permute-start(bf16[64,768]{1,0:T(8,128)(2,1)S(1)} %get-tuple-element.131), channel_id=1, source_target_pairs={{0,1},{1,0},{2,3},{3,2},{4,5},{5,4},{6,7},{7,6},{8,9},{9,8},{10,11... | collective-permute-start | bytes 294920 | tf_op jit(solution)/shard_map/ppermute | solution.py:163
  77.7 6.0 %collective-permute-start.36 = (bf16[64,768]{1,0:T(8,128)(2,1)S(1)}, bf16[64,768]{1,0:T(8,128)(2,1)S(1)}, u32[]{:S(2)}, u32[]{:S(2)}) collective-permute-start(bf16[64,768]{1,0:T(8,128)(2,1)S(1)} %get-tuple-element.132), channel_id=1, source_target_pairs={{0,1},{1,0},{2,3},{3,2},{4,5},{5,4},{6,7},{7,6},{8,9},{9,8},{10,11... | collective-permute-start | bytes 294920 | tf_op jit(solution)/shard_map/ppermute | solution.py:171
  81.1 8.5 %collective-permute-start.39 = (bf16[64,2048]{1,0:T(8,128)(2,1)S(1)}, bf16[64,2048]{1,0:T(8,128)(2,1)S(1)}, u32[]{:S(2)}, u32[]{:S(2)}) collective-permute-start(bf16[64,2048]{1,0:T(8,128)(2,1)S(1)} %shard_map.58), channel_id=1, source_target_pairs={{16,24},{17,25},{18,26},{19,27},{20,28},{21,29},{22,30},{23,31},{2... | collective-permute-start | bytes 786440 | tf_op jit(solution)/shard_map/ppermute | solution.py:279
  84.6 5.4 %collective-permute-start.38 = (bf16[64,768]{1,0:T(8,128)(2,1)S(1)}, bf16[64,768]{1,0:T(8,128)(2,1)S(1)}, u32[]{:S(2)}, u32[]{:S(2)}) collective-permute-start(bf16[64,768]{1,0:T(8,128)(2,1)S(1)} %get-tuple-element.129), channel_id=1, source_target_pairs={{0,1},{1,0},{2,3},{3,2},{4,5},{5,4},{6,7},{7,6},{8,9},{9,8},{10,11... | collective-permute-start | bytes 294920 | tf_op jit(solution)/shard_map/ppermute | solution.py:171
  84.9 5.0 %collective-permute-start.37 = (bf16[64,768]{1,0:T(8,128)(2,1)S(1)}, bf16[64,768]{1,0:T(8,128)(2,1)S(1)}, u32[]{:S(2)}, u32[]{:S(2)}) collective-permute-start(bf16[64,768]{1,0:T(8,128)(2,1)S(1)} %get-tuple-element.130), channel_id=1, source_target_pairs={{0,1},{1,0},{2,3},{3,2},{4,5},{5,4},{6,7},{7,6},{8,9},{9,8},{10,11... | collective-permute-start | bytes 294920 | tf_op jit(solution)/shard_map/ppermute | solution.py:163
  86.6 8.7 %collective-permute-start.43 = (bf16[64,2048]{1,0:T(8,128)(2,1)S(1)}, bf16[64,2048]{1,0:T(8,128)(2,1)S(1)}, u32[]{:S(2)}, u32[]{:S(2)}) collective-permute-start(bf16[64,2048]{1,0:T(8,128)(2,1)S(1)} %shard_map.59), channel_id=1, source_target_pairs={{16,24},{17,25},{18,26},{19,27},{20,28},{21,29},{22,30},{23,31},{2... | collective-permute-start | bytes 786440 | tf_op jit(solution)/shard_map/ppermute | solution.py:279
  90.0 4.8 %collective-permute-start.41 = (bf16[64,768]{1,0:T(8,128)(2,1)S(1)}, bf16[64,768]{1,0:T(8,128)(2,1)S(1)}, u32[]{:S(2)}, u32[]{:S(2)}) collective-permute-start(bf16[64,768]{1,0:T(8,128)(2,1)S(1)} %get-tuple-element.127), channel_id=1, source_target_pairs={{0,1},{1,0},{2,3},{3,2},{4,5},{5,4},{6,7},{7,6},{8,9},{9,8},{10,11... | collective-permute-start | bytes 294920 | tf_op jit(solution)/shard_map/ppermute | solution.py:163
  90.1 4.7 %collective-permute-start.42 = (bf16[64,768]{1,0:T(8,128)(2,1)S(1)}, bf16[64,768]{1,0:T(8,128)(2,1)S(1)}, u32[]{:S(2)}, u32[]{:S(2)}) collective-permute-start(bf16[64,768]{1,0:T(8,128)(2,1)S(1)} %get-tuple-element.128), channel_id=1, source_target_pairs={{0,1},{1,0},{2,3},{3,2},{4,5},{5,4},{6,7},{7,6},{8,9},{9,8},{10,11... | collective-permute-start | bytes 294920 | tf_op jit(solution)/shard_map/ppermute | solution.py:171
  92.2 11.3 %collective-permute-start.40 = (bf16[64,2048]{1,0:T(8,128)(2,1)S(1)}, bf16[64,2048]{1,0:T(8,128)(2,1)S(1)}, u32[]{:S(2)}, u32[]{:S(2)}) collective-permute-start(bf16[64,2048]{1,0:T(8,128)(2,1)S(1)} %shard_map.60), channel_id=1, source_target_pairs={{16,24},{17,25},{18,26},{19,27},{20,28},{21,29},{22,30},{23,31},{2... | collective-permute-start | bytes 786440 | tf_op jit(solution)/shard_map/ppermute | solution.py:279
  95.3 8.1 %collective-permute-start.44 = (bf16[64,768]{1,0:T(8,128)(2,1)S(1)}, bf16[64,768]{1,0:T(8,128)(2,1)S(1)}, u32[]{:S(2)}, u32[]{:S(2)}) collective-permute-start(bf16[64,768]{1,0:T(8,128)(2,1)S(1)} %get-tuple-element.125), channel_id=1, source_target_pairs={{0,1},{1,0},{2,3},{3,2},{4,5},{5,4},{6,7},{7,6},{8,9},{9,8},{10,11... | collective-permute-start | bytes 294920 | tf_op jit(solution)/shard_map/ppermute | solution.py:163
  95.4 8.1 %collective-permute-start.45 = (bf16[64,768]{1,0:T(8,128)(2,1)S(1)}, bf16[64,768]{1,0:T(8,128)(2,1)S(1)}, u32[]{:S(2)}, u32[]{:S(2)}) collective-permute-start(bf16[64,768]{1,0:T(8,128)(2,1)S(1)} %get-tuple-element.126), channel_id=1, source_target_pairs={{0,1},{1,0},{2,3},{3,2},{4,5},{5,4},{6,7},{7,6},{8,9},{9,8},{10,11... | collective-permute-start | bytes 294920 | tf_op jit(solution)/shard_map/ppermute | solution.py:171
  96.5 11.7 %collective-permute-start.48 = (bf16[64,2048]{1,0:T(8,128)(2,1)S(1)}, bf16[64,2048]{1,0:T(8,128)(2,1)S(1)}, u32[]{:S(2)}, u32[]{:S(2)}) collective-permute-start(bf16[64,2048]{1,0:T(8,128)(2,1)S(1)} %shard_map.61), channel_id=1, source_target_pairs={{24,16},{25,17},{26,18},{27,19},{28,20},{29,21},{30,22},{31,23},{1... | collective-permute-start | bytes 786440 | tf_op jit(solution)/shard_map/ppermute | solution.py:279
  103.6 1.4 %collective-permute-start.46 = (bf16[64,768]{1,0:T(8,128)(2,1)S(1)}, bf16[64,768]{1,0:T(8,128)(2,1)S(1)}, u32[]{:S(2)}, u32[]{:S(2)}) collective-permute-start(bf16[64,768]{1,0:T(8,128)(2,1)S(1)} %get-tuple-element.124), channel_id=1, source_target_pairs={{0,1},{1,0},{2,3},{3,2},{4,5},{5,4},{6,7},{7,6},{8,9},{9,8},{10,11... | collective-permute-start | bytes 294920 | tf_op jit(solution)/shard_map/ppermute | solution.py:163
  (4 other events, 38.2 us)

commit v4 on v3

--- a/solution.py
+++ b/solution.py
@@ -50,7 +50,7 @@
         run(1)
 
 
-def layers_kernel(sizes, step, chunks, halo_row, next_place, final, *refs):
+def layers_kernel(sizes, step, chunks, next_place, final, *refs):
     layer_count, block_count, band_count, block, margin, share = sizes
     where_ref, offsets_ref, bias_ref, weights_ref = refs[:4]
     refs = refs[4:]
@@ -74,13 +74,12 @@
     edge = margin * block
     width = block_count * block
     depth = band_count * block
-    rows = pl.ds(halo_row, share)
     active = jnp.logical_and(chunk >= 0, chunk < chunks)
 
     @pl.when(active)
     def _():
         first = buffers[0]
-        near, far = near_ref[rows, :], far_ref[rows, :]
+        near, far = near_ref[...], far_ref[...]
         first[:, :edge] = jnp.where(even, far, near)
         first[:, edge + width :] = jnp.where(even, near, far)
         first[:, edge : edge + width] = source_ref[...]
@@ -183,14 +182,14 @@
     limit = pltpu.CompilerParams(vmem_limit_bytes=8 * 1024 * 1024)
 
     copies, bias_rows, shapes = [[], []], [[], []], []
-    for far in (True, False):
-        for parity in range(2):
-            end = pl.ds(0 if far == (parity == 0) else width - edge, edge)
-            for k in range(AHEAD):
-                batch, target = places[k]
+    for k in range(AHEAD):
+        batch, target = places[k]
+        for far in (True, False):
+            for parity in range(2):
+                end = pl.ds(0 if far == (parity == 0) else width - edge, edge)
                 index = (batch, pl.ds(target * share, share), end)
-                copies[parity].append((len(shapes), pl.ds(k * share, share), "inputs", index))
-        shapes.append((AHEAD * share, edge))
+                copies[parity].append((len(shapes), pl.ds(0, share), "inputs", index))
+            shapes.append((share, edge))
     for layer in range(layer_count - 1):
         side = (layer_count - 1 - layer) * HALO
         for far in (True, False):
@@ -206,31 +205,43 @@
         for parity in range(2):
             copies[parity].append((len(shapes), pl.ds(0, share), "inputs", index))
         shapes.append((share, width))
-    packed = pl.pallas_call(
-        lambda *refs: stage_kernel(copies, bias_rows, *refs),
-        in_specs=[smem, hbm, hbm, hbm],
-        out_specs=[vmem] * len(shapes),
-        out_shape=[pltpu.VMEM(shape, bf16) for shape in shapes],
-        scratch_shapes=[
-            pltpu.VMEM(bias.shape, bf16),
-            pltpu.SemaphoreType.DMA,
-            pltpu.SemaphoreType.DMA((len(copies[0]),)),
-        ],
-        compiler_params=limit,
-    )(
-        where,
-        in_hbm(bias),
-        in_hbm(weights.reshape(layer_count, block_count * depth, block)),
-        in_hbm(inputs),
-    )
-    first_far = send_far(packed[0], [0])
-    tables = []
-    for layer in range(layer_count - 1):
-        far = send_far(packed[2 + 2 * layer])
-        tables += [send_near(packed[3 + 2 * layer]), far]
-    first_halo = [send_near(packed[1]), first_far]
-
-    def run(step, halo_row, source, halo, finished=None):
+    def stage(wanted, first):
+        at = {k: i for i, k in enumerate(wanted)}
+        my_copies = [[(at[c[0]], *c[1:]) for c in side if c[0] in at] for side in copies]
+        my_rows = [[(at[c[0]], *c[1:]) for c in side if c[0] in at] for side in bias_rows]
+        return pl.pallas_call(
+            lambda *refs: stage_kernel(my_copies, my_rows, *refs),
+            in_specs=[smem, hbm, hbm, hbm],
+            out_specs=[vmem] * len(wanted),
+            out_shape=[pltpu.VMEM(shapes[k], bf16) for k in wanted],
+            scratch_shapes=[
+                pltpu.VMEM(bias.shape, bf16),
+                pltpu.SemaphoreType.DMA,
+                pltpu.SemaphoreType.DMA((len(my_copies[0]),)),
+            ],
+            compiler_params=limit,
+        )(
+            tie(where, *first),
+            in_hbm(bias),
+            in_hbm(weights.reshape(layer_count, block_count * depth, block)),
+            in_hbm(inputs),
+        )
+
+    urgent = list(range(2 * AHEAD, 2 * AHEAD + 2 * (layer_count - 1), 2))
+    packed = dict(zip(urgent, stage(urgent, ())))
+    others = [k for k in range(len(shapes)) if k not in urgent]
+    packed.update(zip(others, stage(others, packed.values())))
+    halos = {}
+    for k in range(AHEAD):
+        if k == 1:
+            tables = []
+            for layer in range(layer_count - 1):
+                far = send_far(packed[2 * AHEAD + 2 * layer])
+                tables += [send_near(packed[2 * AHEAD + 1 + 2 * layer]), far]
+        far = send_far(packed[2 * k], [0])
+        halos[k] = [send_near(packed[2 * k + 1]), far]
+
+    def run(step, source, halo, finished=None):
         scratch = [pltpu.VMEM((share, width + 2 * edge), bf16)]
         for layer in range(1, layer_count):
             side = (layer_count - layer) * HALO
@@ -251,7 +262,7 @@
             in_specs += [vmem] * len(finished)
             out_shape = [jax.ShapeDtypeStruct((batches, share, width), bf16)]
         return pl.pallas_call(
-            lambda *refs: layers_kernel(sizes, step, chunks, halo_row, next_place, final, *refs),
+            lambda *refs: layers_kernel(sizes, step, chunks, next_place, final, *refs),
             in_specs=in_specs,
             out_specs=[vmem] * len(out_shape),
             out_shape=out_shape,
@@ -269,6 +280,9 @@
         idle = [s for s in range(sections) if s not in [a for a, _ in moves]]
         open_ = [s for s in range(sections) if s not in [b for _, b in moves]]
         pairs = [(a * neurons + n, b * neurons + n) for a, b in moves for n in range(neurons)]
+        if 0 < step <= LAG:
+            idle = [s for s in idle if s in open_]
+            open_ = idle
         for a, b in zip(
             [s for s in idle if s not in open_] + [s for s in idle if s in open_],
             [s for s in open_ if s not in idle] + [s for s in open_ if s in idle],
@@ -279,21 +293,22 @@
         return lax.ppermute(out, both, pairs)
 
     steps = chunks + LAG * last
-    own = {k: packed[k - AHEAD] for k in range(AHEAD)}
-    sources, halos, sent, hops = {}, {}, {}, {}
+    own = {k: packed[len(shapes) - AHEAD + k] for k in range(AHEAD)}
+    sources, sent, hops = {}, {}, {}
     finished = [None] * batches
     ended = []
     for step in range(steps):
         if step < AHEAD:
-            source, halo, halo_row = own[step], first_halo, step * share
+            source = own[step]
         else:
-            source, halo, halo_row = sources[step], halos[step], 0
+            source = sources[step]
+        halo = halos[step]
         source = tie(source, *halo, *sent.get(step + 1, ()))
         ending = step == steps - 1
         if ending:
-            (result,) = run(step, halo_row, source, halo, finished + [jnp.stack(ended)])
+            (result,) = run(step, source, halo, finished + [jnp.stack(ended)])
             return result
-        out, *following = run(step, halo_row, source, halo)
+        out, *following = run(step, source, halo)
         if following:
             own[step + AHEAD] = following[0]
         done = step - LAG * last
@@ -303,7 +318,7 @@
             ended.append(out)
         coming = step + AHEAD
         if coming < steps:
-            after = (out, *halos.get(coming - 1, ()))
+            after = (out, *halos[coming - 1]) if coming < steps - 1 else (out,)
             if coming < LAG:
                 here = tie(own[coming], *after)
             else:

time: 111 us -> 108 us (0.973)
  starting transfers between devices: 58.6 us -> 47.6 us
  waiting for transfers between devices: 23.2 us -> 30.3 us
  Pallas kernels: 26.9 us -> 28.2 us
    ppermute x15, starting transfers between devices: 40.6 us -> 28.5 us  [hop(): return lax.ppermute(out, both, pairs)]
    ppermute x15, waiting for transfers between devices: 13 us -> 18 us  [hop(): return lax.ppermute(out, both, pairs)]
    ppermute x17 -> x18, waiting for transfers between devices: 9.16 us -> 11.3 us  [send_far(): return lax.ppermute(value, both, pairs)]
    pallas_call x18 -> x19, Pallas kernels: 26.9 us -> 28.2 us  [the longest x17 24.7 us: run(): pl.pallas_call(lambda *refs: layers_kernel(sizes, step, chunks, next_plac...]
    ppermute x17 -> x18, starting transfers between devices: 3.03 us -> 3.9 us  [send_near(): return lax.ppermute(value, both, pairs)]
    ppermute x17 -> x18, starting transfers between devices: 15 us -> 15.2 us  [send_far(): return lax.ppermute(value, both, pairs)]
  transfers between devices with their start and end apart: 49 -> 51, of which waited for: 21 -> 21; matrix products, arithmetic and copies ran while one was open for 0% -> 0% of each run, Pallas kernels for 20% -> 24%
where the time goes in v4:
time: 108 us; the launch traced here: 107 us
  starting transfers between devices  47.6 us (44%)
  waiting for transfers between devices  30.3 us (28%)
  Pallas kernels  28.2 us (26%)
    ppermute x15, starting transfers between devices, hop(): return lax.ppermute(out, both, pairs)  28.5 us
    pallas_call x17, Pallas kernels, run(): pl.pallas_call(lambda *refs: layers_kernel(sizes, step, chunks, next_plac...  24.7 us
    ppermute x15, waiting for transfers between devices, hop(): return lax.ppermute(out, both, pairs)  18 us
    ppermute x18, starting transfers between devices, send_far(): return lax.ppermute(value, both, pairs)  15.2 us
    ppermute x18, waiting for transfers between devices, send_far(): return lax.ppermute(value, both, pairs)  11.3 us
    ppermute x18, starting transfers between devices, send_near(): return lax.ppermute(value, both, pairs)  3.9 us
    pallas_call x2, Pallas kernels, stage(): pl.pallas_call(lambda *refs: stage_kernel(my_copies, my_rows, *refs), in_...  3.48 us
  transfers between devices with their start and end apart: 51, of which 21 were waited for; matrix products, arithmetic and copies ran while one was open for 0% of the time, Pallas kernels for 24%

profile of v4, /device:TPU:16, one launch (start us, length us, event | category | flops | bytes accessed | tf_op | source)
XLA Modules:
  0.0 107.2 jit_solution(9193768623644996670)
XLA Ops:
  0.1 1.5 %shard_map.46 = bf16[1168,128]{1,0:T(8,128)(2,1)S(1)} custom-call(s32[2]{0:T(128)S(1)} %pad_add_fusion.refs_0_, bf16[2,2048]{1,0:T(2,128)(2,1)} %refs_2_.16, bf16[2,6144,128]{2,1,0:T(8,128)(2,1)} %bitcast.4, bf16[2,256,2048]{2,1,0:T(8,128)(2,1)} %refs_9_.5), custom_call_target="tpu_custom_call" | custom-call | tf_op jit(solution)/shard_map/pallas_call | solution.py:212
  1.7 2.0 %collective-permute-start.1 = (bf16[1168,128]{1,0:T(8,128)(2,1)S(1)}, bf16[1168,128]{1,0:T(8,128)(2,1)S(1)}, u32[]{:S(2)}, u32[]{:S(2)}) collective-permute-start(bf16[1168,128]{1,0:T(8,128)(2,1)S(1)} %shard_map.46), channel_id=1, source_target_pairs={{0,7},{1,2},{2,1},{3,4},{4,3},{5,6},{6,5},{7,0},{8,15},{9,10},{10,... | collective-permute-start | bytes 897032 | tf_op jit(solution)/shard_map/ppermute | solution.py:170
  3.6 1.9 %shard_map.47 = (bf16[64,768]{1,0:T(8,128)(2,1)S(1)}, bf16[64,768]{1,0:T(8,128)(2,1)S(1)}, bf16[64,768]{1,0:T(8,128)(2,1)S(1)}, bf16[64,768]{1,0:T(8,128)(2,1)S(...) custom-call(s32[2]{0:T(128)S(1)} %pad_add_fusion.refs_0_, ...), custom_call_target="tpu_custom_call" | custom-call | tf_op jit(solution)/shard_map/pallas_call | solution.py:212
  7.5 4.4 %collective-permute-done.1.refs_5_ = bf16[1168,128]{1,0:T(8,128)(2,1)S(1)} collective-permute-done((bf16[1168,128]{1,0:T(8,128)(2,1)S(1)}, bf16[1168,128]{1,0:T(8,128)(2,1)S(1)}, u32[]{:S(2)}, u32[]{:S(2)}) %collective-permute-start.1) | collective-permute-done | bytes 299040 | tf_op jit(solution)/shard_map/ppermute | solution.py:170
  11.9 1.5 %shard_map.48 = (bf16[64,2048]{1,0:T(8,128)(2,1)S(1)}, bf16[64,2048]{1,0:T(8,128)(2,1)S(1)}) custom-call(s32[2]{0:T(128)S(1)} %pad_add_fusion.refs_0_, s32[2,3]{1,0:T(2,128)S(1)} %copy-done.2, bf16[2,2048]{1,0:T(2,128)(2,1)S(1)} %copy-done.1, bf16[2,16,3,128,128]{4,3,2,1,0:T(8,128)(2,1)S(1)} %copy-done, bf16[1168,128]{1,0:T(8,128)(2,1)S(1)} %collective-permute-done.refs_4_, ...), custom_call_target="tpu_custom_call" | custom-call | tf_op jit(solution)/shard_map/pallas_call | solution.py:264
  14.2 1.5 %shard_map.49 = (bf16[64,2048]{1,0:T(8,128)(2,1)S(1)}, bf16[64,2048]{1,0:T(8,128)(2,1)S(1)}) custom-call(s32[2]{0:T(128)S(1)} %pad_add_fusion.refs_0_, s32[2,3]{1,0:T(2,128)S(1)} %copy-done.2, bf16[2,2048]{1,0:T(2,128)(2,1)S(1)} %copy-done.1, bf16[2,16,3,128,128]{4,3,2,1,0:T(8,128)(2,1)S(1)} %copy-done, bf16[1168,128]{1,0:T(8,128)(2,1)S(1)} %collective-permute-done.refs_4_, ...), custom_call_target="tpu_custom_call" | custom-call | tf_op jit(solution)/shard_map/pallas_call | solution.py:264
  15.7 2.3 %collective-permute-start.11 = (bf16[64,2048]{1,0:T(8,128)(2,1)S(1)}, bf16[64,2048]{1,0:T(8,128)(2,1)S(1)}, u32[]{:S(2)}, u32[]{:S(2)}) collective-permute-start(bf16[64,2048]{1,0:T(8,128)(2,1)S(1)} %get-tuple-element.87), channel_id=1, source_target_pairs={{0,8},{1,9},{2,10},{3,11},{4,12},{5,13},{6,14},{7,15},{16,17},{17,... | collective-permute-start | bytes 786440 | tf_op jit(solution)/shard_map/ppermute | solution.py:293
  18.7 1.5 %shard_map.50 = (bf16[64,2048]{1,0:T(8,128)(2,1)S(1)}, bf16[64,2048]{1,0:T(8,128)(2,1)S(1)}) custom-call(s32[2]{0:T(128)S(1)} %pad_add_fusion.refs_0_, s32[2,3]{1,0:T(2,128)S(1)} %copy-done.2, bf16[2,2048]{1,0:T(2,128)(2,1)S(1)} %copy-done.1, bf16[2,16,3,128,128]{4,3,2,1,0:T(8,128)(2,1)S(1)} %copy-done, bf16[1168,128]{1,0:T(8,128)(2,1)S(1)} %collective-permute-done.refs_4_, ...), custom_call_target="tpu_custom_call" | custom-call | tf_op jit(solution)/shard_map/pallas_call | solution.py:264
  20.3 2.0 %collective-permute-start.12 = (bf16[64,2048]{1,0:T(8,128)(2,1)S(1)}, bf16[64,2048]{1,0:T(8,128)(2,1)S(1)}, u32[]{:S(2)}, u32[]{:S(2)}) collective-permute-start(bf16[64,2048]{1,0:T(8,128)(2,1)S(1)} %get-tuple-element.91), channel_id=1, source_target_pairs={{0,8},{1,9},{2,10},{3,11},{4,12},{5,13},{6,14},{7,15},{16,17},{17,... | collective-permute-start | bytes 786440 | tf_op jit(solution)/shard_map/ppermute | solution.py:293
  22.9 1.5 %shard_map.51 = (bf16[64,2048]{1,0:T(8,128)(2,1)S(1)}, bf16[64,2048]{1,0:T(8,128)(2,1)S(1)}) custom-call(s32[2]{0:T(128)S(1)} %pad_add_fusion.refs_0_, s32[2,3]{1,0:T(2,128)S(1)} %copy-done.2, bf16[2,2048]{1,0:T(2,128)(2,1)S(1)} %copy-done.1, bf16[2,16,3,128,128]{4,3,2,1,0:T(8,128)(2,1)S(1)} %copy-done, bf16[1168,128]{1,0:T(8,128)(2,1)S(1)} %collective-permute-done.refs_4_, ...), custom_call_target="tpu_custom_call" | custom-call | tf_op jit(solution)/shard_map/pallas_call | solution.py:264
  24.4 1.3 %collective-permute-start.17 = (bf16[64,2048]{1,0:T(8,128)(2,1)S(1)}, bf16[64,2048]{1,0:T(8,128)(2,1)S(1)}, u32[]{:S(2)}, u32[]{:S(2)}) collective-permute-start(bf16[64,2048]{1,0:T(8,128)(2,1)S(1)} %get-tuple-element.95), channel_id=1, source_target_pairs={{0,8},{1,9},{2,10},{3,11},{4,12},{5,13},{6,14},{7,15},{8,16},{9,17... | collective-permute-start | bytes 786440 | tf_op jit(solution)/shard_map/ppermute | solution.py:293
  26.4 1.5 %shard_map.52 = (bf16[64,2048]{1,0:T(8,128)(2,1)S(1)}, bf16[64,2048]{1,0:T(8,128)(2,1)S(1)}) custom-call(s32[2]{0:T(128)S(1)} %pad_add_fusion.refs_0_, s32[2,3]{1,0:T(2,128)S(1)} %copy-done.2, bf16[2,2048]{1,0:T(2,128)(2,1)S(1)} %copy-done.1, bf16[2,16,3,128,128]{4,3,2,1,0:T(8,128)(2,1)S(1)} %copy-done, bf16[1168,128]{1,0:T(8,128)(2,1)S(1)} %collective-permute-done.refs_4_, ...), custom_call_target="tpu_custom_call" | custom-call | tf_op jit(solution)/shard_map/pallas_call | solution.py:264
  27.9 10.7 %collective-permute-start.18 = (bf16[64,2048]{1,0:T(8,128)(2,1)S(1)}, bf16[64,2048]{1,0:T(8,128)(2,1)S(1)}, u32[]{:S(2)}, u32[]{:S(2)}) collective-permute-start(bf16[64,2048]{1,0:T(8,128)(2,1)S(1)} %get-tuple-element.99), channel_id=1, source_target_pairs={{0,8},{1,9},{2,10},{3,11},{4,12},{5,13},{6,14},{7,15},{8,16},{9,17... | collective-permute-start | bytes 786440 | tf_op jit(solution)/shard_map/ppermute | solution.py:293
  38.7 1.7 %collective-permute-done.17 = bf16[64,2048]{1,0:T(8,128)(2,1)S(1)} collective-permute-done((bf16[64,2048]{1,0:T(8,128)(2,1)S(1)}, bf16[64,2048]{1,0:T(8,128)(2,1)S(1)}, u32[]{:S(2)}, u32[]{:S(2)}) %collective-permute-start.17) | collective-permute-done | bytes 262176 | tf_op jit(solution)/shard_map/ppermute | solution.py:293
  40.5 1.5 %collective-permute-start.20 = (bf16[64,768]{1,0:T(8,128)(2,1)S(1)}, bf16[64,768]{1,0:T(8,128)(2,1)S(1)}, u32[]{:S(2)}, u32[]{:S(2)}) collective-permute-start(bf16[64,768]{1,0:T(8,128)(2,1)S(1)} %get-tuple-element.148), channel_id=1, source_target_pairs={{0,7},{1,2},{2,1},{3,4},{4,3},{5,6},{6,5},{7,0},{8,15},{9,10},{10,... | collective-permute-start | bytes 294920 | tf_op jit(solution)/shard_map/ppermute | solution.py:170
  42.1 1.5 %shard_map.53 = (bf16[64,2048]{1,0:T(8,128)(2,1)S(1)}, bf16[64,2048]{1,0:T(8,128)(2,1)S(1)}) custom-call(s32[2]{0:T(128)S(1)} %pad_add_fusion.refs_0_, s32[2,3]{1,0:T(2,128)S(1)} %copy-done.2, bf16[2,2048]{1,0:T(2,128)(2,1)S(1)} %copy-done.1, bf16[2,16,3,128,128]{4,3,2,1,0:T(8,128)(2,1)S(1)} %copy-done, bf16[1168,128]{1,0:T(8,128)(2,1)S(1)} %collective-permute-done.refs_4_, ...), custom_call_target="tpu_custom_call" | custom-call | tf_op jit(solution)/shard_map/pallas_call | solution.py:264
  43.6 2.5 %collective-permute-start.23 = (bf16[64,2048]{1,0:T(8,128)(2,1)S(1)}, bf16[64,2048]{1,0:T(8,128)(2,1)S(1)}, u32[]{:S(2)}, u32[]{:S(2)}) collective-permute-start(bf16[64,2048]{1,0:T(8,128)(2,1)S(1)} %get-tuple-element.103), channel_id=1, source_target_pairs={{0,8},{1,9},{2,10},{3,11},{4,12},{5,13},{6,14},{7,15},{8,16},{9,17... | collective-permute-start | bytes 786440 | tf_op jit(solution)/shard_map/ppermute | solution.py:293
  46.1 0.8 collective-permute-done.18
  46.9 1.4 %collective-permute-start.22 = (bf16[64,768]{1,0:T(8,128)(2,1)S(1)}, bf16[64,768]{1,0:T(8,128)(2,1)S(1)}, u32[]{:S(2)}, u32[]{:S(2)}) collective-permute-start(bf16[64,768]{1,0:T(8,128)(2,1)S(1)} %get-tuple-element.145), channel_id=1, source_target_pairs={{0,7},{1,2},{2,1},{3,4},{4,3},{5,6},{6,5},{7,0},{8,15},{9,10},{10,... | collective-permute-start | bytes 294920 | tf_op jit(solution)/shard_map/ppermute | solution.py:170
  48.3 1.6 %shard_map.54 = bf16[64,2048]{1,0:T(8,128)(2,1)S(1)} custom-call(s32[2]{0:T(128)S(1)} %pad_add_fusion.refs_0_, s32[2,3]{1,0:T(2,128)S(1)} %copy-done.2, bf16[2,2048]{1,0:T(2,128)(2,1)S(1)} %copy-done.1, bf16[2,16,3,128,128]{4,3,2,1,0:T(8,128)(2,1)S(1)} %copy-done, bf16[1168,128]{1,0:T(8,128)(2,1)S(1)} %collective-permute-done.refs_4_, ...), custom_call_target="tpu_custom_call" | custom-call | tf_op jit(solution)/shard_map/pallas_call | solution.py:264
  50.0 2.3 %collective-permute-done.23.refs_6_ = bf16[64,2048]{1,0:T(8,128)(2,1)S(1)} collective-permute-done((bf16[64,2048]{1,0:T(8,128)(2,1)S(1)}, bf16[64,2048]{1,0:T(8,128)(2,1)S(1)}, u32[]{:S(2)}, u32[]{:S(2)}) %collective-permute-start.23) | collective-permute-done | bytes 262176 | tf_op jit(solution)/shard_map/ppermute | solution.py:293
  53.1 1.9 %collective-permute-start.26 = (bf16[64,768]{1,0:T(8,128)(2,1)S(1)}, bf16[64,768]{1,0:T(8,128)(2,1)S(1)}, u32[]{:S(2)}, u32[]{:S(2)}) collective-permute-start(bf16[64,768]{1,0:T(8,128)(2,1)S(1)} %get-tuple-element.144), channel_id=1, source_target_pairs={{0,1},{1,0},{2,3},{3,2},{4,5},{5,4},{6,7},{7,6},{8,15},{9,10},{10,... | collective-permute-start | bytes 294920 | tf_op jit(solution)/shard_map/ppermute | solution.py:170
  54.9 1.6 %shard_map.55 = bf16[64,2048]{1,0:T(8,128)(2,1)S(1)} custom-call(s32[2]{0:T(128)S(1)} %pad_add_fusion.refs_0_, s32[2,3]{1,0:T(2,128)S(1)} %copy-done.2, bf16[2,2048]{1,0:T(2,128)(2,1)S(1)} %copy-done.1, bf16[2,16,3,128,128]{4,3,2,1,0:T(8,128)(2,1)S(1)} %copy-done, bf16[1168,128]{1,0:T(8,128)(2,1)S(1)} %collective-permute-done.refs_4_, ...), custom_call_target="tpu_custom_call" | custom-call | tf_op jit(solution)/shard_map/pallas_call | solution.py:264
  56.6 2.1 %collective-permute-done.26.refs_8_ = bf16[64,768]{1,0:T(8,128)(2,1)S(1)} collective-permute-done((bf16[64,768]{1,0:T(8,128)(2,1)S(1)}, bf16[64,768]{1,0:T(8,128)(2,1)S(1)}, u32[]{:S(2)}, u32[]{:S(2)}) %collective-permute-start.26) | collective-permute-done | bytes 98336 | tf_op jit(solution)/shard_map/ppermute | solution.py:170
  58.9 1.8 %collective-permute-start.29 = (bf16[64,768]{1,0:T(8,128)(2,1)S(1)}, bf16[64,768]{1,0:T(8,128)(2,1)S(1)}, u32[]{:S(2)}, u32[]{:S(2)}) collective-permute-start(bf16[64,768]{1,0:T(8,128)(2,1)S(1)} %get-tuple-element.142), channel_id=1, source_target_pairs={{0,1},{1,0},{2,3},{3,2},{4,5},{5,4},{6,7},{7,6},{8,15},{9,10},{10,... | collective-permute-start | bytes 294920 | tf_op jit(solution)/shard_map/ppermute | solution.py:170
  60.6 1.8 %shard_map.56 = bf16[64,2048]{1,0:T(8,128)(2,1)S(1)} custom-call(s32[2]{0:T(128)S(1)} %pad_add_fusion.refs_0_, s32[2,3]{1,0:T(2,128)S(1)} %copy-done.2, bf16[2,2048]{1,0:T(2,128)(2,1)S(1)} %copy-done.1, bf16[2,16,3,128,128]{4,3,2,1,0:T(8,128)(2,1)S(1)} %copy-done, bf16[1168,128]{1,0:T(8,128)(2,1)S(1)} %collective-permute-done.refs_4_, ...), custom_call_target="tpu_custom_call" | custom-call | tf_op jit(solution)/shard_map/pallas_call | solution.py:264
  62.5 2.1 %collective-permute-done.24.refs_6_ = bf16[64,2048]{1,0:T(8,128)(2,1)S(1)} collective-permute-done((bf16[64,2048]{1,0:T(8,128)(2,1)S(1)}, bf16[64,2048]{1,0:T(8,128)(2,1)S(1)}, u32[]{:S(2)}, u32[]{:S(2)}) %collective-permute-start.24) | collective-permute-done | bytes 262176 | tf_op jit(solution)/shard_map/ppermute | solution.py:293
  64.7 1.5 %collective-permute-start.31 = (bf16[64,768]{1,0:T(8,128)(2,1)S(1)}, bf16[64,768]{1,0:T(8,128)(2,1)S(1)}, u32[]{:S(2)}, u32[]{:S(2)}) collective-permute-start(bf16[64,768]{1,0:T(8,128)(2,1)S(1)} %get-tuple-element.139), channel_id=1, source_target_pairs={{0,1},{1,0},{2,3},{3,2},{4,5},{5,4},{6,7},{7,6},{8,15},{9,10},{10,... | collective-permute-start | bytes 294920 | tf_op jit(solution)/shard_map/ppermute | solution.py:170
  66.3 1.6 %shard_map.57 = bf16[64,2048]{1,0:T(8,128)(2,1)S(1)} custom-call(s32[2]{0:T(128)S(1)} %pad_add_fusion.refs_0_, s32[2,3]{1,0:T(2,128)S(1)} %copy-done.2, bf16[2,2048]{1,0:T(2,128)(2,1)S(1)} %copy-done.1, bf16[2,16,3,128,128]{4,3,2,1,0:T(8,128)(2,1)S(1)} %copy-done, bf16[1168,128]{1,0:T(8,128)(2,1)S(1)} %collective-permute-done.refs_4_, ...), custom_call_target="tpu_custom_call" | custom-call | tf_op jit(solution)/shard_map/pallas_call | solution.py:264
  68.4 2.0 %collective-permute-done.31.refs_8_ = bf16[64,768]{1,0:T(8,128)(2,1)S(1)} collective-permute-done((bf16[64,768]{1,0:T(8,128)(2,1)S(1)}, bf16[64,768]{1,0:T(8,128)(2,1)S(1)}, u32[]{:S(2)}, u32[]{:S(2)}) %collective-permute-start.31) | collective-permute-done | bytes 98336 | tf_op jit(solution)/shard_map/ppermute | solution.py:170
  70.9 1.7 %collective-permute-start.35 = (bf16[64,768]{1,0:T(8,128)(2,1)S(1)}, bf16[64,768]{1,0:T(8,128)(2,1)S(1)}, u32[]{:S(2)}, u32[]{:S(2)}) collective-permute-start(bf16[64,768]{1,0:T(8,128)(2,1)S(1)} %get-tuple-element.138), channel_id=1, source_target_pairs={{0,1},{1,0},{2,3},{3,2},{4,5},{5,4},{6,7},{7,6},{8,9},{9,8},{10,11... | collective-permute-start | bytes 294920 | tf_op jit(solution)/shard_map/ppermute | solution.py:170
  72.6 1.6 %shard_map.58 = bf16[64,2048]{1,0:T(8,128)(2,1)S(1)} custom-call(s32[2]{0:T(128)S(1)} %pad_add_fusion.refs_0_, s32[2,3]{1,0:T(2,128)S(1)} %copy-done.2, bf16[2,2048]{1,0:T(2,128)(2,1)S(1)} %copy-done.1, bf16[2,16,3,128,128]{4,3,2,1,0:T(8,128)(2,1)S(1)} %copy-done, bf16[1168,128]{1,0:T(8,128)(2,1)S(1)} %collective-permute-done.refs_4_, ...), custom_call_target="tpu_custom_call" | custom-call | tf_op jit(solution)/shard_map/pallas_call | solution.py:264
  74.2 1.4 %collective-permute-start.33 = (bf16[64,2048]{1,0:T(8,128)(2,1)S(1)}, bf16[64,2048]{1,0:T(8,128)(2,1)S(1)}, u32[]{:S(2)}, u32[]{:S(2)}) collective-permute-start(bf16[64,2048]{1,0:T(8,128)(2,1)S(1)} %shard_map.58), channel_id=1, source_target_pairs={{8,16},{9,17},{10,18},{11,19},{12,20},{13,21},{14,22},{15,23},{16,... | collective-permute-start | bytes 786440 | tf_op jit(solution)/shard_map/ppermute | solution.py:293
  75.6 0.9 collective-permute-done.36.refs_6_
  76.9 1.2 %collective-permute-start.38 = (bf16[64,768]{1,0:T(8,128)(2,1)S(1)}, bf16[64,768]{1,0:T(8,128)(2,1)S(1)}, u32[]{:S(2)}, u32[]{:S(2)}) collective-permute-start(bf16[64,768]{1,0:T(8,128)(2,1)S(1)} %get-tuple-element.136), channel_id=1, source_target_pairs={{0,1},{1,0},{2,3},{3,2},{4,5},{5,4},{6,7},{7,6},{8,9},{9,8},{10,11... | collective-permute-start | bytes 294920 | tf_op jit(solution)/shard_map/ppermute | solution.py:170
  78.2 1.6 %shard_map.59 = bf16[64,2048]{1,0:T(8,128)(2,1)S(1)} custom-call(s32[2]{0:T(128)S(1)} %pad_add_fusion.refs_0_, s32[2,3]{1,0:T(2,128)S(1)} %copy-done.2, bf16[2,2048]{1,0:T(2,128)(2,1)S(1)} %copy-done.1, bf16[2,16,3,128,128]{4,3,2,1,0:T(8,128)(2,1)S(1)} %copy-done, bf16[1168,128]{1,0:T(8,128)(2,1)S(1)} %collective-permute-done.refs_4_, ...), custom_call_target="tpu_custom_call" | custom-call | tf_op jit(solution)/shard_map/pallas_call | solution.py:264
  79.8 1.5 %collective-permute-start.41 = (bf16[64,2048]{1,0:T(8,128)(2,1)S(1)}, bf16[64,2048]{1,0:T(8,128)(2,1)S(1)}, u32[]{:S(2)}, u32[]{:S(2)}) collective-permute-start(bf16[64,2048]{1,0:T(8,128)(2,1)S(1)} %shard_map.59), channel_id=1, source_target_pairs={{16,24},{17,25},{18,26},{19,27},{20,28},{21,29},{22,30},{23,31},{2... | collective-permute-start | bytes 786440 | tf_op jit(solution)/shard_map/ppermute | solution.py:293
  81.3 1.6 %collective-permute-done.38.refs_8_ = bf16[64,768]{1,0:T(8,128)(2,1)S(1)} collective-permute-done((bf16[64,768]{1,0:T(8,128)(2,1)S(1)}, bf16[64,768]{1,0:T(8,128)(2,1)S(1)}, u32[]{:S(2)}, u32[]{:S(2)}) %collective-permute-start.38) | collective-permute-done | bytes 98336 | tf_op jit(solution)/shard_map/ppermute | solution.py:170
  84.0 1.6 %shard_map.60 = bf16[64,2048]{1,0:T(8,128)(2,1)S(1)} custom-call(s32[2]{0:T(128)S(1)} %pad_add_fusion.refs_0_, s32[2,3]{1,0:T(2,128)S(1)} %copy-done.2, bf16[2,2048]{1,0:T(2,128)(2,1)S(1)} %copy-done.1, bf16[2,16,3,128,128]{4,3,2,1,0:T(8,128)(2,1)S(1)} %copy-done, bf16[1168,128]{1,0:T(8,128)(2,1)S(1)} %collective-permute-done.refs_4_, ...), custom_call_target="tpu_custom_call" | custom-call | tf_op jit(solution)/shard_map/pallas_call | solution.py:264
  85.6 0.8 collective-permute-start.45
  86.4 2.4 %collective-permute-done.41.refs_6_ = bf16[64,2048]{1,0:T(8,128)(2,1)S(1)} collective-permute-done((bf16[64,2048]{1,0:T(8,128)(2,1)S(1)}, bf16[64,2048]{1,0:T(8,128)(2,1)S(1)}, u32[]{:S(2)}, u32[]{:S(2)}) %collective-permute-start.41) | collective-permute-done | bytes 262176 | tf_op jit(solution)/shard_map/ppermute | solution.py:293
  89.4 1.6 %shard_map.61 = bf16[64,2048]{1,0:T(8,128)(2,1)S(1)} custom-call(s32[2]{0:T(128)S(1)} %pad_add_fusion.refs_0_, s32[2,3]{1,0:T(2,128)S(1)} %copy-done.2, bf16[2,2048]{1,0:T(2,128)(2,1)S(1)} %copy-done.1, bf16[2,16,3,128,128]{4,3,2,1,0:T(8,128)(2,1)S(1)} %copy-done, bf16[1168,128]{1,0:T(8,128)(2,1)S(1)} %collective-permute-done.refs_4_, ...), custom_call_target="tpu_custom_call" | custom-call | tf_op jit(solution)/shard_map/pallas_call | solution.py:264
  91.0 1.8 %collective-permute-start.42 = (bf16[64,2048]{1,0:T(8,128)(2,1)S(1)}, bf16[64,2048]{1,0:T(8,128)(2,1)S(1)}, u32[]{:S(2)}, u32[]{:S(2)}) collective-permute-start(bf16[64,2048]{1,0:T(8,128)(2,1)S(1)} %shard_map.61), channel_id=1, source_target_pairs={{16,24},{17,25},{18,26},{19,27},{20,28},{21,29},{22,30},{23,31},{2... | collective-permute-start | bytes 786440 | tf_op jit(solution)/shard_map/ppermute | solution.py:293
  92.8 1.5 %collective-permute-done.45.refs_6_ = bf16[64,2048]{1,0:T(8,128)(2,1)S(1)} collective-permute-done((bf16[64,2048]{1,0:T(8,128)(2,1)S(1)}, bf16[64,2048]{1,0:T(8,128)(2,1)S(1)}, u32[]{:S(2)}, u32[]{:S(2)}) %collective-permute-start.45) | collective-permute-done | bytes 262176 | tf_op jit(solution)/shard_map/ppermute | solution.py:293
  95.5 3.3 %collective-permute-start.48 = (bf16[64,2048]{1,0:T(8,128)(2,1)S(1)}, bf16[64,2048]{1,0:T(8,128)(2,1)S(1)}, u32[]{:S(2)}, u32[]{:S(2)}) collective-permute-start(bf16[64,2048]{1,0:T(8,128)(2,1)S(1)} %shard_map.62), channel_id=1, source_target_pairs={{24,16},{25,17},{26,18},{27,19},{28,20},{29,21},{30,22},{31,23},{1... | collective-permute-start | bytes 786440 | tf_op jit(solution)/shard_map/ppermute | solution.py:293
  98.8 1.9 %collective-permute-done.42.refs_6_ = bf16[64,2048]{1,0:T(8,128)(2,1)S(1)} collective-permute-done((bf16[64,2048]{1,0:T(8,128)(2,1)S(1)}, bf16[64,2048]{1,0:T(8,128)(2,1)S(1)}, u32[]{:S(2)}, u32[]{:S(2)}) %collective-permute-start.42) | collective-permute-done | bytes 262176 | tf_op jit(solution)/shard_map/ppermute | solution.py:293
  102.3 3.4 %collective-permute-done.48 = bf16[64,2048]{1,0:T(8,128)(2,1)S(1)} collective-permute-done((bf16[64,2048]{1,0:T(8,128)(2,1)S(1)}, bf16[64,2048]{1,0:T(8,128)(2,1)S(1)}, u32[]{:S(2)}, u32[]{:S(2)}) %collective-permute-start.48) | collective-permute-done | bytes 262176 | tf_op jit(solution)/shard_map/ppermute | solution.py:293
  105.8 1.4 %shard_map.64 = bf16[2,64,2048]{2,1,0:T(8,128)(2,1)} custom-call(s32[2]{0:T(128)S(1)} %pad_add_fusion.refs_0_, s32[2,3]{1,0:T(2,128)S(1)} %copy-done.2, bf16[2,2048]{1,0:T(2,128)(2,1)S(1)} %copy-done.1, bf16[2,16,3,128,128]{4,3,2,1,0:T(8,128)(2,1)S(1)} %copy-done, bf16[1168,128]{1,0:T(8,128)(2,1)S(1)} %collective-permute-done.refs_4_, ...), custom_call_target="tpu_custom_call" | custom-call | tf_op jit(solution)/shard_map/pallas_call | solution.py:264
  (102 shorter events, 12.0 us)
Async XLA Ops:
  1.7 10.3 %collective-permute-start.1 = (bf16[1168,128]{1,0:T(8,128)(2,1)S(1)}, bf16[1168,128]{1,0:T(8,128)(2,1)S(1)}, u32[]{:S(2)}, u32[]{:S(2)}) collective-permute-start(bf16[1168,128]{1,0:T(8,128)(2,1)S(1)} %shard_map.46), channel_id=1, source_target_pairs={{0,7},{1,2},{2,1},{3,4},{4,3},{5,6},{6,5},{7,0},{8,15},{9,10},{10,... | collective-permute-start | bytes 897032 | tf_op jit(solution)/shard_map/ppermute | solution.py:170
  5.6 6.3 %collective-permute-start = (bf16[1168,128]{1,0:T(8,128)(2,1)S(1)}, bf16[1168,128]{1,0:T(8,128)(2,1)S(1)}, u32[]{:S(2)}, u32[]{:S(2)}) collective-permute-start(bf16[1168,128]{1,0:T(8,128)(2,1)S(1)} %get-tuple-element.72), channel_id=1, source_target_pairs={{0,1},{1,0},{2,3},{3,2},{4,5},{5,4},{6,7},{7,6},{8,9},{9,8},{10,11... | collective-permute-start | bytes 897032 | tf_op jit(solution)/shard_map/ppermute | solution.py:162
  5.7 1.7 %collective-permute-start.4 = (bf16[64,768]{1,0:T(8,128)(2,1)S(1)}, bf16[64,768]{1,0:T(8,128)(2,1)S(1)}, u32[]{:S(2)}, u32[]{:S(2)}) collective-permute-start(bf16[64,768]{1,0:T(8,128)(2,1)S(1)} %get-tuple-element.79), channel_id=1, source_target_pairs={{0,1},{1,0},{2,3},{3,2},{4,5},{5,4},{6,7},{7,6},{8,9},{9,8},{10,11... | collective-permute-start | bytes 294920 | tf_op jit(solution)/shard_map/ppermute | solution.py:162
  6.2 7.3 %collective-permute-start.2 = (bf16[64,768]{1,0:T(8,128)(2,1)S(1)}, bf16[64,768]{1,0:T(8,128)(2,1)S(1)}, u32[]{:S(2)}, u32[]{:S(2)}) collective-permute-start(bf16[64,768]{1,0:T(8,128)(2,1)S(1)} %get-tuple-element.75), channel_id=1, source_target_pairs={{0,1},{1,0},{2,3},{3,2},{4,5},{5,4},{6,7},{7,6},{8,9},{9,8},{10,11... | collective-permute-start | bytes 294920 | tf_op jit(solution)/shard_map/ppermute | solution.py:162
  7.4 6.2 %collective-permute-start.3 = (bf16[64,768]{1,0:T(8,128)(2,1)S(1)}, bf16[64,768]{1,0:T(8,128)(2,1)S(1)}, u32[]{:S(2)}, u32[]{:S(2)}) collective-permute-start(bf16[64,768]{1,0:T(8,128)(2,1)S(1)} %get-tuple-element.76), channel_id=1, source_target_pairs={{0,7},{1,2},{2,1},{3,4},{4,3},{5,6},{6,5},{7,0},{8,9},{9,8},{10,11... | collective-permute-start | bytes 294920 | tf_op jit(solution)/shard_map/ppermute | solution.py:170
  13.5 4.6 %collective-permute-start.6 = (bf16[64,2048]{1,0:T(8,128)(2,1)S(1)}, bf16[64,2048]{1,0:T(8,128)(2,1)S(1)}, u32[]{:S(2)}, u32[]{:S(2)}) collective-permute-start(bf16[64,2048]{1,0:T(8,128)(2,1)S(1)} %get-tuple-element.83), channel_id=1, source_target_pairs={{0,8},{1,9},{2,10},{3,11},{4,12},{5,13},{6,14},{7,15},{8,0},{9,1},... | collective-permute-start | bytes 786440 | tf_op jit(solution)/shard_map/ppermute | solution.py:293
  13.6 4.5 %collective-permute-start.7 = (bf16[64,768]{1,0:T(8,128)(2,1)S(1)}, bf16[64,768]{1,0:T(8,128)(2,1)S(1)}, u32[]{:S(2)}, u32[]{:S(2)}) collective-permute-start(bf16[64,768]{1,0:T(8,128)(2,1)S(1)} %get-tuple-element.155), channel_id=1, source_target_pairs={{0,1},{1,0},{2,3},{3,2},{4,5},{5,4},{6,7},{7,6},{8,9},{9,8},{10,11... | collective-permute-start | bytes 294920 | tf_op jit(solution)/shard_map/ppermute | solution.py:162
  14.1 4.0 %collective-permute-start.8 = (bf16[64,768]{1,0:T(8,128)(2,1)S(1)}, bf16[64,768]{1,0:T(8,128)(2,1)S(1)}, u32[]{:S(2)}, u32[]{:S(2)}) collective-permute-start(bf16[64,768]{1,0:T(8,128)(2,1)S(1)} %get-tuple-element.156), channel_id=1, source_target_pairs={{0,7},{1,2},{2,1},{3,4},{4,3},{5,6},{6,5},{7,0},{8,9},{9,8},{10,11... | collective-permute-start | bytes 294920 | tf_op jit(solution)/shard_map/ppermute | solution.py:170
  15.7 6.5 %collective-permute-start.11 = (bf16[64,2048]{1,0:T(8,128)(2,1)S(1)}, bf16[64,2048]{1,0:T(8,128)(2,1)S(1)}, u32[]{:S(2)}, u32[]{:S(2)}) collective-permute-start(bf16[64,2048]{1,0:T(8,128)(2,1)S(1)} %get-tuple-element.87), channel_id=1, source_target_pairs={{0,8},{1,9},{2,10},{3,11},{4,12},{5,13},{6,14},{7,15},{16,17},{17,... | collective-permute-start | bytes 786440 | tf_op jit(solution)/shard_map/ppermute | solution.py:293
  18.2 4.1 %collective-permute-start.10 = (bf16[64,768]{1,0:T(8,128)(2,1)S(1)}, bf16[64,768]{1,0:T(8,128)(2,1)S(1)}, u32[]{:S(2)}, u32[]{:S(2)}) collective-permute-start(bf16[64,768]{1,0:T(8,128)(2,1)S(1)} %get-tuple-element.153), channel_id=1, source_target_pairs={{0,7},{1,2},{2,1},{3,4},{4,3},{5,6},{6,5},{7,0},{8,15},{9,10},{10,... | collective-permute-start | bytes 294920 | tf_op jit(solution)/shard_map/ppermute | solution.py:170
  18.3 4.0 %collective-permute-start.9 = (bf16[64,768]{1,0:T(8,128)(2,1)S(1)}, bf16[64,768]{1,0:T(8,128)(2,1)S(1)}, u32[]{:S(2)}, u32[]{:S(2)}) collective-permute-start(bf16[64,768]{1,0:T(8,128)(2,1)S(1)} %get-tuple-element.154), channel_id=1, source_target_pairs={{0,1},{1,0},{2,3},{3,2},{4,5},{5,4},{6,7},{7,6},{8,9},{9,8},{10,11... | collective-permute-start | bytes 294920 | tf_op jit(solution)/shard_map/ppermute | solution.py:162
  20.3 5.5 %collective-permute-start.12 = (bf16[64,2048]{1,0:T(8,128)(2,1)S(1)}, bf16[64,2048]{1,0:T(8,128)(2,1)S(1)}, u32[]{:S(2)}, u32[]{:S(2)}) collective-permute-start(bf16[64,2048]{1,0:T(8,128)(2,1)S(1)} %get-tuple-element.91), channel_id=1, source_target_pairs={{0,8},{1,9},{2,10},{3,11},{4,12},{5,13},{6,14},{7,15},{16,17},{17,... | collective-permute-start | bytes 786440 | tf_op jit(solution)/shard_map/ppermute | solution.py:293
  22.4 3.4 %collective-permute-start.13 = (bf16[64,768]{1,0:T(8,128)(2,1)S(1)}, bf16[64,768]{1,0:T(8,128)(2,1)S(1)}, u32[]{:S(2)}, u32[]{:S(2)}) collective-permute-start(bf16[64,768]{1,0:T(8,128)(2,1)S(1)} %get-tuple-element.151), channel_id=1, source_target_pairs={{0,1},{1,0},{2,3},{3,2},{4,5},{5,4},{6,7},{7,6},{8,9},{9,8},{10,11... | collective-permute-start | bytes 294920 | tf_op jit(solution)/shard_map/ppermute | solution.py:162
  22.9 2.9 %collective-permute-start.14 = (bf16[64,768]{1,0:T(8,128)(2,1)S(1)}, bf16[64,768]{1,0:T(8,128)(2,1)S(1)}, u32[]{:S(2)}, u32[]{:S(2)}) collective-permute-start(bf16[64,768]{1,0:T(8,128)(2,1)S(1)} %get-tuple-element.152), channel_id=1, source_target_pairs={{0,7},{1,2},{2,1},{3,4},{4,3},{5,6},{6,5},{7,0},{8,15},{9,10},{10,... | collective-permute-start | bytes 294920 | tf_op jit(solution)/shard_map/ppermute | solution.py:170
  24.4 15.9 %collective-permute-start.17 = (bf16[64,2048]{1,0:T(8,128)(2,1)S(1)}, bf16[64,2048]{1,0:T(8,128)(2,1)S(1)}, u32[]{:S(2)}, u32[]{:S(2)}) collective-permute-start(bf16[64,2048]{1,0:T(8,128)(2,1)S(1)} %get-tuple-element.95), channel_id=1, source_target_pairs={{0,8},{1,9},{2,10},{3,11},{4,12},{5,13},{6,14},{7,15},{8,16},{9,17... | collective-permute-start | bytes 786440 | tf_op jit(solution)/shard_map/ppermute | solution.py:293
  25.8 14.5 %collective-permute-start.16 = (bf16[64,768]{1,0:T(8,128)(2,1)S(1)}, bf16[64,768]{1,0:T(8,128)(2,1)S(1)}, u32[]{:S(2)}, u32[]{:S(2)}) collective-permute-start(bf16[64,768]{1,0:T(8,128)(2,1)S(1)} %get-tuple-element.149), channel_id=1, source_target_pairs={{0,7},{1,2},{2,1},{3,4},{4,3},{5,6},{6,5},{7,0},{8,15},{9,10},{10,... | collective-permute-start | bytes 294920 | tf_op jit(solution)/shard_map/ppermute | solution.py:170
  26.3 14.0 %collective-permute-start.15 = (bf16[64,768]{1,0:T(8,128)(2,1)S(1)}, bf16[64,768]{1,0:T(8,128)(2,1)S(1)}, u32[]{:S(2)}, u32[]{:S(2)}) collective-permute-start(bf16[64,768]{1,0:T(8,128)(2,1)S(1)} %get-tuple-element.150), channel_id=1, source_target_pairs={{0,1},{1,0},{2,3},{3,2},{4,5},{5,4},{6,7},{7,6},{8,9},{9,8},{10,11... | collective-permute-start | bytes 294920 | tf_op jit(solution)/shard_map/ppermute | solution.py:162
  27.9 18.9 %collective-permute-start.18 = (bf16[64,2048]{1,0:T(8,128)(2,1)S(1)}, bf16[64,2048]{1,0:T(8,128)(2,1)S(1)}, u32[]{:S(2)}, u32[]{:S(2)}) collective-permute-start(bf16[64,2048]{1,0:T(8,128)(2,1)S(1)} %get-tuple-element.99), channel_id=1, source_target_pairs={{0,8},{1,9},{2,10},{3,11},{4,12},{5,13},{6,14},{7,15},{8,16},{9,17... | collective-permute-start | bytes 786440 | tf_op jit(solution)/shard_map/ppermute | solution.py:293
  40.4 5.6 %collective-permute-start.19 = (bf16[64,768]{1,0:T(8,128)(2,1)S(1)}, bf16[64,768]{1,0:T(8,128)(2,1)S(1)}, u32[]{:S(2)}, u32[]{:S(2)}) collective-permute-start(bf16[64,768]{1,0:T(8,128)(2,1)S(1)} %get-tuple-element.147), channel_id=1, source_target_pairs={{0,1},{1,0},{2,3},{3,2},{4,5},{5,4},{6,7},{7,6},{8,9},{9,8},{10,11... | collective-permute-start | bytes 294920 | tf_op jit(solution)/shard_map/ppermute | solution.py:162
  40.5 5.5 %collective-permute-start.20 = (bf16[64,768]{1,0:T(8,128)(2,1)S(1)}, bf16[64,768]{1,0:T(8,128)(2,1)S(1)}, u32[]{:S(2)}, u32[]{:S(2)}) collective-permute-start(bf16[64,768]{1,0:T(8,128)(2,1)S(1)} %get-tuple-element.148), channel_id=1, source_target_pairs={{0,7},{1,2},{2,1},{3,4},{4,3},{5,6},{6,5},{7,0},{8,15},{9,10},{10,... | collective-permute-start | bytes 294920 | tf_op jit(solution)/shard_map/ppermute | solution.py:170
  43.6 8.7 %collective-permute-start.23 = (bf16[64,2048]{1,0:T(8,128)(2,1)S(1)}, bf16[64,2048]{1,0:T(8,128)(2,1)S(1)}, u32[]{:S(2)}, u32[]{:S(2)}) collective-permute-start(bf16[64,2048]{1,0:T(8,128)(2,1)S(1)} %get-tuple-element.103), channel_id=1, source_target_pairs={{0,8},{1,9},{2,10},{3,11},{4,12},{5,13},{6,14},{7,15},{8,16},{9,17... | collective-permute-start | bytes 786440 | tf_op jit(solution)/shard_map/ppermute | solution.py:293
  46.9 6.0 %collective-permute-start.22 = (bf16[64,768]{1,0:T(8,128)(2,1)S(1)}, bf16[64,768]{1,0:T(8,128)(2,1)S(1)}, u32[]{:S(2)}, u32[]{:S(2)}) collective-permute-start(bf16[64,768]{1,0:T(8,128)(2,1)S(1)} %get-tuple-element.145), channel_id=1, source_target_pairs={{0,7},{1,2},{2,1},{3,4},{4,3},{5,6},{6,5},{7,0},{8,15},{9,10},{10,... | collective-permute-start | bytes 294920 | tf_op jit(solution)/shard_map/ppermute | solution.py:170
  48.3 4.6 %collective-permute-start.21 = (bf16[64,768]{1,0:T(8,128)(2,1)S(1)}, bf16[64,768]{1,0:T(8,128)(2,1)S(1)}, u32[]{:S(2)}, u32[]{:S(2)}) collective-permute-start(bf16[64,768]{1,0:T(8,128)(2,1)S(1)} %get-tuple-element.146), channel_id=1, source_target_pairs={{0,1},{1,0},{2,3},{3,2},{4,5},{5,4},{6,7},{7,6},{8,9},{9,8},{10,11... | collective-permute-start | bytes 294920 | tf_op jit(solution)/shard_map/ppermute | solution.py:162
  49.9 8.8 %collective-permute-start.27 = (bf16[64,2048]{1,0:T(8,128)(2,1)S(1)}, bf16[64,2048]{1,0:T(8,128)(2,1)S(1)}, u32[]{:S(2)}, u32[]{:S(2)}) collective-permute-start(bf16[64,2048]{1,0:T(8,128)(2,1)S(1)} %shard_map.54), channel_id=1, source_target_pairs={{0,8},{1,9},{2,10},{3,11},{4,12},{5,13},{6,14},{7,15},{8,16},{9,17... | collective-permute-start | bytes 786440 | tf_op jit(solution)/shard_map/ppermute | solution.py:293
  53.0 3.7 %collective-permute-start.25 = (bf16[64,768]{1,0:T(8,128)(2,1)S(1)}, bf16[64,768]{1,0:T(8,128)(2,1)S(1)}, u32[]{:S(2)}, u32[]{:S(2)}) collective-permute-start(bf16[64,768]{1,0:T(8,128)(2,1)S(1)} %get-tuple-element.143), channel_id=1, source_target_pairs={{0,1},{1,0},{2,3},{3,2},{4,5},{5,4},{6,7},{7,6},{8,9},{9,8},{10,11... | collective-permute-start | bytes 294920 | tf_op jit(solution)/shard_map/ppermute | solution.py:162
  53.1 5.7 %collective-permute-start.26 = (bf16[64,768]{1,0:T(8,128)(2,1)S(1)}, bf16[64,768]{1,0:T(8,128)(2,1)S(1)}, u32[]{:S(2)}, u32[]{:S(2)}) collective-permute-start(bf16[64,768]{1,0:T(8,128)(2,1)S(1)} %get-tuple-element.144), channel_id=1, source_target_pairs={{0,1},{1,0},{2,3},{3,2},{4,5},{5,4},{6,7},{7,6},{8,15},{9,10},{10,... | collective-permute-start | bytes 294920 | tf_op jit(solution)/shard_map/ppermute | solution.py:170
  56.6 8.0 %collective-permute-start.24 = (bf16[64,2048]{1,0:T(8,128)(2,1)S(1)}, bf16[64,2048]{1,0:T(8,128)(2,1)S(1)}, u32[]{:S(2)}, u32[]{:S(2)}) collective-permute-start(bf16[64,2048]{1,0:T(8,128)(2,1)S(1)} %shard_map.55), channel_id=1, source_target_pairs={{0,8},{1,9},{2,10},{3,11},{4,12},{5,13},{6,14},{7,15},{8,16},{9,17... | collective-permute-start | bytes 786440 | tf_op jit(solution)/shard_map/ppermute | solution.py:293
  58.8 5.8 %collective-permute-start.28 = (bf16[64,768]{1,0:T(8,128)(2,1)S(1)}, bf16[64,768]{1,0:T(8,128)(2,1)S(1)}, u32[]{:S(2)}, u32[]{:S(2)}) collective-permute-start(bf16[64,768]{1,0:T(8,128)(2,1)S(1)} %get-tuple-element.141), channel_id=1, source_target_pairs={{0,1},{1,0},{2,3},{3,2},{4,5},{5,4},{6,7},{7,6},{8,9},{9,8},{10,11... | collective-permute-start | bytes 294920 | tf_op jit(solution)/shard_map/ppermute | solution.py:162
  58.9 5.8 %collective-permute-start.29 = (bf16[64,768]{1,0:T(8,128)(2,1)S(1)}, bf16[64,768]{1,0:T(8,128)(2,1)S(1)}, u32[]{:S(2)}, u32[]{:S(2)}) collective-permute-start(bf16[64,768]{1,0:T(8,128)(2,1)S(1)} %get-tuple-element.142), channel_id=1, source_target_pairs={{0,1},{1,0},{2,3},{3,2},{4,5},{5,4},{6,7},{7,6},{8,15},{9,10},{10,... | collective-permute-start | bytes 294920 | tf_op jit(solution)/shard_map/ppermute | solution.py:170
  62.4 8.4 %collective-permute-start.32 = (bf16[64,2048]{1,0:T(8,128)(2,1)S(1)}, bf16[64,2048]{1,0:T(8,128)(2,1)S(1)}, u32[]{:S(2)}, u32[]{:S(2)}) collective-permute-start(bf16[64,2048]{1,0:T(8,128)(2,1)S(1)} %shard_map.56), channel_id=1, source_target_pairs={{8,16},{9,17},{10,18},{11,19},{12,20},{13,21},{14,22},{15,23},{16,... | collective-permute-start | bytes 786440 | tf_op jit(solution)/shard_map/ppermute | solution.py:293
  64.7 5.7 %collective-permute-start.31 = (bf16[64,768]{1,0:T(8,128)(2,1)S(1)}, bf16[64,768]{1,0:T(8,128)(2,1)S(1)}, u32[]{:S(2)}, u32[]{:S(2)}) collective-permute-start(bf16[64,768]{1,0:T(8,128)(2,1)S(1)} %get-tuple-element.139), channel_id=1, source_target_pairs={{0,1},{1,0},{2,3},{3,2},{4,5},{5,4},{6,7},{7,6},{8,15},{9,10},{10,... | collective-permute-start | bytes 294920 | tf_op jit(solution)/shard_map/ppermute | solution.py:170
  66.1 4.3 %collective-permute-start.30 = (bf16[64,768]{1,0:T(8,128)(2,1)S(1)}, bf16[64,768]{1,0:T(8,128)(2,1)S(1)}, u32[]{:S(2)}, u32[]{:S(2)}) collective-permute-start(bf16[64,768]{1,0:T(8,128)(2,1)S(1)} %get-tuple-element.140), channel_id=1, source_target_pairs={{0,1},{1,0},{2,3},{3,2},{4,5},{5,4},{6,7},{7,6},{8,9},{9,8},{10,11... | collective-permute-start | bytes 294920 | tf_op jit(solution)/shard_map/ppermute | solution.py:162
  67.9 8.7 %collective-permute-start.36 = (bf16[64,2048]{1,0:T(8,128)(2,1)S(1)}, bf16[64,2048]{1,0:T(8,128)(2,1)S(1)}, u32[]{:S(2)}, u32[]{:S(2)}) collective-permute-start(bf16[64,2048]{1,0:T(8,128)(2,1)S(1)} %shard_map.57), channel_id=1, source_target_pairs={{8,16},{9,17},{10,18},{11,19},{12,20},{13,21},{14,22},{15,23},{16,... | collective-permute-start | bytes 786440 | tf_op jit(solution)/shard_map/ppermute | solution.py:293
  70.8 5.7 %collective-permute-start.34 = (bf16[64,768]{1,0:T(8,128)(2,1)S(1)}, bf16[64,768]{1,0:T(8,128)(2,1)S(1)}, u32[]{:S(2)}, u32[]{:S(2)}) collective-permute-start(bf16[64,768]{1,0:T(8,128)(2,1)S(1)} %get-tuple-element.137), channel_id=1, source_target_pairs={{0,1},{1,0},{2,3},{3,2},{4,5},{5,4},{6,7},{7,6},{8,9},{9,8},{10,11... | collective-permute-start | bytes 294920 | tf_op jit(solution)/shard_map/ppermute | solution.py:162
  70.9 5.9 %collective-permute-start.35 = (bf16[64,768]{1,0:T(8,128)(2,1)S(1)}, bf16[64,768]{1,0:T(8,128)(2,1)S(1)}, u32[]{:S(2)}, u32[]{:S(2)}) collective-permute-start(bf16[64,768]{1,0:T(8,128)(2,1)S(1)} %get-tuple-element.138), channel_id=1, source_target_pairs={{0,1},{1,0},{2,3},{3,2},{4,5},{5,4},{6,7},{7,6},{8,9},{9,8},{10,11... | collective-permute-start | bytes 294920 | tf_op jit(solution)/shard_map/ppermute | solution.py:170
  74.2 9.4 %collective-permute-start.33 = (bf16[64,2048]{1,0:T(8,128)(2,1)S(1)}, bf16[64,2048]{1,0:T(8,128)(2,1)S(1)}, u32[]{:S(2)}, u32[]{:S(2)}) collective-permute-start(bf16[64,2048]{1,0:T(8,128)(2,1)S(1)} %shard_map.58), channel_id=1, source_target_pairs={{8,16},{9,17},{10,18},{11,19},{12,20},{13,21},{14,22},{15,23},{16,... | collective-permute-start | bytes 786440 | tf_op jit(solution)/shard_map/ppermute | solution.py:293
  76.8 4.4 %collective-permute-start.37 = (bf16[64,768]{1,0:T(8,128)(2,1)S(1)}, bf16[64,768]{1,0:T(8,128)(2,1)S(1)}, u32[]{:S(2)}, u32[]{:S(2)}) collective-permute-start(bf16[64,768]{1,0:T(8,128)(2,1)S(1)} %get-tuple-element.135), channel_id=1, source_target_pairs={{0,1},{1,0},{2,3},{3,2},{4,5},{5,4},{6,7},{7,6},{8,9},{9,8},{10,11... | collective-permute-start | bytes 294920 | tf_op jit(solution)/shard_map/ppermute | solution.py:162
  76.9 6.0 %collective-permute-start.38 = (bf16[64,768]{1,0:T(8,128)(2,1)S(1)}, bf16[64,768]{1,0:T(8,128)(2,1)S(1)}, u32[]{:S(2)}, u32[]{:S(2)}) collective-permute-start(bf16[64,768]{1,0:T(8,128)(2,1)S(1)} %get-tuple-element.136), channel_id=1, source_target_pairs={{0,1},{1,0},{2,3},{3,2},{4,5},{5,4},{6,7},{7,6},{8,9},{9,8},{10,11... | collective-permute-start | bytes 294920 | tf_op jit(solution)/shard_map/ppermute | solution.py:170
  79.8 9.0 %collective-permute-start.41 = (bf16[64,2048]{1,0:T(8,128)(2,1)S(1)}, bf16[64,2048]{1,0:T(8,128)(2,1)S(1)}, u32[]{:S(2)}, u32[]{:S(2)}) collective-permute-start(bf16[64,2048]{1,0:T(8,128)(2,1)S(1)} %shard_map.59), channel_id=1, source_target_pairs={{16,24},{17,25},{18,26},{19,27},{20,28},{21,29},{22,30},{23,31},{2... | collective-permute-start | bytes 786440 | tf_op jit(solution)/shard_map/ppermute | solution.py:293
  83.6 5.2 %collective-permute-start.40 = (bf16[64,768]{1,0:T(8,128)(2,1)S(1)}, bf16[64,768]{1,0:T(8,128)(2,1)S(1)}, u32[]{:S(2)}, u32[]{:S(2)}) collective-permute-start(bf16[64,768]{1,0:T(8,128)(2,1)S(1)} %get-tuple-element.133), channel_id=1, source_target_pairs={{0,1},{1,0},{2,3},{3,2},{4,5},{5,4},{6,7},{7,6},{8,9},{9,8},{10,11... | collective-permute-start | bytes 294920 | tf_op jit(solution)/shard_map/ppermute | solution.py:170
  83.8 5.1 %collective-permute-start.39 = (bf16[64,768]{1,0:T(8,128)(2,1)S(1)}, bf16[64,768]{1,0:T(8,128)(2,1)S(1)}, u32[]{:S(2)}, u32[]{:S(2)}) collective-permute-start(bf16[64,768]{1,0:T(8,128)(2,1)S(1)} %get-tuple-element.134), channel_id=1, source_target_pairs={{0,1},{1,0},{2,3},{3,2},{4,5},{5,4},{6,7},{7,6},{8,9},{9,8},{10,11... | collective-permute-start | bytes 294920 | tf_op jit(solution)/shard_map/ppermute | solution.py:162
  85.6 8.7 %collective-permute-start.45 = (bf16[64,2048]{1,0:T(8,128)(2,1)S(1)}, bf16[64,2048]{1,0:T(8,128)(2,1)S(1)}, u32[]{:S(2)}, u32[]{:S(2)}) collective-permute-start(bf16[64,2048]{1,0:T(8,128)(2,1)S(1)} %shard_map.60), channel_id=1, source_target_pairs={{16,24},{17,25},{18,26},{19,27},{20,28},{21,29},{22,30},{23,31},{2... | collective-permute-start | bytes 786440 | tf_op jit(solution)/shard_map/ppermute | solution.py:293
  88.8 4.0 %collective-permute-start.43 = (bf16[64,768]{1,0:T(8,128)(2,1)S(1)}, bf16[64,768]{1,0:T(8,128)(2,1)S(1)}, u32[]{:S(2)}, u32[]{:S(2)}) collective-permute-start(bf16[64,768]{1,0:T(8,128)(2,1)S(1)} %get-tuple-element.131), channel_id=1, source_target_pairs={{0,1},{1,0},{2,3},{3,2},{4,5},{5,4},{6,7},{7,6},{8,9},{9,8},{10,11... | collective-permute-start | bytes 294920 | tf_op jit(solution)/shard_map/ppermute | solution.py:162
  88.9 3.9 %collective-permute-start.44 = (bf16[64,768]{1,0:T(8,128)(2,1)S(1)}, bf16[64,768]{1,0:T(8,128)(2,1)S(1)}, u32[]{:S(2)}, u32[]{:S(2)}) collective-permute-start(bf16[64,768]{1,0:T(8,128)(2,1)S(1)} %get-tuple-element.132), channel_id=1, source_target_pairs={{0,1},{1,0},{2,3},{3,2},{4,5},{5,4},{6,7},{7,6},{8,9},{9,8},{10,11... | collective-permute-start | bytes 294920 | tf_op jit(solution)/shard_map/ppermute | solution.py:170
  91.0 9.7 %collective-permute-start.42 = (bf16[64,2048]{1,0:T(8,128)(2,1)S(1)}, bf16[64,2048]{1,0:T(8,128)(2,1)S(1)}, u32[]{:S(2)}, u32[]{:S(2)}) collective-permute-start(bf16[64,2048]{1,0:T(8,128)(2,1)S(1)} %shard_map.61), channel_id=1, source_target_pairs={{16,24},{17,25},{18,26},{19,27},{20,28},{21,29},{22,30},{23,31},{2... | collective-permute-start | bytes 786440 | tf_op jit(solution)/shard_map/ppermute | solution.py:293
  94.3 7.0 %collective-permute-start.49 = (bf16[64,768]{1,0:T(8,128)(2,1)S(1)}, bf16[64,768]{1,0:T(8,128)(2,1)S(1)}, u32[]{:S(2)}, u32[]{:S(2)}) collective-permute-start(bf16[64,768]{1,0:T(8,128)(2,1)S(1)} %get-tuple-element.129), channel_id=1, source_target_pairs={{0,1},{1,0},{2,3},{3,2},{4,5},{5,4},{6,7},{7,6},{8,9},{9,8},{10,11... | collective-permute-start | bytes 294920 | tf_op jit(solution)/shard_map/ppermute | solution.py:162
  94.4 6.9 %collective-permute-start.50 = (bf16[64,768]{1,0:T(8,128)(2,1)S(1)}, bf16[64,768]{1,0:T(8,128)(2,1)S(1)}, u32[]{:S(2)}, u32[]{:S(2)}) collective-permute-start(bf16[64,768]{1,0:T(8,128)(2,1)S(1)} %get-tuple-element.130), channel_id=1, source_target_pairs={{0,1},{1,0},{2,3},{3,2},{4,5},{5,4},{6,7},{7,6},{8,9},{9,8},{10,11... | collective-permute-start | bytes 294920 | tf_op jit(solution)/shard_map/ppermute | solution.py:170
  95.5 10.2 %collective-permute-start.48 = (bf16[64,2048]{1,0:T(8,128)(2,1)S(1)}, bf16[64,2048]{1,0:T(8,128)(2,1)S(1)}, u32[]{:S(2)}, u32[]{:S(2)}) collective-permute-start(bf16[64,2048]{1,0:T(8,128)(2,1)S(1)} %shard_map.62), channel_id=1, source_target_pairs={{24,16},{25,17},{26,18},{27,19},{28,20},{29,21},{30,22},{31,23},{1... | collective-permute-start | bytes 786440 | tf_op jit(solution)/shard_map/ppermute | solution.py:293
  (6 other events, 35.0 us)

commit v5 on v4

--- a/solution.py
+++ b/solution.py
@@ -318,7 +318,7 @@
             ended.append(out)
         coming = step + AHEAD
         if coming < steps:
-            after = (out, *halos[coming - 1]) if coming < steps - 1 else (out,)
+            after = (out, *halos[coming - 1][1:]) if coming < steps - 1 else (out,)
             if coming < LAG:
                 here = tie(own[coming], *after)
             else:

time: 108 us -> 107 us (level)
  starting transfers between devices: 47.6 us -> 45 us
  waiting for transfers between devices: 30.3 us -> 32.5 us
    ppermute x18, starting transfers between devices: 15.2 us -> 11.5 us  [send_far(): return lax.ppermute(value, both, pairs)]
    ppermute x15, waiting for transfers between devices: 18 us -> 21.3 us  [hop(): return lax.ppermute(out, both, pairs)]
    ppermute x18, starting transfers between devices: 3.9 us -> 6.76 us  [send_near(): return lax.ppermute(value, both, pairs)]
    ppermute x15, starting transfers between devices: 28.5 us -> 26.7 us  [hop(): return lax.ppermute(out, both, pairs)]
  transfers between devices with their start and end apart: 51 -> 51, of which waited for: 21 -> 19; matrix products, arithmetic and copies ran while one was open for 0% -> 0% of each run, Pallas kernels for 24% -> 24%
where the time goes in v5:
time: 107 us
  starting transfers between devices  45 us (42%)
  waiting for transfers between devices  32.5 us (30%)
  Pallas kernels  28.2 us (26%)
    ppermute x15, starting transfers between devices, hop(): return lax.ppermute(out, both, pairs)  26.7 us
    pallas_call x17, Pallas kernels, run(): pl.pallas_call(lambda *refs: layers_kernel(sizes, step, chunks, next_plac...  24.7 us
    ppermute x15, waiting for transfers between devices, hop(): return lax.ppermute(out, both, pairs)  21.3 us
    ppermute x18, starting transfers between devices, send_far(): return lax.ppermute(value, both, pairs)  11.5 us
    ppermute x18, waiting for transfers between devices, send_far(): return lax.ppermute(value, both, pairs)  10.3 us
    ppermute x18, starting transfers between devices, send_near(): return lax.ppermute(value, both, pairs)  6.76 us
    pallas_call x2, Pallas kernels, stage(): pl.pallas_call(lambda *refs: stage_kernel(my_copies, my_rows, *refs), in_...  3.48 us
  transfers between devices with their start and end apart: 51, of which 19 were waited for; matrix products, arithmetic and copies ran while one was open for 0% of the time, Pallas kernels for 24%

profile of v5, /device:TPU:16, one launch (start us, length us, event | category | flops | bytes accessed | tf_op | source)
XLA Modules:
  0.0 106.7 jit_solution(1269452355461518438)
XLA Ops:
  0.1 1.5 %shard_map.46 = bf16[1168,128]{1,0:T(8,128)(2,1)S(1)} custom-call(s32[2]{0:T(128)S(1)} %pad_add_fusion.refs_0_, bf16[2,2048]{1,0:T(2,128)(2,1)} %refs_2_.16, bf16[2,6144,128]{2,1,0:T(8,128)(2,1)} %bitcast.4, bf16[2,256,2048]{2,1,0:T(8,128)(2,1)} %refs_9_.5), custom_call_target="tpu_custom_call" | custom-call | tf_op jit(solution)/shard_map/pallas_call | solution.py:212
  1.7 2.0 %collective-permute-start.1 = (bf16[1168,128]{1,0:T(8,128)(2,1)S(1)}, bf16[1168,128]{1,0:T(8,128)(2,1)S(1)}, u32[]{:S(2)}, u32[]{:S(2)}) collective-permute-start(bf16[1168,128]{1,0:T(8,128)(2,1)S(1)} %shard_map.46), channel_id=1, source_target_pairs={{0,7},{1,2},{2,1},{3,4},{4,3},{5,6},{6,5},{7,0},{8,15},{9,10},{10,... | collective-permute-start | bytes 897032 | tf_op jit(solution)/shard_map/ppermute | solution.py:170
  3.6 1.9 %shard_map.47 = (bf16[64,768]{1,0:T(8,128)(2,1)S(1)}, bf16[64,768]{1,0:T(8,128)(2,1)S(1)}, bf16[64,768]{1,0:T(8,128)(2,1)S(1)}, bf16[64,768]{1,0:T(8,128)(2,1)S(...) custom-call(s32[2]{0:T(128)S(1)} %pad_add_fusion.refs_0_, ...), custom_call_target="tpu_custom_call" | custom-call | tf_op jit(solution)/shard_map/pallas_call | solution.py:212
  7.5 4.4 %collective-permute-done.1.refs_5_ = bf16[1168,128]{1,0:T(8,128)(2,1)S(1)} collective-permute-done((bf16[1168,128]{1,0:T(8,128)(2,1)S(1)}, bf16[1168,128]{1,0:T(8,128)(2,1)S(1)}, u32[]{:S(2)}, u32[]{:S(2)}) %collective-permute-start.1) | collective-permute-done | bytes 299040 | tf_op jit(solution)/shard_map/ppermute | solution.py:170
  11.9 1.5 %shard_map.48 = (bf16[64,2048]{1,0:T(8,128)(2,1)S(1)}, bf16[64,2048]{1,0:T(8,128)(2,1)S(1)}) custom-call(s32[2]{0:T(128)S(1)} %pad_add_fusion.refs_0_, s32[2,3]{1,0:T(2,128)S(1)} %copy-done.2, bf16[2,2048]{1,0:T(2,128)(2,1)S(1)} %copy-done.1, bf16[2,16,3,128,128]{4,3,2,1,0:T(8,128)(2,1)S(1)} %copy-done, bf16[1168,128]{1,0:T(8,128)(2,1)S(1)} %collective-permute-done.refs_4_, ...), custom_call_target="tpu_custom_call" | custom-call | tf_op jit(solution)/shard_map/pallas_call | solution.py:264
  14.2 1.5 %shard_map.49 = (bf16[64,2048]{1,0:T(8,128)(2,1)S(1)}, bf16[64,2048]{1,0:T(8,128)(2,1)S(1)}) custom-call(s32[2]{0:T(128)S(1)} %pad_add_fusion.refs_0_, s32[2,3]{1,0:T(2,128)S(1)} %copy-done.2, bf16[2,2048]{1,0:T(2,128)(2,1)S(1)} %copy-done.1, bf16[2,16,3,128,128]{4,3,2,1,0:T(8,128)(2,1)S(1)} %copy-done, bf16[1168,128]{1,0:T(8,128)(2,1)S(1)} %collective-permute-done.refs_4_, ...), custom_call_target="tpu_custom_call" | custom-call | tf_op jit(solution)/shard_map/pallas_call | solution.py:264
  15.7 2.3 %collective-permute-start.11 = (bf16[64,2048]{1,0:T(8,128)(2,1)S(1)}, bf16[64,2048]{1,0:T(8,128)(2,1)S(1)}, u32[]{:S(2)}, u32[]{:S(2)}) collective-permute-start(bf16[64,2048]{1,0:T(8,128)(2,1)S(1)} %get-tuple-element.87), channel_id=1, source_target_pairs={{0,8},{1,9},{2,10},{3,11},{4,12},{5,13},{6,14},{7,15},{16,17},{17,... | collective-permute-start | bytes 786440 | tf_op jit(solution)/shard_map/ppermute | solution.py:293
  18.7 1.5 %shard_map.50 = (bf16[64,2048]{1,0:T(8,128)(2,1)S(1)}, bf16[64,2048]{1,0:T(8,128)(2,1)S(1)}) custom-call(s32[2]{0:T(128)S(1)} %pad_add_fusion.refs_0_, s32[2,3]{1,0:T(2,128)S(1)} %copy-done.2, bf16[2,2048]{1,0:T(2,128)(2,1)S(1)} %copy-done.1, bf16[2,16,3,128,128]{4,3,2,1,0:T(8,128)(2,1)S(1)} %copy-done, bf16[1168,128]{1,0:T(8,128)(2,1)S(1)} %collective-permute-done.refs_4_, ...), custom_call_target="tpu_custom_call" | custom-call | tf_op jit(solution)/shard_map/pallas_call | solution.py:264
  20.3 2.0 %collective-permute-start.12 = (bf16[64,2048]{1,0:T(8,128)(2,1)S(1)}, bf16[64,2048]{1,0:T(8,128)(2,1)S(1)}, u32[]{:S(2)}, u32[]{:S(2)}) collective-permute-start(bf16[64,2048]{1,0:T(8,128)(2,1)S(1)} %get-tuple-element.91), channel_id=1, source_target_pairs={{0,8},{1,9},{2,10},{3,11},{4,12},{5,13},{6,14},{7,15},{16,17},{17,... | collective-permute-start | bytes 786440 | tf_op jit(solution)/shard_map/ppermute | solution.py:293
  22.9 1.5 %shard_map.51 = (bf16[64,2048]{1,0:T(8,128)(2,1)S(1)}, bf16[64,2048]{1,0:T(8,128)(2,1)S(1)}) custom-call(s32[2]{0:T(128)S(1)} %pad_add_fusion.refs_0_, s32[2,3]{1,0:T(2,128)S(1)} %copy-done.2, bf16[2,2048]{1,0:T(2,128)(2,1)S(1)} %copy-done.1, bf16[2,16,3,128,128]{4,3,2,1,0:T(8,128)(2,1)S(1)} %copy-done, bf16[1168,128]{1,0:T(8,128)(2,1)S(1)} %collective-permute-done.refs_4_, ...), custom_call_target="tpu_custom_call" | custom-call | tf_op jit(solution)/shard_map/pallas_call | solution.py:264
  24.4 1.3 %collective-permute-start.17 = (bf16[64,2048]{1,0:T(8,128)(2,1)S(1)}, bf16[64,2048]{1,0:T(8,128)(2,1)S(1)}, u32[]{:S(2)}, u32[]{:S(2)}) collective-permute-start(bf16[64,2048]{1,0:T(8,128)(2,1)S(1)} %get-tuple-element.95), channel_id=1, source_target_pairs={{0,8},{1,9},{2,10},{3,11},{4,12},{5,13},{6,14},{7,15},{8,16},{9,17... | collective-permute-start | bytes 786440 | tf_op jit(solution)/shard_map/ppermute | solution.py:293
  26.4 1.5 %shard_map.52 = (bf16[64,2048]{1,0:T(8,128)(2,1)S(1)}, bf16[64,2048]{1,0:T(8,128)(2,1)S(1)}) custom-call(s32[2]{0:T(128)S(1)} %pad_add_fusion.refs_0_, s32[2,3]{1,0:T(2,128)S(1)} %copy-done.2, bf16[2,2048]{1,0:T(2,128)(2,1)S(1)} %copy-done.1, bf16[2,16,3,128,128]{4,3,2,1,0:T(8,128)(2,1)S(1)} %copy-done, bf16[1168,128]{1,0:T(8,128)(2,1)S(1)} %collective-permute-done.refs_4_, ...), custom_call_target="tpu_custom_call" | custom-call | tf_op jit(solution)/shard_map/pallas_call | solution.py:264
  27.9 11.4 %collective-permute-start.18 = (bf16[64,2048]{1,0:T(8,128)(2,1)S(1)}, bf16[64,2048]{1,0:T(8,128)(2,1)S(1)}, u32[]{:S(2)}, u32[]{:S(2)}) collective-permute-start(bf16[64,2048]{1,0:T(8,128)(2,1)S(1)} %get-tuple-element.99), channel_id=1, source_target_pairs={{0,8},{1,9},{2,10},{3,11},{4,12},{5,13},{6,14},{7,15},{8,16},{9,17... | collective-permute-start | bytes 786440 | tf_op jit(solution)/shard_map/ppermute | solution.py:293
  39.3 1.7 %collective-permute-done.17 = bf16[64,2048]{1,0:T(8,128)(2,1)S(1)} collective-permute-done((bf16[64,2048]{1,0:T(8,128)(2,1)S(1)}, bf16[64,2048]{1,0:T(8,128)(2,1)S(1)}, u32[]{:S(2)}, u32[]{:S(2)}) %collective-permute-start.17) | collective-permute-done | bytes 262176 | tf_op jit(solution)/shard_map/ppermute | solution.py:293
  41.1 1.6 %collective-permute-start.23 = (bf16[64,768]{1,0:T(8,128)(2,1)S(1)}, bf16[64,768]{1,0:T(8,128)(2,1)S(1)}, u32[]{:S(2)}, u32[]{:S(2)}) collective-permute-start(bf16[64,768]{1,0:T(8,128)(2,1)S(1)} %get-tuple-element.147), channel_id=1, source_target_pairs={{0,1},{1,0},{2,3},{3,2},{4,5},{5,4},{6,7},{7,6},{8,9},{9,8},{10,11... | collective-permute-start | bytes 294920 | tf_op jit(solution)/shard_map/ppermute | solution.py:162
  42.7 1.5 %shard_map.53 = (bf16[64,2048]{1,0:T(8,128)(2,1)S(1)}, bf16[64,2048]{1,0:T(8,128)(2,1)S(1)}) custom-call(s32[2]{0:T(128)S(1)} %pad_add_fusion.refs_0_, s32[2,3]{1,0:T(2,128)S(1)} %copy-done.2, bf16[2,2048]{1,0:T(2,128)(2,1)S(1)} %copy-done.1, bf16[2,16,3,128,128]{4,3,2,1,0:T(8,128)(2,1)S(1)} %copy-done, bf16[1168,128]{1,0:T(8,128)(2,1)S(1)} %collective-permute-done.refs_4_, ...), custom_call_target="tpu_custom_call" | custom-call | tf_op jit(solution)/shard_map/pallas_call | solution.py:264
  44.2 1.0 collective-permute-start.22
  45.2 1.1 %collective-permute-done.19.refs_8_ = bf16[64,768]{1,0:T(8,128)(2,1)S(1)} collective-permute-done((bf16[64,768]{1,0:T(8,128)(2,1)S(1)}, bf16[64,768]{1,0:T(8,128)(2,1)S(1)}, u32[]{:S(2)}, u32[]{:S(2)}) %collective-permute-start.19) | collective-permute-done | bytes 98336 | tf_op jit(solution)/shard_map/ppermute | solution.py:170
  46.6 1.6 %collective-permute-start.21 = (bf16[64,768]{1,0:T(8,128)(2,1)S(1)}, bf16[64,768]{1,0:T(8,128)(2,1)S(1)}, u32[]{:S(2)}, u32[]{:S(2)}) collective-permute-start(bf16[64,768]{1,0:T(8,128)(2,1)S(1)} %get-tuple-element.145), channel_id=1, source_target_pairs={{0,7},{1,2},{2,1},{3,4},{4,3},{5,6},{6,5},{7,0},{8,15},{9,10},{10,... | collective-permute-start | bytes 294920 | tf_op jit(solution)/shard_map/ppermute | solution.py:170
  48.2 1.6 %shard_map.54 = bf16[64,2048]{1,0:T(8,128)(2,1)S(1)} custom-call(s32[2]{0:T(128)S(1)} %pad_add_fusion.refs_0_, s32[2,3]{1,0:T(2,128)S(1)} %copy-done.2, bf16[2,2048]{1,0:T(2,128)(2,1)S(1)} %copy-done.1, bf16[2,16,3,128,128]{4,3,2,1,0:T(8,128)(2,1)S(1)} %copy-done, bf16[1168,128]{1,0:T(8,128)(2,1)S(1)} %collective-permute-done.refs_4_, ...), custom_call_target="tpu_custom_call" | custom-call | tf_op jit(solution)/shard_map/pallas_call | solution.py:264
  49.9 2.7 %collective-permute-done.22.refs_6_ = bf16[64,2048]{1,0:T(8,128)(2,1)S(1)} collective-permute-done((bf16[64,2048]{1,0:T(8,128)(2,1)S(1)}, bf16[64,2048]{1,0:T(8,128)(2,1)S(1)}, u32[]{:S(2)}, u32[]{:S(2)}) %collective-permute-start.22) | collective-permute-done | bytes 262176 | tf_op jit(solution)/shard_map/ppermute | solution.py:293
  52.6 1.2 %collective-permute-start.26 = (bf16[64,768]{1,0:T(8,128)(2,1)S(1)}, bf16[64,768]{1,0:T(8,128)(2,1)S(1)}, u32[]{:S(2)}, u32[]{:S(2)}) collective-permute-start(bf16[64,768]{1,0:T(8,128)(2,1)S(1)} %get-tuple-element.144), channel_id=1, source_target_pairs={{0,1},{1,0},{2,3},{3,2},{4,5},{5,4},{6,7},{7,6},{8,15},{9,10},{10,... | collective-permute-start | bytes 294920 | tf_op jit(solution)/shard_map/ppermute | solution.py:170
  54.7 1.6 %shard_map.55 = bf16[64,2048]{1,0:T(8,128)(2,1)S(1)} custom-call(s32[2]{0:T(128)S(1)} %pad_add_fusion.refs_0_, s32[2,3]{1,0:T(2,128)S(1)} %copy-done.2, bf16[2,2048]{1,0:T(2,128)(2,1)S(1)} %copy-done.1, bf16[2,16,3,128,128]{4,3,2,1,0:T(8,128)(2,1)S(1)} %copy-done, bf16[1168,128]{1,0:T(8,128)(2,1)S(1)} %collective-permute-done.refs_4_, ...), custom_call_target="tpu_custom_call" | custom-call | tf_op jit(solution)/shard_map/pallas_call | solution.py:264
  56.3 2.2 %collective-permute-done.26.refs_8_ = bf16[64,768]{1,0:T(8,128)(2,1)S(1)} collective-permute-done((bf16[64,768]{1,0:T(8,128)(2,1)S(1)}, bf16[64,768]{1,0:T(8,128)(2,1)S(1)}, u32[]{:S(2)}, u32[]{:S(2)}) %collective-permute-start.26) | collective-permute-done | bytes 98336 | tf_op jit(solution)/shard_map/ppermute | solution.py:170
  58.6 1.1 %collective-permute-start.28 = (bf16[64,768]{1,0:T(8,128)(2,1)S(1)}, bf16[64,768]{1,0:T(8,128)(2,1)S(1)}, u32[]{:S(2)}, u32[]{:S(2)}) collective-permute-start(bf16[64,768]{1,0:T(8,128)(2,1)S(1)} %get-tuple-element.142), channel_id=1, source_target_pairs={{0,1},{1,0},{2,3},{3,2},{4,5},{5,4},{6,7},{7,6},{8,15},{9,10},{10,... | collective-permute-start | bytes 294920 | tf_op jit(solution)/shard_map/ppermute | solution.py:170
  60.3 1.8 %shard_map.56 = bf16[64,2048]{1,0:T(8,128)(2,1)S(1)} custom-call(s32[2]{0:T(128)S(1)} %pad_add_fusion.refs_0_, s32[2,3]{1,0:T(2,128)S(1)} %copy-done.2, bf16[2,2048]{1,0:T(2,128)(2,1)S(1)} %copy-done.1, bf16[2,16,3,128,128]{4,3,2,1,0:T(8,128)(2,1)S(1)} %copy-done, bf16[1168,128]{1,0:T(8,128)(2,1)S(1)} %collective-permute-done.refs_4_, ...), custom_call_target="tpu_custom_call" | custom-call | tf_op jit(solution)/shard_map/pallas_call | solution.py:264
  62.2 2.4 %collective-permute-done.24.refs_6_ = bf16[64,2048]{1,0:T(8,128)(2,1)S(1)} collective-permute-done((bf16[64,2048]{1,0:T(8,128)(2,1)S(1)}, bf16[64,2048]{1,0:T(8,128)(2,1)S(1)}, u32[]{:S(2)}, u32[]{:S(2)}) %collective-permute-start.24) | collective-permute-done | bytes 262176 | tf_op jit(solution)/shard_map/ppermute | solution.py:293
  64.6 1.1 %collective-permute-start.30 = (bf16[64,768]{1,0:T(8,128)(2,1)S(1)}, bf16[64,768]{1,0:T(8,128)(2,1)S(1)}, u32[]{:S(2)}, u32[]{:S(2)}) collective-permute-start(bf16[64,768]{1,0:T(8,128)(2,1)S(1)} %get-tuple-element.139), channel_id=1, source_target_pairs={{0,1},{1,0},{2,3},{3,2},{4,5},{5,4},{6,7},{7,6},{8,15},{9,10},{10,... | collective-permute-start | bytes 294920 | tf_op jit(solution)/shard_map/ppermute | solution.py:170
  65.7 1.6 %shard_map.57 = bf16[64,2048]{1,0:T(8,128)(2,1)S(1)} custom-call(s32[2]{0:T(128)S(1)} %pad_add_fusion.refs_0_, s32[2,3]{1,0:T(2,128)S(1)} %copy-done.2, bf16[2,2048]{1,0:T(2,128)(2,1)S(1)} %copy-done.1, bf16[2,16,3,128,128]{4,3,2,1,0:T(8,128)(2,1)S(1)} %copy-done, bf16[1168,128]{1,0:T(8,128)(2,1)S(1)} %collective-permute-done.refs_4_, ...), custom_call_target="tpu_custom_call" | custom-call | tf_op jit(solution)/shard_map/pallas_call | solution.py:264
  67.3 1.0 collective-permute-start.36
  68.3 1.3 %collective-permute-done.30.refs_8_ = bf16[64,768]{1,0:T(8,128)(2,1)S(1)} collective-permute-done((bf16[64,768]{1,0:T(8,128)(2,1)S(1)}, bf16[64,768]{1,0:T(8,128)(2,1)S(1)}, u32[]{:S(2)}, u32[]{:S(2)}) %collective-permute-start.30) | collective-permute-done | bytes 98336 | tf_op jit(solution)/shard_map/ppermute | solution.py:170
  71.6 1.6 %shard_map.58 = bf16[64,2048]{1,0:T(8,128)(2,1)S(1)} custom-call(s32[2]{0:T(128)S(1)} %pad_add_fusion.refs_0_, s32[2,3]{1,0:T(2,128)S(1)} %copy-done.2, bf16[2,2048]{1,0:T(2,128)(2,1)S(1)} %copy-done.1, bf16[2,16,3,128,128]{4,3,2,1,0:T(8,128)(2,1)S(1)} %copy-done, bf16[1168,128]{1,0:T(8,128)(2,1)S(1)} %collective-permute-done.refs_4_, ...), custom_call_target="tpu_custom_call" | custom-call | tf_op jit(solution)/shard_map/pallas_call | solution.py:264
  73.3 1.4 %collective-permute-start.33 = (bf16[64,2048]{1,0:T(8,128)(2,1)S(1)}, bf16[64,2048]{1,0:T(8,128)(2,1)S(1)}, u32[]{:S(2)}, u32[]{:S(2)}) collective-permute-start(bf16[64,2048]{1,0:T(8,128)(2,1)S(1)} %shard_map.58), channel_id=1, source_target_pairs={{8,16},{9,17},{10,18},{11,19},{12,20},{13,21},{14,22},{15,23},{16,... | collective-permute-start | bytes 786440 | tf_op jit(solution)/shard_map/ppermute | solution.py:293
  74.7 1.4 %collective-permute-done.36.refs_6_ = bf16[64,2048]{1,0:T(8,128)(2,1)S(1)} collective-permute-done((bf16[64,2048]{1,0:T(8,128)(2,1)S(1)}, bf16[64,2048]{1,0:T(8,128)(2,1)S(1)}, u32[]{:S(2)}, u32[]{:S(2)}) %collective-permute-start.36) | collective-permute-done | bytes 262176 | tf_op jit(solution)/shard_map/ppermute | solution.py:293
  77.3 1.6 %shard_map.59 = bf16[64,2048]{1,0:T(8,128)(2,1)S(1)} custom-call(s32[2]{0:T(128)S(1)} %pad_add_fusion.refs_0_, s32[2,3]{1,0:T(2,128)S(1)} %copy-done.2, bf16[2,2048]{1,0:T(2,128)(2,1)S(1)} %copy-done.1, bf16[2,16,3,128,128]{4,3,2,1,0:T(8,128)(2,1)S(1)} %copy-done, bf16[1168,128]{1,0:T(8,128)(2,1)S(1)} %collective-permute-done.refs_4_, ...), custom_call_target="tpu_custom_call" | custom-call | tf_op jit(solution)/shard_map/pallas_call | solution.py:264
  78.9 1.4 %collective-permute-start.40 = (bf16[64,2048]{1,0:T(8,128)(2,1)S(1)}, bf16[64,2048]{1,0:T(8,128)(2,1)S(1)}, u32[]{:S(2)}, u32[]{:S(2)}) collective-permute-start(bf16[64,2048]{1,0:T(8,128)(2,1)S(1)} %shard_map.59), channel_id=1, source_target_pairs={{16,24},{17,25},{18,26},{19,27},{20,28},{21,29},{22,30},{23,31},{2... | collective-permute-start | bytes 786440 | tf_op jit(solution)/shard_map/ppermute | solution.py:293
  80.3 1.0 collective-permute-done.37.refs_8_
  81.3 1.9 %collective-permute-done.33.refs_6_ = bf16[64,2048]{1,0:T(8,128)(2,1)S(1)} collective-permute-done((bf16[64,2048]{1,0:T(8,128)(2,1)S(1)}, bf16[64,2048]{1,0:T(8,128)(2,1)S(1)}, u32[]{:S(2)}, u32[]{:S(2)}) %collective-permute-start.33) | collective-permute-done | bytes 262176 | tf_op jit(solution)/shard_map/ppermute | solution.py:293
  83.3 1.0 collective-permute-start.38
  84.3 1.6 %shard_map.60 = bf16[64,2048]{1,0:T(8,128)(2,1)S(1)} custom-call(s32[2]{0:T(128)S(1)} %pad_add_fusion.refs_0_, s32[2,3]{1,0:T(2,128)S(1)} %copy-done.2, bf16[2,2048]{1,0:T(2,128)(2,1)S(1)} %copy-done.1, bf16[2,16,3,128,128]{4,3,2,1,0:T(8,128)(2,1)S(1)} %copy-done, bf16[1168,128]{1,0:T(8,128)(2,1)S(1)} %collective-permute-done.refs_4_, ...), custom_call_target="tpu_custom_call" | custom-call | tf_op jit(solution)/shard_map/pallas_call | solution.py:264
  86.0 2.3 %collective-permute-done.40.refs_6_ = bf16[64,2048]{1,0:T(8,128)(2,1)S(1)} collective-permute-done((bf16[64,2048]{1,0:T(8,128)(2,1)S(1)}, bf16[64,2048]{1,0:T(8,128)(2,1)S(1)}, u32[]{:S(2)}, u32[]{:S(2)}) %collective-permute-start.40) | collective-permute-done | bytes 262176 | tf_op jit(solution)/shard_map/ppermute | solution.py:293
  88.4 1.6 %shard_map.61 = bf16[64,2048]{1,0:T(8,128)(2,1)S(1)} custom-call(s32[2]{0:T(128)S(1)} %pad_add_fusion.refs_0_, s32[2,3]{1,0:T(2,128)S(1)} %copy-done.2, bf16[2,2048]{1,0:T(2,128)(2,1)S(1)} %copy-done.1, bf16[2,16,3,128,128]{4,3,2,1,0:T(8,128)(2,1)S(1)} %copy-done, bf16[1168,128]{1,0:T(8,128)(2,1)S(1)} %collective-permute-done.refs_4_, ...), custom_call_target="tpu_custom_call" | custom-call | tf_op jit(solution)/shard_map/pallas_call | solution.py:264
  90.0 1.3 %collective-permute-start.42 = (bf16[64,2048]{1,0:T(8,128)(2,1)S(1)}, bf16[64,2048]{1,0:T(8,128)(2,1)S(1)}, u32[]{:S(2)}, u32[]{:S(2)}) collective-permute-start(bf16[64,2048]{1,0:T(8,128)(2,1)S(1)} %shard_map.61), channel_id=1, source_target_pairs={{16,24},{17,25},{18,26},{19,27},{20,28},{21,29},{22,30},{23,31},{2... | collective-permute-start | bytes 786440 | tf_op jit(solution)/shard_map/ppermute | solution.py:293
  91.3 2.9 %collective-permute-done.45.refs_6_ = bf16[64,2048]{1,0:T(8,128)(2,1)S(1)} collective-permute-done((bf16[64,2048]{1,0:T(8,128)(2,1)S(1)}, bf16[64,2048]{1,0:T(8,128)(2,1)S(1)}, u32[]{:S(2)}, u32[]{:S(2)}) %collective-permute-start.45) | collective-permute-done | bytes 262176 | tf_op jit(solution)/shard_map/ppermute | solution.py:293
  95.3 3.4 %collective-permute-start.48 = (bf16[64,2048]{1,0:T(8,128)(2,1)S(1)}, bf16[64,2048]{1,0:T(8,128)(2,1)S(1)}, u32[]{:S(2)}, u32[]{:S(2)}) collective-permute-start(bf16[64,2048]{1,0:T(8,128)(2,1)S(1)} %shard_map.62), channel_id=1, source_target_pairs={{24,16},{25,17},{26,18},{27,19},{28,20},{29,21},{30,22},{31,23},{1... | collective-permute-start | bytes 786440 | tf_op jit(solution)/shard_map/ppermute | solution.py:293
  98.8 1.5 %collective-permute-done.42.refs_6_ = bf16[64,2048]{1,0:T(8,128)(2,1)S(1)} collective-permute-done((bf16[64,2048]{1,0:T(8,128)(2,1)S(1)}, bf16[64,2048]{1,0:T(8,128)(2,1)S(1)}, u32[]{:S(2)}, u32[]{:S(2)}) %collective-permute-start.42) | collective-permute-done | bytes 262176 | tf_op jit(solution)/shard_map/ppermute | solution.py:293
  101.8 3.5 %collective-permute-done.48 = bf16[64,2048]{1,0:T(8,128)(2,1)S(1)} collective-permute-done((bf16[64,2048]{1,0:T(8,128)(2,1)S(1)}, bf16[64,2048]{1,0:T(8,128)(2,1)S(1)}, u32[]{:S(2)}, u32[]{:S(2)}) %collective-permute-start.48) | collective-permute-done | bytes 262176 | tf_op jit(solution)/shard_map/ppermute | solution.py:293
  105.3 1.4 %shard_map.64 = bf16[2,64,2048]{2,1,0:T(8,128)(2,1)} custom-call(s32[2]{0:T(128)S(1)} %pad_add_fusion.refs_0_, s32[2,3]{1,0:T(2,128)S(1)} %copy-done.2, bf16[2,2048]{1,0:T(2,128)(2,1)S(1)} %copy-done.1, bf16[2,16,3,128,128]{4,3,2,1,0:T(8,128)(2,1)S(1)} %copy-done, bf16[1168,128]{1,0:T(8,128)(2,1)S(1)} %collective-permute-done.refs_4_, ...), custom_call_target="tpu_custom_call" | custom-call | tf_op jit(solution)/shard_map/pallas_call | solution.py:264
  (102 shorter events, 13.2 us)
Async XLA Ops:
  1.7 10.3 %collective-permute-start.1 = (bf16[1168,128]{1,0:T(8,128)(2,1)S(1)}, bf16[1168,128]{1,0:T(8,128)(2,1)S(1)}, u32[]{:S(2)}, u32[]{:S(2)}) collective-permute-start(bf16[1168,128]{1,0:T(8,128)(2,1)S(1)} %shard_map.46), channel_id=1, source_target_pairs={{0,7},{1,2},{2,1},{3,4},{4,3},{5,6},{6,5},{7,0},{8,15},{9,10},{10,... | collective-permute-start | bytes 897032 | tf_op jit(solution)/shard_map/ppermute | solution.py:170
  5.6 6.3 %collective-permute-start = (bf16[1168,128]{1,0:T(8,128)(2,1)S(1)}, bf16[1168,128]{1,0:T(8,128)(2,1)S(1)}, u32[]{:S(2)}, u32[]{:S(2)}) collective-permute-start(bf16[1168,128]{1,0:T(8,128)(2,1)S(1)} %get-tuple-element.72), channel_id=1, source_target_pairs={{0,1},{1,0},{2,3},{3,2},{4,5},{5,4},{6,7},{7,6},{8,9},{9,8},{10,11... | collective-permute-start | bytes 897032 | tf_op jit(solution)/shard_map/ppermute | solution.py:162
  5.7 1.7 %collective-permute-start.4 = (bf16[64,768]{1,0:T(8,128)(2,1)S(1)}, bf16[64,768]{1,0:T(8,128)(2,1)S(1)}, u32[]{:S(2)}, u32[]{:S(2)}) collective-permute-start(bf16[64,768]{1,0:T(8,128)(2,1)S(1)} %get-tuple-element.79), channel_id=1, source_target_pairs={{0,1},{1,0},{2,3},{3,2},{4,5},{5,4},{6,7},{7,6},{8,9},{9,8},{10,11... | collective-permute-start | bytes 294920 | tf_op jit(solution)/shard_map/ppermute | solution.py:162
  6.2 7.3 %collective-permute-start.3 = (bf16[64,768]{1,0:T(8,128)(2,1)S(1)}, bf16[64,768]{1,0:T(8,128)(2,1)S(1)}, u32[]{:S(2)}, u32[]{:S(2)}) collective-permute-start(bf16[64,768]{1,0:T(8,128)(2,1)S(1)} %get-tuple-element.76), channel_id=1, source_target_pairs={{0,7},{1,2},{2,1},{3,4},{4,3},{5,6},{6,5},{7,0},{8,9},{9,8},{10,11... | collective-permute-start | bytes 294920 | tf_op jit(solution)/shard_map/ppermute | solution.py:170
  7.4 6.8 %collective-permute-start.2 = (bf16[64,768]{1,0:T(8,128)(2,1)S(1)}, bf16[64,768]{1,0:T(8,128)(2,1)S(1)}, u32[]{:S(2)}, u32[]{:S(2)}) collective-permute-start(bf16[64,768]{1,0:T(8,128)(2,1)S(1)} %get-tuple-element.75), channel_id=1, source_target_pairs={{0,1},{1,0},{2,3},{3,2},{4,5},{5,4},{6,7},{7,6},{8,9},{9,8},{10,11... | collective-permute-start | bytes 294920 | tf_op jit(solution)/shard_map/ppermute | solution.py:162
  13.5 4.6 %collective-permute-start.6 = (bf16[64,2048]{1,0:T(8,128)(2,1)S(1)}, bf16[64,2048]{1,0:T(8,128)(2,1)S(1)}, u32[]{:S(2)}, u32[]{:S(2)}) collective-permute-start(bf16[64,2048]{1,0:T(8,128)(2,1)S(1)} %get-tuple-element.83), channel_id=1, source_target_pairs={{0,8},{1,9},{2,10},{3,11},{4,12},{5,13},{6,14},{7,15},{8,0},{9,1},... | collective-permute-start | bytes 786440 | tf_op jit(solution)/shard_map/ppermute | solution.py:293
  13.6 4.5 %collective-permute-start.7 = (bf16[64,768]{1,0:T(8,128)(2,1)S(1)}, bf16[64,768]{1,0:T(8,128)(2,1)S(1)}, u32[]{:S(2)}, u32[]{:S(2)}) collective-permute-start(bf16[64,768]{1,0:T(8,128)(2,1)S(1)} %get-tuple-element.156), channel_id=1, source_target_pairs={{0,7},{1,2},{2,1},{3,4},{4,3},{5,6},{6,5},{7,0},{8,9},{9,8},{10,11... | collective-permute-start | bytes 294920 | tf_op jit(solution)/shard_map/ppermute | solution.py:170
  14.1 4.6 %collective-permute-start.10 = (bf16[64,768]{1,0:T(8,128)(2,1)S(1)}, bf16[64,768]{1,0:T(8,128)(2,1)S(1)}, u32[]{:S(2)}, u32[]{:S(2)}) collective-permute-start(bf16[64,768]{1,0:T(8,128)(2,1)S(1)} %get-tuple-element.155), channel_id=1, source_target_pairs={{0,1},{1,0},{2,3},{3,2},{4,5},{5,4},{6,7},{7,6},{8,9},{9,8},{10,11... | collective-permute-start | bytes 294920 | tf_op jit(solution)/shard_map/ppermute | solution.py:162
  15.7 6.5 %collective-permute-start.11 = (bf16[64,2048]{1,0:T(8,128)(2,1)S(1)}, bf16[64,2048]{1,0:T(8,128)(2,1)S(1)}, u32[]{:S(2)}, u32[]{:S(2)}) collective-permute-start(bf16[64,2048]{1,0:T(8,128)(2,1)S(1)} %get-tuple-element.87), channel_id=1, source_target_pairs={{0,8},{1,9},{2,10},{3,11},{4,12},{5,13},{6,14},{7,15},{16,17},{17,... | collective-permute-start | bytes 786440 | tf_op jit(solution)/shard_map/ppermute | solution.py:293
  18.2 4.1 %collective-permute-start.9 = (bf16[64,768]{1,0:T(8,128)(2,1)S(1)}, bf16[64,768]{1,0:T(8,128)(2,1)S(1)}, u32[]{:S(2)}, u32[]{:S(2)}) collective-permute-start(bf16[64,768]{1,0:T(8,128)(2,1)S(1)} %get-tuple-element.153), channel_id=1, source_target_pairs={{0,7},{1,2},{2,1},{3,4},{4,3},{5,6},{6,5},{7,0},{8,15},{9,10},{10,... | collective-permute-start | bytes 294920 | tf_op jit(solution)/shard_map/ppermute | solution.py:170
  18.3 4.6 %collective-permute-start.8 = (bf16[64,768]{1,0:T(8,128)(2,1)S(1)}, bf16[64,768]{1,0:T(8,128)(2,1)S(1)}, u32[]{:S(2)}, u32[]{:S(2)}) collective-permute-start(bf16[64,768]{1,0:T(8,128)(2,1)S(1)} %get-tuple-element.154), channel_id=1, source_target_pairs={{0,1},{1,0},{2,3},{3,2},{4,5},{5,4},{6,7},{7,6},{8,9},{9,8},{10,11... | collective-permute-start | bytes 294920 | tf_op jit(solution)/shard_map/ppermute | solution.py:162
  20.3 5.5 %collective-permute-start.12 = (bf16[64,2048]{1,0:T(8,128)(2,1)S(1)}, bf16[64,2048]{1,0:T(8,128)(2,1)S(1)}, u32[]{:S(2)}, u32[]{:S(2)}) collective-permute-start(bf16[64,2048]{1,0:T(8,128)(2,1)S(1)} %get-tuple-element.91), channel_id=1, source_target_pairs={{0,8},{1,9},{2,10},{3,11},{4,12},{5,13},{6,14},{7,15},{16,17},{17,... | collective-permute-start | bytes 786440 | tf_op jit(solution)/shard_map/ppermute | solution.py:293
  22.3 3.4 %collective-permute-start.13 = (bf16[64,768]{1,0:T(8,128)(2,1)S(1)}, bf16[64,768]{1,0:T(8,128)(2,1)S(1)}, u32[]{:S(2)}, u32[]{:S(2)}) collective-permute-start(bf16[64,768]{1,0:T(8,128)(2,1)S(1)} %get-tuple-element.152), channel_id=1, source_target_pairs={{0,7},{1,2},{2,1},{3,4},{4,3},{5,6},{6,5},{7,0},{8,15},{9,10},{10,... | collective-permute-start | bytes 294920 | tf_op jit(solution)/shard_map/ppermute | solution.py:170
  22.8 3.6 %collective-permute-start.16 = (bf16[64,768]{1,0:T(8,128)(2,1)S(1)}, bf16[64,768]{1,0:T(8,128)(2,1)S(1)}, u32[]{:S(2)}, u32[]{:S(2)}) collective-permute-start(bf16[64,768]{1,0:T(8,128)(2,1)S(1)} %get-tuple-element.151), channel_id=1, source_target_pairs={{0,1},{1,0},{2,3},{3,2},{4,5},{5,4},{6,7},{7,6},{8,9},{9,8},{10,11... | collective-permute-start | bytes 294920 | tf_op jit(solution)/shard_map/ppermute | solution.py:162
  24.4 16.5 %collective-permute-start.17 = (bf16[64,2048]{1,0:T(8,128)(2,1)S(1)}, bf16[64,2048]{1,0:T(8,128)(2,1)S(1)}, u32[]{:S(2)}, u32[]{:S(2)}) collective-permute-start(bf16[64,2048]{1,0:T(8,128)(2,1)S(1)} %get-tuple-element.95), channel_id=1, source_target_pairs={{0,8},{1,9},{2,10},{3,11},{4,12},{5,13},{6,14},{7,15},{8,16},{9,17... | collective-permute-start | bytes 786440 | tf_op jit(solution)/shard_map/ppermute | solution.py:293
  25.8 15.1 %collective-permute-start.15 = (bf16[64,768]{1,0:T(8,128)(2,1)S(1)}, bf16[64,768]{1,0:T(8,128)(2,1)S(1)}, u32[]{:S(2)}, u32[]{:S(2)}) collective-permute-start(bf16[64,768]{1,0:T(8,128)(2,1)S(1)} %get-tuple-element.149), channel_id=1, source_target_pairs={{0,7},{1,2},{2,1},{3,4},{4,3},{5,6},{6,5},{7,0},{8,15},{9,10},{10,... | collective-permute-start | bytes 294920 | tf_op jit(solution)/shard_map/ppermute | solution.py:170
  26.3 16.3 %collective-permute-start.14 = (bf16[64,768]{1,0:T(8,128)(2,1)S(1)}, bf16[64,768]{1,0:T(8,128)(2,1)S(1)}, u32[]{:S(2)}, u32[]{:S(2)}) collective-permute-start(bf16[64,768]{1,0:T(8,128)(2,1)S(1)} %get-tuple-element.150), channel_id=1, source_target_pairs={{0,1},{1,0},{2,3},{3,2},{4,5},{5,4},{6,7},{7,6},{8,9},{9,8},{10,11... | collective-permute-start | bytes 294920 | tf_op jit(solution)/shard_map/ppermute | solution.py:162
  27.9 18.7 %collective-permute-start.18 = (bf16[64,2048]{1,0:T(8,128)(2,1)S(1)}, bf16[64,2048]{1,0:T(8,128)(2,1)S(1)}, u32[]{:S(2)}, u32[]{:S(2)}) collective-permute-start(bf16[64,2048]{1,0:T(8,128)(2,1)S(1)} %get-tuple-element.99), channel_id=1, source_target_pairs={{0,8},{1,9},{2,10},{3,11},{4,12},{5,13},{6,14},{7,15},{8,16},{9,17... | collective-permute-start | bytes 786440 | tf_op jit(solution)/shard_map/ppermute | solution.py:293
  41.0 5.2 %collective-permute-start.19 = (bf16[64,768]{1,0:T(8,128)(2,1)S(1)}, bf16[64,768]{1,0:T(8,128)(2,1)S(1)}, u32[]{:S(2)}, u32[]{:S(2)}) collective-permute-start(bf16[64,768]{1,0:T(8,128)(2,1)S(1)} %get-tuple-element.148), channel_id=1, source_target_pairs={{0,7},{1,2},{2,1},{3,4},{4,3},{5,6},{6,5},{7,0},{8,15},{9,10},{10,... | collective-permute-start | bytes 294920 | tf_op jit(solution)/shard_map/ppermute | solution.py:170
  41.1 7.1 %collective-permute-start.23 = (bf16[64,768]{1,0:T(8,128)(2,1)S(1)}, bf16[64,768]{1,0:T(8,128)(2,1)S(1)}, u32[]{:S(2)}, u32[]{:S(2)}) collective-permute-start(bf16[64,768]{1,0:T(8,128)(2,1)S(1)} %get-tuple-element.147), channel_id=1, source_target_pairs={{0,1},{1,0},{2,3},{3,2},{4,5},{5,4},{6,7},{7,6},{8,9},{9,8},{10,11... | collective-permute-start | bytes 294920 | tf_op jit(solution)/shard_map/ppermute | solution.py:162
  44.2 8.4 %collective-permute-start.22 = (bf16[64,2048]{1,0:T(8,128)(2,1)S(1)}, bf16[64,2048]{1,0:T(8,128)(2,1)S(1)}, u32[]{:S(2)}, u32[]{:S(2)}) collective-permute-start(bf16[64,2048]{1,0:T(8,128)(2,1)S(1)} %get-tuple-element.103), channel_id=1, source_target_pairs={{0,8},{1,9},{2,10},{3,11},{4,12},{5,13},{6,14},{7,15},{8,16},{9,17... | collective-permute-start | bytes 786440 | tf_op jit(solution)/shard_map/ppermute | solution.py:293
  46.6 6.0 %collective-permute-start.21 = (bf16[64,768]{1,0:T(8,128)(2,1)S(1)}, bf16[64,768]{1,0:T(8,128)(2,1)S(1)}, u32[]{:S(2)}, u32[]{:S(2)}) collective-permute-start(bf16[64,768]{1,0:T(8,128)(2,1)S(1)} %get-tuple-element.145), channel_id=1, source_target_pairs={{0,7},{1,2},{2,1},{3,4},{4,3},{5,6},{6,5},{7,0},{8,15},{9,10},{10,... | collective-permute-start | bytes 294920 | tf_op jit(solution)/shard_map/ppermute | solution.py:170
  48.2 6.5 %collective-permute-start.20 = (bf16[64,768]{1,0:T(8,128)(2,1)S(1)}, bf16[64,768]{1,0:T(8,128)(2,1)S(1)}, u32[]{:S(2)}, u32[]{:S(2)}) collective-permute-start(bf16[64,768]{1,0:T(8,128)(2,1)S(1)} %get-tuple-element.146), channel_id=1, source_target_pairs={{0,1},{1,0},{2,3},{3,2},{4,5},{5,4},{6,7},{7,6},{8,9},{9,8},{10,11... | collective-permute-start | bytes 294920 | tf_op jit(solution)/shard_map/ppermute | solution.py:162
  49.8 8.8 %collective-permute-start.27 = (bf16[64,2048]{1,0:T(8,128)(2,1)S(1)}, bf16[64,2048]{1,0:T(8,128)(2,1)S(1)}, u32[]{:S(2)}, u32[]{:S(2)}) collective-permute-start(bf16[64,2048]{1,0:T(8,128)(2,1)S(1)} %shard_map.54), channel_id=1, source_target_pairs={{0,8},{1,9},{2,10},{3,11},{4,12},{5,13},{6,14},{7,15},{8,16},{9,17... | collective-permute-start | bytes 786440 | tf_op jit(solution)/shard_map/ppermute | solution.py:293
  52.6 6.0 %collective-permute-start.26 = (bf16[64,768]{1,0:T(8,128)(2,1)S(1)}, bf16[64,768]{1,0:T(8,128)(2,1)S(1)}, u32[]{:S(2)}, u32[]{:S(2)}) collective-permute-start(bf16[64,768]{1,0:T(8,128)(2,1)S(1)} %get-tuple-element.144), channel_id=1, source_target_pairs={{0,1},{1,0},{2,3},{3,2},{4,5},{5,4},{6,7},{7,6},{8,15},{9,10},{10,... | collective-permute-start | bytes 294920 | tf_op jit(solution)/shard_map/ppermute | solution.py:170
  53.8 6.5 %collective-permute-start.25 = (bf16[64,768]{1,0:T(8,128)(2,1)S(1)}, bf16[64,768]{1,0:T(8,128)(2,1)S(1)}, u32[]{:S(2)}, u32[]{:S(2)}) collective-permute-start(bf16[64,768]{1,0:T(8,128)(2,1)S(1)} %get-tuple-element.143), channel_id=1, source_target_pairs={{0,1},{1,0},{2,3},{3,2},{4,5},{5,4},{6,7},{7,6},{8,9},{9,8},{10,11... | collective-permute-start | bytes 294920 | tf_op jit(solution)/shard_map/ppermute | solution.py:162
  56.3 8.3 %collective-permute-start.24 = (bf16[64,2048]{1,0:T(8,128)(2,1)S(1)}, bf16[64,2048]{1,0:T(8,128)(2,1)S(1)}, u32[]{:S(2)}, u32[]{:S(2)}) collective-permute-start(bf16[64,2048]{1,0:T(8,128)(2,1)S(1)} %shard_map.55), channel_id=1, source_target_pairs={{0,8},{1,9},{2,10},{3,11},{4,12},{5,13},{6,14},{7,15},{8,16},{9,17... | collective-permute-start | bytes 786440 | tf_op jit(solution)/shard_map/ppermute | solution.py:293
  58.6 5.9 %collective-permute-start.28 = (bf16[64,768]{1,0:T(8,128)(2,1)S(1)}, bf16[64,768]{1,0:T(8,128)(2,1)S(1)}, u32[]{:S(2)}, u32[]{:S(2)}) collective-permute-start(bf16[64,768]{1,0:T(8,128)(2,1)S(1)} %get-tuple-element.142), channel_id=1, source_target_pairs={{0,1},{1,0},{2,3},{3,2},{4,5},{5,4},{6,7},{7,6},{8,15},{9,10},{10,... | collective-permute-start | bytes 294920 | tf_op jit(solution)/shard_map/ppermute | solution.py:170
  59.7 6.0 %collective-permute-start.32 = (bf16[64,768]{1,0:T(8,128)(2,1)S(1)}, bf16[64,768]{1,0:T(8,128)(2,1)S(1)}, u32[]{:S(2)}, u32[]{:S(2)}) collective-permute-start(bf16[64,768]{1,0:T(8,128)(2,1)S(1)} %get-tuple-element.141), channel_id=1, source_target_pairs={{0,1},{1,0},{2,3},{3,2},{4,5},{5,4},{6,7},{7,6},{8,9},{9,8},{10,11... | collective-permute-start | bytes 294920 | tf_op jit(solution)/shard_map/ppermute | solution.py:162
  62.1 8.3 %collective-permute-start.31 = (bf16[64,2048]{1,0:T(8,128)(2,1)S(1)}, bf16[64,2048]{1,0:T(8,128)(2,1)S(1)}, u32[]{:S(2)}, u32[]{:S(2)}) collective-permute-start(bf16[64,2048]{1,0:T(8,128)(2,1)S(1)} %shard_map.56), channel_id=1, source_target_pairs={{8,16},{9,17},{10,18},{11,19},{12,20},{13,21},{14,22},{15,23},{16,... | collective-permute-start | bytes 786440 | tf_op jit(solution)/shard_map/ppermute | solution.py:293
  64.6 5.0 %collective-permute-start.30 = (bf16[64,768]{1,0:T(8,128)(2,1)S(1)}, bf16[64,768]{1,0:T(8,128)(2,1)S(1)}, u32[]{:S(2)}, u32[]{:S(2)}) collective-permute-start(bf16[64,768]{1,0:T(8,128)(2,1)S(1)} %get-tuple-element.139), channel_id=1, source_target_pairs={{0,1},{1,0},{2,3},{3,2},{4,5},{5,4},{6,7},{7,6},{8,15},{9,10},{10,... | collective-permute-start | bytes 294920 | tf_op jit(solution)/shard_map/ppermute | solution.py:170
  65.7 5.9 %collective-permute-start.29 = (bf16[64,768]{1,0:T(8,128)(2,1)S(1)}, bf16[64,768]{1,0:T(8,128)(2,1)S(1)}, u32[]{:S(2)}, u32[]{:S(2)}) collective-permute-start(bf16[64,768]{1,0:T(8,128)(2,1)S(1)} %get-tuple-element.140), channel_id=1, source_target_pairs={{0,1},{1,0},{2,3},{3,2},{4,5},{5,4},{6,7},{7,6},{8,9},{9,8},{10,11... | collective-permute-start | bytes 294920 | tf_op jit(solution)/shard_map/ppermute | solution.py:162
  67.3 8.8 %collective-permute-start.36 = (bf16[64,2048]{1,0:T(8,128)(2,1)S(1)}, bf16[64,2048]{1,0:T(8,128)(2,1)S(1)}, u32[]{:S(2)}, u32[]{:S(2)}) collective-permute-start(bf16[64,2048]{1,0:T(8,128)(2,1)S(1)} %shard_map.57), channel_id=1, source_target_pairs={{8,16},{9,17},{10,18},{11,19},{12,20},{13,21},{14,22},{15,23},{16,... | collective-permute-start | bytes 786440 | tf_op jit(solution)/shard_map/ppermute | solution.py:293
  70.4 5.7 %collective-permute-start.35 = (bf16[64,768]{1,0:T(8,128)(2,1)S(1)}, bf16[64,768]{1,0:T(8,128)(2,1)S(1)}, u32[]{:S(2)}, u32[]{:S(2)}) collective-permute-start(bf16[64,768]{1,0:T(8,128)(2,1)S(1)} %get-tuple-element.138), channel_id=1, source_target_pairs={{0,1},{1,0},{2,3},{3,2},{4,5},{5,4},{6,7},{7,6},{8,9},{9,8},{10,11... | collective-permute-start | bytes 294920 | tf_op jit(solution)/shard_map/ppermute | solution.py:170
  71.1 6.2 %collective-permute-start.34 = (bf16[64,768]{1,0:T(8,128)(2,1)S(1)}, bf16[64,768]{1,0:T(8,128)(2,1)S(1)}, u32[]{:S(2)}, u32[]{:S(2)}) collective-permute-start(bf16[64,768]{1,0:T(8,128)(2,1)S(1)} %get-tuple-element.137), channel_id=1, source_target_pairs={{0,1},{1,0},{2,3},{3,2},{4,5},{5,4},{6,7},{7,6},{8,9},{9,8},{10,11... | collective-permute-start | bytes 294920 | tf_op jit(solution)/shard_map/ppermute | solution.py:162
  73.3 10.0 %collective-permute-start.33 = (bf16[64,2048]{1,0:T(8,128)(2,1)S(1)}, bf16[64,2048]{1,0:T(8,128)(2,1)S(1)}, u32[]{:S(2)}, u32[]{:S(2)}) collective-permute-start(bf16[64,2048]{1,0:T(8,128)(2,1)S(1)} %shard_map.58), channel_id=1, source_target_pairs={{8,16},{9,17},{10,18},{11,19},{12,20},{13,21},{14,22},{15,23},{16,... | collective-permute-start | bytes 786440 | tf_op jit(solution)/shard_map/ppermute | solution.py:293
  76.1 5.2 %collective-permute-start.37 = (bf16[64,768]{1,0:T(8,128)(2,1)S(1)}, bf16[64,768]{1,0:T(8,128)(2,1)S(1)}, u32[]{:S(2)}, u32[]{:S(2)}) collective-permute-start(bf16[64,768]{1,0:T(8,128)(2,1)S(1)} %get-tuple-element.136), channel_id=1, source_target_pairs={{0,1},{1,0},{2,3},{3,2},{4,5},{5,4},{6,7},{7,6},{8,9},{9,8},{10,11... | collective-permute-start | bytes 294920 | tf_op jit(solution)/shard_map/ppermute | solution.py:170
  77.0 7.3 %collective-permute-start.41 = (bf16[64,768]{1,0:T(8,128)(2,1)S(1)}, bf16[64,768]{1,0:T(8,128)(2,1)S(1)}, u32[]{:S(2)}, u32[]{:S(2)}) collective-permute-start(bf16[64,768]{1,0:T(8,128)(2,1)S(1)} %get-tuple-element.135), channel_id=1, source_target_pairs={{0,1},{1,0},{2,3},{3,2},{4,5},{5,4},{6,7},{7,6},{8,9},{9,8},{10,11... | collective-permute-start | bytes 294920 | tf_op jit(solution)/shard_map/ppermute | solution.py:162
  78.9 9.4 %collective-permute-start.40 = (bf16[64,2048]{1,0:T(8,128)(2,1)S(1)}, bf16[64,2048]{1,0:T(8,128)(2,1)S(1)}, u32[]{:S(2)}, u32[]{:S(2)}) collective-permute-start(bf16[64,2048]{1,0:T(8,128)(2,1)S(1)} %shard_map.59), channel_id=1, source_target_pairs={{16,24},{17,25},{18,26},{19,27},{20,28},{21,29},{22,30},{23,31},{2... | collective-permute-start | bytes 786440 | tf_op jit(solution)/shard_map/ppermute | solution.py:293
  83.3 5.0 %collective-permute-start.39 = (bf16[64,768]{1,0:T(8,128)(2,1)S(1)}, bf16[64,768]{1,0:T(8,128)(2,1)S(1)}, u32[]{:S(2)}, u32[]{:S(2)}) collective-permute-start(bf16[64,768]{1,0:T(8,128)(2,1)S(1)} %get-tuple-element.133), channel_id=1, source_target_pairs={{0,1},{1,0},{2,3},{3,2},{4,5},{5,4},{6,7},{7,6},{8,9},{9,8},{10,11... | collective-permute-start | bytes 294920 | tf_op jit(solution)/shard_map/ppermute | solution.py:170
  83.3 5.1 %collective-permute-start.38 = (bf16[64,768]{1,0:T(8,128)(2,1)S(1)}, bf16[64,768]{1,0:T(8,128)(2,1)S(1)}, u32[]{:S(2)}, u32[]{:S(2)}) collective-permute-start(bf16[64,768]{1,0:T(8,128)(2,1)S(1)} %get-tuple-element.134), channel_id=1, source_target_pairs={{0,1},{1,0},{2,3},{3,2},{4,5},{5,4},{6,7},{7,6},{8,9},{9,8},{10,11... | collective-permute-start | bytes 294920 | tf_op jit(solution)/shard_map/ppermute | solution.py:162
  85.9 8.3 %collective-permute-start.45 = (bf16[64,2048]{1,0:T(8,128)(2,1)S(1)}, bf16[64,2048]{1,0:T(8,128)(2,1)S(1)}, u32[]{:S(2)}, u32[]{:S(2)}) collective-permute-start(bf16[64,2048]{1,0:T(8,128)(2,1)S(1)} %shard_map.60), channel_id=1, source_target_pairs={{16,24},{17,25},{18,26},{19,27},{20,28},{21,29},{22,30},{23,31},{2... | collective-permute-start | bytes 786440 | tf_op jit(solution)/shard_map/ppermute | solution.py:293
  88.3 3.0 %collective-permute-start.44 = (bf16[64,768]{1,0:T(8,128)(2,1)S(1)}, bf16[64,768]{1,0:T(8,128)(2,1)S(1)}, u32[]{:S(2)}, u32[]{:S(2)}) collective-permute-start(bf16[64,768]{1,0:T(8,128)(2,1)S(1)} %get-tuple-element.132), channel_id=1, source_target_pairs={{0,1},{1,0},{2,3},{3,2},{4,5},{5,4},{6,7},{7,6},{8,9},{9,8},{10,11... | collective-permute-start | bytes 294920 | tf_op jit(solution)/shard_map/ppermute | solution.py:170
  90.0 10.2 %collective-permute-start.42 = (bf16[64,2048]{1,0:T(8,128)(2,1)S(1)}, bf16[64,2048]{1,0:T(8,128)(2,1)S(1)}, u32[]{:S(2)}, u32[]{:S(2)}) collective-permute-start(bf16[64,2048]{1,0:T(8,128)(2,1)S(1)} %shard_map.61), channel_id=1, source_target_pairs={{16,24},{17,25},{18,26},{19,27},{20,28},{21,29},{22,30},{23,31},{2... | collective-permute-start | bytes 786440 | tf_op jit(solution)/shard_map/ppermute | solution.py:293
  91.3 3.5 %collective-permute-start.43 = (bf16[64,768]{1,0:T(8,128)(2,1)S(1)}, bf16[64,768]{1,0:T(8,128)(2,1)S(1)}, u32[]{:S(2)}, u32[]{:S(2)}) collective-permute-start(bf16[64,768]{1,0:T(8,128)(2,1)S(1)} %get-tuple-element.131), channel_id=1, source_target_pairs={{0,1},{1,0},{2,3},{3,2},{4,5},{5,4},{6,7},{7,6},{8,9},{9,8},{10,11... | collective-permute-start | bytes 294920 | tf_op jit(solution)/shard_map/ppermute | solution.py:162
  94.2 6.7 %collective-permute-start.49 = (bf16[64,768]{1,0:T(8,128)(2,1)S(1)}, bf16[64,768]{1,0:T(8,128)(2,1)S(1)}, u32[]{:S(2)}, u32[]{:S(2)}) collective-permute-start(bf16[64,768]{1,0:T(8,128)(2,1)S(1)} %get-tuple-element.129), channel_id=1, source_target_pairs={{0,1},{1,0},{2,3},{3,2},{4,5},{5,4},{6,7},{7,6},{8,9},{9,8},{10,11... | collective-permute-start | bytes 294920 | tf_op jit(solution)/shard_map/ppermute | solution.py:162
  94.3 6.6 %collective-permute-start.50 = (bf16[64,768]{1,0:T(8,128)(2,1)S(1)}, bf16[64,768]{1,0:T(8,128)(2,1)S(1)}, u32[]{:S(2)}, u32[]{:S(2)}) collective-permute-start(bf16[64,768]{1,0:T(8,128)(2,1)S(1)} %get-tuple-element.130), channel_id=1, source_target_pairs={{0,1},{1,0},{2,3},{3,2},{4,5},{5,4},{6,7},{7,6},{8,9},{9,8},{10,11... | collective-permute-start | bytes 294920 | tf_op jit(solution)/shard_map/ppermute | solution.py:170
  95.3 9.9 %collective-permute-start.48 = (bf16[64,2048]{1,0:T(8,128)(2,1)S(1)}, bf16[64,2048]{1,0:T(8,128)(2,1)S(1)}, u32[]{:S(2)}, u32[]{:S(2)}) collective-permute-start(bf16[64,2048]{1,0:T(8,128)(2,1)S(1)} %shard_map.62), channel_id=1, source_target_pairs={{24,16},{25,17},{26,18},{27,19},{28,20},{29,21},{30,22},{31,23},{1... | collective-permute-start | bytes 786440 | tf_op jit(solution)/shard_map/ppermute | solution.py:293
  (6 other events, 35.0 us)

commit v6 on v5

--- a/solution.py
+++ b/solution.py
@@ -280,7 +280,7 @@
         idle = [s for s in range(sections) if s not in [a for a, _ in moves]]
         open_ = [s for s in range(sections) if s not in [b for _, b in moves]]
         pairs = [(a * neurons + n, b * neurons + n) for a, b in moves for n in range(neurons)]
-        if 0 < step <= LAG:
+        if 0 < step < LAG:
             idle = [s for s in idle if s in open_]
             open_ = idle
         for a, b in zip(

time: 107 us -> 108 us (level)
  waiting for transfers between devices: 32.5 us -> 28.2 us
  starting transfers between devices: 45 us -> 49.3 us
    ppermute x18, starting transfers between devices: 11.5 us -> 15.1 us  [send_far(): return lax.ppermute(value, both, pairs)]
    ppermute x15, waiting for transfers between devices: 21.3 us -> 17.8 us  [hop(): return lax.ppermute(out, both, pairs)]
    ppermute x15, starting transfers between devices: 26.7 us -> 28.5 us  [hop(): return lax.ppermute(out, both, pairs)]
  transfers between devices with their start and end apart: 51 -> 51, of which waited for: 19 -> 20; matrix products, arithmetic and copies ran while one was open for 0% -> 0% of each run, Pallas kernels for 24% -> 24%
where the time goes in v6:
time: 108 us; the launch traced here: 107 us
  starting transfers between devices  49.3 us (46%)
  Pallas kernels  28.2 us (26%)
  waiting for transfers between devices  28.2 us (26%)
    ppermute x15, starting transfers between devices, hop(): return lax.ppermute(out, both, pairs)  28.5 us
    pallas_call x17, Pallas kernels, run(): pl.pallas_call(lambda *refs: layers_kernel(sizes, step, chunks, next_plac...  24.7 us
    ppermute x15, waiting for transfers between devices, hop(): return lax.ppermute(out, both, pairs)  17.8 us
    ppermute x18, starting transfers between devices, send_far(): return lax.ppermute(value, both, pairs)  15.1 us
    ppermute x18, waiting for transfers between devices, send_far(): return lax.ppermute(value, both, pairs)  9.48 us
    ppermute x18, starting transfers between devices, send_near(): return lax.ppermute(value, both, pairs)  5.7 us
    pallas_call x2, Pallas kernels, stage(): pl.pallas_call(lambda *refs: stage_kernel(my_copies, my_rows, *refs), in_...  3.48 us
  transfers between devices with their start and end apart: 51, of which 20 were waited for; matrix products, arithmetic and copies ran while one was open for 0% of the time, Pallas kernels for 24%

profile of v6, /device:TPU:16, one launch (start us, length us, event | category | flops | bytes accessed | tf_op | source)
XLA Modules:
  0.0 106.8 jit_solution(10881321711393623939)
XLA Ops:
  0.1 1.5 %shard_map.46 = bf16[1168,128]{1,0:T(8,128)(2,1)S(1)} custom-call(s32[2]{0:T(128)S(1)} %pad_add_fusion.refs_0_, bf16[2,2048]{1,0:T(2,128)(2,1)} %refs_2_.16, bf16[2,6144,128]{2,1,0:T(8,128)(2,1)} %bitcast.4, bf16[2,256,2048]{2,1,0:T(8,128)(2,1)} %refs_9_.5), custom_call_target="tpu_custom_call" | custom-call | tf_op jit(solution)/shard_map/pallas_call | solution.py:212
  1.7 2.0 %collective-permute-start.1 = (bf16[1168,128]{1,0:T(8,128)(2,1)S(1)}, bf16[1168,128]{1,0:T(8,128)(2,1)S(1)}, u32[]{:S(2)}, u32[]{:S(2)}) collective-permute-start(bf16[1168,128]{1,0:T(8,128)(2,1)S(1)} %shard_map.46), channel_id=1, source_target_pairs={{0,7},{1,2},{2,1},{3,4},{4,3},{5,6},{6,5},{7,0},{8,15},{9,10},{10,... | collective-permute-start | bytes 897032 | tf_op jit(solution)/shard_map/ppermute | solution.py:170
  3.6 1.9 %shard_map.47 = (bf16[64,768]{1,0:T(8,128)(2,1)S(1)}, bf16[64,768]{1,0:T(8,128)(2,1)S(1)}, bf16[64,768]{1,0:T(8,128)(2,1)S(1)}, bf16[64,768]{1,0:T(8,128)(2,1)S(...) custom-call(s32[2]{0:T(128)S(1)} %pad_add_fusion.refs_0_, ...), custom_call_target="tpu_custom_call" | custom-call | tf_op jit(solution)/shard_map/pallas_call | solution.py:212
  7.5 4.4 %collective-permute-done.1.refs_5_ = bf16[1168,128]{1,0:T(8,128)(2,1)S(1)} collective-permute-done((bf16[1168,128]{1,0:T(8,128)(2,1)S(1)}, bf16[1168,128]{1,0:T(8,128)(2,1)S(1)}, u32[]{:S(2)}, u32[]{:S(2)}) %collective-permute-start.1) | collective-permute-done | bytes 299040 | tf_op jit(solution)/shard_map/ppermute | solution.py:170
  11.9 1.5 %shard_map.48 = (bf16[64,2048]{1,0:T(8,128)(2,1)S(1)}, bf16[64,2048]{1,0:T(8,128)(2,1)S(1)}) custom-call(s32[2]{0:T(128)S(1)} %pad_add_fusion.refs_0_, s32[2,3]{1,0:T(2,128)S(1)} %copy-done.2, bf16[2,2048]{1,0:T(2,128)(2,1)S(1)} %copy-done.1, bf16[2,16,3,128,128]{4,3,2,1,0:T(8,128)(2,1)S(1)} %copy-done, bf16[1168,128]{1,0:T(8,128)(2,1)S(1)} %collective-permute-done.refs_4_, ...), custom_call_target="tpu_custom_call" | custom-call | tf_op jit(solution)/shard_map/pallas_call | solution.py:264
  14.2 1.5 %shard_map.49 = (bf16[64,2048]{1,0:T(8,128)(2,1)S(1)}, bf16[64,2048]{1,0:T(8,128)(2,1)S(1)}) custom-call(s32[2]{0:T(128)S(1)} %pad_add_fusion.refs_0_, s32[2,3]{1,0:T(2,128)S(1)} %copy-done.2, bf16[2,2048]{1,0:T(2,128)(2,1)S(1)} %copy-done.1, bf16[2,16,3,128,128]{4,3,2,1,0:T(8,128)(2,1)S(1)} %copy-done, bf16[1168,128]{1,0:T(8,128)(2,1)S(1)} %collective-permute-done.refs_4_, ...), custom_call_target="tpu_custom_call" | custom-call | tf_op jit(solution)/shard_map/pallas_call | solution.py:264
  15.7 2.3 %collective-permute-start.11 = (bf16[64,2048]{1,0:T(8,128)(2,1)S(1)}, bf16[64,2048]{1,0:T(8,128)(2,1)S(1)}, u32[]{:S(2)}, u32[]{:S(2)}) collective-permute-start(bf16[64,2048]{1,0:T(8,128)(2,1)S(1)} %get-tuple-element.87), channel_id=1, source_target_pairs={{0,8},{1,9},{2,10},{3,11},{4,12},{5,13},{6,14},{7,15},{16,17},{17,... | collective-permute-start | bytes 786440 | tf_op jit(solution)/shard_map/ppermute | solution.py:293
  18.7 1.5 %shard_map.50 = (bf16[64,2048]{1,0:T(8,128)(2,1)S(1)}, bf16[64,2048]{1,0:T(8,128)(2,1)S(1)}) custom-call(s32[2]{0:T(128)S(1)} %pad_add_fusion.refs_0_, s32[2,3]{1,0:T(2,128)S(1)} %copy-done.2, bf16[2,2048]{1,0:T(2,128)(2,1)S(1)} %copy-done.1, bf16[2,16,3,128,128]{4,3,2,1,0:T(8,128)(2,1)S(1)} %copy-done, bf16[1168,128]{1,0:T(8,128)(2,1)S(1)} %collective-permute-done.refs_4_, ...), custom_call_target="tpu_custom_call" | custom-call | tf_op jit(solution)/shard_map/pallas_call | solution.py:264
  20.3 2.0 %collective-permute-start.12 = (bf16[64,2048]{1,0:T(8,128)(2,1)S(1)}, bf16[64,2048]{1,0:T(8,128)(2,1)S(1)}, u32[]{:S(2)}, u32[]{:S(2)}) collective-permute-start(bf16[64,2048]{1,0:T(8,128)(2,1)S(1)} %get-tuple-element.91), channel_id=1, source_target_pairs={{0,8},{1,9},{2,10},{3,11},{4,12},{5,13},{6,14},{7,15},{16,17},{17,... | collective-permute-start | bytes 786440 | tf_op jit(solution)/shard_map/ppermute | solution.py:293
  22.9 1.5 %shard_map.51 = (bf16[64,2048]{1,0:T(8,128)(2,1)S(1)}, bf16[64,2048]{1,0:T(8,128)(2,1)S(1)}) custom-call(s32[2]{0:T(128)S(1)} %pad_add_fusion.refs_0_, s32[2,3]{1,0:T(2,128)S(1)} %copy-done.2, bf16[2,2048]{1,0:T(2,128)(2,1)S(1)} %copy-done.1, bf16[2,16,3,128,128]{4,3,2,1,0:T(8,128)(2,1)S(1)} %copy-done, bf16[1168,128]{1,0:T(8,128)(2,1)S(1)} %collective-permute-done.refs_4_, ...), custom_call_target="tpu_custom_call" | custom-call | tf_op jit(solution)/shard_map/pallas_call | solution.py:264
  24.4 8.6 %collective-permute-start.17 = (bf16[64,2048]{1,0:T(8,128)(2,1)S(1)}, bf16[64,2048]{1,0:T(8,128)(2,1)S(1)}, u32[]{:S(2)}, u32[]{:S(2)}) collective-permute-start(bf16[64,2048]{1,0:T(8,128)(2,1)S(1)} %get-tuple-element.95), channel_id=1, source_target_pairs={{0,8},{1,9},{2,10},{3,11},{4,12},{5,13},{6,14},{7,15},{8,16},{9,17... | collective-permute-start | bytes 786440 | tf_op jit(solution)/shard_map/ppermute | solution.py:293
  33.7 1.5 %shard_map.52 = (bf16[64,2048]{1,0:T(8,128)(2,1)S(1)}, bf16[64,2048]{1,0:T(8,128)(2,1)S(1)}) custom-call(s32[2]{0:T(128)S(1)} %pad_add_fusion.refs_0_, s32[2,3]{1,0:T(2,128)S(1)} %copy-done.2, bf16[2,2048]{1,0:T(2,128)(2,1)S(1)} %copy-done.1, bf16[2,16,3,128,128]{4,3,2,1,0:T(8,128)(2,1)S(1)} %copy-done, bf16[1168,128]{1,0:T(8,128)(2,1)S(1)} %collective-permute-done.refs_4_, ...), custom_call_target="tpu_custom_call" | custom-call | tf_op jit(solution)/shard_map/pallas_call | solution.py:264
  35.2 3.7 %collective-permute-start.18 = (bf16[64,2048]{1,0:T(8,128)(2,1)S(1)}, bf16[64,2048]{1,0:T(8,128)(2,1)S(1)}, u32[]{:S(2)}, u32[]{:S(2)}) collective-permute-start(bf16[64,2048]{1,0:T(8,128)(2,1)S(1)} %get-tuple-element.99), channel_id=1, source_target_pairs={{0,8},{1,9},{2,10},{3,11},{4,12},{5,13},{6,14},{7,15},{8,16},{9,17... | collective-permute-start | bytes 786440 | tf_op jit(solution)/shard_map/ppermute | solution.py:293
  39.4 1.7 %collective-permute-start.19 = (bf16[64,768]{1,0:T(8,128)(2,1)S(1)}, bf16[64,768]{1,0:T(8,128)(2,1)S(1)}, u32[]{:S(2)}, u32[]{:S(2)}) collective-permute-start(bf16[64,768]{1,0:T(8,128)(2,1)S(1)} %get-tuple-element.148), channel_id=1, source_target_pairs={{0,7},{1,2},{2,1},{3,4},{4,3},{5,6},{6,5},{7,0},{8,15},{9,10},{10,... | collective-permute-start | bytes 294920 | tf_op jit(solution)/shard_map/ppermute | solution.py:170
  41.4 1.5 %shard_map.53 = (bf16[64,2048]{1,0:T(8,128)(2,1)S(1)}, bf16[64,2048]{1,0:T(8,128)(2,1)S(1)}) custom-call(s32[2]{0:T(128)S(1)} %pad_add_fusion.refs_0_, s32[2,3]{1,0:T(2,128)S(1)} %copy-done.2, bf16[2,2048]{1,0:T(2,128)(2,1)S(1)} %copy-done.1, bf16[2,16,3,128,128]{4,3,2,1,0:T(8,128)(2,1)S(1)} %copy-done, bf16[1168,128]{1,0:T(8,128)(2,1)S(1)} %collective-permute-done.refs_4_, ...), custom_call_target="tpu_custom_call" | custom-call | tf_op jit(solution)/shard_map/pallas_call | solution.py:264
  43.0 2.7 %collective-permute-start.22 = (bf16[64,2048]{1,0:T(8,128)(2,1)S(1)}, bf16[64,2048]{1,0:T(8,128)(2,1)S(1)}, u32[]{:S(2)}, u32[]{:S(2)}) collective-permute-start(bf16[64,2048]{1,0:T(8,128)(2,1)S(1)} %get-tuple-element.103), channel_id=1, source_target_pairs={{0,8},{1,9},{2,10},{3,11},{4,12},{5,13},{6,14},{7,15},{8,16},{9,17... | collective-permute-start | bytes 786440 | tf_op jit(solution)/shard_map/ppermute | solution.py:293
  45.6 1.0 collective-permute-done.18
  46.7 1.6 %collective-permute-start.21 = (bf16[64,768]{1,0:T(8,128)(2,1)S(1)}, bf16[64,768]{1,0:T(8,128)(2,1)S(1)}, u32[]{:S(2)}, u32[]{:S(2)}) collective-permute-start(bf16[64,768]{1,0:T(8,128)(2,1)S(1)} %get-tuple-element.145), channel_id=1, source_target_pairs={{0,7},{1,2},{2,1},{3,4},{4,3},{5,6},{6,5},{7,0},{8,15},{9,10},{10,... | collective-permute-start | bytes 294920 | tf_op jit(solution)/shard_map/ppermute | solution.py:170
  48.3 1.0 collective-permute-start.20
  49.3 1.6 %shard_map.54 = bf16[64,2048]{1,0:T(8,128)(2,1)S(1)} custom-call(s32[2]{0:T(128)S(1)} %pad_add_fusion.refs_0_, s32[2,3]{1,0:T(2,128)S(1)} %copy-done.2, bf16[2,2048]{1,0:T(2,128)(2,1)S(1)} %copy-done.1, bf16[2,16,3,128,128]{4,3,2,1,0:T(8,128)(2,1)S(1)} %copy-done, bf16[1168,128]{1,0:T(8,128)(2,1)S(1)} %collective-permute-done.refs_4_, ...), custom_call_target="tpu_custom_call" | custom-call | tf_op jit(solution)/shard_map/pallas_call | solution.py:264
  51.0 1.4 %collective-permute-done.22.refs_6_ = bf16[64,2048]{1,0:T(8,128)(2,1)S(1)} collective-permute-done((bf16[64,2048]{1,0:T(8,128)(2,1)S(1)}, bf16[64,2048]{1,0:T(8,128)(2,1)S(1)}, u32[]{:S(2)}, u32[]{:S(2)}) %collective-permute-start.22) | collective-permute-done | bytes 262176 | tf_op jit(solution)/shard_map/ppermute | solution.py:293
  52.5 1.6 %collective-permute-start.26 = (bf16[64,768]{1,0:T(8,128)(2,1)S(1)}, bf16[64,768]{1,0:T(8,128)(2,1)S(1)}, u32[]{:S(2)}, u32[]{:S(2)}) collective-permute-start(bf16[64,768]{1,0:T(8,128)(2,1)S(1)} %get-tuple-element.144), channel_id=1, source_target_pairs={{0,1},{1,0},{2,3},{3,2},{4,5},{5,4},{6,7},{7,6},{8,15},{9,10},{10,... | collective-permute-start | bytes 294920 | tf_op jit(solution)/shard_map/ppermute | solution.py:170
  54.7 1.6 %shard_map.55 = bf16[64,2048]{1,0:T(8,128)(2,1)S(1)} custom-call(s32[2]{0:T(128)S(1)} %pad_add_fusion.refs_0_, s32[2,3]{1,0:T(2,128)S(1)} %copy-done.2, bf16[2,2048]{1,0:T(2,128)(2,1)S(1)} %copy-done.1, bf16[2,16,3,128,128]{4,3,2,1,0:T(8,128)(2,1)S(1)} %copy-done, bf16[1168,128]{1,0:T(8,128)(2,1)S(1)} %collective-permute-done.refs_4_, ...), custom_call_target="tpu_custom_call" | custom-call | tf_op jit(solution)/shard_map/pallas_call | solution.py:264
  56.4 2.1 %collective-permute-done.26.refs_8_ = bf16[64,768]{1,0:T(8,128)(2,1)S(1)} collective-permute-done((bf16[64,768]{1,0:T(8,128)(2,1)S(1)}, bf16[64,768]{1,0:T(8,128)(2,1)S(1)}, u32[]{:S(2)}, u32[]{:S(2)}) %collective-permute-start.26) | collective-permute-done | bytes 98336 | tf_op jit(solution)/shard_map/ppermute | solution.py:170
  58.5 0.9 collective-permute-done.27.refs_6_
  60.3 1.8 %shard_map.56 = bf16[64,2048]{1,0:T(8,128)(2,1)S(1)} custom-call(s32[2]{0:T(128)S(1)} %pad_add_fusion.refs_0_, s32[2,3]{1,0:T(2,128)S(1)} %copy-done.2, bf16[2,2048]{1,0:T(2,128)(2,1)S(1)} %copy-done.1, bf16[2,16,3,128,128]{4,3,2,1,0:T(8,128)(2,1)S(1)} %copy-done, bf16[1168,128]{1,0:T(8,128)(2,1)S(1)} %collective-permute-done.refs_4_, ...), custom_call_target="tpu_custom_call" | custom-call | tf_op jit(solution)/shard_map/pallas_call | solution.py:264
  62.2 2.6 %collective-permute-done.24.refs_6_ = bf16[64,2048]{1,0:T(8,128)(2,1)S(1)} collective-permute-done((bf16[64,2048]{1,0:T(8,128)(2,1)S(1)}, bf16[64,2048]{1,0:T(8,128)(2,1)S(1)}, u32[]{:S(2)}, u32[]{:S(2)}) %collective-permute-start.24) | collective-permute-done | bytes 262176 | tf_op jit(solution)/shard_map/ppermute | solution.py:293
  64.8 0.9 collective-permute-start.30
  65.8 1.6 %shard_map.57 = bf16[64,2048]{1,0:T(8,128)(2,1)S(1)} custom-call(s32[2]{0:T(128)S(1)} %pad_add_fusion.refs_0_, s32[2,3]{1,0:T(2,128)S(1)} %copy-done.2, bf16[2,2048]{1,0:T(2,128)(2,1)S(1)} %copy-done.1, bf16[2,16,3,128,128]{4,3,2,1,0:T(8,128)(2,1)S(1)} %copy-done, bf16[1168,128]{1,0:T(8,128)(2,1)S(1)} %collective-permute-done.refs_4_, ...), custom_call_target="tpu_custom_call" | custom-call | tf_op jit(solution)/shard_map/pallas_call | solution.py:264
  67.4 1.2 %collective-permute-start.36 = (bf16[64,2048]{1,0:T(8,128)(2,1)S(1)}, bf16[64,2048]{1,0:T(8,128)(2,1)S(1)}, u32[]{:S(2)}, u32[]{:S(2)}) collective-permute-start(bf16[64,2048]{1,0:T(8,128)(2,1)S(1)} %shard_map.57), channel_id=1, source_target_pairs={{8,16},{9,17},{10,18},{11,19},{12,20},{13,21},{14,22},{15,23},{16,... | collective-permute-start | bytes 786440 | tf_op jit(solution)/shard_map/ppermute | solution.py:293
  68.6 1.3 %collective-permute-done.30.refs_8_ = bf16[64,768]{1,0:T(8,128)(2,1)S(1)} collective-permute-done((bf16[64,768]{1,0:T(8,128)(2,1)S(1)}, bf16[64,768]{1,0:T(8,128)(2,1)S(1)}, u32[]{:S(2)}, u32[]{:S(2)}) %collective-permute-start.30) | collective-permute-done | bytes 98336 | tf_op jit(solution)/shard_map/ppermute | solution.py:170
  69.9 0.9 collective-permute-done.31.refs_6_
  71.9 1.6 %shard_map.58 = bf16[64,2048]{1,0:T(8,128)(2,1)S(1)} custom-call(s32[2]{0:T(128)S(1)} %pad_add_fusion.refs_0_, s32[2,3]{1,0:T(2,128)S(1)} %copy-done.2, bf16[2,2048]{1,0:T(2,128)(2,1)S(1)} %copy-done.1, bf16[2,16,3,128,128]{4,3,2,1,0:T(8,128)(2,1)S(1)} %copy-done, bf16[1168,128]{1,0:T(8,128)(2,1)S(1)} %collective-permute-done.refs_4_, ...), custom_call_target="tpu_custom_call" | custom-call | tf_op jit(solution)/shard_map/pallas_call | solution.py:264
  73.5 1.6 %collective-permute-start.33 = (bf16[64,2048]{1,0:T(8,128)(2,1)S(1)}, bf16[64,2048]{1,0:T(8,128)(2,1)S(1)}, u32[]{:S(2)}, u32[]{:S(2)}) collective-permute-start(bf16[64,2048]{1,0:T(8,128)(2,1)S(1)} %shard_map.58), channel_id=1, source_target_pairs={{8,16},{9,17},{10,18},{11,19},{12,20},{13,21},{14,22},{15,23},{16,... | collective-permute-start | bytes 786440 | tf_op jit(solution)/shard_map/ppermute | solution.py:293
  75.1 1.2 %collective-permute-done.36.refs_6_ = bf16[64,2048]{1,0:T(8,128)(2,1)S(1)} collective-permute-done((bf16[64,2048]{1,0:T(8,128)(2,1)S(1)}, bf16[64,2048]{1,0:T(8,128)(2,1)S(1)}, u32[]{:S(2)}, u32[]{:S(2)}) %collective-permute-start.36) | collective-permute-done | bytes 262176 | tf_op jit(solution)/shard_map/ppermute | solution.py:293
  77.6 1.6 %shard_map.59 = bf16[64,2048]{1,0:T(8,128)(2,1)S(1)} custom-call(s32[2]{0:T(128)S(1)} %pad_add_fusion.refs_0_, s32[2,3]{1,0:T(2,128)S(1)} %copy-done.2, bf16[2,2048]{1,0:T(2,128)(2,1)S(1)} %copy-done.1, bf16[2,16,3,128,128]{4,3,2,1,0:T(8,128)(2,1)S(1)} %copy-done, bf16[1168,128]{1,0:T(8,128)(2,1)S(1)} %collective-permute-done.refs_4_, ...), custom_call_target="tpu_custom_call" | custom-call | tf_op jit(solution)/shard_map/pallas_call | solution.py:264
  79.2 1.5 %collective-permute-start.40 = (bf16[64,2048]{1,0:T(8,128)(2,1)S(1)}, bf16[64,2048]{1,0:T(8,128)(2,1)S(1)}, u32[]{:S(2)}, u32[]{:S(2)}) collective-permute-start(bf16[64,2048]{1,0:T(8,128)(2,1)S(1)} %shard_map.59), channel_id=1, source_target_pairs={{16,24},{17,25},{18,26},{19,27},{20,28},{21,29},{22,30},{23,31},{2... | collective-permute-start | bytes 786440 | tf_op jit(solution)/shard_map/ppermute | solution.py:293
  80.7 1.2 %collective-permute-done.37.refs_8_ = bf16[64,768]{1,0:T(8,128)(2,1)S(1)} collective-permute-done((bf16[64,768]{1,0:T(8,128)(2,1)S(1)}, bf16[64,768]{1,0:T(8,128)(2,1)S(1)}, u32[]{:S(2)}, u32[]{:S(2)}) %collective-permute-start.37) | collective-permute-done | bytes 98336 | tf_op jit(solution)/shard_map/ppermute | solution.py:170
  81.9 2.3 %collective-permute-start.39 = (bf16[64,768]{1,0:T(8,128)(2,1)S(1)}, bf16[64,768]{1,0:T(8,128)(2,1)S(1)}, u32[]{:S(2)}, u32[]{:S(2)}) collective-permute-start(bf16[64,768]{1,0:T(8,128)(2,1)S(1)} %get-tuple-element.133), channel_id=1, source_target_pairs={{0,1},{1,0},{2,3},{3,2},{4,5},{5,4},{6,7},{7,6},{8,9},{9,8},{10,11... | collective-permute-start | bytes 294920 | tf_op jit(solution)/shard_map/ppermute | solution.py:170
  84.8 1.6 %shard_map.60 = bf16[64,2048]{1,0:T(8,128)(2,1)S(1)} custom-call(s32[2]{0:T(128)S(1)} %pad_add_fusion.refs_0_, s32[2,3]{1,0:T(2,128)S(1)} %copy-done.2, bf16[2,2048]{1,0:T(2,128)(2,1)S(1)} %copy-done.1, bf16[2,16,3,128,128]{4,3,2,1,0:T(8,128)(2,1)S(1)} %copy-done, bf16[1168,128]{1,0:T(8,128)(2,1)S(1)} %collective-permute-done.refs_4_, ...), custom_call_target="tpu_custom_call" | custom-call | tf_op jit(solution)/shard_map/pallas_call | solution.py:264
  86.5 1.2 %collective-permute-done.40.refs_6_ = bf16[64,2048]{1,0:T(8,128)(2,1)S(1)} collective-permute-done((bf16[64,2048]{1,0:T(8,128)(2,1)S(1)}, bf16[64,2048]{1,0:T(8,128)(2,1)S(1)}, u32[]{:S(2)}, u32[]{:S(2)}) %collective-permute-start.40) | collective-permute-done | bytes 262176 | tf_op jit(solution)/shard_map/ppermute | solution.py:293
  88.2 1.6 %shard_map.61 = bf16[64,2048]{1,0:T(8,128)(2,1)S(1)} custom-call(s32[2]{0:T(128)S(1)} %pad_add_fusion.refs_0_, s32[2,3]{1,0:T(2,128)S(1)} %copy-done.2, bf16[2,2048]{1,0:T(2,128)(2,1)S(1)} %copy-done.1, bf16[2,16,3,128,128]{4,3,2,1,0:T(8,128)(2,1)S(1)} %copy-done, bf16[1168,128]{1,0:T(8,128)(2,1)S(1)} %collective-permute-done.refs_4_, ...), custom_call_target="tpu_custom_call" | custom-call | tf_op jit(solution)/shard_map/pallas_call | solution.py:264
  89.8 2.0 %collective-permute-start.42 = (bf16[64,2048]{1,0:T(8,128)(2,1)S(1)}, bf16[64,2048]{1,0:T(8,128)(2,1)S(1)}, u32[]{:S(2)}, u32[]{:S(2)}) collective-permute-start(bf16[64,2048]{1,0:T(8,128)(2,1)S(1)} %shard_map.61), channel_id=1, source_target_pairs={{16,24},{17,25},{18,26},{19,27},{20,28},{21,29},{22,30},{23,31},{2... | collective-permute-start | bytes 786440 | tf_op jit(solution)/shard_map/ppermute | solution.py:293
  91.7 3.0 %collective-permute-done.45.refs_6_ = bf16[64,2048]{1,0:T(8,128)(2,1)S(1)} collective-permute-done((bf16[64,2048]{1,0:T(8,128)(2,1)S(1)}, bf16[64,2048]{1,0:T(8,128)(2,1)S(1)}, u32[]{:S(2)}, u32[]{:S(2)}) %collective-permute-start.45) | collective-permute-done | bytes 262176 | tf_op jit(solution)/shard_map/ppermute | solution.py:293
  95.9 2.6 %collective-permute-start.48 = (bf16[64,2048]{1,0:T(8,128)(2,1)S(1)}, bf16[64,2048]{1,0:T(8,128)(2,1)S(1)}, u32[]{:S(2)}, u32[]{:S(2)}) collective-permute-start(bf16[64,2048]{1,0:T(8,128)(2,1)S(1)} %shard_map.62), channel_id=1, source_target_pairs={{24,16},{25,17},{26,18},{27,19},{28,20},{29,21},{30,22},{31,23},{1... | collective-permute-start | bytes 786440 | tf_op jit(solution)/shard_map/ppermute | solution.py:293
  98.5 1.6 %collective-permute-done.42.refs_6_ = bf16[64,2048]{1,0:T(8,128)(2,1)S(1)} collective-permute-done((bf16[64,2048]{1,0:T(8,128)(2,1)S(1)}, bf16[64,2048]{1,0:T(8,128)(2,1)S(1)}, u32[]{:S(2)}, u32[]{:S(2)}) %collective-permute-start.42) | collective-permute-done | bytes 262176 | tf_op jit(solution)/shard_map/ppermute | solution.py:293
  101.6 3.7 %collective-permute-done.48 = bf16[64,2048]{1,0:T(8,128)(2,1)S(1)} collective-permute-done((bf16[64,2048]{1,0:T(8,128)(2,1)S(1)}, bf16[64,2048]{1,0:T(8,128)(2,1)S(1)}, u32[]{:S(2)}, u32[]{:S(2)}) %collective-permute-start.48) | collective-permute-done | bytes 262176 | tf_op jit(solution)/shard_map/ppermute | solution.py:293
  105.4 1.4 %shard_map.64 = bf16[2,64,2048]{2,1,0:T(8,128)(2,1)} custom-call(s32[2]{0:T(128)S(1)} %pad_add_fusion.refs_0_, s32[2,3]{1,0:T(2,128)S(1)} %copy-done.2, bf16[2,2048]{1,0:T(2,128)(2,1)S(1)} %copy-done.1, bf16[2,16,3,128,128]{4,3,2,1,0:T(8,128)(2,1)S(1)} %copy-done, bf16[1168,128]{1,0:T(8,128)(2,1)S(1)} %collective-permute-done.refs_4_, ...), custom_call_target="tpu_custom_call" | custom-call | tf_op jit(solution)/shard_map/pallas_call | solution.py:264
  (102 shorter events, 13.7 us)
Async XLA Ops:
  1.7 10.3 %collective-permute-start.1 = (bf16[1168,128]{1,0:T(8,128)(2,1)S(1)}, bf16[1168,128]{1,0:T(8,128)(2,1)S(1)}, u32[]{:S(2)}, u32[]{:S(2)}) collective-permute-start(bf16[1168,128]{1,0:T(8,128)(2,1)S(1)} %shard_map.46), channel_id=1, source_target_pairs={{0,7},{1,2},{2,1},{3,4},{4,3},{5,6},{6,5},{7,0},{8,15},{9,10},{10,... | collective-permute-start | bytes 897032 | tf_op jit(solution)/shard_map/ppermute | solution.py:170
  5.6 6.3 %collective-permute-start = (bf16[1168,128]{1,0:T(8,128)(2,1)S(1)}, bf16[1168,128]{1,0:T(8,128)(2,1)S(1)}, u32[]{:S(2)}, u32[]{:S(2)}) collective-permute-start(bf16[1168,128]{1,0:T(8,128)(2,1)S(1)} %get-tuple-element.72), channel_id=1, source_target_pairs={{0,1},{1,0},{2,3},{3,2},{4,5},{5,4},{6,7},{7,6},{8,9},{9,8},{10,11... | collective-permute-start | bytes 897032 | tf_op jit(solution)/shard_map/ppermute | solution.py:162
  5.7 1.7 %collective-permute-start.4 = (bf16[64,768]{1,0:T(8,128)(2,1)S(1)}, bf16[64,768]{1,0:T(8,128)(2,1)S(1)}, u32[]{:S(2)}, u32[]{:S(2)}) collective-permute-start(bf16[64,768]{1,0:T(8,128)(2,1)S(1)} %get-tuple-element.79), channel_id=1, source_target_pairs={{0,1},{1,0},{2,3},{3,2},{4,5},{5,4},{6,7},{7,6},{8,9},{9,8},{10,11... | collective-permute-start | bytes 294920 | tf_op jit(solution)/shard_map/ppermute | solution.py:162
  6.2 7.3 %collective-permute-start.3 = (bf16[64,768]{1,0:T(8,128)(2,1)S(1)}, bf16[64,768]{1,0:T(8,128)(2,1)S(1)}, u32[]{:S(2)}, u32[]{:S(2)}) collective-permute-start(bf16[64,768]{1,0:T(8,128)(2,1)S(1)} %get-tuple-element.76), channel_id=1, source_target_pairs={{0,7},{1,2},{2,1},{3,4},{4,3},{5,6},{6,5},{7,0},{8,9},{9,8},{10,11... | collective-permute-start | bytes 294920 | tf_op jit(solution)/shard_map/ppermute | solution.py:170
  7.4 6.8 %collective-permute-start.2 = (bf16[64,768]{1,0:T(8,128)(2,1)S(1)}, bf16[64,768]{1,0:T(8,128)(2,1)S(1)}, u32[]{:S(2)}, u32[]{:S(2)}) collective-permute-start(bf16[64,768]{1,0:T(8,128)(2,1)S(1)} %get-tuple-element.75), channel_id=1, source_target_pairs={{0,1},{1,0},{2,3},{3,2},{4,5},{5,4},{6,7},{7,6},{8,9},{9,8},{10,11... | collective-permute-start | bytes 294920 | tf_op jit(solution)/shard_map/ppermute | solution.py:162
  13.5 4.6 %collective-permute-start.6 = (bf16[64,2048]{1,0:T(8,128)(2,1)S(1)}, bf16[64,2048]{1,0:T(8,128)(2,1)S(1)}, u32[]{:S(2)}, u32[]{:S(2)}) collective-permute-start(bf16[64,2048]{1,0:T(8,128)(2,1)S(1)} %get-tuple-element.83), channel_id=1, source_target_pairs={{0,8},{1,9},{2,10},{3,11},{4,12},{5,13},{6,14},{7,15},{8,0},{9,1},... | collective-permute-start | bytes 786440 | tf_op jit(solution)/shard_map/ppermute | solution.py:293
  13.6 4.5 %collective-permute-start.7 = (bf16[64,768]{1,0:T(8,128)(2,1)S(1)}, bf16[64,768]{1,0:T(8,128)(2,1)S(1)}, u32[]{:S(2)}, u32[]{:S(2)}) collective-permute-start(bf16[64,768]{1,0:T(8,128)(2,1)S(1)} %get-tuple-element.156), channel_id=1, source_target_pairs={{0,7},{1,2},{2,1},{3,4},{4,3},{5,6},{6,5},{7,0},{8,9},{9,8},{10,11... | collective-permute-start | bytes 294920 | tf_op jit(solution)/shard_map/ppermute | solution.py:170
  14.1 4.6 %collective-permute-start.10 = (bf16[64,768]{1,0:T(8,128)(2,1)S(1)}, bf16[64,768]{1,0:T(8,128)(2,1)S(1)}, u32[]{:S(2)}, u32[]{:S(2)}) collective-permute-start(bf16[64,768]{1,0:T(8,128)(2,1)S(1)} %get-tuple-element.155), channel_id=1, source_target_pairs={{0,1},{1,0},{2,3},{3,2},{4,5},{5,4},{6,7},{7,6},{8,9},{9,8},{10,11... | collective-permute-start | bytes 294920 | tf_op jit(solution)/shard_map/ppermute | solution.py:162
  15.7 6.5 %collective-permute-start.11 = (bf16[64,2048]{1,0:T(8,128)(2,1)S(1)}, bf16[64,2048]{1,0:T(8,128)(2,1)S(1)}, u32[]{:S(2)}, u32[]{:S(2)}) collective-permute-start(bf16[64,2048]{1,0:T(8,128)(2,1)S(1)} %get-tuple-element.87), channel_id=1, source_target_pairs={{0,8},{1,9},{2,10},{3,11},{4,12},{5,13},{6,14},{7,15},{16,17},{17,... | collective-permute-start | bytes 786440 | tf_op jit(solution)/shard_map/ppermute | solution.py:293
  18.2 4.1 %collective-permute-start.9 = (bf16[64,768]{1,0:T(8,128)(2,1)S(1)}, bf16[64,768]{1,0:T(8,128)(2,1)S(1)}, u32[]{:S(2)}, u32[]{:S(2)}) collective-permute-start(bf16[64,768]{1,0:T(8,128)(2,1)S(1)} %get-tuple-element.153), channel_id=1, source_target_pairs={{0,7},{1,2},{2,1},{3,4},{4,3},{5,6},{6,5},{7,0},{8,15},{9,10},{10,... | collective-permute-start | bytes 294920 | tf_op jit(solution)/shard_map/ppermute | solution.py:170
  18.3 4.6 %collective-permute-start.8 = (bf16[64,768]{1,0:T(8,128)(2,1)S(1)}, bf16[64,768]{1,0:T(8,128)(2,1)S(1)}, u32[]{:S(2)}, u32[]{:S(2)}) collective-permute-start(bf16[64,768]{1,0:T(8,128)(2,1)S(1)} %get-tuple-element.154), channel_id=1, source_target_pairs={{0,1},{1,0},{2,3},{3,2},{4,5},{5,4},{6,7},{7,6},{8,9},{9,8},{10,11... | collective-permute-start | bytes 294920 | tf_op jit(solution)/shard_map/ppermute | solution.py:162
  20.3 12.8 %collective-permute-start.12 = (bf16[64,2048]{1,0:T(8,128)(2,1)S(1)}, bf16[64,2048]{1,0:T(8,128)(2,1)S(1)}, u32[]{:S(2)}, u32[]{:S(2)}) collective-permute-start(bf16[64,2048]{1,0:T(8,128)(2,1)S(1)} %get-tuple-element.91), channel_id=1, source_target_pairs={{0,8},{1,9},{2,10},{3,11},{4,12},{5,13},{6,14},{7,15},{16,17},{17,... | collective-permute-start | bytes 786440 | tf_op jit(solution)/shard_map/ppermute | solution.py:293
  22.3 10.7 %collective-permute-start.13 = (bf16[64,768]{1,0:T(8,128)(2,1)S(1)}, bf16[64,768]{1,0:T(8,128)(2,1)S(1)}, u32[]{:S(2)}, u32[]{:S(2)}) collective-permute-start(bf16[64,768]{1,0:T(8,128)(2,1)S(1)} %get-tuple-element.152), channel_id=1, source_target_pairs={{0,7},{1,2},{2,1},{3,4},{4,3},{5,6},{6,5},{7,0},{8,15},{9,10},{10,... | collective-permute-start | bytes 294920 | tf_op jit(solution)/shard_map/ppermute | solution.py:170
  22.8 10.9 %collective-permute-start.16 = (bf16[64,768]{1,0:T(8,128)(2,1)S(1)}, bf16[64,768]{1,0:T(8,128)(2,1)S(1)}, u32[]{:S(2)}, u32[]{:S(2)}) collective-permute-start(bf16[64,768]{1,0:T(8,128)(2,1)S(1)} %get-tuple-element.151), channel_id=1, source_target_pairs={{0,1},{1,0},{2,3},{3,2},{4,5},{5,4},{6,7},{7,6},{8,9},{9,8},{10,11... | collective-permute-start | bytes 294920 | tf_op jit(solution)/shard_map/ppermute | solution.py:162
  24.4 14.9 %collective-permute-start.17 = (bf16[64,2048]{1,0:T(8,128)(2,1)S(1)}, bf16[64,2048]{1,0:T(8,128)(2,1)S(1)}, u32[]{:S(2)}, u32[]{:S(2)}) collective-permute-start(bf16[64,2048]{1,0:T(8,128)(2,1)S(1)} %get-tuple-element.95), channel_id=1, source_target_pairs={{0,8},{1,9},{2,10},{3,11},{4,12},{5,13},{6,14},{7,15},{8,16},{9,17... | collective-permute-start | bytes 786440 | tf_op jit(solution)/shard_map/ppermute | solution.py:293
  33.1 6.2 %collective-permute-start.15 = (bf16[64,768]{1,0:T(8,128)(2,1)S(1)}, bf16[64,768]{1,0:T(8,128)(2,1)S(1)}, u32[]{:S(2)}, u32[]{:S(2)}) collective-permute-start(bf16[64,768]{1,0:T(8,128)(2,1)S(1)} %get-tuple-element.149), channel_id=1, source_target_pairs={{0,7},{1,2},{2,1},{3,4},{4,3},{5,6},{6,5},{7,0},{8,15},{9,10},{10,... | collective-permute-start | bytes 294920 | tf_op jit(solution)/shard_map/ppermute | solution.py:170
  33.4 8.0 %collective-permute-start.14 = (bf16[64,768]{1,0:T(8,128)(2,1)S(1)}, bf16[64,768]{1,0:T(8,128)(2,1)S(1)}, u32[]{:S(2)}, u32[]{:S(2)}) collective-permute-start(bf16[64,768]{1,0:T(8,128)(2,1)S(1)} %get-tuple-element.150), channel_id=1, source_target_pairs={{0,1},{1,0},{2,3},{3,2},{4,5},{5,4},{6,7},{7,6},{8,9},{9,8},{10,11... | collective-permute-start | bytes 294920 | tf_op jit(solution)/shard_map/ppermute | solution.py:162
  35.2 11.4 %collective-permute-start.18 = (bf16[64,2048]{1,0:T(8,128)(2,1)S(1)}, bf16[64,2048]{1,0:T(8,128)(2,1)S(1)}, u32[]{:S(2)}, u32[]{:S(2)}) collective-permute-start(bf16[64,2048]{1,0:T(8,128)(2,1)S(1)} %get-tuple-element.99), channel_id=1, source_target_pairs={{0,8},{1,9},{2,10},{3,11},{4,12},{5,13},{6,14},{7,15},{8,16},{9,17... | collective-permute-start | bytes 786440 | tf_op jit(solution)/shard_map/ppermute | solution.py:293
  39.4 6.3 %collective-permute-start.19 = (bf16[64,768]{1,0:T(8,128)(2,1)S(1)}, bf16[64,768]{1,0:T(8,128)(2,1)S(1)}, u32[]{:S(2)}, u32[]{:S(2)}) collective-permute-start(bf16[64,768]{1,0:T(8,128)(2,1)S(1)} %get-tuple-element.148), channel_id=1, source_target_pairs={{0,7},{1,2},{2,1},{3,4},{4,3},{5,6},{6,5},{7,0},{8,15},{9,10},{10,... | collective-permute-start | bytes 294920 | tf_op jit(solution)/shard_map/ppermute | solution.py:170
  41.1 8.2 %collective-permute-start.23 = (bf16[64,768]{1,0:T(8,128)(2,1)S(1)}, bf16[64,768]{1,0:T(8,128)(2,1)S(1)}, u32[]{:S(2)}, u32[]{:S(2)}) collective-permute-start(bf16[64,768]{1,0:T(8,128)(2,1)S(1)} %get-tuple-element.147), channel_id=1, source_target_pairs={{0,1},{1,0},{2,3},{3,2},{4,5},{5,4},{6,7},{7,6},{8,9},{9,8},{10,11... | collective-permute-start | bytes 294920 | tf_op jit(solution)/shard_map/ppermute | solution.py:162
  43.0 9.4 %collective-permute-start.22 = (bf16[64,2048]{1,0:T(8,128)(2,1)S(1)}, bf16[64,2048]{1,0:T(8,128)(2,1)S(1)}, u32[]{:S(2)}, u32[]{:S(2)}) collective-permute-start(bf16[64,2048]{1,0:T(8,128)(2,1)S(1)} %get-tuple-element.103), channel_id=1, source_target_pairs={{0,8},{1,9},{2,10},{3,11},{4,12},{5,13},{6,14},{7,15},{8,16},{9,17... | collective-permute-start | bytes 786440 | tf_op jit(solution)/shard_map/ppermute | solution.py:293
  46.7 5.8 %collective-permute-start.21 = (bf16[64,768]{1,0:T(8,128)(2,1)S(1)}, bf16[64,768]{1,0:T(8,128)(2,1)S(1)}, u32[]{:S(2)}, u32[]{:S(2)}) collective-permute-start(bf16[64,768]{1,0:T(8,128)(2,1)S(1)} %get-tuple-element.145), channel_id=1, source_target_pairs={{0,7},{1,2},{2,1},{3,4},{4,3},{5,6},{6,5},{7,0},{8,15},{9,10},{10,... | collective-permute-start | bytes 294920 | tf_op jit(solution)/shard_map/ppermute | solution.py:170
  48.3 6.4 %collective-permute-start.20 = (bf16[64,768]{1,0:T(8,128)(2,1)S(1)}, bf16[64,768]{1,0:T(8,128)(2,1)S(1)}, u32[]{:S(2)}, u32[]{:S(2)}) collective-permute-start(bf16[64,768]{1,0:T(8,128)(2,1)S(1)} %get-tuple-element.146), channel_id=1, source_target_pairs={{0,1},{1,0},{2,3},{3,2},{4,5},{5,4},{6,7},{7,6},{8,9},{9,8},{10,11... | collective-permute-start | bytes 294920 | tf_op jit(solution)/shard_map/ppermute | solution.py:162
  50.9 8.4 %collective-permute-start.27 = (bf16[64,2048]{1,0:T(8,128)(2,1)S(1)}, bf16[64,2048]{1,0:T(8,128)(2,1)S(1)}, u32[]{:S(2)}, u32[]{:S(2)}) collective-permute-start(bf16[64,2048]{1,0:T(8,128)(2,1)S(1)} %shard_map.54), channel_id=1, source_target_pairs={{0,8},{1,9},{2,10},{3,11},{4,12},{5,13},{6,14},{7,15},{8,16},{9,17... | collective-permute-start | bytes 786440 | tf_op jit(solution)/shard_map/ppermute | solution.py:293
  52.5 5.9 %collective-permute-start.26 = (bf16[64,768]{1,0:T(8,128)(2,1)S(1)}, bf16[64,768]{1,0:T(8,128)(2,1)S(1)}, u32[]{:S(2)}, u32[]{:S(2)}) collective-permute-start(bf16[64,768]{1,0:T(8,128)(2,1)S(1)} %get-tuple-element.144), channel_id=1, source_target_pairs={{0,1},{1,0},{2,3},{3,2},{4,5},{5,4},{6,7},{7,6},{8,15},{9,10},{10,... | collective-permute-start | bytes 294920 | tf_op jit(solution)/shard_map/ppermute | solution.py:170
  54.1 6.2 %collective-permute-start.25 = (bf16[64,768]{1,0:T(8,128)(2,1)S(1)}, bf16[64,768]{1,0:T(8,128)(2,1)S(1)}, u32[]{:S(2)}, u32[]{:S(2)}) collective-permute-start(bf16[64,768]{1,0:T(8,128)(2,1)S(1)} %get-tuple-element.143), channel_id=1, source_target_pairs={{0,1},{1,0},{2,3},{3,2},{4,5},{5,4},{6,7},{7,6},{8,9},{9,8},{10,11... | collective-permute-start | bytes 294920 | tf_op jit(solution)/shard_map/ppermute | solution.py:162
  56.3 8.5 %collective-permute-start.24 = (bf16[64,2048]{1,0:T(8,128)(2,1)S(1)}, bf16[64,2048]{1,0:T(8,128)(2,1)S(1)}, u32[]{:S(2)}, u32[]{:S(2)}) collective-permute-start(bf16[64,2048]{1,0:T(8,128)(2,1)S(1)} %shard_map.55), channel_id=1, source_target_pairs={{0,8},{1,9},{2,10},{3,11},{4,12},{5,13},{6,14},{7,15},{8,16},{9,17... | collective-permute-start | bytes 786440 | tf_op jit(solution)/shard_map/ppermute | solution.py:293
  59.4 5.5 %collective-permute-start.28 = (bf16[64,768]{1,0:T(8,128)(2,1)S(1)}, bf16[64,768]{1,0:T(8,128)(2,1)S(1)}, u32[]{:S(2)}, u32[]{:S(2)}) collective-permute-start(bf16[64,768]{1,0:T(8,128)(2,1)S(1)} %get-tuple-element.142), channel_id=1, source_target_pairs={{0,1},{1,0},{2,3},{3,2},{4,5},{5,4},{6,7},{7,6},{8,15},{9,10},{10,... | collective-permute-start | bytes 294920 | tf_op jit(solution)/shard_map/ppermute | solution.py:170
  60.1 5.7 %collective-permute-start.32 = (bf16[64,768]{1,0:T(8,128)(2,1)S(1)}, bf16[64,768]{1,0:T(8,128)(2,1)S(1)}, u32[]{:S(2)}, u32[]{:S(2)}) collective-permute-start(bf16[64,768]{1,0:T(8,128)(2,1)S(1)} %get-tuple-element.141), channel_id=1, source_target_pairs={{0,1},{1,0},{2,3},{3,2},{4,5},{5,4},{6,7},{7,6},{8,9},{9,8},{10,11... | collective-permute-start | bytes 294920 | tf_op jit(solution)/shard_map/ppermute | solution.py:162
  62.2 8.6 %collective-permute-start.31 = (bf16[64,2048]{1,0:T(8,128)(2,1)S(1)}, bf16[64,2048]{1,0:T(8,128)(2,1)S(1)}, u32[]{:S(2)}, u32[]{:S(2)}) collective-permute-start(bf16[64,2048]{1,0:T(8,128)(2,1)S(1)} %shard_map.56), channel_id=1, source_target_pairs={{8,16},{9,17},{10,18},{11,19},{12,20},{13,21},{14,22},{15,23},{16,... | collective-permute-start | bytes 786440 | tf_op jit(solution)/shard_map/ppermute | solution.py:293
  64.8 5.1 %collective-permute-start.30 = (bf16[64,768]{1,0:T(8,128)(2,1)S(1)}, bf16[64,768]{1,0:T(8,128)(2,1)S(1)}, u32[]{:S(2)}, u32[]{:S(2)}) collective-permute-start(bf16[64,768]{1,0:T(8,128)(2,1)S(1)} %get-tuple-element.139), channel_id=1, source_target_pairs={{0,1},{1,0},{2,3},{3,2},{4,5},{5,4},{6,7},{7,6},{8,15},{9,10},{10,... | collective-permute-start | bytes 294920 | tf_op jit(solution)/shard_map/ppermute | solution.py:170
  65.7 6.2 %collective-permute-start.29 = (bf16[64,768]{1,0:T(8,128)(2,1)S(1)}, bf16[64,768]{1,0:T(8,128)(2,1)S(1)}, u32[]{:S(2)}, u32[]{:S(2)}) collective-permute-start(bf16[64,768]{1,0:T(8,128)(2,1)S(1)} %get-tuple-element.140), channel_id=1, source_target_pairs={{0,1},{1,0},{2,3},{3,2},{4,5},{5,4},{6,7},{7,6},{8,9},{9,8},{10,11... | collective-permute-start | bytes 294920 | tf_op jit(solution)/shard_map/ppermute | solution.py:162
  67.4 8.9 %collective-permute-start.36 = (bf16[64,2048]{1,0:T(8,128)(2,1)S(1)}, bf16[64,2048]{1,0:T(8,128)(2,1)S(1)}, u32[]{:S(2)}, u32[]{:S(2)}) collective-permute-start(bf16[64,2048]{1,0:T(8,128)(2,1)S(1)} %shard_map.57), channel_id=1, source_target_pairs={{8,16},{9,17},{10,18},{11,19},{12,20},{13,21},{14,22},{15,23},{16,... | collective-permute-start | bytes 786440 | tf_op jit(solution)/shard_map/ppermute | solution.py:293
  70.8 5.7 %collective-permute-start.35 = (bf16[64,768]{1,0:T(8,128)(2,1)S(1)}, bf16[64,768]{1,0:T(8,128)(2,1)S(1)}, u32[]{:S(2)}, u32[]{:S(2)}) collective-permute-start(bf16[64,768]{1,0:T(8,128)(2,1)S(1)} %get-tuple-element.138), channel_id=1, source_target_pairs={{0,1},{1,0},{2,3},{3,2},{4,5},{5,4},{6,7},{7,6},{8,9},{9,8},{10,11... | collective-permute-start | bytes 294920 | tf_op jit(solution)/shard_map/ppermute | solution.py:170
  71.4 6.2 %collective-permute-start.34 = (bf16[64,768]{1,0:T(8,128)(2,1)S(1)}, bf16[64,768]{1,0:T(8,128)(2,1)S(1)}, u32[]{:S(2)}, u32[]{:S(2)}) collective-permute-start(bf16[64,768]{1,0:T(8,128)(2,1)S(1)} %get-tuple-element.137), channel_id=1, source_target_pairs={{0,1},{1,0},{2,3},{3,2},{4,5},{5,4},{6,7},{7,6},{8,9},{9,8},{10,11... | collective-permute-start | bytes 294920 | tf_op jit(solution)/shard_map/ppermute | solution.py:162
  73.5 8.4 %collective-permute-start.33 = (bf16[64,2048]{1,0:T(8,128)(2,1)S(1)}, bf16[64,2048]{1,0:T(8,128)(2,1)S(1)}, u32[]{:S(2)}, u32[]{:S(2)}) collective-permute-start(bf16[64,2048]{1,0:T(8,128)(2,1)S(1)} %shard_map.58), channel_id=1, source_target_pairs={{8,16},{9,17},{10,18},{11,19},{12,20},{13,21},{14,22},{15,23},{16,... | collective-permute-start | bytes 786440 | tf_op jit(solution)/shard_map/ppermute | solution.py:293
  76.5 5.4 %collective-permute-start.37 = (bf16[64,768]{1,0:T(8,128)(2,1)S(1)}, bf16[64,768]{1,0:T(8,128)(2,1)S(1)}, u32[]{:S(2)}, u32[]{:S(2)}) collective-permute-start(bf16[64,768]{1,0:T(8,128)(2,1)S(1)} %get-tuple-element.136), channel_id=1, source_target_pairs={{0,1},{1,0},{2,3},{3,2},{4,5},{5,4},{6,7},{7,6},{8,9},{9,8},{10,11... | collective-permute-start | bytes 294920 | tf_op jit(solution)/shard_map/ppermute | solution.py:170
  77.3 7.5 %collective-permute-start.41 = (bf16[64,768]{1,0:T(8,128)(2,1)S(1)}, bf16[64,768]{1,0:T(8,128)(2,1)S(1)}, u32[]{:S(2)}, u32[]{:S(2)}) collective-permute-start(bf16[64,768]{1,0:T(8,128)(2,1)S(1)} %get-tuple-element.135), channel_id=1, source_target_pairs={{0,1},{1,0},{2,3},{3,2},{4,5},{5,4},{6,7},{7,6},{8,9},{9,8},{10,11... | collective-permute-start | bytes 294920 | tf_op jit(solution)/shard_map/ppermute | solution.py:162
  79.2 8.5 %collective-permute-start.40 = (bf16[64,2048]{1,0:T(8,128)(2,1)S(1)}, bf16[64,2048]{1,0:T(8,128)(2,1)S(1)}, u32[]{:S(2)}, u32[]{:S(2)}) collective-permute-start(bf16[64,2048]{1,0:T(8,128)(2,1)S(1)} %shard_map.59), channel_id=1, source_target_pairs={{16,24},{17,25},{18,26},{19,27},{20,28},{21,29},{22,30},{23,31},{2... | collective-permute-start | bytes 786440 | tf_op jit(solution)/shard_map/ppermute | solution.py:293
  81.9 5.8 %collective-permute-start.39 = (bf16[64,768]{1,0:T(8,128)(2,1)S(1)}, bf16[64,768]{1,0:T(8,128)(2,1)S(1)}, u32[]{:S(2)}, u32[]{:S(2)}) collective-permute-start(bf16[64,768]{1,0:T(8,128)(2,1)S(1)} %get-tuple-element.133), channel_id=1, source_target_pairs={{0,1},{1,0},{2,3},{3,2},{4,5},{5,4},{6,7},{7,6},{8,9},{9,8},{10,11... | collective-permute-start | bytes 294920 | tf_op jit(solution)/shard_map/ppermute | solution.py:170
  84.2 4.0 %collective-permute-start.38 = (bf16[64,768]{1,0:T(8,128)(2,1)S(1)}, bf16[64,768]{1,0:T(8,128)(2,1)S(1)}, u32[]{:S(2)}, u32[]{:S(2)}) collective-permute-start(bf16[64,768]{1,0:T(8,128)(2,1)S(1)} %get-tuple-element.134), channel_id=1, source_target_pairs={{0,1},{1,0},{2,3},{3,2},{4,5},{5,4},{6,7},{7,6},{8,9},{9,8},{10,11... | collective-permute-start | bytes 294920 | tf_op jit(solution)/shard_map/ppermute | solution.py:162
  86.4 8.3 %collective-permute-start.45 = (bf16[64,2048]{1,0:T(8,128)(2,1)S(1)}, bf16[64,2048]{1,0:T(8,128)(2,1)S(1)}, u32[]{:S(2)}, u32[]{:S(2)}) collective-permute-start(bf16[64,2048]{1,0:T(8,128)(2,1)S(1)} %shard_map.60), channel_id=1, source_target_pairs={{16,24},{17,25},{18,26},{19,27},{20,28},{21,29},{22,30},{23,31},{2... | collective-permute-start | bytes 786440 | tf_op jit(solution)/shard_map/ppermute | solution.py:293
  87.7 4.0 %collective-permute-start.44 = (bf16[64,768]{1,0:T(8,128)(2,1)S(1)}, bf16[64,768]{1,0:T(8,128)(2,1)S(1)}, u32[]{:S(2)}, u32[]{:S(2)}) collective-permute-start(bf16[64,768]{1,0:T(8,128)(2,1)S(1)} %get-tuple-element.132), channel_id=1, source_target_pairs={{0,1},{1,0},{2,3},{3,2},{4,5},{5,4},{6,7},{7,6},{8,9},{9,8},{10,11... | collective-permute-start | bytes 294920 | tf_op jit(solution)/shard_map/ppermute | solution.py:170
  89.8 10.3 %collective-permute-start.42 = (bf16[64,2048]{1,0:T(8,128)(2,1)S(1)}, bf16[64,2048]{1,0:T(8,128)(2,1)S(1)}, u32[]{:S(2)}, u32[]{:S(2)}) collective-permute-start(bf16[64,2048]{1,0:T(8,128)(2,1)S(1)} %shard_map.61), channel_id=1, source_target_pairs={{16,24},{17,25},{18,26},{19,27},{20,28},{21,29},{22,30},{23,31},{2... | collective-permute-start | bytes 786440 | tf_op jit(solution)/shard_map/ppermute | solution.py:293
  91.7 3.6 %collective-permute-start.43 = (bf16[64,768]{1,0:T(8,128)(2,1)S(1)}, bf16[64,768]{1,0:T(8,128)(2,1)S(1)}, u32[]{:S(2)}, u32[]{:S(2)}) collective-permute-start(bf16[64,768]{1,0:T(8,128)(2,1)S(1)} %get-tuple-element.131), channel_id=1, source_target_pairs={{0,1},{1,0},{2,3},{3,2},{4,5},{5,4},{6,7},{7,6},{8,9},{9,8},{10,11... | collective-permute-start | bytes 294920 | tf_op jit(solution)/shard_map/ppermute | solution.py:162
  94.7 6.0 %collective-permute-start.49 = (bf16[64,768]{1,0:T(8,128)(2,1)S(1)}, bf16[64,768]{1,0:T(8,128)(2,1)S(1)}, u32[]{:S(2)}, u32[]{:S(2)}) collective-permute-start(bf16[64,768]{1,0:T(8,128)(2,1)S(1)} %get-tuple-element.129), channel_id=1, source_target_pairs={{0,1},{1,0},{2,3},{3,2},{4,5},{5,4},{6,7},{7,6},{8,9},{9,8},{10,11... | collective-permute-start | bytes 294920 | tf_op jit(solution)/shard_map/ppermute | solution.py:162
  94.8 5.9 %collective-permute-start.50 = (bf16[64,768]{1,0:T(8,128)(2,1)S(1)}, bf16[64,768]{1,0:T(8,128)(2,1)S(1)}, u32[]{:S(2)}, u32[]{:S(2)}) collective-permute-start(bf16[64,768]{1,0:T(8,128)(2,1)S(1)} %get-tuple-element.130), channel_id=1, source_target_pairs={{0,1},{1,0},{2,3},{3,2},{4,5},{5,4},{6,7},{7,6},{8,9},{9,8},{10,11... | collective-permute-start | bytes 294920 | tf_op jit(solution)/shard_map/ppermute | solution.py:170
  95.9 9.4 %collective-permute-start.48 = (bf16[64,2048]{1,0:T(8,128)(2,1)S(1)}, bf16[64,2048]{1,0:T(8,128)(2,1)S(1)}, u32[]{:S(2)}, u32[]{:S(2)}) collective-permute-start(bf16[64,2048]{1,0:T(8,128)(2,1)S(1)} %shard_map.62), channel_id=1, source_target_pairs={{24,16},{25,17},{26,18},{27,19},{28,20},{29,21},{30,22},{31,23},{1... | collective-permute-start | bytes 786440 | tf_op jit(solution)/shard_map/ppermute | solution.py:293
  (6 other events, 35.0 us)
